TPU v7x, 256 devices: a whole 4x4x8 slice. The times are simulated.
256 devices in a mesh: pipe: 4 (over x), sp: 64 (over y, z, core).
Axes of the slice: x: 4, y: 4, z: 8, core: 2. Of those that a mesh axis runs over, the one named last changes fastest.
Arguments:
- latent: bfloat16 [32, 64, 3072], P(None, 'sp'), may hold values from -6 to 6
- modulation: float32 [4, 3, 3072], P('pipe'), may hold values from 0.5 to 3
- w_qkv: bfloat16 [4, 3072, 9216], P('pipe', 'sp'), may hold values from -0.109375 to 0.109375
- w_out: bfloat16 [4, 3072, 3072], P('pipe', None, 'sp'), may hold values from -0.109375 to 0.109375
- stale: bfloat16 [4, 32, 64, 2, 3072], P('pipe', None, 'sp'), may hold values from -4 to 4
Outputs:
- hidden: bfloat16 [4, 32, 64, 3072], P('pipe', None, 'sp')
All inputs are finite; a program needn't handle non-finite values.
Results may differ from a plain program's by a relative error of at most 0.022.
Values may be sent and summed in bfloat16 or wider, within the bound.
No kernel may reach another device: no remote copies, remote signals or barrier semaphores. Data moves between devices by JAX's collectives and lax.ppermute only.
A program may use at most 128 MiB of HBM per device.

v0:
```python
import math

import jax
import jax.numpy as jnp
from jax import lax
from jax.sharding import PartitionSpec as P

D = 3072
HEADS = 24
HD = 128
PT = 64
PATCHES = 32


def passed_along(array, axis, by):
    peers = lax.axis_size(axis)
    pairs = [(i, i + by) for i in range(peers) if 0 <= i + by < peers]
    return lax.ppermute(array, axis, pairs)


def modulate(block_rows, shift_term, scale_term):
    widened = block_rows.astype(jnp.float32)
    average = jnp.mean(widened, axis=-1, keepdims=True)
    centered = widened - average
    variance = jnp.mean(centered * centered, axis=-1, keepdims=True)
    return (centered * lax.rsqrt(variance + 1e-06) * (1.0 + scale_term) + shift_term).astype(
        jnp.bfloat16
    )


def head_norm(head_values):
    return (
        head_values * lax.rsqrt(jnp.mean(head_values * head_values, axis=-1, keepdims=True) + 1e-06)
    ).astype(jnp.bfloat16)


def body(latent, modulation, w_qkv, w_out, stale):
    devices = lax.axis_size("sp")
    sp_index = lax.axis_index("sp")
    section_index = lax.axis_index("pipe")
    section_count = lax.axis_size("pipe")
    patch_group = min(8, devices // 2)
    head_groups = devices // patch_group
    heads_each = HEADS // head_groups
    block_width = heads_each * HD
    own_rows = latent.shape[1]
    weight_rows = w_qkv.shape[1]
    weight_cols = w_out.shape[2]
    group_count = PATCHES // patch_group
    round_count = group_count + section_count - 1
    patch_slot = sp_index % patch_group

    def spread_heads(member):
        return jnp.broadcast_to(member[:, None], (head_groups, patch_group) + member.shape[1:])

    def spread_rows(member):
        return jnp.broadcast_to(member[None], (head_groups,) + member.shape)

    def merge_heads(received):
        return jnp.sum(received.reshape(own_rows, head_groups, patch_group, D), axis=1).transpose(
            1, 0, 2
        )

    qkv_local = w_qkv[0].reshape(weight_rows, 3, head_groups, block_width).transpose(2, 0, 1, 3)
    out_local = w_out[0].reshape(head_groups, block_width, weight_cols).transpose(0, 2, 1)
    stale_local = (
        stale[0].reshape(PATCHES, own_rows, 2, head_groups, block_width).transpose(3, 1, 0, 2, 4)
    )
    qkv_send = spread_heads(qkv_local).reshape(devices * weight_rows, 3, block_width)
    out_send = spread_heads(out_local).reshape(devices * weight_cols, block_width)
    stale_send = spread_heads(stale_local).reshape(devices * own_rows, PATCHES, 2, block_width)
    qkv_block, out_block, key_store = (
        lax.all_to_all(qkv_send, "sp", split_axis=0, concat_axis=0, tiled=True),
        lax.all_to_all(out_send, "sp", split_axis=0, concat_axis=0, tiled=True),
        lax.all_to_all(stale_send, "sp", split_axis=0, concat_axis=0, tiled=True),
    )
    qkv_flat = qkv_block.reshape(D, 3 * block_width)
    modulators = modulation[0]

    def one_round(step_number, state_pair):
        incoming, results = state_pair
        group_index = step_number - section_index
        valid = (group_index >= 0) & (group_index < group_count)
        clipped = jnp.clip(group_index, 0, group_count - 1)
        first_patch = clipped * patch_group
        entering = lax.dynamic_slice_in_dim(latent, first_patch, patch_group, 0)
        block_rows = jnp.where(section_index == 0, entering, incoming)
        normed = modulate(block_rows, modulators[0], modulators[1])
        outgoing = spread_rows(normed).reshape(devices * own_rows, D)
        patch_rows = lax.all_to_all(outgoing, "sp", split_axis=0, concat_axis=0, tiled=True)
        projected = jnp.dot(patch_rows, qkv_flat, preferred_element_type=jnp.float32).reshape(
            PT, 3, heads_each, HD
        )
        queries = head_norm(projected[:, 0])
        keys_new = head_norm(projected[:, 1])
        values_new = projected[:, 2].astype(jnp.bfloat16)
        fresh_pair = jnp.stack([keys_new, values_new], 1).reshape(PT, 1, 2, block_width)
        patch_index = first_patch + patch_slot
        zero_index = jnp.zeros((), jnp.int32)
        key_table = lax.dynamic_update_slice(
            key_store, fresh_pair, (zero_index, patch_index, zero_index, zero_index)
        )
        all_keys = key_table[:, :, 0].reshape(PT, PATCHES, heads_each, HD)
        all_values = key_table[:, :, 1].reshape(PT, PATCHES, heads_each, HD)
        scores = jnp.einsum(
            "qhd,tphd->hqtp", queries, all_keys, preferred_element_type=jnp.float32
        ) / math.sqrt(HD)
        numerator = jnp.exp(scores)
        row_total = jnp.sum(numerator, axis=(2, 3))
        weights = numerator.astype(jnp.bfloat16)
        attended = (
            jnp.einsum("hqtp,tphd->qhd", weights, all_values, preferred_element_type=jnp.float32)
            / row_total.T[:, :, None]
        )
        attention = attended.astype(jnp.bfloat16).reshape(PT, block_width)
        partial_value = lax.dot_general(
            attention, out_block, (((1,), (1,)), ((), ())), preferred_element_type=jnp.float32
        ).astype(jnp.bfloat16)
        returned = lax.all_to_all(
            partial_value.reshape(PT, 1, D), "sp", split_axis=0, concat_axis=1, tiled=True
        )
        summed = merge_heads(returned.astype(jnp.float32))
        updated = (block_rows.astype(jnp.float32) + modulators[2] * summed).astype(jnp.bfloat16)
        current = lax.dynamic_slice_in_dim(results, first_patch, patch_group, 0)
        results = lax.dynamic_update_slice_in_dim(
            results, jnp.where(valid, updated, current), first_patch, 0
        )
        incoming = passed_along(updated, "pipe", 1)
        return (incoming, results)

    start_rows = jnp.zeros((patch_group, own_rows, D), jnp.bfloat16)
    start_results = jnp.zeros((PATCHES, own_rows, D), jnp.bfloat16)
    final_pair = lax.fori_loop(0, round_count, one_round, (start_rows, start_results))
    return final_pair[1][None]


def solution(mesh):
    return jax.shard_map(
        body,
        mesh=mesh,
        in_specs=(
            P(None, "sp", None),
            P("pipe", None, None),
            P("pipe", "sp", None),
            P("pipe", None, "sp"),
            P("pipe", None, "sp", None, None),
        ),
        out_specs=P("pipe", None, "sp", None),
        check_vma=False,
    )
```

profile of v0, /device:TPU:1, one launch (start us, length us, event | category | flops | bytes accessed | tf_op | source)
XLA Modules:
  0.0 1023.2 jit_solution(13872692560084082442)
XLA Ops:
  3.5 13.2 %all-to-all-start.3 = ((bf16[64,32,2,384]{3,1,2,0:T(8,128)(2,1)}), bf16[64,32,2,384]{3,1,2,0:T(8,128)(2,1)S(1)}, u32[]{:S(2)}, u32[]{:S(2)}) async-start(bf16[64,32,2,384]{3,1,2,0:T(8,128)(2,1)} %bitcast.139), calls=%async_computation.3 | async-start | bytes 6291456 | tf_op jit(solution)/shard_map/all_to_all | solution.py:75
  18.7 47.3 %copy.55 = bf16[3072,3,384]{2,1,0:T(4,128)(2,1)} copy(bf16[3072,3,384]{2,0,1:T(8,128)(2,1)S(1)} %bitcast.138) | data formatting | bytes 14155776 | tf_op jit(solution)/shard_map/reshape | solution.py:69
  66.0 24.2 %all-to-all-done.3 = bf16[64,32,2,384]{3,1,2,0:T(8,128)(2,1)S(1)} async-done(((bf16[64,32,2,384]{3,1,2,0:T(8,128)(2,1)}), bf16[64,32,2,384]{3,1,2,0:T(8,128)(2,1)S(1)}, u32[]{:S(2)}, u32[]{:S(2)}) %all-to-all-start.3) | async-done | bytes 3145760 | tf_op jit(solution)/shard_map/all_to_all | solution.py:75
  91.9 6.2 all-to-all-start.2
  98.2 208.2 %all-to-all-done.2 = bf16[3072,3,384]{2,1,0:T(4,128)(2,1)} async-done(((bf16[3072,3,384]{2,1,0:T(4,128)(2,1)}), bf16[3072,3,384]{2,1,0:T(4,128)(2,1)}, u32[]{:S(2)}, u32[]{:S(2)}) %all-to-all-start.2) | async-done | bytes 7077920 | tf_op jit(solution)/shard_map/all_to_all | solution.py:73
  308.0 6.0 all-to-all-start.4
  318.6 14.6 %copy.56 = bf16[3072,3,384]{0,2,1:T(8,128)(2,1)} copy(bf16[3072,3,384]{2,1,0:T(4,128)(2,1)} %all-to-all-done.2) | data formatting | bytes 14155776 | tf_op jit(solution)/shard_map/all_to_all | solution.py:73
  333.1 37.5 %all-to-all-done.4 = bf16[64,48,384]{2,1,0:T(8,128)(2,1)S(1)} async-done(((bf16[64,48,384]{2,1,0:T(8,128)(2,1)}), bf16[64,48,384]{2,1,0:T(8,128)(2,1)S(1)}, u32[]{:S(2)}, u32[]{:S(2)}) %all-to-all-start.4) | async-done | bytes 2359328 | tf_op jit(solution)/shard_map/all_to_all | solution.py:74
  371.4 651.9 %while.16 = (s32[]{:T(128)}, bf16[8,1,3072]{2,0,1:T(8,128)(2,1)S(1)}, bf16[32,1,3072]{2,0,1:T(8,128)(2,1)}, pred[]{:T(512)}, s32[]{:T(128)}, /*index=5*/bf16[32,...) while((s32[]{:T(128)}, ...), condition=%wide.region_7.8_spmd, body=%wide.region_0.7_spmd.sunk | while | flops 808185088 | bytes 66921072 | solution.py:133
  376.7 6.0 all-to-all-start
  384.6 12.7 %all-to-all-done = bf16[64,2,1536]{2,1,0:T(2,128)(2,1)S(1)} async-done(((bf16[64,2,1536]{2,1,0:T(2,128)(2,1)}), bf16[64,2,1536]{2,1,0:T(2,128)(2,1)S(1)}, u32[]{:S(2)}, u32[]{:S(2)}) %all-to-all-start) | async-done | bytes 393248 | tf_op jit(solution)/shard_map/while/body/eval_jaxpr/all_to_all | solution.py:90
  398.4 5.5 fusion.74
  407.3 5.2 dynamic_update_slice.20
  414.5 5.1 squeeze.48
  423.6 4.1 fusion.76
  435.0 6.2 all-to-all-start.1
  441.3 14.6 %all-to-all-done.1 = bf16[64,2,1536]{2,1,0:T(2,128)(2,1)S(1)} async-done(((bf16[64,2,1536]{2,1,0:T(2,128)(2,1)}), bf16[64,2,1536]{2,1,0:T(2,128)(2,1)S(1)}, u32[]{:S(2)}, u32[]{:S(2)}) %all-to-all-start.1) | async-done | bytes 393248 | tf_op jit(solution)/shard_map/while/body/eval_jaxpr/all_to_all | solution.py:119
  468.2 7.1 all-to-all-start
  477.2 12.7 %all-to-all-done = bf16[64,2,1536]{2,1,0:T(2,128)(2,1)S(1)} async-done(((bf16[64,2,1536]{2,1,0:T(2,128)(2,1)}), bf16[64,2,1536]{2,1,0:T(2,128)(2,1)S(1)}, u32[]{:S(2)}, u32[]{:S(2)}) %all-to-all-start) | async-done | bytes 393248 | tf_op jit(solution)/shard_map/while/body/eval_jaxpr/all_to_all | solution.py:90
  490.9 5.5 fusion.74
  499.8 5.2 dynamic_update_slice.20
  507.1 5.1 squeeze.48
  516.1 4.1 fusion.76
  527.6 6.2 all-to-all-start.1
  533.8 14.6 %all-to-all-done.1 = bf16[64,2,1536]{2,1,0:T(2,128)(2,1)S(1)} async-done(((bf16[64,2,1536]{2,1,0:T(2,128)(2,1)}), bf16[64,2,1536]{2,1,0:T(2,128)(2,1)S(1)}, u32[]{:S(2)}, u32[]{:S(2)}) %all-to-all-start.1) | async-done | bytes 393248 | tf_op jit(solution)/shard_map/while/body/eval_jaxpr/all_to_all | solution.py:119
  561.6 7.1 all-to-all-start
  570.5 12.7 %all-to-all-done = bf16[64,2,1536]{2,1,0:T(2,128)(2,1)S(1)} async-done(((bf16[64,2,1536]{2,1,0:T(2,128)(2,1)}), bf16[64,2,1536]{2,1,0:T(2,128)(2,1)S(1)}, u32[]{:S(2)}, u32[]{:S(2)}) %all-to-all-start) | async-done | bytes 393248 | tf_op jit(solution)/shard_map/while/body/eval_jaxpr/all_to_all | solution.py:90
  584.3 5.5 fusion.74
  593.2 5.2 dynamic_update_slice.20
  600.4 5.1 squeeze.48
  609.5 4.1 fusion.76
  621.0 6.2 all-to-all-start.1
  627.2 14.6 %all-to-all-done.1 = bf16[64,2,1536]{2,1,0:T(2,128)(2,1)S(1)} async-done(((bf16[64,2,1536]{2,1,0:T(2,128)(2,1)}), bf16[64,2,1536]{2,1,0:T(2,128)(2,1)S(1)}, u32[]{:S(2)}, u32[]{:S(2)}) %all-to-all-start.1) | async-done | bytes 393248 | tf_op jit(solution)/shard_map/while/body/eval_jaxpr/all_to_all | solution.py:119
  655.0 7.1 all-to-all-start
  663.9 12.7 %all-to-all-done = bf16[64,2,1536]{2,1,0:T(2,128)(2,1)S(1)} async-done(((bf16[64,2,1536]{2,1,0:T(2,128)(2,1)}), bf16[64,2,1536]{2,1,0:T(2,128)(2,1)S(1)}, u32[]{:S(2)}, u32[]{:S(2)}) %all-to-all-start) | async-done | bytes 393248 | tf_op jit(solution)/shard_map/while/body/eval_jaxpr/all_to_all | solution.py:90
  677.7 5.5 fusion.74
  686.6 5.2 dynamic_update_slice.20
  693.8 5.1 squeeze.48
  702.9 4.1 fusion.76
  714.4 6.2 all-to-all-start.1
  720.6 14.6 %all-to-all-done.1 = bf16[64,2,1536]{2,1,0:T(2,128)(2,1)S(1)} async-done(((bf16[64,2,1536]{2,1,0:T(2,128)(2,1)}), bf16[64,2,1536]{2,1,0:T(2,128)(2,1)S(1)}, u32[]{:S(2)}, u32[]{:S(2)}) %all-to-all-start.1) | async-done | bytes 393248 | tf_op jit(solution)/shard_map/while/body/eval_jaxpr/all_to_all | solution.py:119
  748.4 7.1 all-to-all-start
  757.3 12.7 %all-to-all-done = bf16[64,2,1536]{2,1,0:T(2,128)(2,1)S(1)} async-done(((bf16[64,2,1536]{2,1,0:T(2,128)(2,1)}), bf16[64,2,1536]{2,1,0:T(2,128)(2,1)S(1)}, u32[]{:S(2)}, u32[]{:S(2)}) %all-to-all-start) | async-done | bytes 393248 | tf_op jit(solution)/shard_map/while/body/eval_jaxpr/all_to_all | solution.py:90
  771.1 5.5 fusion.74
  780.0 5.2 dynamic_update_slice.20
  787.2 5.1 squeeze.48
  796.3 4.1 fusion.76
  807.7 6.2 all-to-all-start.1
  814.0 14.6 %all-to-all-done.1 = bf16[64,2,1536]{2,1,0:T(2,128)(2,1)S(1)} async-done(((bf16[64,2,1536]{2,1,0:T(2,128)(2,1)}), bf16[64,2,1536]{2,1,0:T(2,128)(2,1)S(1)}, u32[]{:S(2)}, u32[]{:S(2)}) %all-to-all-start.1) | async-done | bytes 393248 | tf_op jit(solution)/shard_map/while/body/eval_jaxpr/all_to_all | solution.py:119
  841.7 7.1 all-to-all-start
  850.7 12.7 %all-to-all-done = bf16[64,2,1536]{2,1,0:T(2,128)(2,1)S(1)} async-done(((bf16[64,2,1536]{2,1,0:T(2,128)(2,1)}), bf16[64,2,1536]{2,1,0:T(2,128)(2,1)S(1)}, u32[]{:S(2)}, u32[]{:S(2)}) %all-to-all-start) | async-done | bytes 393248 | tf_op jit(solution)/shard_map/while/body/eval_jaxpr/all_to_all | solution.py:90
  864.5 5.5 fusion.74
  873.4 5.2 dynamic_update_slice.20
  880.6 5.1 squeeze.48
  889.7 4.1 fusion.76
  901.1 6.2 all-to-all-start.1
  907.4 14.6 %all-to-all-done.1 = bf16[64,2,1536]{2,1,0:T(2,128)(2,1)S(1)} async-done(((bf16[64,2,1536]{2,1,0:T(2,128)(2,1)}), bf16[64,2,1536]{2,1,0:T(2,128)(2,1)S(1)}, u32[]{:S(2)}, u32[]{:S(2)}) %all-to-all-start.1) | async-done | bytes 393248 | tf_op jit(solution)/shard_map/while/body/eval_jaxpr/all_to_all | solution.py:119
  935.1 7.1 all-to-all-start
  944.1 12.7 %all-to-all-done = bf16[64,2,1536]{2,1,0:T(2,128)(2,1)S(1)} async-done(((bf16[64,2,1536]{2,1,0:T(2,128)(2,1)}), bf16[64,2,1536]{2,1,0:T(2,128)(2,1)S(1)}, u32[]{:S(2)}, u32[]{:S(2)}) %all-to-all-start) | async-done | bytes 393248 | tf_op jit(solution)/shard_map/while/body/eval_jaxpr/all_to_all | solution.py:90
  957.9 5.5 fusion.74
  966.8 5.2 dynamic_update_slice.20
  974.0 5.1 squeeze.48
  994.5 6.2 all-to-all-start.1
  1000.7 14.6 %all-to-all-done.1 = bf16[64,2,1536]{2,1,0:T(2,128)(2,1)S(1)} async-done(((bf16[64,2,1536]{2,1,0:T(2,128)(2,1)}), bf16[64,2,1536]{2,1,0:T(2,128)(2,1)S(1)}, u32[]{:S(2)}, u32[]{:S(2)}) %all-to-all-start.1) | async-done | bytes 393248 | tf_op jit(solution)/shard_map/while/body/eval_jaxpr/all_to_all | solution.py:119
  (349 shorter events, 246.7 us)
Async XLA Ops:
  3.5 86.7 %all-to-all-start.3 = ((bf16[64,32,2,384]{3,1,2,0:T(8,128)(2,1)}), bf16[64,32,2,384]{3,1,2,0:T(8,128)(2,1)S(1)}, u32[]{:S(2)}, u32[]{:S(2)}) async-start(bf16[64,32,2,384]{3,1,2,0:T(8,128)(2,1)} %bitcast.139), calls=%async_computation.3 | async-start | bytes 6291456 | tf_op jit(solution)/shard_map/all_to_all | solution.py:75
  66.0 32.1 %copy-start.5 = (bf16[1,3072,48]{1,2,0:T(8,128)(2,1)S(1)}, bf16[1,3072,48]{1,2,0:T(8,128)(2,1)}, u32[]{:S(2)}) copy-start(bf16[1,3072,48]{1,2,0:T(8,128)(2,1)} %param.10) | copy-start | bytes 884740
  90.2 1.7 copy-start.3
  91.9 214.5 %all-to-all-start.2 = ((bf16[3072,3,384]{2,1,0:T(4,128)(2,1)}), bf16[3072,3,384]{2,1,0:T(4,128)(2,1)}, u32[]{:S(2)}, u32[]{:S(2)}) async-start(bf16[3072,3,384]{2,1,0:T(4,128)(2,1)} %copy.55), calls=%async_computation.2 | async-start | bytes 18874368 | tf_op jit(solution)/shard_map/all_to_all | solution.py:73
  98.2 215.8 %copy-start.7 = (f32[1,3,3072]{2,0,1:T(1,128)S(1)}, f32[1,3,3072]{2,0,1:T(1,128)}, u32[]{:S(2)}) copy-start(f32[1,3,3072]{2,0,1:T(1,128)} %param.8) | copy-start | bytes 110596
  308.0 62.6 %all-to-all-start.4 = ((bf16[64,48,384]{2,1,0:T(8,128)(2,1)}), bf16[64,48,384]{2,1,0:T(8,128)(2,1)S(1)}, u32[]{:S(2)}, u32[]{:S(2)}) async-start(bf16[64,48,384]{2,1,0:T(8,128)(2,1)} %bitcast.140), calls=%async_computation.4 | async-start | bytes 4718592 | tf_op jit(solution)/shard_map/all_to_all | solution.py:74
  371.4 11.4 %copy-start = (bf16[3072,384]{1,0:T(8,128)(2,1)}, bf16[3072,384]{1,0:T(8,128)(2,1)S(1)}, u32[]{:S(2)}) copy-start(bf16[3072,384]{1,0:T(8,128)(2,1)S(1)} %get-tuple-element.412) | copy-start | bytes 7077892 | tf_op jit(solution)/shard_map/while
  372.4 1.8 copy-start.2
  376.7 20.6 %all-to-all-start = ((bf16[64,2,1536]{2,1,0:T(2,128)(2,1)}), bf16[64,2,1536]{2,1,0:T(2,128)(2,1)S(1)}, u32[]{:S(2)}, u32[]{:S(2)}) async-start(bf16[64,2,1536]{2,1,0:T(2,128)(2,1)} %reshape.233), calls=%async_computation | async-start | bytes 786432 | tf_op jit(solution)/shard_map/while/body/eval_jaxpr/all_to_all | solution.py:90
  414.5 5.1 copy-start.6
  432.5 24.7 %copy-start.4 = (f32[1,3072]{1,0:T(1,128)S(1)}, f32[1,3072]{1,0:T(1,128)}, u32[]{:S(2)}) copy-start(f32[1,3072]{1,0:T(1,128)} %get-tuple-element.361) | copy-start | bytes 36868 | tf_op jit(solution)/shard_map/while
  433.0 29.9 %copy-start.1 = (bf16[3072,384]{1,0:T(8,128)(2,1)S(1)}, bf16[3072,384]{1,0:T(8,128)(2,1)}, u32[]{:S(2)}) copy-start(bf16[3072,384]{1,0:T(8,128)(2,1)} %copy-done) | copy-start | bytes 7077892 | tf_op jit(solution)/shard_map/while
  435.0 20.8 %all-to-all-start.1 = ((bf16[64,2,1536]{2,1,0:T(2,128)(2,1)}), bf16[64,2,1536]{2,1,0:T(2,128)(2,1)S(1)}, u32[]{:S(2)}, u32[]{:S(2)}) async-start(bf16[64,2,1536]{2,1,0:T(2,128)(2,1)} %reshape.235), calls=%async_computation.1 | async-start | bytes 786432 | tf_op jit(solution)/shard_map/while/body/eval_jaxpr/all_to_all | solution.py:119
  458.6 4.3 collective-permute-start
  462.9 12.4 %copy-start = (bf16[3072,384]{1,0:T(8,128)(2,1)}, bf16[3072,384]{1,0:T(8,128)(2,1)S(1)}, u32[]{:S(2)}) copy-start(bf16[3072,384]{1,0:T(8,128)(2,1)S(1)} %get-tuple-element.412) | copy-start | bytes 7077892 | tf_op jit(solution)/shard_map/while
  463.9 1.8 copy-start.2
  468.2 21.7 %all-to-all-start = ((bf16[64,2,1536]{2,1,0:T(2,128)(2,1)}), bf16[64,2,1536]{2,1,0:T(2,128)(2,1)S(1)}, u32[]{:S(2)}, u32[]{:S(2)}) async-start(bf16[64,2,1536]{2,1,0:T(2,128)(2,1)} %reshape.233), calls=%async_computation | async-start | bytes 786432 | tf_op jit(solution)/shard_map/while/body/eval_jaxpr/all_to_all | solution.py:90
  507.0 5.1 copy-start.6
  525.0 24.7 %copy-start.4 = (f32[1,3072]{1,0:T(1,128)S(1)}, f32[1,3072]{1,0:T(1,128)}, u32[]{:S(2)}) copy-start(f32[1,3072]{1,0:T(1,128)} %get-tuple-element.361) | copy-start | bytes 36868 | tf_op jit(solution)/shard_map/while
  525.5 30.7 %copy-start.1 = (bf16[3072,384]{1,0:T(8,128)(2,1)S(1)}, bf16[3072,384]{1,0:T(8,128)(2,1)}, u32[]{:S(2)}) copy-start(bf16[3072,384]{1,0:T(8,128)(2,1)} %copy-done) | copy-start | bytes 7077892 | tf_op jit(solution)/shard_map/while
  527.6 20.8 %all-to-all-start.1 = ((bf16[64,2,1536]{2,1,0:T(2,128)(2,1)}), bf16[64,2,1536]{2,1,0:T(2,128)(2,1)S(1)}, u32[]{:S(2)}, u32[]{:S(2)}) async-start(bf16[64,2,1536]{2,1,0:T(2,128)(2,1)} %reshape.235), calls=%async_computation.1 | async-start | bytes 786432 | tf_op jit(solution)/shard_map/while/body/eval_jaxpr/all_to_all | solution.py:119
  551.2 5.1 collective-permute-start
  556.3 12.4 %copy-start = (bf16[3072,384]{1,0:T(8,128)(2,1)}, bf16[3072,384]{1,0:T(8,128)(2,1)S(1)}, u32[]{:S(2)}) copy-start(bf16[3072,384]{1,0:T(8,128)(2,1)S(1)} %get-tuple-element.412) | copy-start | bytes 7077892 | tf_op jit(solution)/shard_map/while
  557.2 1.8 copy-start.2
  561.6 21.7 %all-to-all-start = ((bf16[64,2,1536]{2,1,0:T(2,128)(2,1)}), bf16[64,2,1536]{2,1,0:T(2,128)(2,1)S(1)}, u32[]{:S(2)}, u32[]{:S(2)}) async-start(bf16[64,2,1536]{2,1,0:T(2,128)(2,1)} %reshape.233), calls=%async_computation | async-start | bytes 786432 | tf_op jit(solution)/shard_map/while/body/eval_jaxpr/all_to_all | solution.py:90
  600.4 5.1 copy-start.6
  618.4 24.7 %copy-start.4 = (f32[1,3072]{1,0:T(1,128)S(1)}, f32[1,3072]{1,0:T(1,128)}, u32[]{:S(2)}) copy-start(f32[1,3072]{1,0:T(1,128)} %get-tuple-element.361) | copy-start | bytes 36868 | tf_op jit(solution)/shard_map/while
  618.9 30.7 %copy-start.1 = (bf16[3072,384]{1,0:T(8,128)(2,1)S(1)}, bf16[3072,384]{1,0:T(8,128)(2,1)}, u32[]{:S(2)}) copy-start(bf16[3072,384]{1,0:T(8,128)(2,1)} %copy-done) | copy-start | bytes 7077892 | tf_op jit(solution)/shard_map/while
  621.0 20.8 %all-to-all-start.1 = ((bf16[64,2,1536]{2,1,0:T(2,128)(2,1)}), bf16[64,2,1536]{2,1,0:T(2,128)(2,1)S(1)}, u32[]{:S(2)}, u32[]{:S(2)}) async-start(bf16[64,2,1536]{2,1,0:T(2,128)(2,1)} %reshape.235), calls=%async_computation.1 | async-start | bytes 786432 | tf_op jit(solution)/shard_map/while/body/eval_jaxpr/all_to_all | solution.py:119
  644.5 5.1 collective-permute-start
  649.7 12.4 %copy-start = (bf16[3072,384]{1,0:T(8,128)(2,1)}, bf16[3072,384]{1,0:T(8,128)(2,1)S(1)}, u32[]{:S(2)}) copy-start(bf16[3072,384]{1,0:T(8,128)(2,1)S(1)} %get-tuple-element.412) | copy-start | bytes 7077892 | tf_op jit(solution)/shard_map/while
  650.6 1.8 copy-start.2
  655.0 21.7 %all-to-all-start = ((bf16[64,2,1536]{2,1,0:T(2,128)(2,1)}), bf16[64,2,1536]{2,1,0:T(2,128)(2,1)S(1)}, u32[]{:S(2)}, u32[]{:S(2)}) async-start(bf16[64,2,1536]{2,1,0:T(2,128)(2,1)} %reshape.233), calls=%async_computation | async-start | bytes 786432 | tf_op jit(solution)/shard_map/while/body/eval_jaxpr/all_to_all | solution.py:90
  693.8 5.1 copy-start.6
  711.8 24.7 %copy-start.4 = (f32[1,3072]{1,0:T(1,128)S(1)}, f32[1,3072]{1,0:T(1,128)}, u32[]{:S(2)}) copy-start(f32[1,3072]{1,0:T(1,128)} %get-tuple-element.361) | copy-start | bytes 36868 | tf_op jit(solution)/shard_map/while
  712.3 30.7 %copy-start.1 = (bf16[3072,384]{1,0:T(8,128)(2,1)S(1)}, bf16[3072,384]{1,0:T(8,128)(2,1)}, u32[]{:S(2)}) copy-start(bf16[3072,384]{1,0:T(8,128)(2,1)} %copy-done) | copy-start | bytes 7077892 | tf_op jit(solution)/shard_map/while
  714.4 20.8 %all-to-all-start.1 = ((bf16[64,2,1536]{2,1,0:T(2,128)(2,1)}), bf16[64,2,1536]{2,1,0:T(2,128)(2,1)S(1)}, u32[]{:S(2)}, u32[]{:S(2)}) async-start(bf16[64,2,1536]{2,1,0:T(2,128)(2,1)} %reshape.235), calls=%async_computation.1 | async-start | bytes 786432 | tf_op jit(solution)/shard_map/while/body/eval_jaxpr/all_to_all | solution.py:119
  737.9 5.1 collective-permute-start
  743.1 12.4 %copy-start = (bf16[3072,384]{1,0:T(8,128)(2,1)}, bf16[3072,384]{1,0:T(8,128)(2,1)S(1)}, u32[]{:S(2)}) copy-start(bf16[3072,384]{1,0:T(8,128)(2,1)S(1)} %get-tuple-element.412) | copy-start | bytes 7077892 | tf_op jit(solution)/shard_map/while
  744.0 1.8 copy-start.2
  748.4 21.7 %all-to-all-start = ((bf16[64,2,1536]{2,1,0:T(2,128)(2,1)}), bf16[64,2,1536]{2,1,0:T(2,128)(2,1)S(1)}, u32[]{:S(2)}, u32[]{:S(2)}) async-start(bf16[64,2,1536]{2,1,0:T(2,128)(2,1)} %reshape.233), calls=%async_computation | async-start | bytes 786432 | tf_op jit(solution)/shard_map/while/body/eval_jaxpr/all_to_all | solution.py:90
  787.2 5.1 copy-start.6
  805.2 24.7 %copy-start.4 = (f32[1,3072]{1,0:T(1,128)S(1)}, f32[1,3072]{1,0:T(1,128)}, u32[]{:S(2)}) copy-start(f32[1,3072]{1,0:T(1,128)} %get-tuple-element.361) | copy-start | bytes 36868 | tf_op jit(solution)/shard_map/while
  805.7 30.7 %copy-start.1 = (bf16[3072,384]{1,0:T(8,128)(2,1)S(1)}, bf16[3072,384]{1,0:T(8,128)(2,1)}, u32[]{:S(2)}) copy-start(bf16[3072,384]{1,0:T(8,128)(2,1)} %copy-done) | copy-start | bytes 7077892 | tf_op jit(solution)/shard_map/while
  807.7 20.8 %all-to-all-start.1 = ((bf16[64,2,1536]{2,1,0:T(2,128)(2,1)}), bf16[64,2,1536]{2,1,0:T(2,128)(2,1)S(1)}, u32[]{:S(2)}, u32[]{:S(2)}) async-start(bf16[64,2,1536]{2,1,0:T(2,128)(2,1)} %reshape.235), calls=%async_computation.1 | async-start | bytes 786432 | tf_op jit(solution)/shard_map/while/body/eval_jaxpr/all_to_all | solution.py:119
  831.3 5.1 collective-permute-start
  836.4 12.4 %copy-start = (bf16[3072,384]{1,0:T(8,128)(2,1)}, bf16[3072,384]{1,0:T(8,128)(2,1)S(1)}, u32[]{:S(2)}) copy-start(bf16[3072,384]{1,0:T(8,128)(2,1)S(1)} %get-tuple-element.412) | copy-start | bytes 7077892 | tf_op jit(solution)/shard_map/while
  837.4 1.8 copy-start.2
  841.7 21.7 %all-to-all-start = ((bf16[64,2,1536]{2,1,0:T(2,128)(2,1)}), bf16[64,2,1536]{2,1,0:T(2,128)(2,1)S(1)}, u32[]{:S(2)}, u32[]{:S(2)}) async-start(bf16[64,2,1536]{2,1,0:T(2,128)(2,1)} %reshape.233), calls=%async_computation | async-start | bytes 786432 | tf_op jit(solution)/shard_map/while/body/eval_jaxpr/all_to_all | solution.py:90
  880.6 5.1 copy-start.6
  898.5 24.7 %copy-start.4 = (f32[1,3072]{1,0:T(1,128)S(1)}, f32[1,3072]{1,0:T(1,128)}, u32[]{:S(2)}) copy-start(f32[1,3072]{1,0:T(1,128)} %get-tuple-element.361) | copy-start | bytes 36868 | tf_op jit(solution)/shard_map/while
  899.1 30.7 %copy-start.1 = (bf16[3072,384]{1,0:T(8,128)(2,1)S(1)}, bf16[3072,384]{1,0:T(8,128)(2,1)}, u32[]{:S(2)}) copy-start(bf16[3072,384]{1,0:T(8,128)(2,1)} %copy-done) | copy-start | bytes 7077892 | tf_op jit(solution)/shard_map/while
  901.1 20.8 %all-to-all-start.1 = ((bf16[64,2,1536]{2,1,0:T(2,128)(2,1)}), bf16[64,2,1536]{2,1,0:T(2,128)(2,1)S(1)}, u32[]{:S(2)}, u32[]{:S(2)}) async-start(bf16[64,2,1536]{2,1,0:T(2,128)(2,1)} %reshape.235), calls=%async_computation.1 | async-start | bytes 786432 | tf_op jit(solution)/shard_map/while/body/eval_jaxpr/all_to_all | solution.py:119
  924.7 5.1 collective-permute-start
  929.8 12.4 %copy-start = (bf16[3072,384]{1,0:T(8,128)(2,1)}, bf16[3072,384]{1,0:T(8,128)(2,1)S(1)}, u32[]{:S(2)}) copy-start(bf16[3072,384]{1,0:T(8,128)(2,1)S(1)} %get-tuple-element.412) | copy-start | bytes 7077892 | tf_op jit(solution)/shard_map/while
  930.8 1.8 copy-start.2
  935.1 21.7 %all-to-all-start = ((bf16[64,2,1536]{2,1,0:T(2,128)(2,1)}), bf16[64,2,1536]{2,1,0:T(2,128)(2,1)S(1)}, u32[]{:S(2)}, u32[]{:S(2)}) async-start(bf16[64,2,1536]{2,1,0:T(2,128)(2,1)} %reshape.233), calls=%async_computation | async-start | bytes 786432 | tf_op jit(solution)/shard_map/while/body/eval_jaxpr/all_to_all | solution.py:90
  974.0 5.1 copy-start.6
  991.9 24.7 %copy-start.4 = (f32[1,3072]{1,0:T(1,128)S(1)}, f32[1,3072]{1,0:T(1,128)}, u32[]{:S(2)}) copy-start(f32[1,3072]{1,0:T(1,128)} %get-tuple-element.361) | copy-start | bytes 36868 | tf_op jit(solution)/shard_map/while
  992.5 30.7 %copy-start.1 = (bf16[3072,384]{1,0:T(8,128)(2,1)S(1)}, bf16[3072,384]{1,0:T(8,128)(2,1)}, u32[]{:S(2)}) copy-start(bf16[3072,384]{1,0:T(8,128)(2,1)} %copy-done) | copy-start | bytes 7077892 | tf_op jit(solution)/shard_map/while
  994.5 20.8 %all-to-all-start.1 = ((bf16[64,2,1536]{2,1,0:T(2,128)(2,1)}), bf16[64,2,1536]{2,1,0:T(2,128)(2,1)S(1)}, u32[]{:S(2)}, u32[]{:S(2)}) async-start(bf16[64,2,1536]{2,1,0:T(2,128)(2,1)} %reshape.235), calls=%async_computation.1 | async-start | bytes 786432 | tf_op jit(solution)/shard_map/while/body/eval_jaxpr/all_to_all | solution.py:119
  1018.1 5.1 collective-permute-start
where the time goes:
time: 1030 us; the launch traced here: 1020 us
  waiting for transfers between devices  469 us (46%)
  local copies, waits for them, and re-layouts  246 us (24%)
  starting transfers between devices  144 us (14%)
  matrix products  101 us (10%)
  other arithmetic  61.6 us (6%)
    all_to_all x1, waiting for transfers between devices, body(): lax.all_to_all(qkv_send, 'sp', split_axis=0, concat_axis=0, tiled=True)  208 us
    all_to_all x7, waiting for transfers between devices, one_round(): lax.all_to_all(partial_value.reshape(PT, 1, D), 'sp', split_axis=0, conca...  102 us
    all_to_all x7, waiting for transfers between devices, one_round(): lax.all_to_all(outgoing, 'sp', split_axis=0, concat_axis=0, tiled=True)  88.9 us
    all_to_all x7, starting transfers between devices, one_round(): lax.all_to_all(outgoing, 'sp', split_axis=0, concat_axis=0, tiled=True)  48.3 us
    reshape x1, local copies, waits for them, and re-layouts, body(): spread_heads(qkv_local).reshape(devices * weight_rows, 3, block_width)  47.3 us
    all_to_all x7, starting transfers between devices, one_round(): lax.all_to_all(partial_value.reshape(PT, 1, D), 'sp', split_axis=0, conca...  43.4 us
    dot_general x7, matrix products, one_round(): jnp.dot(patch_rows, qkv_flat, preferred_element_type=jnp.float32)  38.6 us
    all_to_all x1, waiting for transfers between devices, body(): lax.all_to_all(out_send, 'sp', split_axis=0, concat_axis=0, tiled=True)  37.5 us
  transfers between devices with their start and end apart: 24, of which 24 were waited for; matrix products, arithmetic and copies ran while one was open for 8% of the time, Pallas kernels for 0%

commit v1 on v0

v1 whole, which is shorter than its diff:
```python
import math

import jax
import jax.numpy as jnp
from jax import lax
from jax.experimental import pallas as pl
from jax.experimental.pallas import tpu as pltpu
from jax.sharding import Mesh
from jax.sharding import PartitionSpec as P

D = 3072
HEADS = 24
HD = 128
PT = 64
PATCHES = 32
BLOCKS = 4
NX, NY, NZ, NC = 4, 4, 8, 2
SP = ("y", "z", "c")
HEAD_AXES = ("x", "y")
REST_AXES = ("z", "c")
MEMBERS = NX * NY
SOURCES = NY * NZ * NC
ROWS = D // SOURCES
PAIR = 2 * HD
OWN = 8
LOCAL = 2 * PT
AT_V_W, AT_OUT, AT_K, AT_V = 2 * ROWS, 3 * ROWS, 4 * ROWS, 4 * ROWS + PATCHES
PIECE = 4 * ROWS + 2 * PATCHES
VMEM = pl.BlockSpec(memory_space=pltpu.VMEM)
PARAMS = pltpu.CompilerParams(vmem_limit_bytes=48 * 1024 * 1024)


def head_norm(values):
    return (
        values * lax.rsqrt(jnp.mean(values * values, axis=-1, keepdims=True) + 1e-06)
    ).astype(jnp.bfloat16)


def modulate(rows, shift_term, scale_term):
    average = jnp.mean(rows, axis=-1, keepdims=True)
    centered = rows - average
    variance = jnp.mean(centered * centered, axis=-1, keepdims=True)
    return (centered * lax.rsqrt(variance + 1e-06) * (1.0 + scale_term) + shift_term).astype(
        jnp.bfloat16
    )


def pack_kernel(qkv_ref, out_ref, stale_ref, sent_ref):
    for member in range(MEMBERS):
        triple, half = divmod(member, 2)
        for lane, head in ((0, 3 * triple + 2 * half), (HD, 3 * triple + 1)):
            for part in range(3):
                sent_ref[member, part * ROWS : (part + 1) * ROWS, lane : lane + HD] = qkv_ref[
                    :, part * D + head * HD : part * D + (head + 1) * HD
                ]
            columns = slice(head * HD, (head + 1) * HD)
            sent_ref[member, AT_OUT:AT_K, lane : lane + HD] = out_ref[:, columns]
            sent_ref[member, AT_K:AT_V, lane : lane + HD] = stale_ref[0, :, columns]
            sent_ref[member, AT_V:PIECE, lane : lane + HD] = stale_ref[1, :, columns]


def first_kernel(rows_ref, shift_ref, scale_ref, normed_ref):
    normed = modulate(rows_ref[...].astype(jnp.float32), shift_ref[...], scale_ref[...])
    twice = jnp.concatenate([normed, normed], axis=0)
    for at in range(0, LOCAL, 2 * OWN):
        normed_ref[at : at + 2 * OWN, :] = twice


def sum_rows(parts_ref, rows_ref, gate_ref):
    total = jnp.zeros((2 * OWN, D), jnp.float32)
    for at in range(0, LOCAL, 2 * OWN):
        total = total + parts_ref[at : at + 2 * OWN, :].astype(jnp.float32)
    summed = total[:OWN] + total[OWN:]
    return (rows_ref[...].astype(jnp.float32) + gate_ref[...] * summed).astype(jnp.bfloat16)


def middle_kernel(parts_ref, rows_ref, gate_ref, shift_ref, scale_ref, updated_ref, normed_ref):
    updated = sum_rows(parts_ref, rows_ref, gate_ref)
    updated_ref[...] = updated
    normed = modulate(updated.astype(jnp.float32), shift_ref[...], scale_ref[...])
    twice = jnp.concatenate([normed, normed], axis=0)
    for at in range(0, LOCAL, 2 * OWN):
        normed_ref[at : at + 2 * OWN, :] = twice


def last_kernel(parts_ref, rows_ref, gate_ref, updated_ref):
    updated_ref[...] = sum_rows(parts_ref, rows_ref, gate_ref)


def across(left, right):
    return lax.dot_general(
        left, right, (((1,), (1,)), ((), ())), preferred_element_type=jnp.float32
    )


def block_kernel(
    place_ref, rows_ref, pieces_ref, partial_ref, w_q, w_k, w_v, w_o, keys, values, sems
):
    copies = [
        pltpu.make_async_copy(pieces_ref.at[:, low : low + count, :], target, sems.at[number])
        for number, (target, low, count) in enumerate(
            (
                (w_q, 0, ROWS),
                (w_k, ROWS, ROWS),
                (w_v, AT_V_W, ROWS),
                (keys, AT_K, PATCHES),
                (values, AT_V, PATCHES),
                (w_o, AT_OUT, ROWS),
            )
        )
    ]
    for copy in copies:
        copy.start()
    first_patch, half = place_ref[0], place_ref[1]
    rows = rows_ref[...]

    def project(weight):
        return jnp.dot(
            rows, weight[...].reshape(D, PAIR), preferred_element_type=jnp.float32
        )

    copies[0].wait()
    q = project(w_q)
    copies[1].wait()
    k = project(w_k)
    copies[2].wait()
    v = project(w_v).astype(jnp.bfloat16)
    queries = [head_norm(q[:, :HD]), head_norm(q[:, HD:])]
    fresh_keys = [head_norm(k[:, :HD]), head_norm(k[:, HD:])]
    fresh_values = [v[:, :HD], v[:, HD:]]
    for own in (queries, fresh_keys, fresh_values):
        own[1] = jnp.where(half == 0, own[1][:PT], own[1][PT:])
    copies[3].wait()
    copies[4].wait()
    scale = 1.0 / math.sqrt(HD)
    step = 16
    results = []
    for at in range(2):
        asking = queries[at]
        count = asking.shape[0]
        lanes = slice(at * HD, (at + 1) * HD)
        fresh = jnp.exp(across(asking, fresh_keys[at]) * scale)
        row_at = lax.broadcasted_iota(jnp.int32, (count, 1), 0)
        if at == 0:
            row_patch = first_patch + (row_at >= PT).astype(jnp.int32)
            column_at = lax.broadcasted_iota(jnp.int32, (count, count), 1)
            fresh = jnp.where((row_at >= PT) == (column_at >= PT), fresh, 0.0)
        else:
            row_patch = jnp.full((count, 1), first_patch + half, jnp.int32)
        total = jnp.sum(fresh, axis=1, keepdims=True)
        gathered = jnp.dot(
            fresh.astype(jnp.bfloat16), fresh_values[at], preferred_element_type=jnp.float32
        )
        patch_of = lax.broadcasted_iota(jnp.int32, (count, step * PATCHES), 1) % PATCHES
        stale_here = patch_of != row_patch
        for low in range(0, SOURCES, step):
            some_keys = keys[low : low + step, :, lanes].reshape(step * PATCHES, HD)
            some_values = values[low : low + step, :, lanes].reshape(step * PATCHES, HD)
            numerator = jnp.where(stale_here, jnp.exp(across(asking, some_keys) * scale), 0.0)
            total = total + jnp.sum(numerator, axis=1, keepdims=True)
            gathered = gathered + jnp.dot(
                numerator.astype(jnp.bfloat16), some_values, preferred_element_type=jnp.float32
            )
        results.append((gathered / total).astype(jnp.bfloat16))
    shared = results[1]
    nothing = jnp.zeros_like(shared)
    shared = jnp.concatenate(
        [jnp.where(half == 0, shared, nothing), jnp.where(half == 0, nothing, shared)], axis=0
    )
    attention = jnp.concatenate([results[0], shared], axis=1)
    copies[5].wait()
    for low in range(0, SOURCES, 8):
        some = w_o[low : low + 8].reshape(8 * ROWS, PAIR)
        partial_ref[:, low * ROWS : (low + 8) * ROWS] = across(attention, some).astype(
            jnp.bfloat16
        )


def to_own_order(array):
    lead = array.shape[:-1]
    split = array.reshape(lead + (NY, NZ * NC, ROWS))
    return jnp.swapaxes(split, -3, -2).reshape(lead + (D,))


def to_given_order(array):
    lead = array.shape[:-1]
    split = array.reshape(lead + (NZ * NC, NY, ROWS))
    return jnp.swapaxes(split, -3, -2).reshape(lead + (D,))


def exchange(array, axes):
    return lax.all_to_all(array, axes, split_axis=0, concat_axis=0, tiled=True)


def body(latent, modulation, w_qkv, w_out, stale):
    x_at, y_at = lax.axis_index("x"), lax.axis_index("y")
    pair_at = lax.axis_index("z") * NC + lax.axis_index("c")
    place = jnp.stack([2 * pair_at, y_at % 2]).astype(jnp.int32)

    sent = pl.pallas_call(
        pack_kernel,
        out_shape=jax.ShapeDtypeStruct((MEMBERS, PIECE, PAIR), jnp.bfloat16),
        in_specs=[VMEM] * 3,
        out_specs=VMEM,
        compiler_params=PARAMS,
        name="pack",
    )(w_qkv[0], w_out[0].T, jnp.swapaxes(stale[0, :, 0], 0, 1))
    received = exchange(sent, HEAD_AXES).reshape(BLOCKS, NY, PIECE, PAIR)

    def gather(block):
        return lax.all_gather(received[block], REST_AXES, axis=0, tiled=True)

    pieces = [gather(block) for block in range(BLOCKS)]

    terms = to_own_order(lax.all_gather(modulation[0], "x", axis=0, tiled=False))
    mine = exchange(latent[:, 0], REST_AXES).reshape(NZ * NC, 2, D)
    mine = jnp.swapaxes(mine, 0, 1).reshape(NZ * NC * 2, D)
    current = to_own_order(lax.dynamic_slice_in_dim(mine, x_at * OWN, OWN, 0))

    def term(block, which):
        return terms[block, which][None]

    spread = jax.ShapeDtypeStruct((LOCAL, D), jnp.bfloat16)
    owned = jax.ShapeDtypeStruct((OWN, D), jnp.bfloat16)
    normed = pl.pallas_call(
        first_kernel,
        out_shape=spread,
        in_specs=[VMEM] * 3,
        out_specs=VMEM,
        compiler_params=PARAMS,
        name="first",
    )(current, term(0, 0), term(0, 1))
    outputs = []
    for block in range(BLOCKS):
        rows = exchange(normed, HEAD_AXES)
        partial = pl.pallas_call(
            block_kernel,
            out_shape=spread,
            in_specs=[
                pl.BlockSpec(memory_space=pltpu.SMEM),
                VMEM,
                pl.BlockSpec(memory_space=pl.ANY),
            ],
            out_specs=VMEM,
            scratch_shapes=[pltpu.VMEM((SOURCES, ROWS, PAIR), jnp.bfloat16)] * 4
            + [pltpu.VMEM((SOURCES, PATCHES, PAIR), jnp.bfloat16)] * 2
            + [pltpu.SemaphoreType.DMA((6,))],
            compiler_params=PARAMS,
            cost_estimate=pl.CostEstimate(
                flops=2 * LOCAL * D * PAIR * 4 + 4 * 3 * PT * 2048 * HD,
                bytes_accessed=SOURCES * PIECE * PAIR * 2 + 4 * LOCAL * D,
                transcendentals=3 * PT * 2048,
            ),
            name="block",
        )(place, rows, pieces[block])
        parts = exchange(partial, HEAD_AXES)
        if block + 1 < BLOCKS:
            current, normed = pl.pallas_call(
                middle_kernel,
                out_shape=(owned, spread),
                in_specs=[VMEM] * 5,
                out_specs=(VMEM, VMEM),
                compiler_params=PARAMS,
                name="middle",
            )(parts, current, term(block, 2), term(block + 1, 0), term(block + 1, 1))
        else:
            current = pl.pallas_call(
                last_kernel,
                out_shape=owned,
                in_specs=[VMEM] * 3,
                out_specs=VMEM,
                compiler_params=PARAMS,
                name="last",
            )(parts, current, term(block, 2))
        outputs.append(to_given_order(current))
    placed = exchange(jnp.concatenate(outputs, axis=0), "x")
    placed = jnp.swapaxes(placed.reshape(2, NZ * NC, D), 0, 1).reshape(PATCHES, D)
    placed = exchange(placed, REST_AXES)
    return placed[None, :, None]


def solution(mesh):
    own_mesh = Mesh(mesh.devices.reshape(NX, NY, NZ, NC), ("x",) + SP)
    return jax.shard_map(
        body,
        mesh=own_mesh,
        in_specs=(
            P(None, SP, None),
            P("x", None, None),
            P("x", SP, None),
            P("x", None, SP),
            P("x", None, SP, None, None),
        ),
        out_specs=P("x", None, SP, None),
        check_vma=False,
    )
```

time: 1030 us -> 336 us (0.33)
  waiting for transfers between devices: 469 us -> 122 us
  local copies, waits for them, and re-layouts: 246 us -> 9.18 us
  blocking collectives: 0 us -> 128 us
  starting transfers between devices: 144 us -> 32.7 us
  matrix products: 101 us -> 0 us
  other arithmetic: 61.6 us -> 0.09 us
  Pallas kernels: 0 us -> 30.1 us
  between operations: 0.12 us -> 13.4 us
    all_to_all x17 -> x6, waiting for transfers between devices: 461 us -> 25.1 us  [exchange(): return lax.all_to_all(array, axes, split_axis=0, concat_axis=0, tiled=True)]
    all_to_all x0 -> x6, blocking collectives: none -> 117 us  [exchange(): return lax.all_to_all(array, axes, split_axis=0, concat_axis=0, tiled=True)]
    dot_general x28 -> x0, matrix products: 101 us -> none  [the longest x7 38.6 us: one_round(): jnp.dot(patch_rows, qkv_flat, preferred_element_type=jnp.float32)]
    all_gather x0 -> x4, waiting for transfers between devices: none -> 95 us  [gather(): return lax.all_gather(received[block], REST_AXES, axis=0, tiled=True)]
    all_to_all x17 -> x6, starting transfers between devices: 117 us -> 32.6 us  [exchange(): return lax.all_to_all(array, axes, split_axis=0, concat_axis=0, tiled=True)]
    squeeze x14 -> x0, local copies, waits for them, and re-layouts: 63.2 us -> none  [the longest x7 35.8 us: one_round(): all_keys = key_table[:, :, 0].reshape(PT, PATCHES, heads_each, HD)]
    reshape x8 -> x16, local copies, waits for them, and re-layouts: 51.1 us -> 2.43 us  [the longest x4 0.76 us: to_given_order(): return jnp.swapaxes(split, -3, -2).reshape(lead + (D,))]
    while x106 -> x0, local copies, waits for them, and re-layouts: 41.3 us -> none
  transfers between devices with their start and end apart: 24 -> 10, of which waited for: 24 -> 7; matrix products, arithmetic and copies ran while one was open for 8% -> 1% of each run, Pallas kernels for 0% -> 7%
where the time goes in v1:
time: 336 us; the launch traced here: 335 us
  blocking collectives  128 us (38%)
  waiting for transfers between devices  122 us (36%)
  starting transfers between devices  32.7 us (10%)
  Pallas kernels  30.1 us (9%)
  between operations  13.4 us (4%)
  local copies, waits for them, and re-layouts  9.18 us (3%)
    all_to_all x6, blocking collectives, exchange(): return lax.all_to_all(array, axes, split_axis=0, concat_axis=0, tiled=True)  117 us
    all_gather x4, waiting for transfers between devices, gather(): return lax.all_gather(received[block], REST_AXES, axis=0, tiled=True)  95 us
    all_to_all x6, starting transfers between devices, exchange(): return lax.all_to_all(array, axes, split_axis=0, concat_axis=0, tiled=True)  32.6 us
    all_to_all x6, waiting for transfers between devices, exchange(): return lax.all_to_all(array, axes, split_axis=0, concat_axis=0, tiled=True)  25.1 us
    pallas_call x4, Pallas kernels, body(): pl.pallas_call(block_kernel, out_shape=spread, in_specs=[pl.BlockSpec(mem...  24.4 us
    all_gather x1, blocking collectives, body(): lax.all_gather(modulation[0], 'x', axis=0, tiled=False)  10.5 us
  transfers between devices with their start and end apart: 10, of which 7 were waited for; matrix products, arithmetic and copies ran while one was open for 1% of the time, Pallas kernels for 7%

profile of v1, /device:TPU:1, one launch (start us, length us, event | category | flops | bytes accessed | tf_op | source)
XLA Modules:
  0.0 335.1 jit_solution(16586935498470337689)
XLA Ops:
  6.5 1.1 copy.49
  7.6 0.0 copy-start
  7.7 1.2 copy-done
  8.8 1.0 copy-done.1
  9.8 0.3 pack.1
  10.1 33.9 %all_to_all.117 = bf16[16,256,256]{2,1,0:T(8,128)(2,1)S(1)} all-to-all(bf16[16,256,256]{2,1,0:T(8,128)(2,1)S(1)} %pack.1), channel_id=1, replica_groups=mesh['x'=4,'y'=4,'z'=8,'c'=2] {'x','y'}, dimensions={0} | all-to-all | bytes 4194304 | tf_op jit(solution)/shard_map/all_to_all | solution.py:192
  44.0 1.3 fusion
  45.3 0.0 all-gather.5.cloned.1.call-update
  45.4 0.0 all-gather.7.cloned.1.call-start
  45.4 0.7 all-gather.7.cloned.1.call-update
  46.1 0.0 all-gather.9.cloned.1.call-start
  46.2 0.7 all-gather.9.cloned.1.call-update
  46.8 0.0 all-gather.11.cloned.1.call-start
  46.9 0.5 all-gather.11.cloned.1.call-update
  47.4 0.8 all_to_all.75
  48.2 11.2 %all-to-all-start = ((bf16[16,2,3072]{2,1,0:T(2,128)(2,1)}), bf16[16,2,3072]{2,1,0:T(2,128)(2,1)S(1)}, u32[]{:S(2)}, u32[]{:S(2)}) async-start(bf16[16,2,3072]{2,1,0:T(2,128)(2,1)} %all_to_all.75), calls=%async_computation | async-start | bytes 393216 | tf_op jit(solution)/shard_map/all_to_all | solution.py:192
  59.4 10.5 %all_gather.15 = f32[4,3,3072]{2,1,0:T(4,128)S(1)} all-gather(f32[1,3,3072]{2,1,0:T(4,128)S(1)} %copy.35), channel_id=1, replica_groups=mesh['x'=4,'y'=4,'z'=8,'c'=2] {'x'}, dimensions={0}, use_global_device_ids=true | all-gather | bytes 184320 | tf_op jit(solution)/shard_map/all_gather | solution.py:215
  69.9 0.1 copy.36
  70.0 0.2 reshape.83
  70.2 0.2 copy.37
  70.3 0.4 reshape.84
  70.7 0.1 slice_bitcast_fusion
  70.8 1.0 all-to-all-done
  71.8 0.2 reshape.81
  72.0 0.1 copy.34
  72.1 0.2 reshape.82.rows_ref
  72.3 1.2 first.1
  73.4 3.6 %all-to-all-start.1 = ((bf16[16,8,3072]{2,1,0:T(8,128)(2,1)}), bf16[16,8,3072]{2,1,0:T(8,128)(2,1)S(1)}, u32[]{:S(2)}, u32[]{:S(2)}) async-start(bf16[16,8,3072]{2,1,0:T(8,128)(2,1)} %bitcast.8), calls=%async_computation.1 | async-start | bytes 1572864 | tf_op jit(solution)/shard_map/all_to_all | solution.py:192
  77.1 0.1 pad_add_fusion.place_ref
  77.2 12.7 %all-to-all-done.1 = bf16[16,8,3072]{2,1,0:T(8,128)(2,1)S(1)} async-done(((bf16[16,8,3072]{2,1,0:T(8,128)(2,1)}), bf16[16,8,3072]{2,1,0:T(8,128)(2,1)S(1)}, u32[]{:S(2)}, u32[]{:S(2)}) %all-to-all-start.1) | async-done | bytes 786464 | tf_op jit(solution)/shard_map/all_to_all | solution.py:192
  89.8 18.0 %all-gather.5.cloned.1.call-done.pieces_ref = bf16[64,256,256]{2,1,0:T(8,128)(2,1)} async-done(((bf16[4,256,256]{2,1,0:T(8,128)(2,1)}), bf16[64,256,256]{2,1,0:T(8,128)(2,1)}) %all-gather.5.cloned.1.call-update) | async-done | bytes 8388624 | tf_op jit(solution)/shard_map/all_gather | solution.py:211
  107.9 5.9 %block.4 = bf16[128,3072]{1,0:T(8,128)(2,1)S(1)} custom-call(s32[2]{0:T(128)S(1)} %pad_add_fusion.place_ref, bf16[128,3072]{1,0:T(8,128)(2,1)S(1)} %bitcast.86, bf16[64,256,256]{2,1,0:T(8,128)(2,1)} %all-gather.5.cloned.1.call-done.pieces_ref), custom_call_target="tpu_custom_call" | custom-call | flops 1006632960 | bytes 9961472 | tf_op jit(solution)/shard_map/block/pallas_call | solution.py:236
  113.7 17.7 %all_to_all.118 = bf16[16,8,3072]{2,1,0:T(8,128)(2,1)S(1)} all-to-all(bf16[16,8,3072]{2,1,0:T(8,128)(2,1)S(1)} %bitcast.90), channel_id=1, replica_groups=mesh['x'=4,'y'=4,'z'=8,'c'=2] {'x','y'}, dimensions={0} | all-to-all | bytes 1572864 | tf_op jit(solution)/shard_map/all_to_all | solution.py:192
  131.5 1.4 middle.3
  132.8 3.7 %all-to-all-start.4 = ((bf16[16,8,3072]{2,1,0:T(8,128)(2,1)}), bf16[16,8,3072]{2,1,0:T(8,128)(2,1)S(1)}, u32[]{:S(2)}, u32[]{:S(2)}) async-start(bf16[16,8,3072]{2,1,0:T(8,128)(2,1)} %bitcast.21), calls=%async_computation.4 | async-start | bytes 1572864 | tf_op jit(solution)/shard_map/all_to_all | solution.py:192
  136.6 25.9 %all-gather.7.cloned.1.call-done.pieces_ref = bf16[64,256,256]{2,1,0:T(8,128)(2,1)} async-done(((bf16[4,256,256]{2,1,0:T(8,128)(2,1)}), bf16[64,256,256]{2,1,0:T(8,128)(2,1)}) %all-gather.7.cloned.1.call-update) | async-done | bytes 8388624 | tf_op jit(solution)/shard_map/all_gather | solution.py:211
  162.4 0.0 all-to-all-done.4
  162.4 5.9 %block.5 = bf16[128,3072]{1,0:T(8,128)(2,1)S(1)} custom-call(s32[2]{0:T(128)S(1)} %pad_add_fusion.place_ref, bf16[128,3072]{1,0:T(8,128)(2,1)S(1)} %bitcast.88, bf16[64,256,256]{2,1,0:T(8,128)(2,1)} %all-gather.7.cloned.1.call-done.pieces_ref), custom_call_target="tpu_custom_call" | custom-call | flops 1006632960 | bytes 9961472 | tf_op jit(solution)/shard_map/block/pallas_call | solution.py:236
  168.3 19.7 %all_to_all.119 = bf16[16,8,3072]{2,1,0:T(8,128)(2,1)S(1)} all-to-all(bf16[16,8,3072]{2,1,0:T(8,128)(2,1)S(1)} %bitcast.91), channel_id=1, replica_groups=mesh['x'=4,'y'=4,'z'=8,'c'=2] {'x','y'}, dimensions={0} | all-to-all | bytes 1572864 | tf_op jit(solution)/shard_map/all_to_all | solution.py:192
  188.0 1.3 middle.4
  189.4 3.8 %all-to-all-start.6 = ((bf16[16,8,3072]{2,1,0:T(8,128)(2,1)}), bf16[16,8,3072]{2,1,0:T(8,128)(2,1)S(1)}, u32[]{:S(2)}, u32[]{:S(2)}) async-start(bf16[16,8,3072]{2,1,0:T(8,128)(2,1)} %bitcast.29), calls=%async_computation.6 | async-start | bytes 1572864 | tf_op jit(solution)/shard_map/all_to_all | solution.py:192
  193.2 25.6 %all-gather.9.cloned.1.call-done.pieces_ref = bf16[64,256,256]{2,1,0:T(8,128)(2,1)} async-done(((bf16[4,256,256]{2,1,0:T(8,128)(2,1)}), bf16[64,256,256]{2,1,0:T(8,128)(2,1)}) %all-gather.9.cloned.1.call-update) | async-done | bytes 8388624 | tf_op jit(solution)/shard_map/all_gather | solution.py:211
  218.8 0.0 all-to-all-done.6
  218.8 5.9 %block.6 = bf16[128,3072]{1,0:T(8,128)(2,1)S(1)} custom-call(s32[2]{0:T(128)S(1)} %pad_add_fusion.place_ref, bf16[128,3072]{1,0:T(8,128)(2,1)S(1)} %bitcast.89, bf16[64,256,256]{2,1,0:T(8,128)(2,1)} %all-gather.9.cloned.1.call-done.pieces_ref), custom_call_target="tpu_custom_call" | custom-call | flops 1006632960 | bytes 9961472 | tf_op jit(solution)/shard_map/block/pallas_call | solution.py:236
  224.6 19.7 %all_to_all.120 = bf16[16,8,3072]{2,1,0:T(8,128)(2,1)S(1)} all-to-all(bf16[16,8,3072]{2,1,0:T(8,128)(2,1)S(1)} %bitcast.92), channel_id=1, replica_groups=mesh['x'=4,'y'=4,'z'=8,'c'=2] {'x','y'}, dimensions={0} | all-to-all | bytes 1572864 | tf_op jit(solution)/shard_map/all_to_all | solution.py:192
  244.4 1.4 middle.5
  245.8 3.7 %all-to-all-start.8 = ((bf16[16,8,3072]{2,1,0:T(8,128)(2,1)}), bf16[16,8,3072]{2,1,0:T(8,128)(2,1)S(1)}, u32[]{:S(2)}, u32[]{:S(2)}) async-start(bf16[16,8,3072]{2,1,0:T(8,128)(2,1)} %bitcast.37), calls=%async_computation.8 | async-start | bytes 1572864 | tf_op jit(solution)/shard_map/all_to_all | solution.py:192
  249.5 25.5 %all-gather.11.cloned.1.call-done.pieces_ref = bf16[64,256,256]{2,1,0:T(8,128)(2,1)} async-done(((bf16[4,256,256]{2,1,0:T(8,128)(2,1)}), bf16[64,256,256]{2,1,0:T(8,128)(2,1)}) %all-gather.11.cloned.1.call-update) | async-done | bytes 8388624 | tf_op jit(solution)/shard_map/all_gather | solution.py:211
  275.0 6.8 %block.7 = bf16[128,3072]{1,0:T(8,128)(2,1)} custom-call(s32[2]{0:T(128)S(1)} %pad_add_fusion.place_ref, bf16[128,3072]{1,0:T(8,128)(2,1)S(1)} %bitcast.87, bf16[64,256,256]{2,1,0:T(8,128)(2,1)} %all-gather.11.cloned.1.call-done.pieces_ref), custom_call_target="tpu_custom_call" | custom-call | flops 1006632960 | bytes 9961472 | tf_op jit(solution)/shard_map/block/pallas_call | solution.py:236
  281.8 6.5 %all-to-all-start.9 = ((bf16[16,8,3072]{2,1,0:T(8,128)(2,1)}), bf16[16,8,3072]{2,1,0:T(8,128)(2,1)S(1)}, u32[]{:S(2)}, u32[]{:S(2)}) async-start(bf16[16,8,3072]{2,1,0:T(8,128)(2,1)} %bitcast.39), calls=%async_computation.9 | async-start | bytes 1572864 | tf_op jit(solution)/shard_map/all_to_all | solution.py:192
  288.4 0.2 reshape.85
  288.6 0.2 reshape.86
  288.8 0.2 reshape.87
  289.0 0.2 reshape.88
  289.2 0.2 reshape.89
  289.4 0.2 reshape.90
  289.6 11.5 %all-to-all-done.9 = bf16[16,8,3072]{2,1,0:T(8,128)(2,1)S(1)} async-done(((bf16[16,8,3072]{2,1,0:T(8,128)(2,1)}), bf16[16,8,3072]{2,1,0:T(8,128)(2,1)S(1)}, u32[]{:S(2)}, u32[]{:S(2)}) %all-to-all-start.9) | async-done | bytes 786464 | tf_op jit(solution)/shard_map/all_to_all | solution.py:192
  301.0 0.1 last.1
  301.2 0.2 reshape.91
  301.4 0.2 reshape.92
  301.6 7.8 %all_to_all.121 = bf16[4,8,3072]{2,1,0:T(8,128)(2,1)S(1)} all-to-all(bf16[4,8,3072]{2,1,0:T(8,128)(2,1)S(1)} %maximum_bitcast_fusion), channel_id=1, replica_groups=mesh['x'=4,'y'=4,'z'=8,'c'=2] {'x'}, dimensions={0} | all-to-all | bytes 393216 | tf_op jit(solution)/shard_map/all_to_all | solution.py:192
  309.4 0.2 copy.43
  309.6 18.2 %all_to_all.122 = bf16[16,2,3072]{2,1,0:T(2,128)(2,1)S(1)} all-to-all(bf16[16,2,3072]{2,1,0:T(2,128)(2,1)S(1)} %copy.43), channel_id=1, replica_groups=mesh['x'=4,'y'=4,'z'=8,'c'=2] {'z','c'}, dimensions={0} | all-to-all | bytes 393216 | tf_op jit(solution)/shard_map/all_to_all | solution.py:192
  327.8 0.8 broadcast_in_dim.3
  (15 shorter events, 0.2 us)
Async XLA Ops:
  6.5 40.9 %copy-start.2 = (bf16[32,1,3072]{2,0,1:T(8,128)(2,1)S(1)}, bf16[32,1,3072]{2,0,1:T(8,128)(2,1)}, u32[]{:S(2)}) copy-start(bf16[32,1,3072]{2,0,1:T(8,128)(2,1)} %param.5) | copy-start | bytes 589828
  6.5 52.8 %copy-start.3 = (f32[1,3,3072]{2,0,1:T(1,128)S(1)}, f32[1,3,3072]{2,0,1:T(1,128)}, u32[]{:S(2)}) copy-start(f32[1,3,3072]{2,0,1:T(1,128)} %param.6) | copy-start | bytes 110596
  6.5 101.3 %all-gather.5.cloned.1.call-start = ((), (), s32[]{:S(2)}) async-start(), calls=%async_computation.12 | async-start | bytes 8912896 | tf_op jit(solution)/shard_map/all_gather | solution.py:211
  7.6 1.2 copy-start
  8.8 1.0 copy-start.1
  45.4 117.1 %all-gather.7.cloned.1.call-start = ((), (), s32[]{:S(2)}) async-start(), calls=%async_computation.13 | async-start | bytes 8912896 | tf_op jit(solution)/shard_map/all_gather | solution.py:211
  46.1 172.7 %all-gather.9.cloned.1.call-start = ((), (), s32[]{:S(2)}) async-start(), calls=%async_computation.14 | async-start | bytes 8912896 | tf_op jit(solution)/shard_map/all_gather | solution.py:211
  46.8 228.2 %all-gather.11.cloned.1.call-start = ((), (), s32[]{:S(2)}) async-start(), calls=%async_computation.15 | async-start | bytes 8912896 | tf_op jit(solution)/shard_map/all_gather | solution.py:211
  48.2 23.6 %all-to-all-start = ((bf16[16,2,3072]{2,1,0:T(2,128)(2,1)}), bf16[16,2,3072]{2,1,0:T(2,128)(2,1)S(1)}, u32[]{:S(2)}, u32[]{:S(2)}) async-start(bf16[16,2,3072]{2,1,0:T(2,128)(2,1)} %all_to_all.75), calls=%async_computation | async-start | bytes 393216 | tf_op jit(solution)/shard_map/all_to_all | solution.py:192
  73.4 16.4 %all-to-all-start.1 = ((bf16[16,8,3072]{2,1,0:T(8,128)(2,1)}), bf16[16,8,3072]{2,1,0:T(8,128)(2,1)S(1)}, u32[]{:S(2)}, u32[]{:S(2)}) async-start(bf16[16,8,3072]{2,1,0:T(8,128)(2,1)} %bitcast.8), calls=%async_computation.1 | async-start | bytes 1572864 | tf_op jit(solution)/shard_map/all_to_all | solution.py:192
  132.8 29.6 %all-to-all-start.4 = ((bf16[16,8,3072]{2,1,0:T(8,128)(2,1)}), bf16[16,8,3072]{2,1,0:T(8,128)(2,1)S(1)}, u32[]{:S(2)}, u32[]{:S(2)}) async-start(bf16[16,8,3072]{2,1,0:T(8,128)(2,1)} %bitcast.21), calls=%async_computation.4 | async-start | bytes 1572864 | tf_op jit(solution)/shard_map/all_to_all | solution.py:192
  189.4 29.4 %all-to-all-start.6 = ((bf16[16,8,3072]{2,1,0:T(8,128)(2,1)}), bf16[16,8,3072]{2,1,0:T(8,128)(2,1)S(1)}, u32[]{:S(2)}, u32[]{:S(2)}) async-start(bf16[16,8,3072]{2,1,0:T(8,128)(2,1)} %bitcast.29), calls=%async_computation.6 | async-start | bytes 1572864 | tf_op jit(solution)/shard_map/all_to_all | solution.py:192
  245.8 29.3 %all-to-all-start.8 = ((bf16[16,8,3072]{2,1,0:T(8,128)(2,1)}), bf16[16,8,3072]{2,1,0:T(8,128)(2,1)S(1)}, u32[]{:S(2)}, u32[]{:S(2)}) async-start(bf16[16,8,3072]{2,1,0:T(8,128)(2,1)} %bitcast.37), calls=%async_computation.8 | async-start | bytes 1572864 | tf_op jit(solution)/shard_map/all_to_all | solution.py:192
  281.8 19.2 %all-to-all-start.9 = ((bf16[16,8,3072]{2,1,0:T(8,128)(2,1)}), bf16[16,8,3072]{2,1,0:T(8,128)(2,1)S(1)}, u32[]{:S(2)}, u32[]{:S(2)}) async-start(bf16[16,8,3072]{2,1,0:T(8,128)(2,1)} %bitcast.39), calls=%async_computation.9 | async-start | bytes 1572864 | tf_op jit(solution)/shard_map/all_to_all | solution.py:192
Sparse Core Ops, SparseCore 0:
  45.5 62.3 all-gather.4
  109.7 52.6 all-gather.6
  164.3 54.4 all-gather.8
  220.4 54.5 all-gather.10

commit v2 on v1

v2 whole, which is shorter than its diff:
```python
import math

import jax
import jax.numpy as jnp
from jax import lax
from jax.experimental import pallas as pl
from jax.experimental.pallas import tpu as pltpu
from jax.sharding import Mesh
from jax.sharding import PartitionSpec as P

D = 3072
HEADS = 24
HD = 128
PT = 64
PATCHES = 32
BLOCKS = 4
NX, NY, NZ, NC = 4, 4, 8, 2
SP = ("y", "z", "c")
HEAD_AXES = ("x", "y")
REST_AXES = ("z", "c")
MEMBERS = NX * NY
SOURCES = NY * NZ * NC
ROWS = D // SOURCES
OWN = 8
LOCAL = 2 * PT
AT_OUT, AT_K, AT_V, AT_HALF = 3 * ROWS, 4 * ROWS, 4 * ROWS + PATCHES, 4 * ROWS + 2 * PATCHES
HALF = 2 * ROWS + PATCHES
PIECE = AT_HALF + HALF
VMEM = pl.BlockSpec(memory_space=pltpu.VMEM)
ANY = pl.BlockSpec(memory_space=pl.ANY)
SMEM = pl.BlockSpec(memory_space=pltpu.SMEM)
PARAMS = pltpu.CompilerParams(vmem_limit_bytes=48 * 1024 * 1024)


def head_norm(values):
    return (
        values * lax.rsqrt(jnp.mean(values * values, axis=-1, keepdims=True) + 1e-06)
    ).astype(jnp.bfloat16)


def modulate(rows, shift_term, scale_term):
    average = jnp.mean(rows, axis=-1, keepdims=True)
    centered = rows - average
    variance = jnp.mean(centered * centered, axis=-1, keepdims=True)
    return (centered * lax.rsqrt(variance + 1e-06) * (1.0 + scale_term) + shift_term).astype(
        jnp.bfloat16
    )


def pack_kernel(qkv_ref, out_ref, stale_ref, sent_ref):
    def columns(head):
        return slice(head * HD, (head + 1) * HD)

    def weight(part, head):
        if part == 3:
            return out_ref[:, columns(head)]
        return qkv_ref[:, columns(part * HEADS + head)]

    for member in range(MEMBERS):
        triple, half = divmod(member, 2)
        own, shared = 3 * triple + 2 * half, 3 * triple + 1
        for part in range(4):
            sent_ref[member, part * ROWS : (part + 1) * ROWS, :] = weight(part, own)
        sent_ref[member, AT_K:AT_V, :] = stale_ref[0, :, columns(own)]
        sent_ref[member, AT_V:AT_HALF, :] = stale_ref[1, :, columns(own)]
        for at in range(2):
            low = AT_HALF + at * ROWS
            sent_ref[member, low : low + ROWS, :] = weight(2 * half + at, shared)
        sent_ref[member, AT_HALF + 2 * ROWS : PIECE, :] = stale_ref[half, :, columns(shared)]


def first_kernel(place_ref, rows_ref, shift_ref, scale_ref, normed_ref, core_ref):
    core_ref[0] = place_ref[2]
    normed = modulate(rows_ref[...].astype(jnp.float32), shift_ref[...], scale_ref[...])
    twice = jnp.concatenate([normed, normed], axis=0)
    for at in range(0, LOCAL, 2 * OWN):
        normed_ref[at : at + 2 * OWN, :] = twice


def sum_rows(parts_ref, rows_ref, gate_ref):
    total = jnp.zeros((2 * OWN, D), jnp.float32)
    for at in range(0, LOCAL, 2 * OWN):
        total = total + parts_ref[at : at + 2 * OWN, :].astype(jnp.float32)
    summed = total[:OWN] + total[OWN:]
    return (rows_ref[...].astype(jnp.float32) + gate_ref[...] * summed).astype(jnp.bfloat16)


def middle_kernel(
    place_ref,
    parts_ref,
    rows_ref,
    gate_ref,
    shift_ref,
    scale_ref,
    updated_ref,
    normed_ref,
    core_ref,
):
    core_ref[0] = place_ref[2]
    updated = sum_rows(parts_ref, rows_ref, gate_ref)
    updated_ref[...] = updated
    normed = modulate(updated.astype(jnp.float32), shift_ref[...], scale_ref[...])
    twice = jnp.concatenate([normed, normed], axis=0)
    for at in range(0, LOCAL, 2 * OWN):
        normed_ref[at : at + 2 * OWN, :] = twice


def after_kernel(array_ref, earlier_ref, same_ref):
    del array_ref, earlier_ref, same_ref


def last_kernel(parts_ref, rows_ref, gate_ref, updated_ref):
    updated_ref[...] = sum_rows(parts_ref, rows_ref, gate_ref)


def across(left, right):
    return lax.dot_general(
        left, right, (((1,), (1,)), ((), ())), preferred_element_type=jnp.float32
    )


def block_kernel(
    place_ref,
    rows_ref,
    pieces_ref,
    near_ref,
    far_ref,
    partial_ref,
    w_q,
    w_k,
    w_v,
    w_o,
    keys,
    values,
    w_qv,
    w_ko,
    shared,
    sems,
):
    first_patch, half, core = place_ref[0], place_ref[1], place_ref[2]
    copies = []

    def fetch(source, target):
        copies.append(pltpu.make_async_copy(source, target, sems.at[len(copies)]))

    def fetch_half(target, low, count):
        fetch(pieces_ref.at[:, :, :, AT_HALF + low : AT_HALF + low + count, :], target.at[half])
        fetch(near_ref.at[:, :, low : low + count, :], target.at[1 - half, :, core])
        fetch(far_ref.at[:, :, low : low + count, :], target.at[1 - half, :, 1 - core])

    for number, target in enumerate((w_q, w_k, w_v)):
        fetch(pieces_ref.at[:, :, :, number * ROWS : (number + 1) * ROWS, :], target)
    fetch_half(w_qv, 0, ROWS)
    fetch_half(w_ko, ROWS, ROWS)
    fetch(pieces_ref.at[:, :, :, AT_K:AT_V, :], keys)
    fetch(pieces_ref.at[:, :, :, AT_V:AT_HALF, :], values)
    fetch_half(shared, 2 * ROWS, PATCHES)
    fetch(pieces_ref.at[:, :, :, AT_OUT:AT_K, :], w_o)
    for copy in copies:
        copy.start()
    rows = rows_ref[...]

    def both(own, other):
        return jnp.concatenate([own.reshape(D, HD), other.reshape(D, HD)], axis=1)

    def project(own, other):
        return jnp.dot(rows, both(own, other), preferred_element_type=jnp.float32)

    for copy in copies[:9]:
        copy.wait()
    q = project(w_q[...], w_qv[0])
    k = project(w_k[...], w_ko[0])
    v = project(w_v[...], w_qv[1]).astype(jnp.bfloat16)
    queries = [head_norm(q[:, :HD]), head_norm(q[:, HD:])]
    fresh_keys = [head_norm(k[:, :HD]), head_norm(k[:, HD:])]
    fresh_values = [v[:, :HD], v[:, HD:]]
    for own in (queries, fresh_keys, fresh_values):
        own[1] = jnp.where(half == 0, own[1][:PT], own[1][PT:])
    for copy in copies[9:14]:
        copy.wait()
    scale = 1.0 / math.sqrt(HD)
    step = 2
    some = step * NC * NY * PATCHES
    results = []
    for at in range(2):
        asking = queries[at]
        count = asking.shape[0]
        fresh = jnp.exp(across(asking, fresh_keys[at]) * scale)
        row_at = lax.broadcasted_iota(jnp.int32, (count, 1), 0)
        if at == 0:
            row_patch = first_patch + (row_at >= PT).astype(jnp.int32)
            column_at = lax.broadcasted_iota(jnp.int32, (count, count), 1)
            fresh = jnp.where((row_at >= PT) == (column_at >= PT), fresh, 0.0)
        else:
            row_patch = jnp.full((count, 1), first_patch + half, jnp.int32)
        total = jnp.sum(fresh, axis=1, keepdims=True)
        gathered = jnp.dot(
            fresh.astype(jnp.bfloat16), fresh_values[at], preferred_element_type=jnp.float32
        )
        patch_of = lax.broadcasted_iota(jnp.int32, (count, some), 1) % PATCHES
        stale_here = patch_of != row_patch
        for low in range(0, NZ, step):
            if at == 0:
                some_keys, some_values = keys[low : low + step], values[low : low + step]
            else:
                some_keys, some_values = shared[0, low : low + step], shared[1, low : low + step]
            some_keys, some_values = some_keys.reshape(some, HD), some_values.reshape(some, HD)
            numerator = jnp.where(stale_here, jnp.exp(across(asking, some_keys) * scale), 0.0)
            total = total + jnp.sum(numerator, axis=1, keepdims=True)
            gathered = gathered + jnp.dot(
                numerator.astype(jnp.bfloat16), some_values, preferred_element_type=jnp.float32
            )
        results.append((gathered / total).astype(jnp.bfloat16))
    answer = results[1]
    nothing = jnp.zeros_like(answer)
    answer = jnp.concatenate(
        [jnp.where(half == 0, answer, nothing), jnp.where(half == 0, nothing, answer)], axis=0
    )
    attention = jnp.concatenate([results[0], answer], axis=1)
    copies[14].wait()
    width = NC * NY * ROWS
    for low in range(NZ):
        weight = jnp.concatenate(
            [w_o[low].reshape(width, HD), w_ko[1, low].reshape(width, HD)], axis=1
        )
        partial_ref[:, low * width : (low + 1) * width] = across(attention, weight).astype(
            jnp.bfloat16
        )


def to_own_order(array):
    lead = array.shape[:-1]
    split = array.reshape(lead + (NY, NZ * NC, ROWS))
    return jnp.swapaxes(split, -3, -2).reshape(lead + (D,))


def to_given_order(array):
    lead = array.shape[:-1]
    split = array.reshape(lead + (NZ * NC, NY, ROWS))
    return jnp.swapaxes(split, -3, -2).reshape(lead + (D,))


def exchange(array, axes):
    return lax.all_to_all(array, axes, split_axis=0, concat_axis=0, tiled=True)


def body(latent, modulation, w_qkv, w_out, stale):
    x_at, y_at = lax.axis_index("x"), lax.axis_index("y")
    pair_at = lax.axis_index("z") * NC + lax.axis_index("c")
    core_at = lax.axis_index("c")
    place = jnp.stack([2 * pair_at, y_at % 2, core_at]).astype(jnp.int32)

    sent = pl.pallas_call(
        pack_kernel,
        out_shape=jax.ShapeDtypeStruct((MEMBERS, PIECE, HD), jnp.bfloat16),
        in_specs=[VMEM] * 3,
        out_specs=VMEM,
        compiler_params=PARAMS,
        name="pack",
    )(w_qkv[0], w_out[0].T, jnp.swapaxes(stale[0, :, 0], 0, 1))
    received = exchange(sent, HEAD_AXES).reshape(BLOCKS, NY, PIECE, HD)

    def gather(block):
        gathered = lax.all_gather(received[block], REST_AXES, axis=0, tiled=True)
        return gathered.reshape(NZ, NC, NY, PIECE, HD)

    def after(array, earlier):
        return pl.pallas_call(
            after_kernel,
            out_shape=jax.ShapeDtypeStruct(array.shape, array.dtype),
            in_specs=[ANY, ANY],
            out_specs=ANY,
            input_output_aliases={0: 0},
            name="after",
        )(array, earlier)

    pieces = [gather(block) for block in range(BLOCKS)]

    terms = to_own_order(lax.all_gather(modulation[0], "x", axis=0, tiled=False))
    mine = exchange(latent[:, 0], REST_AXES).reshape(NZ * NC, 2, D)
    mine = jnp.swapaxes(mine, 0, 1).reshape(NZ * NC * 2, D)
    current = to_own_order(lax.dynamic_slice_in_dim(mine, x_at * OWN, OWN, 0))

    def term(block, which):
        return terms[block, which][None]

    spread = jax.ShapeDtypeStruct((LOCAL, D), jnp.bfloat16)
    owned = jax.ShapeDtypeStruct((OWN, D), jnp.bfloat16)
    index = jax.ShapeDtypeStruct((1,), jnp.int32)
    normed, core = pl.pallas_call(
        first_kernel,
        out_shape=(spread, index),
        in_specs=[SMEM] + [VMEM] * 3,
        out_specs=(VMEM, SMEM),
        compiler_params=PARAMS,
        name="first",
    )(place, current, term(0, 0), term(0, 1))
    outputs = []
    for block in range(BLOCKS):
        half = lax.dynamic_slice(
            pieces[block], (0, core[0], 0, AT_HALF, 0), (NZ, 1, NY, HALF, HD)
        ).reshape(NZ, NY, HALF, HD)
        near = lax.ppermute(half, "y", [(at, at ^ 1) for at in range(NY)])
        rows = exchange(normed, HEAD_AXES)
        near = after(near, rows)
        far = lax.ppermute(near, "c", [(0, 1), (1, 0)])
        partial = pl.pallas_call(
            block_kernel,
            out_shape=spread,
            in_specs=[
                SMEM,
                VMEM,
                ANY,
                ANY,
                ANY,
            ],
            out_specs=VMEM,
            scratch_shapes=[pltpu.VMEM((NZ, NC, NY, ROWS, HD), jnp.bfloat16)] * 4
            + [pltpu.VMEM((NZ, NC, NY, PATCHES, HD), jnp.bfloat16)] * 2
            + [pltpu.VMEM((2, NZ, NC, NY, ROWS, HD), jnp.bfloat16)] * 2
            + [pltpu.VMEM((2, NZ, NC, NY, PATCHES, HD), jnp.bfloat16)]
            + [pltpu.SemaphoreType.DMA((15,))],
            compiler_params=PARAMS,
            cost_estimate=pl.CostEstimate(
                flops=2 * LOCAL * D * 2 * HD * 4 + 4 * 3 * PT * 2048 * HD,
                bytes_accessed=SOURCES * PIECE * HD * 2 + 4 * LOCAL * D,
                transcendentals=3 * PT * 2048,
            ),
            name="block",
        )(place, rows, pieces[block], near, far)
        parts = exchange(partial, HEAD_AXES)
        if block + 1 < BLOCKS:
            current, normed, core = pl.pallas_call(
                middle_kernel,
                out_shape=(owned, spread, index),
                in_specs=[SMEM] + [VMEM] * 5,
                out_specs=(VMEM, VMEM, SMEM),
                compiler_params=PARAMS,
                name="middle",
            )(place, parts, current, term(block, 2), term(block + 1, 0), term(block + 1, 1))
        else:
            current = pl.pallas_call(
                last_kernel,
                out_shape=owned,
                in_specs=[VMEM] * 3,
                out_specs=VMEM,
                compiler_params=PARAMS,
                name="last",
            )(parts, current, term(block, 2))
        outputs.append(to_given_order(current))
    placed = exchange(jnp.concatenate(outputs, axis=0), "x")
    placed = jnp.swapaxes(placed.reshape(2, NZ * NC, D), 0, 1).reshape(PATCHES, D)
    placed = exchange(placed, REST_AXES)
    return placed[None, :, None]


def solution(mesh):
    own_mesh = Mesh(mesh.devices.reshape(NX, NY, NZ, NC), ("x",) + SP)
    return jax.shard_map(
        body,
        mesh=own_mesh,
        in_specs=(
            P(None, SP, None),
            P("x", None, None),
            P("x", SP, None),
            P("x", None, SP),
            P("x", None, SP, None, None),
        ),
        out_specs=P("x", None, SP, None),
        check_vma=False,
    )
```

time: 336 us -> 400 us (1.19)
  blocking collectives: 128 us -> 244 us
  waiting for transfers between devices: 122 us -> 47.1 us
  local copies, waits for them, and re-layouts: 9.18 us -> 27.7 us
  between operations: 13.4 us -> 21.2 us
  starting transfers between devices: 32.7 us -> 28.2 us
    all_to_all x6 -> x10, blocking collectives: 117 us -> 234 us  [exchange(): return lax.all_to_all(array, axes, split_axis=0, concat_axis=0, tiled=True)]
    all_gather x4, waiting for transfers between devices: 95 us -> 22.8 us  [gather(): gathered = lax.all_gather(received[block], REST_AXES, axis=0, tiled=True)]
    all_to_all x6 -> x2, starting transfers between devices: 32.6 us -> 15.1 us  [exchange(): return lax.all_to_all(array, axes, split_axis=0, concat_axis=0, tiled=True)]
    unnamed x10 -> x34, local copies, waits for them, and re-layouts: 3.25 us -> 16.7 us
    ppermute x0 -> x8, starting transfers between devices: none -> 13 us  [the longest x4 10.7 us: body(): far = lax.ppermute(near, 'c', [(0, 1), (1, 0)])]
    all_to_all x6 -> x2, waiting for transfers between devices: 25.1 us -> 12.4 us  [exchange(): return lax.all_to_all(array, axes, split_axis=0, concat_axis=0, tiled=True)]
    ppermute x0 -> x8, waiting for transfers between devices: none -> 10 us  [the longest x4 9.99 us: body(): far = lax.ppermute(near, 'c', [(0, 1), (1, 0)])]
    reshape x0 -> x4, local copies, waits for them, and re-layouts: none -> 5.26 us  [body(): half = lax.dynamic_slice(pieces[block], (0, core[0], 0, AT_HALF, 0), (NZ,...]
  transfers between devices with their start and end apart: 10 -> 14, of which waited for: 7 -> 7; matrix products, arithmetic and copies ran while one was open for 1% -> 2% of each run, Pallas kernels for 7% -> 6%
where the time goes in v2:
time: 400 us; the launch traced here: 398 us
  blocking collectives  244 us (61%)
  waiting for transfers between devices  47.1 us (12%)
  Pallas kernels  30 us (8%)
  starting transfers between devices  28.2 us (7%)
  local copies, waits for them, and re-layouts  27.7 us (7%)
  between operations  21.2 us (5%)
    all_to_all x10, blocking collectives, exchange(): return lax.all_to_all(array, axes, split_axis=0, concat_axis=0, tiled=True)  234 us
    pallas_call x4, Pallas kernels, body(): pl.pallas_call(block_kernel, out_shape=spread, in_specs=[SMEM, VMEM, ANY,...  24.9 us
    all_gather x4, waiting for transfers between devices, gather(): gathered = lax.all_gather(received[block], REST_AXES, axis=0, tiled=True)  22.8 us
    unnamed x34, local copies, waits for them, and re-layouts  16.7 us
    all_to_all x2, starting transfers between devices, exchange(): return lax.all_to_all(array, axes, split_axis=0, concat_axis=0, tiled=True)  15.1 us
    all_to_all x2, waiting for transfers between devices, exchange(): return lax.all_to_all(array, axes, split_axis=0, concat_axis=0, tiled=True)  12.4 us
    ppermute x4, starting transfers between devices, body(): far = lax.ppermute(near, 'c', [(0, 1), (1, 0)])  10.7 us
    all_gather x1, blocking collectives, body(): lax.all_gather(modulation[0], 'x', axis=0, tiled=False)  10.5 us
  transfers between devices with their start and end apart: 14, of which 7 were waited for; matrix products, arithmetic and copies ran while one was open for 2% of the time, Pallas kernels for 6%

profile of v2, /device:TPU:1, one launch (start us, length us, event | category | flops | bytes accessed | tf_op | source)
XLA Modules:
  0.0 398.4 jit_solution(5367856983339016902)
XLA Ops:
  6.5 1.1 copy.53
  7.7 1.2 copy-done.12
  8.8 1.0 copy-done.13
  9.8 0.3 pack.1
  10.1 28.9 %all_to_all.117 = bf16[16,384,128]{2,1,0:T(8,128)(2,1)S(1)} all-to-all(bf16[16,384,128]{2,1,0:T(8,128)(2,1)S(1)} %pack.1), channel_id=1, replica_groups=mesh['x'=4,'y'=4,'z'=8,'c'=2] {'x','y'}, dimensions={0} | all-to-all | bytes 3145728 | tf_op jit(solution)/shard_map/all_to_all | solution.py:244
  38.9 1.2 fusion
  40.2 0.7 all-gather.7.cloned.1.call-update
  41.0 0.7 all-gather.9.cloned.1.call-update
  41.7 0.5 all-gather.11.cloned.1.call-update
  42.2 0.8 all_to_all.75
  43.0 10.5 %all-to-all-start = ((bf16[16,2,3072]{2,1,0:T(2,128)(2,1)}), bf16[16,2,3072]{2,1,0:T(2,128)(2,1)S(1)}, u32[]{:S(2)}, u32[]{:S(2)}) async-start(bf16[16,2,3072]{2,1,0:T(2,128)(2,1)} %all_to_all.75), calls=%async_computation | async-start | bytes 393216 | tf_op jit(solution)/shard_map/all_to_all | solution.py:244
  53.5 10.5 %all_gather.15 = f32[4,3,3072]{2,1,0:T(4,128)S(1)} all-gather(f32[1,3,3072]{2,1,0:T(4,128)S(1)} %copy.39), channel_id=1, replica_groups=mesh['x'=4,'y'=4,'z'=8,'c'=2] {'x'}, dimensions={0}, use_global_device_ids=true | all-gather | bytes 184320 | tf_op jit(solution)/shard_map/all_gather | solution.py:279
  64.4 0.4 reshape.108
  65.0 0.9 all-to-all-done
  66.4 1.1 first.1
  69.4 22.7 %all-gather.5.cloned.1.call-done = bf16[64,384,128]{2,1,0:T(8,128)(2,1)} async-done(((bf16[4,384,128]{2,1,0:T(8,128)(2,1)}), bf16[64,384,128]{2,1,0:T(8,128)(2,1)}) %all-gather.5.cloned.1.call-update) | async-done | bytes 6291472 | tf_op jit(solution)/shard_map/all_gather | solution.py:264
  92.1 1.3 dynamic-slice_bitcast_fusion.3
  93.4 1.1 collective-permute-start
  94.5 33.0 %all_to_all.118 = bf16[16,8,3072]{2,1,0:T(8,128)(2,1)} all-to-all(bf16[16,8,3072]{2,1,0:T(8,128)(2,1)S(1)} %bitcast.123), channel_id=1, replica_groups=mesh['x'=4,'y'=4,'z'=8,'c'=2] {'x','y'}, dimensions={0} | all-to-all | bytes 1572864 | tf_op jit(solution)/shard_map/all_to_all | solution.py:244
  127.6 1.0 copy-done.4
  128.5 1.3 collective-permute-start.1
  129.8 2.5 collective-permute-done.1.far_ref
  132.3 1.1 copy-done.1
  133.4 1.2 copy-done.5
  134.6 6.0 %block.4 = bf16[128,3072]{1,0:T(8,128)(2,1)S(1)} custom-call(s32[3]{0:T(128)S(1)} %pad_add_fusion.place_ref, bf16[128,3072]{1,0:T(8,128)(2,1)S(1)} %bitcast.106, bf16[8,2,4,384,128]{4,3,2,1,0:T(8,128)(2,1)} %bitcast.132, bf16[8,4,128,128]{3,2,1,0:T(8,128)(2,1)S(1)} %copy-done.5, bf16[8,4,128,128]{3,2,1,0:T(8,128)(2,1)S(1)} %collective-permute-done.1.far_ref), custom_call_target="tpu_custom_call" | custom-call | flops 1006632960 | bytes 7864320 | tf_op jit(solution)/shard_map/block/pallas_call | solution.py:307
  140.6 17.6 %all_to_all.119 = bf16[16,8,3072]{2,1,0:T(8,128)(2,1)S(1)} all-to-all(bf16[16,8,3072]{2,1,0:T(8,128)(2,1)S(1)} %bitcast.111), channel_id=1, replica_groups=mesh['x'=4,'y'=4,'z'=8,'c'=2] {'x','y'}, dimensions={0} | all-to-all | bytes 1572864 | tf_op jit(solution)/shard_map/all_to_all | solution.py:244
  158.2 1.2 middle.3
  161.4 1.4 dynamic-slice_bitcast_fusion.2
  162.8 0.4 collective-permute-start.2
  163.2 30.9 %all_to_all.120 = bf16[16,8,3072]{2,1,0:T(8,128)(2,1)} all-to-all(bf16[16,8,3072]{2,1,0:T(8,128)(2,1)S(1)} %bitcast.121), channel_id=1, replica_groups=mesh['x'=4,'y'=4,'z'=8,'c'=2] {'x','y'}, dimensions={0} | all-to-all | bytes 1572864 | tf_op jit(solution)/shard_map/all_to_all | solution.py:244
  194.0 1.0 copy-done.6
  195.0 3.2 collective-permute-start.3
  198.2 2.5 collective-permute-done.3.far_ref
  200.7 1.2 copy-done.2
  201.8 1.2 copy-done.7
  203.1 6.1 %block.5 = bf16[128,3072]{1,0:T(8,128)(2,1)S(1)} custom-call(s32[3]{0:T(128)S(1)} %pad_add_fusion.place_ref, bf16[128,3072]{1,0:T(8,128)(2,1)S(1)} %bitcast.108, bf16[8,2,4,384,128]{4,3,2,1,0:T(8,128)(2,1)} %bitcast.130, bf16[8,4,128,128]{3,2,1,0:T(8,128)(2,1)S(1)} %copy-done.7, bf16[8,4,128,128]{3,2,1,0:T(8,128)(2,1)S(1)} %collective-permute-done.3.far_ref), custom_call_target="tpu_custom_call" | custom-call | flops 1006632960 | bytes 7864320 | tf_op jit(solution)/shard_map/block/pallas_call | solution.py:307
  209.2 17.5 %all_to_all.121 = bf16[16,8,3072]{2,1,0:T(8,128)(2,1)S(1)} all-to-all(bf16[16,8,3072]{2,1,0:T(8,128)(2,1)S(1)} %bitcast.112), channel_id=1, replica_groups=mesh['x'=4,'y'=4,'z'=8,'c'=2] {'x','y'}, dimensions={0} | all-to-all | bytes 1572864 | tf_op jit(solution)/shard_map/all_to_all | solution.py:244
  226.7 1.2 middle.4
  229.9 1.3 dynamic-slice_bitcast_fusion.1
  231.2 0.4 collective-permute-start.4
  231.6 30.9 %all_to_all.122 = bf16[16,8,3072]{2,1,0:T(8,128)(2,1)} all-to-all(bf16[16,8,3072]{2,1,0:T(8,128)(2,1)S(1)} %bitcast.122), channel_id=1, replica_groups=mesh['x'=4,'y'=4,'z'=8,'c'=2] {'x','y'}, dimensions={0} | all-to-all | bytes 1572864 | tf_op jit(solution)/shard_map/all_to_all | solution.py:244
  262.5 1.0 copy-done.8
  263.4 3.2 collective-permute-start.5
  266.6 2.5 collective-permute-done.5.far_ref
  269.1 1.1 copy-done.3
  270.3 1.2 copy-done.9
  271.5 6.0 %block.6 = bf16[128,3072]{1,0:T(8,128)(2,1)S(1)} custom-call(s32[3]{0:T(128)S(1)} %pad_add_fusion.place_ref, bf16[128,3072]{1,0:T(8,128)(2,1)S(1)} %bitcast.110, bf16[8,2,4,384,128]{4,3,2,1,0:T(8,128)(2,1)} %bitcast.128, bf16[8,4,128,128]{3,2,1,0:T(8,128)(2,1)S(1)} %copy-done.9, bf16[8,4,128,128]{3,2,1,0:T(8,128)(2,1)S(1)} %collective-permute-done.5.far_ref), custom_call_target="tpu_custom_call" | custom-call | flops 1006632960 | bytes 7864320 | tf_op jit(solution)/shard_map/block/pallas_call | solution.py:307
  277.5 17.5 %all_to_all.123 = bf16[16,8,3072]{2,1,0:T(8,128)(2,1)S(1)} all-to-all(bf16[16,8,3072]{2,1,0:T(8,128)(2,1)S(1)} %bitcast.113), channel_id=1, replica_groups=mesh['x'=4,'y'=4,'z'=8,'c'=2] {'x','y'}, dimensions={0} | all-to-all | bytes 1572864 | tf_op jit(solution)/shard_map/all_to_all | solution.py:244
  295.0 1.2 middle.5
  298.1 1.3 dynamic-slice_bitcast_fusion
  299.4 0.4 collective-permute-start.6
  299.8 30.9 %all_to_all.124 = bf16[16,8,3072]{2,1,0:T(8,128)(2,1)} all-to-all(bf16[16,8,3072]{2,1,0:T(8,128)(2,1)S(1)} %bitcast.120), channel_id=1, replica_groups=mesh['x'=4,'y'=4,'z'=8,'c'=2] {'x','y'}, dimensions={0} | all-to-all | bytes 1572864 | tf_op jit(solution)/shard_map/all_to_all | solution.py:244
  330.8 1.0 copy-done.10
  331.8 3.1 collective-permute-start.7
  334.9 2.5 collective-permute-done.7.far_ref
  337.4 1.1 copy-done
  338.5 1.2 copy-done.11
  339.7 6.9 %block.7 = bf16[128,3072]{1,0:T(8,128)(2,1)} custom-call(s32[3]{0:T(128)S(1)} %pad_add_fusion.place_ref, bf16[128,3072]{1,0:T(8,128)(2,1)S(1)} %bitcast.104, bf16[8,2,4,384,128]{4,3,2,1,0:T(8,128)(2,1)} %bitcast.126, bf16[8,4,128,128]{3,2,1,0:T(8,128)(2,1)S(1)} %copy-done.11, bf16[8,4,128,128]{3,2,1,0:T(8,128)(2,1)S(1)} %collective-permute-done.7.far_ref), custom_call_target="tpu_custom_call" | custom-call | flops 1006632960 | bytes 7864320 | tf_op jit(solution)/shard_map/block/pallas_call | solution.py:307
  346.6 4.6 %all-to-all-start.9 = ((bf16[16,8,3072]{2,1,0:T(8,128)(2,1)}), bf16[16,8,3072]{2,1,0:T(8,128)(2,1)S(1)}, u32[]{:S(2)}, u32[]{:S(2)}) async-start(bf16[16,8,3072]{2,1,0:T(8,128)(2,1)} %bitcast.52), calls=%async_computation.9 | async-start | bytes 1572864 | tf_op jit(solution)/shard_map/all_to_all | solution.py:244
  352.4 11.5 %all-to-all-done.9 = bf16[16,8,3072]{2,1,0:T(8,128)(2,1)S(1)} async-done(((bf16[16,8,3072]{2,1,0:T(8,128)(2,1)}), bf16[16,8,3072]{2,1,0:T(8,128)(2,1)S(1)}, u32[]{:S(2)}, u32[]{:S(2)}) %all-to-all-start.9) | async-done | bytes 786464 | tf_op jit(solution)/shard_map/all_to_all | solution.py:244
  364.5 7.6 %all_to_all.125 = bf16[4,8,3072]{2,1,0:T(8,128)(2,1)S(1)} all-to-all(bf16[4,8,3072]{2,1,0:T(8,128)(2,1)S(1)} %maximum_bitcast_fusion), channel_id=1, replica_groups=mesh['x'=4,'y'=4,'z'=8,'c'=2] {'x'}, dimensions={0} | all-to-all | bytes 393216 | tf_op jit(solution)/shard_map/all_to_all | solution.py:244
  372.1 0.2 copy.47
  372.3 18.9 %all_to_all.126 = bf16[16,2,3072]{2,1,0:T(2,128)(2,1)S(1)} all-to-all(bf16[16,2,3072]{2,1,0:T(2,128)(2,1)S(1)} %copy.47), channel_id=1, replica_groups=mesh['x'=4,'y'=4,'z'=8,'c'=2] {'z','c'}, dimensions={0} | all-to-all | bytes 393216 | tf_op jit(solution)/shard_map/all_to_all | solution.py:244
  391.1 0.8 broadcast_in_dim.3
  (59 shorter events, 3.0 us)
Async XLA Ops:
  6.5 35.7 %copy-start.14 = (bf16[32,1,3072]{2,0,1:T(8,128)(2,1)S(1)}, bf16[32,1,3072]{2,0,1:T(8,128)(2,1)}, u32[]{:S(2)}) copy-start(bf16[32,1,3072]{2,0,1:T(8,128)(2,1)} %param.5) | copy-start | bytes 589828
  6.5 46.9 %copy-start.15 = (f32[1,3,3072]{2,0,1:T(1,128)S(1)}, f32[1,3,3072]{2,0,1:T(1,128)}, u32[]{:S(2)}) copy-start(f32[1,3,3072]{2,0,1:T(1,128)} %param.6) | copy-start | bytes 110596
  6.5 85.6 %all-gather.5.cloned.1.call-start = ((), (), s32[]{:S(2)}) async-start(), calls=%async_computation.12 | async-start | bytes 6684672 | tf_op jit(solution)/shard_map/all_gather | solution.py:264
  7.6 1.2 copy-start.12
  8.8 1.0 copy-start.13
  40.2 121.2 %all-gather.7.cloned.1.call-start = ((), (), s32[]{:S(2)}) async-start(), calls=%async_computation.13 | async-start | bytes 6684672 | tf_op jit(solution)/shard_map/all_gather | solution.py:264
  40.9 189.0 %all-gather.9.cloned.1.call-start = ((), (), s32[]{:S(2)}) async-start(), calls=%async_computation.14 | async-start | bytes 6684672 | tf_op jit(solution)/shard_map/all_gather | solution.py:264
  41.6 256.5 %all-gather.11.cloned.1.call-start = ((), (), s32[]{:S(2)}) async-start(), calls=%async_computation.15 | async-start | bytes 6684672 | tf_op jit(solution)/shard_map/all_gather | solution.py:264
  43.0 22.9 %all-to-all-start = ((bf16[16,2,3072]{2,1,0:T(2,128)(2,1)}), bf16[16,2,3072]{2,1,0:T(2,128)(2,1)S(1)}, u32[]{:S(2)}, u32[]{:S(2)}) async-start(bf16[16,2,3072]{2,1,0:T(2,128)(2,1)} %all_to_all.75), calls=%async_computation | async-start | bytes 393216 | tf_op jit(solution)/shard_map/all_to_all | solution.py:244
  93.4 34.1 %collective-permute-start = (bf16[8,4,128,128]{3,2,1,0:T(8,128)(2,1)S(1)}, bf16[8,4,128,128]{3,2,1,0:T(8,128)(2,1)S(1)}, u32[]{:S(2)}, u32[]{:S(2)}) collective-permute-start(bf16[8,4,128,128]{3,2,1,0:T(8,128)(2,1)S(1)} %dynamic-slice_bitcast_fusion.3), channel_id=1, source_target_pairs={{0,16},{16,0},{32,48},{48,32},{1,17},{17,1},{33,49},{49,33},{2,18}... | collective-permute-start | bytes 3145736 | tf_op jit(solution)/shard_map/ppermute | solution.py:303
  127.6 1.0 copy-start.4
  128.5 3.7 collective-permute-start.1
  132.3 1.1 copy-start.1
  133.4 1.2 copy-start.5
  162.8 31.3 %collective-permute-start.2 = (bf16[8,4,128,128]{3,2,1,0:T(8,128)(2,1)S(1)}, bf16[8,4,128,128]{3,2,1,0:T(8,128)(2,1)S(1)}, u32[]{:S(2)}, u32[]{:S(2)}) collective-permute-start(bf16[8,4,128,128]{3,2,1,0:T(8,128)(2,1)S(1)} %dynamic-slice_bitcast_fusion.2), channel_id=1, source_target_pairs={{0,16},{16,0},{32,48},{48,32},{1,17},{17,1},{33,49},{49,33},{2,18}... | collective-permute-start | bytes 3145736 | tf_op jit(solution)/shard_map/ppermute | solution.py:303
  194.0 1.0 copy-start.6
  195.0 5.7 %collective-permute-start.3 = (bf16[8,4,128,128]{3,2,1,0:T(8,128)(2,1)}, bf16[8,4,128,128]{3,2,1,0:T(8,128)(2,1)S(1)}, u32[]{:S(2)}, u32[]{:S(2)}) collective-permute-start(bf16[8,4,128,128]{3,2,1,0:T(8,128)(2,1)} %after.5.near_ref), channel_id=1, source_target_pairs={{0,1},{1,0},{2,3},{3,2},{4,5},{5,4},{6,7},{7,6},{8,9},{9,8},{10,11... | collective-permute-start | bytes 3145736 | tf_op jit(solution)/shard_map/ppermute | solution.py:306
  200.7 1.2 copy-start.2
  201.8 1.2 copy-start.7
  231.2 31.3 %collective-permute-start.4 = (bf16[8,4,128,128]{3,2,1,0:T(8,128)(2,1)S(1)}, bf16[8,4,128,128]{3,2,1,0:T(8,128)(2,1)S(1)}, u32[]{:S(2)}, u32[]{:S(2)}) collective-permute-start(bf16[8,4,128,128]{3,2,1,0:T(8,128)(2,1)S(1)} %dynamic-slice_bitcast_fusion.1), channel_id=1, source_target_pairs={{0,16},{16,0},{32,48},{48,32},{1,17},{17,1},{33,49},{49,33},{2,18}... | collective-permute-start | bytes 3145736 | tf_op jit(solution)/shard_map/ppermute | solution.py:303
  262.5 1.0 copy-start.8
  263.4 5.7 %collective-permute-start.5 = (bf16[8,4,128,128]{3,2,1,0:T(8,128)(2,1)}, bf16[8,4,128,128]{3,2,1,0:T(8,128)(2,1)S(1)}, u32[]{:S(2)}, u32[]{:S(2)}) collective-permute-start(bf16[8,4,128,128]{3,2,1,0:T(8,128)(2,1)} %after.6.near_ref), channel_id=1, source_target_pairs={{0,1},{1,0},{2,3},{3,2},{4,5},{5,4},{6,7},{7,6},{8,9},{9,8},{10,11... | collective-permute-start | bytes 3145736 | tf_op jit(solution)/shard_map/ppermute | solution.py:306
  269.1 1.1 copy-start.3
  270.2 1.2 copy-start.9
  299.4 31.3 %collective-permute-start.6 = (bf16[8,4,128,128]{3,2,1,0:T(8,128)(2,1)S(1)}, bf16[8,4,128,128]{3,2,1,0:T(8,128)(2,1)S(1)}, u32[]{:S(2)}, u32[]{:S(2)}) collective-permute-start(bf16[8,4,128,128]{3,2,1,0:T(8,128)(2,1)S(1)} %dynamic-slice_bitcast_fusion), channel_id=1, source_target_pairs={{0,16},{16,0},{32,48},{48,32},{1,17},{17,1},{33,49},{49,33},{2,18}... | collective-permute-start | bytes 3145736 | tf_op jit(solution)/shard_map/ppermute | solution.py:303
  330.8 1.0 copy-start.10
  331.8 5.6 %collective-permute-start.7 = (bf16[8,4,128,128]{3,2,1,0:T(8,128)(2,1)}, bf16[8,4,128,128]{3,2,1,0:T(8,128)(2,1)S(1)}, u32[]{:S(2)}, u32[]{:S(2)}) collective-permute-start(bf16[8,4,128,128]{3,2,1,0:T(8,128)(2,1)} %after.7.near_ref), channel_id=1, source_target_pairs={{0,1},{1,0},{2,3},{3,2},{4,5},{5,4},{6,7},{7,6},{8,9},{9,8},{10,11... | collective-permute-start | bytes 3145736 | tf_op jit(solution)/shard_map/ppermute | solution.py:306
  337.4 1.1 copy-start
  338.5 1.2 copy-start.11
  346.6 17.3 %all-to-all-start.9 = ((bf16[16,8,3072]{2,1,0:T(8,128)(2,1)}), bf16[16,8,3072]{2,1,0:T(8,128)(2,1)S(1)}, u32[]{:S(2)}, u32[]{:S(2)}) async-start(bf16[16,8,3072]{2,1,0:T(8,128)(2,1)} %bitcast.52), calls=%async_computation.9 | async-start | bytes 1572864 | tf_op jit(solution)/shard_map/all_to_all | solution.py:244
Sparse Core Ops, SparseCore 0:
  40.3 51.7 all-gather.4
  93.9 42.8 all-gather.6
  138.6 44.6 all-gather.8
  185.0 44.6 all-gather.10

commit v3 on v1

v3 whole, which is shorter than its diff:
```python
import math

import jax
import jax.numpy as jnp
from jax import lax
from jax.experimental import pallas as pl
from jax.experimental.pallas import tpu as pltpu
from jax.sharding import Mesh
from jax.sharding import PartitionSpec as P

D = 3072
HEADS = 24
HD = 128
PT = 64
PATCHES = 32
BLOCKS = 4
NX, NY, NZ, NC = 4, 4, 8, 2
SP = ("y", "z", "c")
HEAD_AXES = ("x", "y")
REST_AXES = ("z", "c")
MEMBERS = NX * NY
SOURCES = NY * NZ * NC
ROWS = D // SOURCES
OWN = 8
LOCAL = 2 * PT
AT_OUT, AT_K, AT_V, AT_SHARED = 3 * ROWS, 4 * ROWS, 4 * ROWS + PATCHES, 4 * ROWS + 2 * PATCHES
AT_SHARED_OUT = AT_SHARED + 2 * ROWS
AT_SHARED_K = AT_SHARED + 3 * ROWS
AT_SHARED_V = AT_SHARED_K + PATCHES
PIECE = AT_SHARED_V + PATCHES
AT_KEPT = 3 * LOCAL
LEFT = AT_KEPT + 2 * PT
ANY = pl.BlockSpec(memory_space=pl.ANY)
SMEM = pl.BlockSpec(memory_space=pltpu.SMEM)
VMEM = pl.BlockSpec(memory_space=pltpu.VMEM)
PARAMS = pltpu.CompilerParams(vmem_limit_bytes=48 * 1024 * 1024)


def head_norm(values):
    return (
        values * lax.rsqrt(jnp.mean(values * values, axis=-1, keepdims=True) + 1e-06)
    ).astype(jnp.bfloat16)


def modulate(rows, shift_term, scale_term):
    average = jnp.mean(rows, axis=-1, keepdims=True)
    centered = rows - average
    variance = jnp.mean(centered * centered, axis=-1, keepdims=True)
    return (centered * lax.rsqrt(variance + 1e-06) * (1.0 + scale_term) + shift_term).astype(
        jnp.bfloat16
    )


def pack_kernel(qkv_from, out_from, stale_ref, sent_ref, qkv_ref, out_ref, sems):
    copies = [
        pltpu.make_async_copy(qkv_from, qkv_ref, sems.at[0]),
        pltpu.make_async_copy(out_from, out_ref, sems.at[1]),
    ]
    for copy in copies:
        copy.start()

    def columns(head):
        return slice(head * HD, (head + 1) * HD)

    def put(member, low, rows):
        sent_ref[member, low : low + rows.shape[0], :] = rows

    def each():
        for member in range(MEMBERS):
            triple, half = divmod(member, 2)
            yield member, half, 3 * triple + 2 * half, 3 * triple + 1

    for member, half, own, shared in each():
        put(member, AT_K, stale_ref[0, :, columns(own)])
        put(member, AT_V, stale_ref[1, :, columns(own)])
        put(member, AT_SHARED_K, stale_ref[0, :, columns(shared)])
        put(member, AT_SHARED_V, stale_ref[1, :, columns(shared)])
    copies[1].wait()
    for member, half, own, shared in each():
        put(member, AT_OUT, out_ref[:, columns(own)])
        put(member, AT_SHARED_OUT, out_ref[:, columns(shared)])
    copies[0].wait()
    for member, half, own, shared in each():
        for part in range(3):
            put(member, part * ROWS, qkv_ref[:, columns(part * HEADS + own)])
        put(member, AT_SHARED, qkv_ref[:, columns(half * HEADS + shared)])
        put(member, AT_SHARED + ROWS, qkv_ref[:, columns(2 * HEADS + shared)])


def first_kernel(rows_ref, shift_ref, scale_ref, normed_ref):
    normed = modulate(rows_ref[...].astype(jnp.float32), shift_ref[...], scale_ref[...])
    twice = jnp.concatenate([normed, normed], axis=0)
    for at in range(0, LOCAL, 2 * OWN):
        normed_ref[at : at + 2 * OWN, :] = twice


def sum_rows(parts_ref, rows_ref, gate_ref):
    total = jnp.zeros((2 * OWN, D), jnp.float32)
    for at in range(0, LOCAL, 2 * OWN):
        total = total + parts_ref[at : at + 2 * OWN, :].astype(jnp.float32)
    summed = total[:OWN] + total[OWN:]
    return (rows_ref[...].astype(jnp.float32) + gate_ref[...] * summed).astype(jnp.bfloat16)


def middle_kernel(parts_ref, rows_ref, gate_ref, shift_ref, scale_ref, updated_ref, normed_ref):
    updated = sum_rows(parts_ref, rows_ref, gate_ref)
    updated_ref[...] = updated
    normed = modulate(updated.astype(jnp.float32), shift_ref[...], scale_ref[...])
    twice = jnp.concatenate([normed, normed], axis=0)
    for at in range(0, LOCAL, 2 * OWN):
        normed_ref[at : at + 2 * OWN, :] = twice


def last_kernel(parts_ref, rows_ref, gate_ref, updated_ref):
    updated_ref[...] = sum_rows(parts_ref, rows_ref, gate_ref)


def across(left, right):
    return lax.dot_general(
        left, right, (((1,), (1,)), ((), ())), preferred_element_type=jnp.float32
    )


def fetch(pieces_ref, sems, wanted):
    copies = [
        pltpu.make_async_copy(
            pieces_ref.at[:, low : low + target.shape[1], :], target, sems.at[number]
        )
        for number, (target, low) in enumerate(wanted)
    ]
    for copy in copies:
        copy.start()
    return copies


def project_kernel(
    place_ref, rows_ref, pieces_ref, left_ref, given_ref, w_q, w_k, w_v, w_qk, w_sv, sems
):
    weights = (w_q, w_k, w_v, w_qk, w_sv)
    lows = (0, ROWS, 2 * ROWS, AT_SHARED, AT_SHARED + ROWS)
    copies = fetch(pieces_ref, sems, list(zip(weights, lows)))
    half = place_ref[1]
    rows = rows_ref[...]

    def project(*parts):
        weight = jnp.concatenate([part[...].reshape(D, HD) for part in parts], axis=1)
        return jnp.dot(rows, weight, preferred_element_type=jnp.float32)

    def mine(both):
        return jnp.where(half == 0, both[:PT], both[PT:])

    copies[0].wait()
    copies[1].wait()
    first = project(w_q, w_k)
    left_ref[:LOCAL] = head_norm(first[:, :HD])
    left_ref[LOCAL : 2 * LOCAL] = head_norm(first[:, HD:])
    copies[3].wait()
    copies[4].wait()
    second = project(w_qk, w_sv)
    shared = head_norm(second[:, :HD])
    left_ref[AT_KEPT : AT_KEPT + PT] = mine(shared)
    given_ref[...] = jnp.where(half == 0, shared[PT:], shared[:PT])
    left_ref[AT_KEPT + PT :] = mine(second[:, HD:].astype(jnp.bfloat16))
    copies[2].wait()
    left_ref[2 * LOCAL : 3 * LOCAL] = project(w_v).astype(jnp.bfloat16)


def attend(queries, fresh_keys, fresh_values, keys, values, row_patch):
    count = queries.shape[0]
    scale = 1.0 / math.sqrt(HD)
    fresh = jnp.exp(across(queries, fresh_keys) * scale)
    if count > PT:
        row_at = lax.broadcasted_iota(jnp.int32, (count, 1), 0)
        column_at = lax.broadcasted_iota(jnp.int32, (count, count), 1)
        fresh = jnp.where((row_at >= PT) == (column_at >= PT), fresh, 0.0)
    total = jnp.sum(fresh, axis=1, keepdims=True)
    gathered = jnp.dot(
        fresh.astype(jnp.bfloat16), fresh_values, preferred_element_type=jnp.float32
    )
    step = 16
    patch_of = lax.broadcasted_iota(jnp.int32, (count, step * PATCHES), 1) % PATCHES
    stale_here = patch_of != row_patch
    for low in range(0, SOURCES, step):
        some_keys = keys[low : low + step].reshape(step * PATCHES, HD)
        some_values = values[low : low + step].reshape(step * PATCHES, HD)
        numerator = jnp.where(stale_here, jnp.exp(across(queries, some_keys) * scale), 0.0)
        total = total + jnp.sum(numerator, axis=1, keepdims=True)
        gathered = gathered + jnp.dot(
            numerator.astype(jnp.bfloat16), some_values, preferred_element_type=jnp.float32
        )
    return (gathered / total).astype(jnp.bfloat16)


def own_kernel(place_ref, left_ref, pieces_ref, attended_ref, keys, values, sems):
    copies = fetch(pieces_ref, sems, [(keys, AT_K), (values, AT_V)])
    second = lax.broadcasted_iota(jnp.int32, (LOCAL, 1), 0) >= PT
    row_patch = place_ref[0] + second.astype(jnp.int32)
    for copy in copies:
        copy.wait()
    attended_ref[...] = attend(
        left_ref[:LOCAL],
        left_ref[LOCAL : 2 * LOCAL],
        left_ref[2 * LOCAL : 3 * LOCAL],
        keys,
        values,
        row_patch,
    )


def finish_kernel(
    place_ref,
    left_ref,
    attended_ref,
    got_ref,
    pieces_ref,
    partial_ref,
    keys,
    values,
    w_own,
    w_shared,
    sems,
):
    copies = fetch(
        pieces_ref,
        sems,
        [(keys, AT_SHARED_K), (values, AT_SHARED_V), (w_own, AT_OUT), (w_shared, AT_SHARED_OUT)],
    )
    half = place_ref[1]
    kept, got = left_ref[AT_KEPT : AT_KEPT + PT], got_ref[...]
    queries = jnp.where(half == 0, kept, got)
    fresh_keys = jnp.where(half == 0, got, kept)
    copies[0].wait()
    copies[1].wait()
    shared = attend(
        queries,
        fresh_keys,
        left_ref[AT_KEPT + PT :],
        keys,
        values,
        jnp.full((PT, 1), place_ref[0] + half, jnp.int32),
    )
    nothing = jnp.zeros_like(shared)
    shared = jnp.concatenate(
        [jnp.where(half == 0, shared, nothing), jnp.where(half == 0, nothing, shared)], axis=0
    )
    attention = jnp.concatenate([attended_ref[...], shared], axis=1)
    copies[2].wait()
    copies[3].wait()
    step = 8
    width = step * ROWS
    for low in range(0, SOURCES, step):
        weight = jnp.concatenate(
            [
                w_own[low : low + step].reshape(width, HD),
                w_shared[low : low + step].reshape(width, HD),
            ],
            axis=1,
        )
        partial_ref[:, low * ROWS : low * ROWS + width] = across(attention, weight).astype(
            jnp.bfloat16
        )


def to_own_order(array):
    lead = array.shape[:-1]
    split = array.reshape(lead + (NY, NZ * NC, ROWS))
    return jnp.swapaxes(split, -3, -2).reshape(lead + (D,))


def to_given_order(array):
    lead = array.shape[:-1]
    split = array.reshape(lead + (NZ * NC, NY, ROWS))
    return jnp.swapaxes(split, -3, -2).reshape(lead + (D,))


def exchange(array, axes):
    return lax.all_to_all(array, axes, split_axis=0, concat_axis=0, tiled=True)


def body(latent, modulation, w_qkv, w_out, stale):
    x_at, y_at = lax.axis_index("x"), lax.axis_index("y")
    pair_at = lax.axis_index("z") * NC + lax.axis_index("c")
    place = jnp.stack([2 * pair_at, y_at % 2]).astype(jnp.int32)

    sent = pl.pallas_call(
        pack_kernel,
        out_shape=jax.ShapeDtypeStruct((MEMBERS, PIECE, HD), jnp.bfloat16),
        in_specs=[ANY, ANY, VMEM],
        out_specs=VMEM,
        scratch_shapes=[
            pltpu.VMEM((ROWS, 3 * D), jnp.bfloat16),
            pltpu.VMEM((ROWS, D), jnp.bfloat16),
            pltpu.SemaphoreType.DMA((2,)),
        ],
        compiler_params=PARAMS,
        name="pack",
    )(w_qkv[0], w_out[0].T, jnp.swapaxes(stale[0, :, 0], 0, 1))
    received = exchange(sent, HEAD_AXES).reshape(BLOCKS, NY, PIECE, HD)

    def gather(block):
        return lax.all_gather(received[block], REST_AXES, axis=0, tiled=True)

    pieces = [gather(block) for block in range(BLOCKS)]

    terms = to_own_order(lax.all_gather(modulation[0], "x", axis=0, tiled=False))
    mine = exchange(latent[:, 0], REST_AXES).reshape(NZ * NC, 2, D)
    mine = jnp.swapaxes(mine, 0, 1).reshape(NZ * NC * 2, D)
    current = to_own_order(lax.dynamic_slice_in_dim(mine, x_at * OWN, OWN, 0))

    def term(block, which):
        return terms[block, which][None]

    spread = jax.ShapeDtypeStruct((LOCAL, D), jnp.bfloat16)
    weight = pltpu.VMEM((SOURCES, ROWS, HD), jnp.bfloat16)
    cache = pltpu.VMEM((SOURCES, PATCHES, HD), jnp.bfloat16)
    owned = jax.ShapeDtypeStruct((OWN, D), jnp.bfloat16)
    normed = pl.pallas_call(
        first_kernel,
        out_shape=spread,
        in_specs=[VMEM] * 3,
        out_specs=VMEM,
        compiler_params=PARAMS,
        name="first",
    )(current, term(0, 0), term(0, 1))
    outputs = []
    for block in range(BLOCKS):
        rows = exchange(normed, HEAD_AXES)
        left, given = pl.pallas_call(
            project_kernel,
            out_shape=(
                jax.ShapeDtypeStruct((LEFT, HD), jnp.bfloat16),
                jax.ShapeDtypeStruct((PT, HD), jnp.bfloat16),
            ),
            in_specs=[SMEM, VMEM, ANY],
            out_specs=(VMEM, VMEM),
            scratch_shapes=[weight] * 5 + [pltpu.SemaphoreType.DMA((5,))],
            compiler_params=PARAMS,
            cost_estimate=pl.CostEstimate(
                flops=2 * LOCAL * D * 5 * HD,
                bytes_accessed=2 * 5 * D * HD + 2 * LOCAL * D,
                transcendentals=0,
            ),
            name="project",
        )(place, rows, pieces[block])
        got = lax.ppermute(given, "y", [(at, at ^ 1) for at in range(NY)])
        attended = pl.pallas_call(
            own_kernel,
            out_shape=jax.ShapeDtypeStruct((LOCAL, HD), jnp.bfloat16),
            in_specs=[SMEM, VMEM, ANY],
            out_specs=VMEM,
            scratch_shapes=[cache] * 2 + [pltpu.SemaphoreType.DMA((2,))],
            compiler_params=PARAMS,
            cost_estimate=pl.CostEstimate(
                flops=4 * LOCAL * PATCHES * PT * HD,
                bytes_accessed=4 * PATCHES * PT * HD,
                transcendentals=LOCAL * PATCHES * PT,
            ),
            name="own",
        )(place, left, pieces[block])
        partial = pl.pallas_call(
            finish_kernel,
            out_shape=spread,
            in_specs=[SMEM, VMEM, VMEM, VMEM, ANY],
            out_specs=VMEM,
            scratch_shapes=[cache] * 2 + [weight] * 2 + [pltpu.SemaphoreType.DMA((4,))],
            compiler_params=PARAMS,
            cost_estimate=pl.CostEstimate(
                flops=4 * PT * PATCHES * PT * HD + 4 * LOCAL * D * HD,
                bytes_accessed=4 * PATCHES * PT * HD + 4 * D * HD + 2 * LOCAL * D,
                transcendentals=PT * PATCHES * PT,
            ),
            name="finish",
        )(place, left, attended, got, pieces[block])
        parts = exchange(partial, HEAD_AXES)
        if block + 1 < BLOCKS:
            current, normed = pl.pallas_call(
                middle_kernel,
                out_shape=(owned, spread),
                in_specs=[VMEM] * 5,
                out_specs=(VMEM, VMEM),
                compiler_params=PARAMS,
                name="middle",
            )(parts, current, term(block, 2), term(block + 1, 0), term(block + 1, 1))
        else:
            current = pl.pallas_call(
                last_kernel,
                out_shape=owned,
                in_specs=[VMEM] * 3,
                out_specs=VMEM,
                compiler_params=PARAMS,
                name="last",
            )(parts, current, term(block, 2))
        outputs.append(to_given_order(current))
    placed = exchange(jnp.concatenate(outputs, axis=0), "x")
    placed = jnp.swapaxes(placed.reshape(2, NZ * NC, D), 0, 1).reshape(PATCHES, D)
    placed = exchange(placed, REST_AXES)
    return placed[None, :, None]


def solution(mesh):
    own_mesh = Mesh(mesh.devices.reshape(NX, NY, NZ, NC), ("x",) + SP)
    return jax.shard_map(
        body,
        mesh=own_mesh,
        in_specs=(
            P(None, SP, None),
            P("x", None, None),
            P("x", SP, None),
            P("x", None, SP),
            P("x", None, SP, None, None),
        ),
        out_specs=P("x", None, SP, None),
        check_vma=False,
    )
```

time: 336 us -> 324 us (0.964)
  waiting for transfers between devices: 122 us -> 94.3 us
  Pallas kernels: 30.1 us -> 45 us
  starting transfers between devices: 32.7 us -> 36.8 us
  blocking collectives: 128 us -> 124 us
    all_gather x4, waiting for transfers between devices: 95 us -> 67.2 us  [gather(): return lax.all_gather(received[block], REST_AXES, axis=0, tiled=True)]
    pallas_call x4 -> x12, Pallas kernels: 24.4 us -> 39.1 us  [the longest x4 14.7 us: body(): pl.pallas_call(project_kernel, out_shape=(jax.ShapeDtypeStruct((LEFT, HD)...]
    ppermute x0 -> x4, starting transfers between devices: none -> 5.15 us  [body(): got = lax.ppermute(given, 'y', [(at, at ^ 1) for at in range(NY)])]
    all_to_all x6, blocking collectives: 117 us -> 114 us  [exchange(): return lax.all_to_all(array, axes, split_axis=0, concat_axis=0, tiled=True)]
  transfers between devices with their start and end apart: 10 -> 14, of which waited for: 7 -> 7; matrix products, arithmetic and copies ran while one was open for 1% -> 1% of each run, Pallas kernels for 7% -> 11%
where the time goes in v3:
time: 324 us; the launch traced here: 323 us
  blocking collectives  124 us (38%)
  waiting for transfers between devices  94.3 us (29%)
  Pallas kernels  45 us (14%)
  starting transfers between devices  36.8 us (11%)
  between operations  13.5 us (4%)
  local copies, waits for them, and re-layouts  9.11 us (3%)
    all_to_all x6, blocking collectives, exchange(): return lax.all_to_all(array, axes, split_axis=0, concat_axis=0, tiled=True)  114 us
    all_gather x4, waiting for transfers between devices, gather(): return lax.all_gather(received[block], REST_AXES, axis=0, tiled=True)  67.2 us
    all_to_all x6, starting transfers between devices, exchange(): return lax.all_to_all(array, axes, split_axis=0, concat_axis=0, tiled=True)  31.6 us
    all_to_all x6, waiting for transfers between devices, exchange(): return lax.all_to_all(array, axes, split_axis=0, concat_axis=0, tiled=True)  25.2 us
    pallas_call x4, Pallas kernels, body(): pl.pallas_call(project_kernel, out_shape=(jax.ShapeDtypeStruct((LEFT, HD)...  14.7 us
    pallas_call x4, Pallas kernels, body(): pl.pallas_call(finish_kernel, out_shape=spread, in_specs=[SMEM, VMEM, VME...  13.7 us
    pallas_call x4, Pallas kernels, body(): pl.pallas_call(own_kernel, out_shape=jax.ShapeDtypeStruct((LOCAL, HD), jn...  10.7 us
    all_gather x1, blocking collectives, body(): lax.all_gather(modulation[0], 'x', axis=0, tiled=False)  10.5 us
  transfers between devices with their start and end apart: 14, of which 7 were waited for; matrix products, arithmetic and copies ran while one was open for 1% of the time, Pallas kernels for 11%

profile of v3, /device:TPU:1, one launch (start us, length us, event | category | flops | bytes accessed | tf_op | source)
XLA Modules:
  0.0 322.8 jit_solution(12102620436152332162)
XLA Ops:
  6.5 1.1 copy.49
  7.7 1.2 copy-done
  8.8 1.0 copy-done.1
  9.8 0.6 pack.1
  10.3 32.2 %all_to_all.117 = bf16[16,464,128]{2,1,0:T(8,128)(2,1)S(1)} all-to-all(bf16[16,464,128]{2,1,0:T(8,128)(2,1)S(1)} %pack.1), channel_id=1, replica_groups=mesh['x'=4,'y'=4,'z'=8,'c'=2] {'x','y'}, dimensions={0} | all-to-all | bytes 3801088 | tf_op jit(solution)/shard_map/all_to_all | solution.py:277
  42.5 1.3 fusion
  43.9 0.7 all-gather.7.cloned.1.call-update
  44.6 0.7 all-gather.9.cloned.1.call-update
  45.3 0.5 all-gather.11.cloned.1.call-update
  45.9 0.8 all_to_all.75
  46.6 10.7 %all-to-all-start = ((bf16[16,2,3072]{2,1,0:T(2,128)(2,1)}), bf16[16,2,3072]{2,1,0:T(2,128)(2,1)S(1)}, u32[]{:S(2)}, u32[]{:S(2)}) async-start(bf16[16,2,3072]{2,1,0:T(2,128)(2,1)} %all_to_all.75), calls=%async_computation | async-start | bytes 393216 | tf_op jit(solution)/shard_map/all_to_all | solution.py:277
  57.3 10.5 %all_gather.15 = f32[4,3,3072]{2,1,0:T(4,128)S(1)} all-gather(f32[1,3,3072]{2,1,0:T(4,128)S(1)} %copy.35), channel_id=1, replica_groups=mesh['x'=4,'y'=4,'z'=8,'c'=2] {'x'}, dimensions={0}, use_global_device_ids=true | all-gather | bytes 184320 | tf_op jit(solution)/shard_map/all_gather | solution.py:305
  67.9 0.2 reshape.83
  68.1 0.2 copy.37
  68.2 0.4 reshape.84
  68.7 1.0 all-to-all-done
  69.7 0.2 reshape.81
  70.0 0.2 reshape.82.rows_ref
  70.2 1.2 first.1
  71.4 3.6 %all-to-all-start.1 = ((bf16[16,8,3072]{2,1,0:T(8,128)(2,1)}), bf16[16,8,3072]{2,1,0:T(8,128)(2,1)S(1)}, u32[]{:S(2)}, u32[]{:S(2)}) async-start(bf16[16,8,3072]{2,1,0:T(8,128)(2,1)} %bitcast.8), calls=%async_computation.1 | async-start | bytes 1572864 | tf_op jit(solution)/shard_map/all_to_all | solution.py:277
  75.1 12.7 %all-to-all-done.1 = bf16[16,8,3072]{2,1,0:T(8,128)(2,1)S(1)} async-done(((bf16[16,8,3072]{2,1,0:T(8,128)(2,1)}), bf16[16,8,3072]{2,1,0:T(8,128)(2,1)S(1)}, u32[]{:S(2)}, u32[]{:S(2)}) %all-to-all-start.1) | async-done | bytes 786464 | tf_op jit(solution)/shard_map/all_to_all | solution.py:277
  87.7 14.4 %all-gather.5.cloned.1.call-done.pieces_ref = bf16[64,464,128]{2,1,0:T(8,128)(2,1)} async-done(((bf16[4,464,128]{2,1,0:T(8,128)(2,1)}), bf16[64,464,128]{2,1,0:T(8,128)(2,1)}) %all-gather.5.cloned.1.call-update) | async-done | bytes 7602192 | tf_op jit(solution)/shard_map/all_gather | solution.py:301
  102.1 3.7 %project.4 = (bf16[512,128]{1,0:T(8,128)(2,1)S(1)}, bf16[64,128]{1,0:T(8,128)(2,1)S(1)}) custom-call(s32[2]{0:T(128)S(1)} %pad_add_fusion.place_ref, bf16[128,3072]{1,0:T(8,128)(2,1)S(1)} %bitcast.86, bf16[64,464,128]{2,1,0:T(8,128)(2,1)} %all-gather.5.cloned.1.call-done.pieces_ref), custom_call_target="tpu_custom_call" | custom-call | flops 503316480 | bytes 4718592 | tf_op jit(solution)/shard_map/project/pallas_call | solution.py:328
  105.8 1.3 collective-permute-start
  107.1 2.7 own.4.attended_ref
  109.8 3.2 finish.4
  113.0 17.0 %all_to_all.118 = bf16[16,8,3072]{2,1,0:T(8,128)(2,1)S(1)} all-to-all(bf16[16,8,3072]{2,1,0:T(8,128)(2,1)S(1)} %bitcast.90), channel_id=1, replica_groups=mesh['x'=4,'y'=4,'z'=8,'c'=2] {'x','y'}, dimensions={0} | all-to-all | bytes 1572864 | tf_op jit(solution)/shard_map/all_to_all | solution.py:277
  130.0 1.3 middle.3
  131.3 3.6 %all-to-all-start.4 = ((bf16[16,8,3072]{2,1,0:T(8,128)(2,1)}), bf16[16,8,3072]{2,1,0:T(8,128)(2,1)S(1)}, u32[]{:S(2)}, u32[]{:S(2)}) async-start(bf16[16,8,3072]{2,1,0:T(8,128)(2,1)} %bitcast.21), calls=%async_computation.4 | async-start | bytes 1572864 | tf_op jit(solution)/shard_map/all_to_all | solution.py:277
  135.0 18.0 %all-gather.7.cloned.1.call-done.pieces_ref = bf16[64,464,128]{2,1,0:T(8,128)(2,1)} async-done(((bf16[4,464,128]{2,1,0:T(8,128)(2,1)}), bf16[64,464,128]{2,1,0:T(8,128)(2,1)}) %all-gather.7.cloned.1.call-update) | async-done | bytes 7602192 | tf_op jit(solution)/shard_map/all_gather | solution.py:301
  153.0 3.7 %project.5 = (bf16[512,128]{1,0:T(8,128)(2,1)S(1)}, bf16[64,128]{1,0:T(8,128)(2,1)S(1)}) custom-call(s32[2]{0:T(128)S(1)} %pad_add_fusion.place_ref, bf16[128,3072]{1,0:T(8,128)(2,1)S(1)} %bitcast.87, bf16[64,464,128]{2,1,0:T(8,128)(2,1)} %all-gather.7.cloned.1.call-done.pieces_ref), custom_call_target="tpu_custom_call" | custom-call | flops 503316480 | bytes 4718592 | tf_op jit(solution)/shard_map/project/pallas_call | solution.py:328
  156.7 1.3 collective-permute-start.1
  158.0 2.7 own.5.attended_ref
  160.7 3.2 finish.5
  163.9 19.3 %all_to_all.119 = bf16[16,8,3072]{2,1,0:T(8,128)(2,1)S(1)} all-to-all(bf16[16,8,3072]{2,1,0:T(8,128)(2,1)S(1)} %bitcast.91), channel_id=1, replica_groups=mesh['x'=4,'y'=4,'z'=8,'c'=2] {'x','y'}, dimensions={0} | all-to-all | bytes 1572864 | tf_op jit(solution)/shard_map/all_to_all | solution.py:277
  183.2 1.3 middle.4
  184.5 3.8 %all-to-all-start.6 = ((bf16[16,8,3072]{2,1,0:T(8,128)(2,1)}), bf16[16,8,3072]{2,1,0:T(8,128)(2,1)S(1)}, u32[]{:S(2)}, u32[]{:S(2)}) async-start(bf16[16,8,3072]{2,1,0:T(8,128)(2,1)} %bitcast.29), calls=%async_computation.6 | async-start | bytes 1572864 | tf_op jit(solution)/shard_map/all_to_all | solution.py:277
  188.3 17.4 %all-gather.9.cloned.1.call-done.pieces_ref = bf16[64,464,128]{2,1,0:T(8,128)(2,1)} async-done(((bf16[4,464,128]{2,1,0:T(8,128)(2,1)}), bf16[64,464,128]{2,1,0:T(8,128)(2,1)}) %all-gather.9.cloned.1.call-update) | async-done | bytes 7602192 | tf_op jit(solution)/shard_map/all_gather | solution.py:301
  205.7 3.7 %project.6 = (bf16[512,128]{1,0:T(8,128)(2,1)S(1)}, bf16[64,128]{1,0:T(8,128)(2,1)S(1)}) custom-call(s32[2]{0:T(128)S(1)} %pad_add_fusion.place_ref, bf16[128,3072]{1,0:T(8,128)(2,1)S(1)} %bitcast.88, bf16[64,464,128]{2,1,0:T(8,128)(2,1)} %all-gather.9.cloned.1.call-done.pieces_ref), custom_call_target="tpu_custom_call" | custom-call | flops 503316480 | bytes 4718592 | tf_op jit(solution)/shard_map/project/pallas_call | solution.py:328
  209.3 1.3 collective-permute-start.2
  210.6 2.7 own.6.attended_ref
  213.3 3.2 finish.6
  216.5 19.3 %all_to_all.120 = bf16[16,8,3072]{2,1,0:T(8,128)(2,1)S(1)} all-to-all(bf16[16,8,3072]{2,1,0:T(8,128)(2,1)S(1)} %bitcast.92), channel_id=1, replica_groups=mesh['x'=4,'y'=4,'z'=8,'c'=2] {'x','y'}, dimensions={0} | all-to-all | bytes 1572864 | tf_op jit(solution)/shard_map/all_to_all | solution.py:277
  235.8 1.4 middle.5
  237.2 3.6 %all-to-all-start.8 = ((bf16[16,8,3072]{2,1,0:T(8,128)(2,1)}), bf16[16,8,3072]{2,1,0:T(8,128)(2,1)S(1)}, u32[]{:S(2)}, u32[]{:S(2)}) async-start(bf16[16,8,3072]{2,1,0:T(8,128)(2,1)} %bitcast.37), calls=%async_computation.8 | async-start | bytes 1572864 | tf_op jit(solution)/shard_map/all_to_all | solution.py:277
  240.8 17.4 %all-gather.11.cloned.1.call-done.pieces_ref = bf16[64,464,128]{2,1,0:T(8,128)(2,1)} async-done(((bf16[4,464,128]{2,1,0:T(8,128)(2,1)}), bf16[64,464,128]{2,1,0:T(8,128)(2,1)}) %all-gather.11.cloned.1.call-update) | async-done | bytes 7602192 | tf_op jit(solution)/shard_map/all_gather | solution.py:301
  258.2 3.7 %project.7 = (bf16[512,128]{1,0:T(8,128)(2,1)S(1)}, bf16[64,128]{1,0:T(8,128)(2,1)S(1)}) custom-call(s32[2]{0:T(128)S(1)} %pad_add_fusion.place_ref, bf16[128,3072]{1,0:T(8,128)(2,1)S(1)} %bitcast.89, bf16[64,464,128]{2,1,0:T(8,128)(2,1)} %all-gather.11.cloned.1.call-done.pieces_ref), custom_call_target="tpu_custom_call" | custom-call | flops 503316480 | bytes 4718592 | tf_op jit(solution)/shard_map/project/pallas_call | solution.py:328
  261.9 1.3 collective-permute-start.3
  263.2 2.7 own.7.attended_ref
  265.8 4.1 %finish.7 = bf16[128,3072]{1,0:T(8,128)(2,1)} custom-call(s32[2]{0:T(128)S(1)} %pad_add_fusion.place_ref, bf16[512,128]{1,0:T(8,128)(2,1)S(1)} %get-tuple-element.31.left_ref, bf16[128,128]{1,0:T(8,128)(2,1)S(1)} %own.7.attended_ref, bf16[64,128]{1,0:T(8,128)(2,1)S(1)} %collective-permute-done.3.got_ref, ...), custom_call_target="tpu_custom_call" | custom-call | flops 268435456 | bytes 3407872 | tf_op jit(solution)/shard_map/finish/pallas_call | solution.py:360
  270.0 6.3 %all-to-all-start.9 = ((bf16[16,8,3072]{2,1,0:T(8,128)(2,1)}), bf16[16,8,3072]{2,1,0:T(8,128)(2,1)S(1)}, u32[]{:S(2)}, u32[]{:S(2)}) async-start(bf16[16,8,3072]{2,1,0:T(8,128)(2,1)} %bitcast.39), calls=%async_computation.9 | async-start | bytes 1572864 | tf_op jit(solution)/shard_map/all_to_all | solution.py:277
  276.2 0.2 reshape.85
  276.4 0.2 reshape.86
  276.6 0.2 reshape.87
  276.8 0.2 reshape.88
  277.0 0.2 reshape.89
  277.2 0.2 reshape.90
  277.4 11.6 %all-to-all-done.9 = bf16[16,8,3072]{2,1,0:T(8,128)(2,1)S(1)} async-done(((bf16[16,8,3072]{2,1,0:T(8,128)(2,1)}), bf16[16,8,3072]{2,1,0:T(8,128)(2,1)S(1)}, u32[]{:S(2)}, u32[]{:S(2)}) %all-to-all-start.9) | async-done | bytes 786464 | tf_op jit(solution)/shard_map/all_to_all | solution.py:277
  289.1 0.2 reshape.91
  289.3 0.2 reshape.92
  289.5 7.5 %all_to_all.121 = bf16[4,8,3072]{2,1,0:T(8,128)(2,1)S(1)} all-to-all(bf16[4,8,3072]{2,1,0:T(8,128)(2,1)S(1)} %maximum_bitcast_fusion), channel_id=1, replica_groups=mesh['x'=4,'y'=4,'z'=8,'c'=2] {'x'}, dimensions={0} | all-to-all | bytes 393216 | tf_op jit(solution)/shard_map/all_to_all | solution.py:277
  297.1 0.2 copy.43
  297.3 18.2 %all_to_all.122 = bf16[16,2,3072]{2,1,0:T(2,128)(2,1)S(1)} all-to-all(bf16[16,2,3072]{2,1,0:T(2,128)(2,1)S(1)} %copy.43), channel_id=1, replica_groups=mesh['x'=4,'y'=4,'z'=8,'c'=2] {'z','c'}, dimensions={0} | all-to-all | bytes 393216 | tf_op jit(solution)/shard_map/all_to_all | solution.py:277
  315.5 0.8 broadcast_in_dim.3
  (31 shorter events, 0.8 us)
Async XLA Ops:
  6.5 39.3 %copy-start.2 = (bf16[32,1,3072]{2,0,1:T(8,128)(2,1)S(1)}, bf16[32,1,3072]{2,0,1:T(8,128)(2,1)}, u32[]{:S(2)}) copy-start(bf16[32,1,3072]{2,0,1:T(8,128)(2,1)} %param.5) | copy-start | bytes 589828
  6.5 50.8 %copy-start.3 = (f32[1,3,3072]{2,0,1:T(1,128)S(1)}, f32[1,3,3072]{2,0,1:T(1,128)}, u32[]{:S(2)}) copy-start(f32[1,3,3072]{2,0,1:T(1,128)} %param.6) | copy-start | bytes 110596
  6.5 95.6 %all-gather.5.cloned.1.call-start = ((), (), s32[]{:S(2)}) async-start(), calls=%async_computation.12 | async-start | bytes 8077312 | tf_op jit(solution)/shard_map/all_gather | solution.py:301
  7.6 1.2 copy-start
  8.8 1.0 copy-start.1
  43.8 109.2 %all-gather.7.cloned.1.call-start = ((), (), s32[]{:S(2)}) async-start(), calls=%async_computation.13 | async-start | bytes 8077312 | tf_op jit(solution)/shard_map/all_gather | solution.py:301
  44.6 161.1 %all-gather.9.cloned.1.call-start = ((), (), s32[]{:S(2)}) async-start(), calls=%async_computation.14 | async-start | bytes 8077312 | tf_op jit(solution)/shard_map/all_gather | solution.py:301
  45.3 212.9 %all-gather.11.cloned.1.call-start = ((), (), s32[]{:S(2)}) async-start(), calls=%async_computation.15 | async-start | bytes 8077312 | tf_op jit(solution)/shard_map/all_gather | solution.py:301
  46.6 23.0 %all-to-all-start = ((bf16[16,2,3072]{2,1,0:T(2,128)(2,1)}), bf16[16,2,3072]{2,1,0:T(2,128)(2,1)S(1)}, u32[]{:S(2)}, u32[]{:S(2)}) async-start(bf16[16,2,3072]{2,1,0:T(2,128)(2,1)} %all_to_all.75), calls=%async_computation | async-start | bytes 393216 | tf_op jit(solution)/shard_map/all_to_all | solution.py:277
  71.4 16.4 %all-to-all-start.1 = ((bf16[16,8,3072]{2,1,0:T(8,128)(2,1)}), bf16[16,8,3072]{2,1,0:T(8,128)(2,1)S(1)}, u32[]{:S(2)}, u32[]{:S(2)}) async-start(bf16[16,8,3072]{2,1,0:T(8,128)(2,1)} %bitcast.8), calls=%async_computation.1 | async-start | bytes 1572864 | tf_op jit(solution)/shard_map/all_to_all | solution.py:277
  105.8 4.0 %collective-permute-start = (bf16[64,128]{1,0:T(8,128)(2,1)S(1)}, bf16[64,128]{1,0:T(8,128)(2,1)S(1)}, u32[]{:S(2)}, u32[]{:S(2)}) collective-permute-start(bf16[64,128]{1,0:T(8,128)(2,1)S(1)} %get-tuple-element.20), channel_id=1, source_target_pairs={{0,16},{16,0},{32,48},{48,32},{1,17},{17,1},{33,49},{49,33},{2,18}... | collective-permute-start | bytes 49160 | tf_op jit(solution)/shard_map/ppermute | solution.py:345
  131.3 21.7 %all-to-all-start.4 = ((bf16[16,8,3072]{2,1,0:T(8,128)(2,1)}), bf16[16,8,3072]{2,1,0:T(8,128)(2,1)S(1)}, u32[]{:S(2)}, u32[]{:S(2)}) async-start(bf16[16,8,3072]{2,1,0:T(8,128)(2,1)} %bitcast.21), calls=%async_computation.4 | async-start | bytes 1572864 | tf_op jit(solution)/shard_map/all_to_all | solution.py:277
  156.7 4.0 %collective-permute-start.1 = (bf16[64,128]{1,0:T(8,128)(2,1)S(1)}, bf16[64,128]{1,0:T(8,128)(2,1)S(1)}, u32[]{:S(2)}, u32[]{:S(2)}) collective-permute-start(bf16[64,128]{1,0:T(8,128)(2,1)S(1)} %get-tuple-element.24), channel_id=1, source_target_pairs={{0,16},{16,0},{32,48},{48,32},{1,17},{17,1},{33,49},{49,33},{2,18}... | collective-permute-start | bytes 49160 | tf_op jit(solution)/shard_map/ppermute | solution.py:345
  184.5 21.2 %all-to-all-start.6 = ((bf16[16,8,3072]{2,1,0:T(8,128)(2,1)}), bf16[16,8,3072]{2,1,0:T(8,128)(2,1)S(1)}, u32[]{:S(2)}, u32[]{:S(2)}) async-start(bf16[16,8,3072]{2,1,0:T(8,128)(2,1)} %bitcast.29), calls=%async_computation.6 | async-start | bytes 1572864 | tf_op jit(solution)/shard_map/all_to_all | solution.py:277
  209.3 4.0 %collective-permute-start.2 = (bf16[64,128]{1,0:T(8,128)(2,1)S(1)}, bf16[64,128]{1,0:T(8,128)(2,1)S(1)}, u32[]{:S(2)}, u32[]{:S(2)}) collective-permute-start(bf16[64,128]{1,0:T(8,128)(2,1)S(1)} %get-tuple-element.28), channel_id=1, source_target_pairs={{0,16},{16,0},{32,48},{48,32},{1,17},{17,1},{33,49},{49,33},{2,18}... | collective-permute-start | bytes 49160 | tf_op jit(solution)/shard_map/ppermute | solution.py:345
  237.2 21.0 %all-to-all-start.8 = ((bf16[16,8,3072]{2,1,0:T(8,128)(2,1)}), bf16[16,8,3072]{2,1,0:T(8,128)(2,1)S(1)}, u32[]{:S(2)}, u32[]{:S(2)}) async-start(bf16[16,8,3072]{2,1,0:T(8,128)(2,1)} %bitcast.37), calls=%async_computation.8 | async-start | bytes 1572864 | tf_op jit(solution)/shard_map/all_to_all | solution.py:277
  261.9 4.0 %collective-permute-start.3 = (bf16[64,128]{1,0:T(8,128)(2,1)S(1)}, bf16[64,128]{1,0:T(8,128)(2,1)S(1)}, u32[]{:S(2)}, u32[]{:S(2)}) collective-permute-start(bf16[64,128]{1,0:T(8,128)(2,1)S(1)} %get-tuple-element.32), channel_id=1, source_target_pairs={{0,16},{16,0},{32,48},{48,32},{1,17},{17,1},{33,49},{49,33},{2,18}... | collective-permute-start | bytes 49160 | tf_op jit(solution)/shard_map/ppermute | solution.py:345
  270.0 19.0 %all-to-all-start.9 = ((bf16[16,8,3072]{2,1,0:T(8,128)(2,1)}), bf16[16,8,3072]{2,1,0:T(8,128)(2,1)S(1)}, u32[]{:S(2)}, u32[]{:S(2)}) async-start(bf16[16,8,3072]{2,1,0:T(8,128)(2,1)} %bitcast.39), calls=%async_computation.9 | async-start | bytes 1572864 | tf_op jit(solution)/shard_map/all_to_all | solution.py:277
Sparse Core Ops, SparseCore 0:
  43.9 58.1 all-gather.4
  104.0 48.9 all-gather.6
  154.8 50.7 all-gather.8
  207.3 50.7 all-gather.10

commit v4 on v3

--- a/solution.py
+++ b/solution.py
@@ -24,12 +24,11 @@
 OWN = 8
 LOCAL = 2 * PT
 AT_OUT, AT_K, AT_V, AT_SHARED = 3 * ROWS, 4 * ROWS, 4 * ROWS + PATCHES, 4 * ROWS + 2 * PATCHES
-AT_SHARED_OUT = AT_SHARED + 2 * ROWS
-AT_SHARED_K = AT_SHARED + 3 * ROWS
-AT_SHARED_V = AT_SHARED_K + PATCHES
-PIECE = AT_SHARED_V + PATCHES
-AT_KEPT = 3 * LOCAL
-LEFT = AT_KEPT + 2 * PT
+AT_SHARED_VO = AT_SHARED + ROWS
+AT_SHARED_K = AT_SHARED + 2 * ROWS
+AT_SHARED_V = AT_SHARED_K + PATCHES // 2
+PIECE = AT_SHARED_V + PATCHES // 2
+HALF = HD // 2
 ANY = pl.BlockSpec(memory_space=pl.ANY)
 SMEM = pl.BlockSpec(memory_space=pltpu.SMEM)
 VMEM = pl.BlockSpec(memory_space=pltpu.VMEM)
@@ -73,18 +72,21 @@
     for member, half, own, shared in each():
         put(member, AT_K, stale_ref[0, :, columns(own)])
         put(member, AT_V, stale_ref[1, :, columns(own)])
-        put(member, AT_SHARED_K, stale_ref[0, :, columns(shared)])
-        put(member, AT_SHARED_V, stale_ref[1, :, columns(shared)])
+        some = slice(half * PATCHES // 2, (half + 1) * PATCHES // 2)
+        put(member, AT_SHARED_K, stale_ref[0, some, columns(shared)])
+        put(member, AT_SHARED_V, stale_ref[1, some, columns(shared)])
     copies[1].wait()
     for member, half, own, shared in each():
         put(member, AT_OUT, out_ref[:, columns(own)])
-        put(member, AT_SHARED_OUT, out_ref[:, columns(shared)])
     copies[0].wait()
     for member, half, own, shared in each():
         for part in range(3):
             put(member, part * ROWS, qkv_ref[:, columns(part * HEADS + own)])
         put(member, AT_SHARED, qkv_ref[:, columns(half * HEADS + shared)])
-        put(member, AT_SHARED + ROWS, qkv_ref[:, columns(2 * HEADS + shared)])
+        w_v = qkv_ref[:, columns(2 * HEADS + shared)]
+        w_o = out_ref[:, columns(shared)]
+        lanes = slice(half * HALF, (half + 1) * HALF)
+        put(member, AT_SHARED_VO, jnp.concatenate([w_v[:, lanes], w_o[:, lanes]], axis=1))
 
 
 def first_kernel(rows_ref, shift_ref, scale_ref, normed_ref):
@@ -133,126 +135,146 @@
     return copies
 
 
-def project_kernel(
-    place_ref, rows_ref, pieces_ref, left_ref, given_ref, w_q, w_k, w_v, w_qk, w_sv, sems
-):
-    weights = (w_q, w_k, w_v, w_qk, w_sv)
-    lows = (0, ROWS, 2 * ROWS, AT_SHARED, AT_SHARED + ROWS)
-    copies = fetch(pieces_ref, sems, list(zip(weights, lows)))
+def project(rows, *parts):
+    weight = jnp.concatenate([part[...].reshape(D, HD) for part in parts], axis=1)
+    return jnp.dot(rows, weight, preferred_element_type=jnp.float32)
+
+
+def low_lanes(rows):
+    return lax.broadcasted_iota(jnp.int32, (rows, HD), 1) < HALF
+
+
+def pick(half, both):
+    return jnp.where(half == 0, both[:PT], both[PT:])
+
+
+def shared_project_kernel(place_ref, rows_ref, pieces_ref, kept_ref, given_ref, w_qk, w_vo, sems):
+    copies = fetch(pieces_ref, sems, [(w_qk, AT_SHARED), (w_vo, AT_SHARED_VO)])
     half = place_ref[1]
     rows = rows_ref[...]
-
-    def project(*parts):
-        weight = jnp.concatenate([part[...].reshape(D, HD) for part in parts], axis=1)
-        return jnp.dot(rows, weight, preferred_element_type=jnp.float32)
-
-    def mine(both):
-        return jnp.where(half == 0, both[:PT], both[PT:])
-
+    for copy in copies:
+        copy.wait()
+    both = project(rows, w_qk, w_vo)
+    normed = head_norm(both[:, :HD])
+    values = jnp.where(low_lanes(LOCAL), both[:, HD:], 0.0).astype(jnp.bfloat16)
+    kept_ref[:LOCAL] = normed
+    kept_ref[LOCAL:] = pick(half, values)
+    given_ref[:LOCAL] = normed
+    given_ref[LOCAL:] = pick(1 - half, values)
+
+
+def own_project_kernel(rows_ref, pieces_ref, own_ref, w_q, w_k, w_v, sems):
+    copies = fetch(pieces_ref, sems, [(w_q, 0), (w_k, ROWS), (w_v, 2 * ROWS)])
+    rows = rows_ref[...]
     copies[0].wait()
     copies[1].wait()
-    first = project(w_q, w_k)
-    left_ref[:LOCAL] = head_norm(first[:, :HD])
-    left_ref[LOCAL : 2 * LOCAL] = head_norm(first[:, HD:])
-    copies[3].wait()
-    copies[4].wait()
-    second = project(w_qk, w_sv)
-    shared = head_norm(second[:, :HD])
-    left_ref[AT_KEPT : AT_KEPT + PT] = mine(shared)
-    given_ref[...] = jnp.where(half == 0, shared[PT:], shared[:PT])
-    left_ref[AT_KEPT + PT :] = mine(second[:, HD:].astype(jnp.bfloat16))
+    both = project(rows, w_q, w_k)
+    own_ref[:LOCAL] = head_norm(both[:, :HD])
+    own_ref[LOCAL : 2 * LOCAL] = head_norm(both[:, HD:])
     copies[2].wait()
-    left_ref[2 * LOCAL : 3 * LOCAL] = project(w_v).astype(jnp.bfloat16)
-
-
-def attend(queries, fresh_keys, fresh_values, keys, values, row_patch):
-    count = queries.shape[0]
-    scale = 1.0 / math.sqrt(HD)
-    fresh = jnp.exp(across(queries, fresh_keys) * scale)
-    if count > PT:
-        row_at = lax.broadcasted_iota(jnp.int32, (count, 1), 0)
-        column_at = lax.broadcasted_iota(jnp.int32, (count, count), 1)
-        fresh = jnp.where((row_at >= PT) == (column_at >= PT), fresh, 0.0)
-    total = jnp.sum(fresh, axis=1, keepdims=True)
-    gathered = jnp.dot(
-        fresh.astype(jnp.bfloat16), fresh_values, preferred_element_type=jnp.float32
-    )
-    step = 16
-    patch_of = lax.broadcasted_iota(jnp.int32, (count, step * PATCHES), 1) % PATCHES
-    stale_here = patch_of != row_patch
+    own_ref[2 * LOCAL :] = project(rows, w_v).astype(jnp.bfloat16)
+
+
+def weigh(queries, keys):
+    return jnp.exp(across(queries, keys) * (1.0 / math.sqrt(HD)))
+
+
+def gather_values(numerator, values):
+    return jnp.dot(numerator.astype(jnp.bfloat16), values, preferred_element_type=jnp.float32)
+
+
+def attend_stale(queries, keys, values, first_column, row_patch, total, gathered):
+    patches = keys.shape[1]
+    step = 512 // patches
+    shape = (queries.shape[0], step * patches)
+    column_patch = first_column + lax.broadcasted_iota(jnp.int32, shape, 1) % patches
+    stale_here = column_patch != row_patch
     for low in range(0, SOURCES, step):
-        some_keys = keys[low : low + step].reshape(step * PATCHES, HD)
-        some_values = values[low : low + step].reshape(step * PATCHES, HD)
-        numerator = jnp.where(stale_here, jnp.exp(across(queries, some_keys) * scale), 0.0)
+        some_keys = keys[low : low + step].reshape(step * patches, HD)
+        some_values = values[low : low + step].reshape(step * patches, HD)
+        numerator = jnp.where(stale_here, weigh(queries, some_keys), 0.0)
         total = total + jnp.sum(numerator, axis=1, keepdims=True)
-        gathered = gathered + jnp.dot(
-            numerator.astype(jnp.bfloat16), some_values, preferred_element_type=jnp.float32
+        gathered = gathered + gather_values(numerator, some_values)
+    return total, gathered
+
+
+def patch_of_rows(place_ref):
+    second = lax.broadcasted_iota(jnp.int32, (LOCAL, 1), 0) >= PT
+    return place_ref[0] + second.astype(jnp.int32)
+
+
+def shared_attend_kernel(
+    place_ref, kept_ref, got_ref, earlier_ref, pieces_ref, sums_ref, given_ref, keys, values, sems
+):
+    del earlier_ref
+    copies = fetch(pieces_ref, sems, [(keys, AT_SHARED_K), (values, AT_SHARED_V)])
+    half = place_ref[1]
+    kept, got = kept_ref[:LOCAL], got_ref[:LOCAL]
+    queries = jnp.where(half == 0, kept, got)
+    fresh_keys = jnp.where(half == 0, got[:PT], kept[PT:])
+    mine, other = kept_ref[LOCAL:].astype(jnp.float32), got_ref[LOCAL:].astype(jnp.float32)
+    low = jnp.where(half == 0, mine, other)
+    high = jnp.where(half == 0, other, mine)
+    fresh_values = jnp.where(low_lanes(PT), low, pltpu.roll(high, HALF, 1)).astype(jnp.bfloat16)
+    fresh = weigh(pick(half, queries), fresh_keys)
+
+    def placed(rows):
+        nothing = jnp.zeros_like(rows)
+        return jnp.concatenate(
+            [jnp.where(half == 0, rows, nothing), jnp.where(half == 0, nothing, rows)], axis=0
         )
-    return (gathered / total).astype(jnp.bfloat16)
-
-
-def own_kernel(place_ref, left_ref, pieces_ref, attended_ref, keys, values, sems):
-    copies = fetch(pieces_ref, sems, [(keys, AT_K), (values, AT_V)])
-    second = lax.broadcasted_iota(jnp.int32, (LOCAL, 1), 0) >= PT
-    row_patch = place_ref[0] + second.astype(jnp.int32)
+
+    total = placed(jnp.sum(fresh, axis=1, keepdims=True))
+    gathered = placed(gather_values(fresh, fresh_values))
     for copy in copies:
         copy.wait()
-    attended_ref[...] = attend(
-        left_ref[:LOCAL],
-        left_ref[LOCAL : 2 * LOCAL],
-        left_ref[2 * LOCAL : 3 * LOCAL],
+    total, gathered = attend_stale(
+        queries,
         keys,
         values,
-        row_patch,
+        half * (PATCHES // 2),
+        patch_of_rows(place_ref),
+        total,
+        gathered,
     )
-
-
-def finish_kernel(
-    place_ref,
-    left_ref,
-    attended_ref,
-    got_ref,
-    pieces_ref,
-    partial_ref,
-    keys,
-    values,
-    w_own,
-    w_shared,
-    sems,
-):
-    copies = fetch(
-        pieces_ref,
-        sems,
-        [(keys, AT_SHARED_K), (values, AT_SHARED_V), (w_own, AT_OUT), (w_shared, AT_SHARED_OUT)],
+    swapped = pltpu.roll(gathered, HALF, 1)
+    first = low_lanes(LOCAL)
+    sums_ref[...] = jnp.where(first, total, jnp.where(half == 0, swapped, gathered))
+    given_ref[...] = jnp.where(first, total, jnp.where(half == 0, gathered, swapped))
+
+
+def own_attend_kernel(place_ref, own_ref, earlier_ref, pieces_ref, attended_ref, keys, values, sems):
+    del earlier_ref
+    copies = fetch(pieces_ref, sems, [(keys, AT_K), (values, AT_V)])
+    queries = own_ref[:LOCAL]
+    fresh = weigh(queries, own_ref[LOCAL : 2 * LOCAL])
+    row_at = lax.broadcasted_iota(jnp.int32, (LOCAL, 1), 0)
+    column_at = lax.broadcasted_iota(jnp.int32, (LOCAL, LOCAL), 1)
+    fresh = jnp.where((row_at >= PT) == (column_at >= PT), fresh, 0.0)
+    total = jnp.sum(fresh, axis=1, keepdims=True)
+    gathered = gather_values(fresh, own_ref[2 * LOCAL :])
+    for copy in copies:
+        copy.wait()
+    total, gathered = attend_stale(
+        queries, keys, values, 0, patch_of_rows(place_ref), total, gathered
     )
-    half = place_ref[1]
-    kept, got = left_ref[AT_KEPT : AT_KEPT + PT], got_ref[...]
-    queries = jnp.where(half == 0, kept, got)
-    fresh_keys = jnp.where(half == 0, got, kept)
-    copies[0].wait()
-    copies[1].wait()
-    shared = attend(
-        queries,
-        fresh_keys,
-        left_ref[AT_KEPT + PT :],
-        keys,
-        values,
-        jnp.full((PT, 1), place_ref[0] + half, jnp.int32),
-    )
-    nothing = jnp.zeros_like(shared)
-    shared = jnp.concatenate(
-        [jnp.where(half == 0, shared, nothing), jnp.where(half == 0, nothing, shared)], axis=0
-    )
+    attended_ref[...] = (gathered / total).astype(jnp.bfloat16)
+
+
+def finish_kernel(attended_ref, sums_ref, got_ref, pieces_ref, partial_ref, w_own, w_vo, sems):
+    copies = fetch(pieces_ref, sems, [(w_own, AT_OUT), (w_vo, AT_SHARED_VO)])
+    sums = sums_ref[...] + got_ref[...]
+    shared = jnp.where(low_lanes(LOCAL), 0.0, sums / sums[:, :1]).astype(jnp.bfloat16)
     attention = jnp.concatenate([attended_ref[...], shared], axis=1)
-    copies[2].wait()
-    copies[3].wait()
+    for copy in copies:
+        copy.wait()
     step = 8
     width = step * ROWS
     for low in range(0, SOURCES, step):
         weight = jnp.concatenate(
             [
                 w_own[low : low + step].reshape(width, HD),
-                w_shared[low : low + step].reshape(width, HD),
+                w_vo[low : low + step].reshape(width, HD),
             ],
             axis=1,
         )
@@ -322,55 +344,53 @@
         compiler_params=PARAMS,
         name="first",
     )(current, term(0, 0), term(0, 1))
+    half_cache = pltpu.VMEM((SOURCES, PATCHES // 2, HD), jnp.bfloat16)
+    sums_of = jax.ShapeDtypeStruct((LOCAL, HD), jnp.float32)
+
+    def rows_of(count):
+        return jax.ShapeDtypeStruct((count, HD), jnp.bfloat16)
+
+    def local(kernel, in_specs, out_specs, out_shape, scratch, elements):
+        return pl.pallas_call(
+            kernel,
+            out_shape=out_shape,
+            in_specs=in_specs,
+            out_specs=out_specs,
+            scratch_shapes=scratch + [pltpu.SemaphoreType.DMA((len(scratch),))],
+            compiler_params=PARAMS,
+            cost_estimate=pl.CostEstimate(
+                flops=2 * LOCAL * elements, bytes_accessed=2 * elements, transcendentals=0
+            ),
+            name=kernel.__name__,
+        )
+
+    def swap(array):
+        return lax.ppermute(array, "y", [(at, at ^ 1) for at in range(NY)])
+
     outputs = []
     for block in range(BLOCKS):
         rows = exchange(normed, HEAD_AXES)
-        left, given = pl.pallas_call(
-            project_kernel,
-            out_shape=(
-                jax.ShapeDtypeStruct((LEFT, HD), jnp.bfloat16),
-                jax.ShapeDtypeStruct((PT, HD), jnp.bfloat16),
-            ),
-            in_specs=[SMEM, VMEM, ANY],
-            out_specs=(VMEM, VMEM),
-            scratch_shapes=[weight] * 5 + [pltpu.SemaphoreType.DMA((5,))],
-            compiler_params=PARAMS,
-            cost_estimate=pl.CostEstimate(
-                flops=2 * LOCAL * D * 5 * HD,
-                bytes_accessed=2 * 5 * D * HD + 2 * LOCAL * D,
-                transcendentals=0,
-            ),
-            name="project",
-        )(place, rows, pieces[block])
-        got = lax.ppermute(given, "y", [(at, at ^ 1) for at in range(NY)])
-        attended = pl.pallas_call(
-            own_kernel,
-            out_shape=jax.ShapeDtypeStruct((LOCAL, HD), jnp.bfloat16),
-            in_specs=[SMEM, VMEM, ANY],
-            out_specs=VMEM,
-            scratch_shapes=[cache] * 2 + [pltpu.SemaphoreType.DMA((2,))],
-            compiler_params=PARAMS,
-            cost_estimate=pl.CostEstimate(
-                flops=4 * LOCAL * PATCHES * PT * HD,
-                bytes_accessed=4 * PATCHES * PT * HD,
-                transcendentals=LOCAL * PATCHES * PT,
-            ),
-            name="own",
-        )(place, left, pieces[block])
-        partial = pl.pallas_call(
-            finish_kernel,
-            out_shape=spread,
-            in_specs=[SMEM, VMEM, VMEM, VMEM, ANY],
-            out_specs=VMEM,
-            scratch_shapes=[cache] * 2 + [weight] * 2 + [pltpu.SemaphoreType.DMA((4,))],
-            compiler_params=PARAMS,
-            cost_estimate=pl.CostEstimate(
-                flops=4 * PT * PATCHES * PT * HD + 4 * LOCAL * D * HD,
-                bytes_accessed=4 * PATCHES * PT * HD + 4 * D * HD + 2 * LOCAL * D,
-                transcendentals=PT * PATCHES * PT,
-            ),
-            name="finish",
-        )(place, left, attended, got, pieces[block])
+        source = pieces[block]
+        kept, given = local(
+            shared_project_kernel, (SMEM, VMEM, ANY), (VMEM, VMEM),
+            (rows_of(LOCAL + PT), rows_of(LOCAL + PT)), [weight] * 2, 2 * D * HD,
+        )(place, rows, source)
+        got = swap(given)
+        own = local(
+            own_project_kernel, (VMEM, ANY), VMEM, rows_of(3 * LOCAL), [weight] * 3, 3 * D * HD,
+        )(rows, source)
+        sums, given = local(
+            shared_attend_kernel, (SMEM, VMEM, VMEM, VMEM, ANY), (VMEM, VMEM),
+            (sums_of, sums_of), [half_cache] * 2, PATCHES * PT * HD,
+        )(place, kept, got, own, source)
+        got = swap(given)
+        attended = local(
+            own_attend_kernel, (SMEM, VMEM, VMEM, ANY), VMEM,
+            rows_of(LOCAL), [cache] * 2, 2 * PATCHES * PT * HD,
+        )(place, own, sums, source)
+        partial = local(
+            finish_kernel, (VMEM, VMEM, VMEM, ANY), VMEM, spread, [weight] * 2, 2 * D * HD,
+        )(attended, sums, got, source)
         parts = exchange(partial, HEAD_AXES)
         if block + 1 < BLOCKS:
             current, normed = pl.pallas_call(

time: 324 us -> 300 us (0.926)
  waiting for transfers between devices: 94.3 us -> 66.8 us
  Pallas kernels: 45 us -> 54 us
  blocking collectives: 124 us -> 116 us
    all_gather x4, waiting for transfers between devices: 67.2 us -> 40.8 us  [gather(): return lax.all_gather(received[block], REST_AXES, axis=0, tiled=True)]
    pallas_call x12 -> x20, Pallas kernels: 39.1 us -> 48.1 us  [the longest x4 10.5 us: body(): local(own_attend_kernel, (SMEM, VMEM, VMEM, ANY), VMEM, rows_of(LOCAL), [...]
    all_to_all x6, blocking collectives: 114 us -> 106 us  [exchange(): return lax.all_to_all(array, axes, split_axis=0, concat_axis=0, tiled=True)]
    ppermute x4 -> x8, starting transfers between devices: 5.15 us -> 6.66 us  [swap(): return lax.ppermute(array, 'y', [(at, at ^ 1) for at in range(NY)])]
  transfers between devices with their start and end apart: 14 -> 18, of which waited for: 7 -> 11; matrix products, arithmetic and copies ran while one was open for 1% -> 1% of each run, Pallas kernels for 11% -> 15%
where the time goes in v4:
time: 300 us; the launch traced here: 298 us
  blocking collectives  116 us (39%)
  waiting for transfers between devices  66.8 us (22%)
  Pallas kernels  54 us (18%)
  starting transfers between devices  38.5 us (13%)
  between operations  13.6 us (5%)
  local copies, waits for them, and re-layouts  9.03 us (3%)
    all_to_all x6, blocking collectives, exchange(): return lax.all_to_all(array, axes, split_axis=0, concat_axis=0, tiled=True)  106 us
    all_gather x4, waiting for transfers between devices, gather(): return lax.all_gather(received[block], REST_AXES, axis=0, tiled=True)  40.8 us
    all_to_all x6, starting transfers between devices, exchange(): return lax.all_to_all(array, axes, split_axis=0, concat_axis=0, tiled=True)  31.7 us
    all_to_all x6, waiting for transfers between devices, exchange(): return lax.all_to_all(array, axes, split_axis=0, concat_axis=0, tiled=True)  23.7 us
    pallas_call x4, Pallas kernels, body(): local(own_attend_kernel, (SMEM, VMEM, VMEM, ANY), VMEM, rows_of(LOCAL), [...  10.5 us
    all_gather x1, blocking collectives, body(): lax.all_gather(modulation[0], 'x', axis=0, tiled=False)  10.5 us
    pallas_call x4, Pallas kernels, body(): local(own_project_kernel, (VMEM, ANY), VMEM, rows_of(3 * LOCAL), [weight]...  10.3 us
    pallas_call x4, Pallas kernels, body(): local(shared_project_kernel, (SMEM, VMEM, ANY), (VMEM, VMEM), (rows_of(LO...  9.58 us
  transfers between devices with their start and end apart: 18, of which 11 were waited for; matrix products, arithmetic and copies ran while one was open for 1% of the time, Pallas kernels for 15%

profile of v4, /device:TPU:1, one launch (start us, length us, event | category | flops | bytes accessed | tf_op | source)
XLA Modules:
  0.0 298.3 jit_solution(15182960369085614843)
XLA Ops:
  6.5 1.1 copy.49
  7.7 1.2 copy-done
  8.8 1.0 copy-done.1
  9.8 0.6 pack.1
  10.4 28.9 %all_to_all.117 = bf16[16,384,128]{2,1,0:T(8,128)(2,1)S(1)} all-to-all(bf16[16,384,128]{2,1,0:T(8,128)(2,1)S(1)} %pack.1), channel_id=1, replica_groups=mesh['x'=4,'y'=4,'z'=8,'c'=2] {'x','y'}, dimensions={0} | all-to-all | bytes 3145728 | tf_op jit(solution)/shard_map/all_to_all | solution.py:299
  39.3 1.2 fusion
  40.5 0.7 all-gather.7.cloned.1.call-update
  41.3 0.7 all-gather.9.cloned.1.call-update
  42.0 0.5 all-gather.11.cloned.1.call-update
  42.6 0.8 all_to_all.75
  43.3 10.5 %all-to-all-start = ((bf16[16,2,3072]{2,1,0:T(2,128)(2,1)}), bf16[16,2,3072]{2,1,0:T(2,128)(2,1)S(1)}, u32[]{:S(2)}, u32[]{:S(2)}) async-start(bf16[16,2,3072]{2,1,0:T(2,128)(2,1)} %all_to_all.75), calls=%async_computation | async-start | bytes 393216 | tf_op jit(solution)/shard_map/all_to_all | solution.py:299
  53.8 10.5 %all_gather.15 = f32[4,3,3072]{2,1,0:T(4,128)S(1)} all-gather(f32[1,3,3072]{2,1,0:T(4,128)S(1)} %copy.35), channel_id=1, replica_groups=mesh['x'=4,'y'=4,'z'=8,'c'=2] {'x'}, dimensions={0}, use_global_device_ids=true | all-gather | bytes 184320 | tf_op jit(solution)/shard_map/all_gather | solution.py:327
  64.8 0.4 reshape.84
  65.2 1.0 all-to-all-done
  66.7 1.2 first.1
  67.9 3.6 %all-to-all-start.1 = ((bf16[16,8,3072]{2,1,0:T(8,128)(2,1)}), bf16[16,8,3072]{2,1,0:T(8,128)(2,1)S(1)}, u32[]{:S(2)}, u32[]{:S(2)}) async-start(bf16[16,8,3072]{2,1,0:T(8,128)(2,1)} %bitcast.8), calls=%async_computation.1 | async-start | bytes 1572864 | tf_op jit(solution)/shard_map/all_to_all | solution.py:299
  71.6 12.7 %all-to-all-done.1 = bf16[16,8,3072]{2,1,0:T(8,128)(2,1)S(1)} async-done(((bf16[16,8,3072]{2,1,0:T(8,128)(2,1)}), bf16[16,8,3072]{2,1,0:T(8,128)(2,1)S(1)}, u32[]{:S(2)}, u32[]{:S(2)}) %all-to-all-start.1) | async-done | bytes 786464 | tf_op jit(solution)/shard_map/all_to_all | solution.py:299
  84.3 8.2 %all-gather.5.cloned.1.call-done.pieces_ref = bf16[64,384,128]{2,1,0:T(8,128)(2,1)} async-done(((bf16[4,384,128]{2,1,0:T(8,128)(2,1)}), bf16[64,384,128]{2,1,0:T(8,128)(2,1)}) %all-gather.5.cloned.1.call-update) | async-done | bytes 6291472 | tf_op jit(solution)/shard_map/all_gather | solution.py:323
  92.4 2.4 shared_project_kernel.4
  94.8 1.1 collective-permute-start
  96.0 2.6 own_project_kernel.4.earlier_ref.own_ref
  98.6 2.2 shared_attend_kernel.4
  100.8 0.5 collective-permute-start.1
  101.3 2.6 own_attend_kernel.4.attended_ref
  104.0 2.0 finish_kernel.4
  106.0 16.0 %all_to_all.118 = bf16[16,8,3072]{2,1,0:T(8,128)(2,1)S(1)} all-to-all(bf16[16,8,3072]{2,1,0:T(8,128)(2,1)S(1)} %bitcast.94), channel_id=1, replica_groups=mesh['x'=4,'y'=4,'z'=8,'c'=2] {'x','y'}, dimensions={0} | all-to-all | bytes 1572864 | tf_op jit(solution)/shard_map/all_to_all | solution.py:299
  122.0 1.3 middle.3
  123.3 3.8 %all-to-all-start.4 = ((bf16[16,8,3072]{2,1,0:T(8,128)(2,1)}), bf16[16,8,3072]{2,1,0:T(8,128)(2,1)S(1)}, u32[]{:S(2)}, u32[]{:S(2)}) async-start(bf16[16,8,3072]{2,1,0:T(8,128)(2,1)} %bitcast.21), calls=%async_computation.4 | async-start | bytes 1572864 | tf_op jit(solution)/shard_map/all_to_all | solution.py:299
  127.2 10.0 %all-gather.7.cloned.1.call-done.pieces_ref = bf16[64,384,128]{2,1,0:T(8,128)(2,1)} async-done(((bf16[4,384,128]{2,1,0:T(8,128)(2,1)}), bf16[64,384,128]{2,1,0:T(8,128)(2,1)}) %all-gather.7.cloned.1.call-update) | async-done | bytes 6291472 | tf_op jit(solution)/shard_map/all_gather | solution.py:323
  137.1 0.7 all-to-all-done.4
  137.8 2.4 shared_project_kernel.5
  140.2 0.7 collective-permute-start.2
  140.9 2.6 own_project_kernel.5.earlier_ref.own_ref
  143.5 2.2 shared_attend_kernel.5
  145.8 1.0 collective-permute-start.3
  146.7 2.6 own_attend_kernel.5.attended_ref
  149.4 2.0 finish_kernel.5
  151.4 16.0 %all_to_all.119 = bf16[16,8,3072]{2,1,0:T(8,128)(2,1)S(1)} all-to-all(bf16[16,8,3072]{2,1,0:T(8,128)(2,1)S(1)} %bitcast.95), channel_id=1, replica_groups=mesh['x'=4,'y'=4,'z'=8,'c'=2] {'x','y'}, dimensions={0} | all-to-all | bytes 1572864 | tf_op jit(solution)/shard_map/all_to_all | solution.py:299
  167.3 1.3 middle.4
  168.6 3.7 %all-to-all-start.6 = ((bf16[16,8,3072]{2,1,0:T(8,128)(2,1)}), bf16[16,8,3072]{2,1,0:T(8,128)(2,1)S(1)}, u32[]{:S(2)}, u32[]{:S(2)}) async-start(bf16[16,8,3072]{2,1,0:T(8,128)(2,1)} %bitcast.29), calls=%async_computation.6 | async-start | bytes 1572864 | tf_op jit(solution)/shard_map/all_to_all | solution.py:299
  172.4 11.3 %all-gather.9.cloned.1.call-done.pieces_ref = bf16[64,384,128]{2,1,0:T(8,128)(2,1)} async-done(((bf16[4,384,128]{2,1,0:T(8,128)(2,1)}), bf16[64,384,128]{2,1,0:T(8,128)(2,1)}) %all-gather.9.cloned.1.call-update) | async-done | bytes 6291472 | tf_op jit(solution)/shard_map/all_gather | solution.py:323
  183.7 2.4 shared_project_kernel.6
  186.1 1.2 collective-permute-start.4
  187.4 2.6 own_project_kernel.6.earlier_ref.own_ref
  190.0 2.2 shared_attend_kernel.6
  192.2 0.4 collective-permute-start.5
  192.6 2.6 own_attend_kernel.6.attended_ref
  195.5 2.0 finish_kernel.6
  197.4 16.3 %all_to_all.120 = bf16[16,8,3072]{2,1,0:T(8,128)(2,1)S(1)} all-to-all(bf16[16,8,3072]{2,1,0:T(8,128)(2,1)S(1)} %bitcast.96), channel_id=1, replica_groups=mesh['x'=4,'y'=4,'z'=8,'c'=2] {'x','y'}, dimensions={0} | all-to-all | bytes 1572864 | tf_op jit(solution)/shard_map/all_to_all | solution.py:299
  213.8 1.3 middle.5
  215.1 3.7 %all-to-all-start.8 = ((bf16[16,8,3072]{2,1,0:T(8,128)(2,1)}), bf16[16,8,3072]{2,1,0:T(8,128)(2,1)S(1)}, u32[]{:S(2)}, u32[]{:S(2)}) async-start(bf16[16,8,3072]{2,1,0:T(8,128)(2,1)} %bitcast.37), calls=%async_computation.8 | async-start | bytes 1572864 | tf_op jit(solution)/shard_map/all_to_all | solution.py:299
  218.8 11.3 %all-gather.11.cloned.1.call-done.pieces_ref = bf16[64,384,128]{2,1,0:T(8,128)(2,1)} async-done(((bf16[4,384,128]{2,1,0:T(8,128)(2,1)}), bf16[64,384,128]{2,1,0:T(8,128)(2,1)}) %all-gather.11.cloned.1.call-update) | async-done | bytes 6291472 | tf_op jit(solution)/shard_map/all_gather | solution.py:323
  230.1 2.4 shared_project_kernel.7
  232.5 1.3 collective-permute-start.6
  233.8 2.6 own_project_kernel.7.earlier_ref.own_ref
  236.4 2.2 shared_attend_kernel.7
  238.6 0.4 collective-permute-start.7
  239.0 2.6 own_attend_kernel.7.attended_ref
  241.8 2.8 finish_kernel.7
  244.7 6.3 %all-to-all-start.9 = ((bf16[16,8,3072]{2,1,0:T(8,128)(2,1)}), bf16[16,8,3072]{2,1,0:T(8,128)(2,1)S(1)}, u32[]{:S(2)}, u32[]{:S(2)}) async-start(bf16[16,8,3072]{2,1,0:T(8,128)(2,1)} %bitcast.39), calls=%async_computation.9 | async-start | bytes 1572864 | tf_op jit(solution)/shard_map/all_to_all | solution.py:299
  252.2 9.4 %all-to-all-done.9 = bf16[16,8,3072]{2,1,0:T(8,128)(2,1)S(1)} async-done(((bf16[16,8,3072]{2,1,0:T(8,128)(2,1)}), bf16[16,8,3072]{2,1,0:T(8,128)(2,1)S(1)}, u32[]{:S(2)}, u32[]{:S(2)}) %all-to-all-start.9) | async-done | bytes 786464 | tf_op jit(solution)/shard_map/all_to_all | solution.py:299
  262.1 7.5 %all_to_all.121 = bf16[4,8,3072]{2,1,0:T(8,128)(2,1)S(1)} all-to-all(bf16[4,8,3072]{2,1,0:T(8,128)(2,1)S(1)} %maximum_bitcast_fusion), channel_id=1, replica_groups=mesh['x'=4,'y'=4,'z'=8,'c'=2] {'x'}, dimensions={0} | all-to-all | bytes 393216 | tf_op jit(solution)/shard_map/all_to_all | solution.py:299
  269.9 21.2 %all_to_all.122 = bf16[16,2,3072]{2,1,0:T(2,128)(2,1)S(1)} all-to-all(bf16[16,2,3072]{2,1,0:T(2,128)(2,1)S(1)} %copy.43), channel_id=1, replica_groups=mesh['x'=4,'y'=4,'z'=8,'c'=2] {'z','c'}, dimensions={0} | all-to-all | bytes 393216 | tf_op jit(solution)/shard_map/all_to_all | solution.py:299
  291.0 0.8 broadcast_in_dim.3
  (47 shorter events, 3.5 us)
Async XLA Ops:
  6.5 36.0 %copy-start.2 = (bf16[32,1,3072]{2,0,1:T(8,128)(2,1)S(1)}, bf16[32,1,3072]{2,0,1:T(8,128)(2,1)}, u32[]{:S(2)}) copy-start(bf16[32,1,3072]{2,0,1:T(8,128)(2,1)} %param.5) | copy-start | bytes 589828
  6.5 47.3 %copy-start.3 = (f32[1,3,3072]{2,0,1:T(1,128)S(1)}, f32[1,3,3072]{2,0,1:T(1,128)}, u32[]{:S(2)}) copy-start(f32[1,3,3072]{2,0,1:T(1,128)} %param.6) | copy-start | bytes 110596
  6.5 85.9 %all-gather.5.cloned.1.call-start = ((), (), s32[]{:S(2)}) async-start(), calls=%async_computation.12 | async-start | bytes 6684672 | tf_op jit(solution)/shard_map/all_gather | solution.py:323
  7.6 1.2 copy-start
  8.8 1.0 copy-start.1
  40.5 96.6 %all-gather.7.cloned.1.call-start = ((), (), s32[]{:S(2)}) async-start(), calls=%async_computation.13 | async-start | bytes 6684672 | tf_op jit(solution)/shard_map/all_gather | solution.py:323
  41.2 142.5 %all-gather.9.cloned.1.call-start = ((), (), s32[]{:S(2)}) async-start(), calls=%async_computation.14 | async-start | bytes 6684672 | tf_op jit(solution)/shard_map/all_gather | solution.py:323
  42.0 188.1 %all-gather.11.cloned.1.call-start = ((), (), s32[]{:S(2)}) async-start(), calls=%async_computation.15 | async-start | bytes 6684672 | tf_op jit(solution)/shard_map/all_gather | solution.py:323
  43.3 22.9 %all-to-all-start = ((bf16[16,2,3072]{2,1,0:T(2,128)(2,1)}), bf16[16,2,3072]{2,1,0:T(2,128)(2,1)S(1)}, u32[]{:S(2)}, u32[]{:S(2)}) async-start(bf16[16,2,3072]{2,1,0:T(2,128)(2,1)} %all_to_all.75), calls=%async_computation | async-start | bytes 393216 | tf_op jit(solution)/shard_map/all_to_all | solution.py:299
  67.9 16.4 %all-to-all-start.1 = ((bf16[16,8,3072]{2,1,0:T(8,128)(2,1)}), bf16[16,8,3072]{2,1,0:T(8,128)(2,1)S(1)}, u32[]{:S(2)}, u32[]{:S(2)}) async-start(bf16[16,8,3072]{2,1,0:T(8,128)(2,1)} %bitcast.8), calls=%async_computation.1 | async-start | bytes 1572864 | tf_op jit(solution)/shard_map/all_to_all | solution.py:299
  94.8 3.7 %collective-permute-start = (bf16[192,128]{1,0:T(8,128)(2,1)S(1)}, bf16[192,128]{1,0:T(8,128)(2,1)S(1)}, u32[]{:S(2)}, u32[]{:S(2)}) collective-permute-start(bf16[192,128]{1,0:T(8,128)(2,1)S(1)} %get-tuple-element.28), channel_id=1, source_target_pairs={{0,16},{16,0},{32,48},{48,32},{1,17},{17,1},{33,49},{49,33},{2,18}... | collective-permute-start | bytes 147464 | tf_op jit(solution)/shard_map/ppermute | solution.py:368
  100.8 3.2 %collective-permute-start.1 = (f32[128,128]{1,0:T(8,128)S(1)}, f32[128,128]{1,0:T(8,128)S(1)}, u32[]{:S(2)}, u32[]{:S(2)}) collective-permute-start(f32[128,128]{1,0:T(8,128)S(1)} %get-tuple-element.30), channel_id=1, source_target_pairs={{0,16},{16,0},{32,48},{48,32},{1,17},{17,1},{33,49},{49,33},{2,18}... | collective-permute-start | bytes 196616 | tf_op jit(solution)/shard_map/ppermute | solution.py:368
  123.3 14.5 %all-to-all-start.4 = ((bf16[16,8,3072]{2,1,0:T(8,128)(2,1)}), bf16[16,8,3072]{2,1,0:T(8,128)(2,1)S(1)}, u32[]{:S(2)}, u32[]{:S(2)}) async-start(bf16[16,8,3072]{2,1,0:T(8,128)(2,1)} %bitcast.21), calls=%async_computation.4 | async-start | bytes 1572864 | tf_op jit(solution)/shard_map/all_to_all | solution.py:299
  140.2 3.3 %collective-permute-start.2 = (bf16[192,128]{1,0:T(8,128)(2,1)S(1)}, bf16[192,128]{1,0:T(8,128)(2,1)S(1)}, u32[]{:S(2)}, u32[]{:S(2)}) collective-permute-start(bf16[192,128]{1,0:T(8,128)(2,1)S(1)} %get-tuple-element.34), channel_id=1, source_target_pairs={{0,16},{16,0},{32,48},{48,32},{1,17},{17,1},{33,49},{49,33},{2,18}... | collective-permute-start | bytes 147464 | tf_op jit(solution)/shard_map/ppermute | solution.py:368
  145.8 3.6 %collective-permute-start.3 = (f32[128,128]{1,0:T(8,128)S(1)}, f32[128,128]{1,0:T(8,128)S(1)}, u32[]{:S(2)}, u32[]{:S(2)}) collective-permute-start(f32[128,128]{1,0:T(8,128)S(1)} %get-tuple-element.36), channel_id=1, source_target_pairs={{0,16},{16,0},{32,48},{48,32},{1,17},{17,1},{33,49},{49,33},{2,18}... | collective-permute-start | bytes 196616 | tf_op jit(solution)/shard_map/ppermute | solution.py:368
  168.6 15.1 %all-to-all-start.6 = ((bf16[16,8,3072]{2,1,0:T(8,128)(2,1)}), bf16[16,8,3072]{2,1,0:T(8,128)(2,1)S(1)}, u32[]{:S(2)}, u32[]{:S(2)}) async-start(bf16[16,8,3072]{2,1,0:T(8,128)(2,1)} %bitcast.29), calls=%async_computation.6 | async-start | bytes 1572864 | tf_op jit(solution)/shard_map/all_to_all | solution.py:299
  186.1 3.8 %collective-permute-start.4 = (bf16[192,128]{1,0:T(8,128)(2,1)S(1)}, bf16[192,128]{1,0:T(8,128)(2,1)S(1)}, u32[]{:S(2)}, u32[]{:S(2)}) collective-permute-start(bf16[192,128]{1,0:T(8,128)(2,1)S(1)} %get-tuple-element.40), channel_id=1, source_target_pairs={{0,16},{16,0},{32,48},{48,32},{1,17},{17,1},{33,49},{49,33},{2,18}... | collective-permute-start | bytes 147464 | tf_op jit(solution)/shard_map/ppermute | solution.py:368
  192.2 3.3 %collective-permute-start.5 = (f32[128,128]{1,0:T(8,128)S(1)}, f32[128,128]{1,0:T(8,128)S(1)}, u32[]{:S(2)}, u32[]{:S(2)}) collective-permute-start(f32[128,128]{1,0:T(8,128)S(1)} %get-tuple-element.42), channel_id=1, source_target_pairs={{0,16},{16,0},{32,48},{48,32},{1,17},{17,1},{33,49},{49,33},{2,18}... | collective-permute-start | bytes 196616 | tf_op jit(solution)/shard_map/ppermute | solution.py:368
  215.1 15.0 %all-to-all-start.8 = ((bf16[16,8,3072]{2,1,0:T(8,128)(2,1)}), bf16[16,8,3072]{2,1,0:T(8,128)(2,1)S(1)}, u32[]{:S(2)}, u32[]{:S(2)}) async-start(bf16[16,8,3072]{2,1,0:T(8,128)(2,1)} %bitcast.37), calls=%async_computation.8 | async-start | bytes 1572864 | tf_op jit(solution)/shard_map/all_to_all | solution.py:299
  232.5 3.9 %collective-permute-start.6 = (bf16[192,128]{1,0:T(8,128)(2,1)S(1)}, bf16[192,128]{1,0:T(8,128)(2,1)S(1)}, u32[]{:S(2)}, u32[]{:S(2)}) collective-permute-start(bf16[192,128]{1,0:T(8,128)(2,1)S(1)} %get-tuple-element.46), channel_id=1, source_target_pairs={{0,16},{16,0},{32,48},{48,32},{1,17},{17,1},{33,49},{49,33},{2,18}... | collective-permute-start | bytes 147464 | tf_op jit(solution)/shard_map/ppermute | solution.py:368
  238.6 3.2 %collective-permute-start.7 = (f32[128,128]{1,0:T(8,128)S(1)}, f32[128,128]{1,0:T(8,128)S(1)}, u32[]{:S(2)}, u32[]{:S(2)}) collective-permute-start(f32[128,128]{1,0:T(8,128)S(1)} %get-tuple-element.48), channel_id=1, source_target_pairs={{0,16},{16,0},{32,48},{48,32},{1,17},{17,1},{33,49},{49,33},{2,18}... | collective-permute-start | bytes 196616 | tf_op jit(solution)/shard_map/ppermute | solution.py:368
  244.7 16.9 %all-to-all-start.9 = ((bf16[16,8,3072]{2,1,0:T(8,128)(2,1)}), bf16[16,8,3072]{2,1,0:T(8,128)(2,1)S(1)}, u32[]{:S(2)}, u32[]{:S(2)}) async-start(bf16[16,8,3072]{2,1,0:T(8,128)(2,1)} %bitcast.39), calls=%async_computation.9 | async-start | bytes 1572864 | tf_op jit(solution)/shard_map/all_to_all | solution.py:299
Sparse Core Ops, SparseCore 0:
  40.6 51.7 all-gather.4
  94.3 42.8 all-gather.6
  139.0 44.7 all-gather.8
  185.4 44.6 all-gather.10

commit v5 on v4

--- a/solution.py
+++ b/solution.py
@@ -32,6 +32,7 @@
 ANY = pl.BlockSpec(memory_space=pl.ANY)
 SMEM = pl.BlockSpec(memory_space=pltpu.SMEM)
 VMEM = pl.BlockSpec(memory_space=pltpu.VMEM)
+SMALL = pltpu.CompilerParams(vmem_limit_bytes=24 * 1024 * 1024)
 PARAMS = pltpu.CompilerParams(vmem_limit_bytes=48 * 1024 * 1024)
 
 
@@ -89,7 +90,9 @@
         put(member, AT_SHARED_VO, jnp.concatenate([w_v[:, lanes], w_o[:, lanes]], axis=1))
 
 
-def first_kernel(rows_ref, shift_ref, scale_ref, normed_ref):
+def first_kernel(place_ref, rows_ref, shift_ref, scale_ref, normed_ref, blocks_ref):
+    for block in range(BLOCKS):
+        blocks_ref[block] = place_ref[2] + block
     normed = modulate(rows_ref[...].astype(jnp.float32), shift_ref[...], scale_ref[...])
     twice = jnp.concatenate([normed, normed], axis=0)
     for at in range(0, LOCAL, 2 * OWN):
@@ -163,8 +166,18 @@
     given_ref[LOCAL:] = pick(1 - half, values)
 
 
-def own_project_kernel(rows_ref, pieces_ref, own_ref, w_q, w_k, w_v, sems):
-    copies = fetch(pieces_ref, sems, [(w_q, 0), (w_k, ROWS), (w_v, 2 * ROWS)])
+def own_project_kernel(rows_ref, pieces_ref, own_ref, keys, values, w_q, w_k, w_v, sems):
+    copies = fetch(
+        pieces_ref,
+        sems,
+        [
+            (w_q, 0),
+            (w_k, ROWS),
+            (w_v, 2 * ROWS),
+            (keys, AT_SHARED_K),
+            (values, AT_SHARED_V),
+        ],
+    )
     rows = rows_ref[...]
     copies[0].wait()
     copies[1].wait()
@@ -173,6 +186,8 @@
     own_ref[LOCAL : 2 * LOCAL] = head_norm(both[:, HD:])
     copies[2].wait()
     own_ref[2 * LOCAL :] = project(rows, w_v).astype(jnp.bfloat16)
+    copies[3].wait()
+    copies[4].wait()
 
 
 def weigh(queries, keys):
@@ -204,10 +219,8 @@
 
 
 def shared_attend_kernel(
-    place_ref, kept_ref, got_ref, earlier_ref, pieces_ref, sums_ref, given_ref, keys, values, sems
+    place_ref, kept_ref, got_ref, keys, values, sums_ref, given_ref
 ):
-    del earlier_ref
-    copies = fetch(pieces_ref, sems, [(keys, AT_SHARED_K), (values, AT_SHARED_V)])
     half = place_ref[1]
     kept, got = kept_ref[:LOCAL], got_ref[:LOCAL]
     queries = jnp.where(half == 0, kept, got)
@@ -226,8 +239,6 @@
 
     total = placed(jnp.sum(fresh, axis=1, keepdims=True))
     gathered = placed(gather_values(fresh, fresh_values))
-    for copy in copies:
-        copy.wait()
     total, gathered = attend_stale(
         queries,
         keys,
@@ -243,9 +254,15 @@
     given_ref[...] = jnp.where(first, total, jnp.where(half == 0, gathered, swapped))
 
 
-def own_attend_kernel(place_ref, own_ref, earlier_ref, pieces_ref, attended_ref, keys, values, sems):
+def own_attend_kernel(
+    place_ref, own_ref, earlier_ref, pieces_ref, attended_ref, w_own, w_vo, keys, values, sems
+):
     del earlier_ref
-    copies = fetch(pieces_ref, sems, [(keys, AT_K), (values, AT_V)])
+    copies = fetch(
+        pieces_ref,
+        sems,
+        [(keys, AT_K), (values, AT_V), (w_own, AT_OUT), (w_vo, AT_SHARED_VO)],
+    )
     queries = own_ref[:LOCAL]
     fresh = weigh(queries, own_ref[LOCAL : 2 * LOCAL])
     row_at = lax.broadcasted_iota(jnp.int32, (LOCAL, 1), 0)
@@ -253,21 +270,20 @@
     fresh = jnp.where((row_at >= PT) == (column_at >= PT), fresh, 0.0)
     total = jnp.sum(fresh, axis=1, keepdims=True)
     gathered = gather_values(fresh, own_ref[2 * LOCAL :])
-    for copy in copies:
-        copy.wait()
+    copies[0].wait()
+    copies[1].wait()
     total, gathered = attend_stale(
         queries, keys, values, 0, patch_of_rows(place_ref), total, gathered
     )
     attended_ref[...] = (gathered / total).astype(jnp.bfloat16)
-
-
-def finish_kernel(attended_ref, sums_ref, got_ref, pieces_ref, partial_ref, w_own, w_vo, sems):
-    copies = fetch(pieces_ref, sems, [(w_own, AT_OUT), (w_vo, AT_SHARED_VO)])
+    copies[2].wait()
+    copies[3].wait()
+
+
+def finish_kernel(attended_ref, sums_ref, got_ref, w_own, w_vo, partial_ref):
     sums = sums_ref[...] + got_ref[...]
     shared = jnp.where(low_lanes(LOCAL), 0.0, sums / sums[:, :1]).astype(jnp.bfloat16)
     attention = jnp.concatenate([attended_ref[...], shared], axis=1)
-    for copy in copies:
-        copy.wait()
     step = 8
     width = step * ROWS
     for low in range(0, SOURCES, step):
@@ -302,7 +318,7 @@
 def body(latent, modulation, w_qkv, w_out, stale):
     x_at, y_at = lax.axis_index("x"), lax.axis_index("y")
     pair_at = lax.axis_index("z") * NC + lax.axis_index("c")
-    place = jnp.stack([2 * pair_at, y_at % 2]).astype(jnp.int32)
+    place = jnp.stack([2 * pair_at, y_at % 2, 0 * y_at]).astype(jnp.int32)
 
     sent = pl.pallas_call(
         pack_kernel,
@@ -320,14 +336,16 @@
     received = exchange(sent, HEAD_AXES).reshape(BLOCKS, NY, PIECE, HD)
 
     def gather(block):
-        return lax.all_gather(received[block], REST_AXES, axis=0, tiled=True)
-
-    pieces = [gather(block) for block in range(BLOCKS)]
+        own_piece = lax.dynamic_index_in_dim(received, block, 0, keepdims=False)
+        return lax.all_gather(own_piece, REST_AXES, axis=0, tiled=True)
+
+    pieces = [gather(0)]
 
     terms = to_own_order(lax.all_gather(modulation[0], "x", axis=0, tiled=False))
-    mine = exchange(latent[:, 0], REST_AXES).reshape(NZ * NC, 2, D)
-    mine = jnp.swapaxes(mine, 0, 1).reshape(NZ * NC * 2, D)
-    current = to_own_order(lax.dynamic_slice_in_dim(mine, x_at * OWN, OWN, 0))
+    wanted = latent.reshape(NZ * NC, 2, D)
+    wanted = lax.dynamic_index_in_dim(wanted, x_at // 2, 1, keepdims=False)
+    mine = exchange(wanted, REST_AXES)
+    current = to_own_order(lax.dynamic_slice_in_dim(mine, (x_at % 2) * OWN, OWN, 0))
 
     def term(block, which):
         return terms[block, which][None]
@@ -336,28 +354,30 @@
     weight = pltpu.VMEM((SOURCES, ROWS, HD), jnp.bfloat16)
     cache = pltpu.VMEM((SOURCES, PATCHES, HD), jnp.bfloat16)
     owned = jax.ShapeDtypeStruct((OWN, D), jnp.bfloat16)
-    normed = pl.pallas_call(
+    normed, blocks = pl.pallas_call(
         first_kernel,
-        out_shape=spread,
-        in_specs=[VMEM] * 3,
-        out_specs=VMEM,
+        out_shape=(spread, jax.ShapeDtypeStruct((BLOCKS,), jnp.int32)),
+        in_specs=[SMEM] + [VMEM] * 3,
+        out_specs=(VMEM, SMEM),
         compiler_params=PARAMS,
         name="first",
-    )(current, term(0, 0), term(0, 1))
-    half_cache = pltpu.VMEM((SOURCES, PATCHES // 2, HD), jnp.bfloat16)
+    )(place, current, term(0, 0), term(0, 1))
+    pieces += [gather(blocks[block]) for block in range(1, BLOCKS)]
+    half_cache = jax.ShapeDtypeStruct((SOURCES, PATCHES // 2, HD), jnp.bfloat16)
+    kept_weight = jax.ShapeDtypeStruct((SOURCES, ROWS, HD), jnp.bfloat16)
     sums_of = jax.ShapeDtypeStruct((LOCAL, HD), jnp.float32)
 
     def rows_of(count):
         return jax.ShapeDtypeStruct((count, HD), jnp.bfloat16)
 
-    def local(kernel, in_specs, out_specs, out_shape, scratch, elements):
+    def local(kernel, in_specs, out_specs, out_shape, scratch, copies, elements):
         return pl.pallas_call(
             kernel,
             out_shape=out_shape,
             in_specs=in_specs,
             out_specs=out_specs,
-            scratch_shapes=scratch + [pltpu.SemaphoreType.DMA((len(scratch),))],
-            compiler_params=PARAMS,
+            scratch_shapes=scratch + [pltpu.SemaphoreType.DMA((copies,))] * (copies > 0),
+            compiler_params=PARAMS if copies else SMALL,
             cost_estimate=pl.CostEstimate(
                 flops=2 * LOCAL * elements, bytes_accessed=2 * elements, transcendentals=0
             ),
@@ -373,24 +393,25 @@
         source = pieces[block]
         kept, given = local(
             shared_project_kernel, (SMEM, VMEM, ANY), (VMEM, VMEM),
-            (rows_of(LOCAL + PT), rows_of(LOCAL + PT)), [weight] * 2, 2 * D * HD,
+            (rows_of(LOCAL + PT), rows_of(LOCAL + PT)), [weight] * 2, 2, 2 * D * HD,
         )(place, rows, source)
         got = swap(given)
-        own = local(
-            own_project_kernel, (VMEM, ANY), VMEM, rows_of(3 * LOCAL), [weight] * 3, 3 * D * HD,
+        own, keys, values = local(
+            own_project_kernel, (VMEM, ANY), (VMEM, VMEM, VMEM),
+            (rows_of(3 * LOCAL), half_cache, half_cache), [weight] * 3, 5, 3 * D * HD,
         )(rows, source)
         sums, given = local(
-            shared_attend_kernel, (SMEM, VMEM, VMEM, VMEM, ANY), (VMEM, VMEM),
-            (sums_of, sums_of), [half_cache] * 2, PATCHES * PT * HD,
-        )(place, kept, got, own, source)
+            shared_attend_kernel, (SMEM,) + (VMEM,) * 4, (VMEM, VMEM),
+            (sums_of, sums_of), [], 0, PATCHES * PT * HD,
+        )(place, kept, got, keys, values)
         got = swap(given)
-        attended = local(
-            own_attend_kernel, (SMEM, VMEM, VMEM, ANY), VMEM,
-            rows_of(LOCAL), [cache] * 2, 2 * PATCHES * PT * HD,
+        attended, w_own, w_vo = local(
+            own_attend_kernel, (SMEM, VMEM, VMEM, ANY), (VMEM, VMEM, VMEM),
+            (rows_of(LOCAL), kept_weight, kept_weight), [cache] * 2, 4, 2 * PATCHES * PT * HD,
         )(place, own, sums, source)
         partial = local(
-            finish_kernel, (VMEM, VMEM, VMEM, ANY), VMEM, spread, [weight] * 2, 2 * D * HD,
-        )(attended, sums, got, source)
+            finish_kernel, (VMEM,) * 5, VMEM, spread, [], 0, 2 * D * HD,
+        )(attended, sums, got, w_own, w_vo)
         parts = exchange(partial, HEAD_AXES)
         if block + 1 < BLOCKS:
             current, normed = pl.pallas_call(

time: 300 us -> 294 us (0.980)
  waiting for transfers between devices: 66.8 us -> 50.1 us
  blocking collectives: 116 us -> 130 us
  Pallas kernels: 54 us -> 44.8 us
  between operations: 13.6 us -> 19.7 us
  starting transfers between devices: 38.5 us -> 35 us
    all_to_all x6 -> x7, blocking collectives: 106 us -> 120 us  [exchange(): return lax.all_to_all(array, axes, split_axis=0, concat_axis=0, tiled=True)]
    all_to_all x6 -> x5, waiting for transfers between devices: 23.7 us -> 10.8 us  [exchange(): return lax.all_to_all(array, axes, split_axis=0, concat_axis=0, tiled=True)]
    pallas_call x17, Pallas kernels: 39.7 us -> 30.6 us  [the longest x4 10.6 us: body(): local(own_attend_kernel, (SMEM, VMEM, VMEM, ANY), (VMEM, VMEM, VMEM), (ro...]
    all_to_all x6 -> x5, starting transfers between devices: 31.7 us -> 28 us  [exchange(): return lax.all_to_all(array, axes, split_axis=0, concat_axis=0, tiled=True)]
    all_gather x4, waiting for transfers between devices: 40.8 us -> 37.6 us  [gather(): return lax.all_gather(own_piece, REST_AXES, axis=0, tiled=True)]
  transfers between devices with their start and end apart: 18 -> 17, of which waited for: 11 -> 7; matrix products, arithmetic and copies ran while one was open for 1% -> 2% of each run, Pallas kernels for 15% -> 13%
where the time goes in v5:
time: 294 us; the launch traced here: 293 us
  blocking collectives  130 us (44%)
  waiting for transfers between devices  50.1 us (17%)
  Pallas kernels  44.8 us (15%)
  starting transfers between devices  35 us (12%)
  between operations  19.7 us (7%)
  local copies, waits for them, and re-layouts  11.4 us (4%)
    all_to_all x7, blocking collectives, exchange(): return lax.all_to_all(array, axes, split_axis=0, concat_axis=0, tiled=True)  120 us
    all_gather x4, waiting for transfers between devices, gather(): return lax.all_gather(own_piece, REST_AXES, axis=0, tiled=True)  37.6 us
    all_to_all x5, starting transfers between devices, exchange(): return lax.all_to_all(array, axes, split_axis=0, concat_axis=0, tiled=True)  28 us
    all_to_all x5, waiting for transfers between devices, exchange(): return lax.all_to_all(array, axes, split_axis=0, concat_axis=0, tiled=True)  10.8 us
    pallas_call x4, Pallas kernels, body(): local(own_attend_kernel, (SMEM, VMEM, VMEM, ANY), (VMEM, VMEM, VMEM), (ro...  10.6 us
    all_gather x1, blocking collectives, body(): lax.all_gather(modulation[0], 'x', axis=0, tiled=False)  10.5 us
    pallas_call x4, Pallas kernels, body(): local(own_project_kernel, (VMEM, ANY), (VMEM, VMEM, VMEM), (rows_of(3 * L...  10.4 us
    pallas_call x4, Pallas kernels, body(): local(shared_project_kernel, (SMEM, VMEM, ANY), (VMEM, VMEM), (rows_of(LO...  9.58 us
  transfers between devices with their start and end apart: 17, of which 7 were waited for; matrix products, arithmetic and copies ran while one was open for 2% of the time, Pallas kernels for 13%

profile of v5, /device:TPU:1, one launch (start us, length us, event | category | flops | bytes accessed | tf_op | source)
XLA Modules:
  0.0 292.6 jit_solution(14674350323956275060)
XLA Ops:
  6.5 1.1 copy.57
  7.7 1.2 copy-done
  8.8 1.0 copy-done.1
  9.8 0.6 pack.1
  10.4 28.9 %all_to_all.114 = bf16[16,384,128]{2,1,0:T(8,128)(2,1)S(1)} all-to-all(bf16[16,384,128]{2,1,0:T(8,128)(2,1)S(1)} %pack.1), channel_id=1, replica_groups=mesh['x'=4,'y'=4,'z'=8,'c'=2] {'x','y'}, dimensions={0} | all-to-all | bytes 3145728 | tf_op jit(solution)/shard_map/all_to_all | solution.py:315
  39.3 0.8 dynamic_slice.27
  40.4 0.5 broadcast.4
  41.0 1.2 reduce.2
  42.2 0.7 reshape.95
  42.8 10.5 %all-to-all-start = ((bf16[16,2,1536]{2,1,0:T(2,128)(2,1)}), bf16[16,2,1536]{2,1,0:T(2,128)(2,1)S(1)}, u32[]{:S(2)}, u32[]{:S(2)}) async-start(bf16[16,2,1536]{2,1,0:T(2,128)(2,1)} %reshape.95), calls=%async_computation | async-start | bytes 196608 | tf_op jit(solution)/shard_map/all_to_all | solution.py:315
  53.4 10.5 %all_gather.15 = f32[4,3,3072]{2,1,0:T(4,128)S(1)} all-gather(f32[1,3,3072]{2,1,0:T(4,128)S(1)} %copy.37), channel_id=1, replica_groups=mesh['x'=4,'y'=4,'z'=8,'c'=2] {'x'}, dimensions={0}, use_global_device_ids=true | all-gather | bytes 184320 | tf_op jit(solution)/shard_map/all_gather | solution.py:344
  64.3 0.4 reshape.80
  65.0 0.3 dynamic-slice_reduce_fusion
  65.7 1.1 first.1
  66.9 0.7 fusion
  73.6 1.1 dynamic-slice_bitcast_fusion
  74.8 0.7 all-gather.12.cloned.1.call-update
  75.5 0.5 all-gather.14.cloned.1.call-update
  76.0 14.8 %all_to_all.115 = bf16[16,8,3072]{2,1,0:T(8,128)(2,1)S(1)} all-to-all(bf16[16,8,3072]{2,1,0:T(8,128)(2,1)S(1)} %bitcast.114), channel_id=1, replica_groups=mesh['x'=4,'y'=4,'z'=8,'c'=2] {'x','y'}, dimensions={0} | all-to-all | bytes 1572864 | tf_op jit(solution)/shard_map/all_to_all | solution.py:315
  90.9 2.4 shared_project_kernel.4
  93.3 0.6 collective-permute-start
  93.8 2.6 own_project_kernel.4
  96.5 1.3 shared_attend_kernel.4
  97.7 1.1 collective-permute-start.1
  98.8 2.7 own_attend_kernel.4
  101.5 0.6 finish_kernel.4
  102.1 13.9 %all_to_all.116 = bf16[16,8,3072]{2,1,0:T(8,128)(2,1)S(1)} all-to-all(bf16[16,8,3072]{2,1,0:T(8,128)(2,1)S(1)} %bitcast.105), channel_id=1, replica_groups=mesh['x'=4,'y'=4,'z'=8,'c'=2] {'x','y'}, dimensions={0} | all-to-all | bytes 1572864 | tf_op jit(solution)/shard_map/all_to_all | solution.py:315
  116.0 1.3 middle.3
  117.3 3.7 %all-to-all-start.4 = ((bf16[16,8,3072]{2,1,0:T(8,128)(2,1)}), bf16[16,8,3072]{2,1,0:T(8,128)(2,1)S(1)}, u32[]{:S(2)}, u32[]{:S(2)}) async-start(bf16[16,8,3072]{2,1,0:T(8,128)(2,1)} %bitcast.19), calls=%async_computation.4 | async-start | bytes 1572864 | tf_op jit(solution)/shard_map/all_to_all | solution.py:315
  121.1 13.5 %all-gather.10.cloned.1.call-done = bf16[1,64,384,128]{3,2,0,1:T(8,128)(2,1)} async-done(((bf16[1,4,384,128]{3,2,0,1:T(8,128)(2,1)}), bf16[1,64,384,128]{3,2,0,1:T(8,128)(2,1)}) %all-gather.10.cloned.1.call-update) | async-done | bytes 6291472 | tf_op jit(solution)/shard_map/all_gather | solution.py:340
  134.6 2.4 shared_project_kernel.5
  137.0 1.3 collective-permute-start.2
  138.3 2.6 own_project_kernel.5
  140.9 1.3 shared_attend_kernel.5
  142.1 0.6 collective-permute-start.3
  142.7 2.7 own_attend_kernel.5
  145.5 0.6 finish_kernel.5
  146.1 18.0 %all_to_all.117 = bf16[16,8,3072]{2,1,0:T(8,128)(2,1)S(1)} all-to-all(bf16[16,8,3072]{2,1,0:T(8,128)(2,1)S(1)} %bitcast.106), channel_id=1, replica_groups=mesh['x'=4,'y'=4,'z'=8,'c'=2] {'x','y'}, dimensions={0} | all-to-all | bytes 1572864 | tf_op jit(solution)/shard_map/all_to_all | solution.py:315
  164.1 1.3 middle.4
  165.4 3.6 %all-to-all-start.6 = ((bf16[16,8,3072]{2,1,0:T(8,128)(2,1)}), bf16[16,8,3072]{2,1,0:T(8,128)(2,1)S(1)}, u32[]{:S(2)}, u32[]{:S(2)}) async-start(bf16[16,8,3072]{2,1,0:T(8,128)(2,1)} %bitcast.30), calls=%async_computation.6 | async-start | bytes 1572864 | tf_op jit(solution)/shard_map/all_to_all | solution.py:315
  169.0 12.1 %all-gather.12.cloned.1.call-done = bf16[1,64,384,128]{3,2,0,1:T(8,128)(2,1)} async-done(((bf16[1,4,384,128]{3,2,0,1:T(8,128)(2,1)}), bf16[1,64,384,128]{3,2,0,1:T(8,128)(2,1)}) %all-gather.12.cloned.1.call-update) | async-done | bytes 6291472 | tf_op jit(solution)/shard_map/all_gather | solution.py:340
  181.1 2.4 shared_project_kernel.6
  183.5 1.3 collective-permute-start.4
  184.8 2.6 own_project_kernel.6
  187.4 1.3 shared_attend_kernel.6
  188.7 0.4 collective-permute-start.5
  189.1 2.7 own_attend_kernel.6
  191.9 0.6 finish_kernel.6
  192.5 17.8 %all_to_all.118 = bf16[16,8,3072]{2,1,0:T(8,128)(2,1)S(1)} all-to-all(bf16[16,8,3072]{2,1,0:T(8,128)(2,1)S(1)} %bitcast.107), channel_id=1, replica_groups=mesh['x'=4,'y'=4,'z'=8,'c'=2] {'x','y'}, dimensions={0} | all-to-all | bytes 1572864 | tf_op jit(solution)/shard_map/all_to_all | solution.py:315
  210.4 1.3 middle.5
  211.7 3.8 %all-to-all-start.8 = ((bf16[16,8,3072]{2,1,0:T(8,128)(2,1)}), bf16[16,8,3072]{2,1,0:T(8,128)(2,1)S(1)}, u32[]{:S(2)}, u32[]{:S(2)}) async-start(bf16[16,8,3072]{2,1,0:T(8,128)(2,1)} %bitcast.40), calls=%async_computation.8 | async-start | bytes 1572864 | tf_op jit(solution)/shard_map/all_to_all | solution.py:315
  215.5 12.0 %all-gather.14.cloned.1.call-done = bf16[1,64,384,128]{3,2,0,1:T(8,128)(2,1)} async-done(((bf16[1,4,384,128]{3,2,0,1:T(8,128)(2,1)}), bf16[1,64,384,128]{3,2,0,1:T(8,128)(2,1)}) %all-gather.14.cloned.1.call-update) | async-done | bytes 6291472 | tf_op jit(solution)/shard_map/all_gather | solution.py:340
  227.5 2.4 shared_project_kernel.7
  229.9 1.3 collective-permute-start.6
  231.2 2.6 own_project_kernel.7
  233.8 1.3 shared_attend_kernel.7
  235.1 0.4 collective-permute-start.7
  235.5 2.7 own_attend_kernel.7
  238.3 1.5 finish_kernel.7
  239.8 6.3 %all-to-all-start.9 = ((bf16[16,8,3072]{2,1,0:T(8,128)(2,1)}), bf16[16,8,3072]{2,1,0:T(8,128)(2,1)S(1)}, u32[]{:S(2)}, u32[]{:S(2)}) async-start(bf16[16,8,3072]{2,1,0:T(8,128)(2,1)} %bitcast.44), calls=%async_computation.9 | async-start | bytes 1572864 | tf_op jit(solution)/shard_map/all_to_all | solution.py:315
  247.4 10.8 %all-to-all-done.9 = bf16[16,8,3072]{2,1,0:T(8,128)(2,1)S(1)} async-done(((bf16[16,8,3072]{2,1,0:T(8,128)(2,1)}), bf16[16,8,3072]{2,1,0:T(8,128)(2,1)S(1)}, u32[]{:S(2)}, u32[]{:S(2)}) %all-to-all-start.9) | async-done | bytes 786464 | tf_op jit(solution)/shard_map/all_to_all | solution.py:315
  258.7 7.5 %all_to_all.119 = bf16[4,8,3072]{2,1,0:T(8,128)(2,1)S(1)} all-to-all(bf16[4,8,3072]{2,1,0:T(8,128)(2,1)S(1)} %maximum_bitcast_fusion), channel_id=1, replica_groups=mesh['x'=4,'y'=4,'z'=8,'c'=2] {'x'}, dimensions={0} | all-to-all | bytes 393216 | tf_op jit(solution)/shard_map/all_to_all | solution.py:315
  266.5 18.9 %all_to_all.120 = bf16[16,2,3072]{2,1,0:T(2,128)(2,1)S(1)} all-to-all(bf16[16,2,3072]{2,1,0:T(2,128)(2,1)S(1)} %copy.48), channel_id=1, replica_groups=mesh['x'=4,'y'=4,'z'=8,'c'=2] {'z','c'}, dimensions={0} | all-to-all | bytes 393216 | tf_op jit(solution)/shard_map/all_to_all | solution.py:315
  285.3 0.8 broadcast_in_dim.3
  (52 shorter events, 3.9 us)
Async XLA Ops:
  6.5 33.6 %copy-start.2 = (bf16[32,1,3072]{2,0,1:T(8,128)(2,1)S(1)}, bf16[32,1,3072]{2,0,1:T(8,128)(2,1)}, u32[]{:S(2)}) copy-start(bf16[32,1,3072]{2,0,1:T(8,128)(2,1)} %param.5) | copy-start | bytes 589828
  6.5 46.8 %copy-start.3 = (f32[1,3,3072]{2,0,1:T(1,128)S(1)}, f32[1,3,3072]{2,0,1:T(1,128)}, u32[]{:S(2)}) copy-start(f32[1,3,3072]{2,0,1:T(1,128)} %param.6) | copy-start | bytes 110596
  6.5 84.3 %all-gather.8.cloned.1.call-start = ((), (), s32[]{:S(2)}) async-start(), calls=%async_computation.12 | async-start | bytes 6684672 | tf_op jit(solution)/shard_map/all_gather | solution.py:340
  7.6 1.2 copy-start
  8.8 1.0 copy-start.1
  42.8 22.1 %all-to-all-start = ((bf16[16,2,1536]{2,1,0:T(2,128)(2,1)}), bf16[16,2,1536]{2,1,0:T(2,128)(2,1)S(1)}, u32[]{:S(2)}, u32[]{:S(2)}) async-start(bf16[16,2,1536]{2,1,0:T(2,128)(2,1)} %reshape.95), calls=%async_computation | async-start | bytes 196608 | tf_op jit(solution)/shard_map/all_to_all | solution.py:315
  53.3 81.2 %all-gather.10.cloned.1.call-start = ((), (), s32[]{:S(2)}) async-start(), calls=%async_computation.13 | async-start | bytes 6684672 | tf_op jit(solution)/shard_map/all_gather | solution.py:340
  74.7 106.4 %all-gather.12.cloned.1.call-start = ((), (), s32[]{:S(2)}) async-start(), calls=%async_computation.14 | async-start | bytes 6684672 | tf_op jit(solution)/shard_map/all_gather | solution.py:340
  75.5 152.1 %all-gather.14.cloned.1.call-start = ((), (), s32[]{:S(2)}) async-start(), calls=%async_computation.15 | async-start | bytes 6684672 | tf_op jit(solution)/shard_map/all_gather | solution.py:340
  93.3 3.2 %collective-permute-start = (bf16[192,128]{1,0:T(8,128)(2,1)S(1)}, bf16[192,128]{1,0:T(8,128)(2,1)S(1)}, u32[]{:S(2)}, u32[]{:S(2)}) collective-permute-start(bf16[192,128]{1,0:T(8,128)(2,1)S(1)} %get-tuple-element.56), channel_id=1, source_target_pairs={{0,16},{16,0},{32,48},{48,32},{1,17},{17,1},{33,49},{49,33},{2,18}... | collective-permute-start | bytes 147464 | tf_op jit(solution)/shard_map/ppermute | solution.py:388
  97.7 3.7 %collective-permute-start.1 = (f32[128,128]{1,0:T(8,128)S(1)}, f32[128,128]{1,0:T(8,128)S(1)}, u32[]{:S(2)}, u32[]{:S(2)}) collective-permute-start(f32[128,128]{1,0:T(8,128)S(1)} %get-tuple-element.61), channel_id=1, source_target_pairs={{0,16},{16,0},{32,48},{48,32},{1,17},{17,1},{33,49},{49,33},{2,18}... | collective-permute-start | bytes 196616 | tf_op jit(solution)/shard_map/ppermute | solution.py:388
  117.3 17.2 %all-to-all-start.4 = ((bf16[16,8,3072]{2,1,0:T(8,128)(2,1)}), bf16[16,8,3072]{2,1,0:T(8,128)(2,1)S(1)}, u32[]{:S(2)}, u32[]{:S(2)}) async-start(bf16[16,8,3072]{2,1,0:T(8,128)(2,1)} %bitcast.19), calls=%async_computation.4 | async-start | bytes 1572864 | tf_op jit(solution)/shard_map/all_to_all | solution.py:315
  137.0 3.9 %collective-permute-start.2 = (bf16[192,128]{1,0:T(8,128)(2,1)S(1)}, bf16[192,128]{1,0:T(8,128)(2,1)S(1)}, u32[]{:S(2)}, u32[]{:S(2)}) collective-permute-start(bf16[192,128]{1,0:T(8,128)(2,1)S(1)} %get-tuple-element.69), channel_id=1, source_target_pairs={{0,16},{16,0},{32,48},{48,32},{1,17},{17,1},{33,49},{49,33},{2,18}... | collective-permute-start | bytes 147464 | tf_op jit(solution)/shard_map/ppermute | solution.py:388
  142.1 3.4 %collective-permute-start.3 = (f32[128,128]{1,0:T(8,128)S(1)}, f32[128,128]{1,0:T(8,128)S(1)}, u32[]{:S(2)}, u32[]{:S(2)}) collective-permute-start(f32[128,128]{1,0:T(8,128)S(1)} %get-tuple-element.74), channel_id=1, source_target_pairs={{0,16},{16,0},{32,48},{48,32},{1,17},{17,1},{33,49},{49,33},{2,18}... | collective-permute-start | bytes 196616 | tf_op jit(solution)/shard_map/ppermute | solution.py:388
  165.4 15.7 %all-to-all-start.6 = ((bf16[16,8,3072]{2,1,0:T(8,128)(2,1)}), bf16[16,8,3072]{2,1,0:T(8,128)(2,1)S(1)}, u32[]{:S(2)}, u32[]{:S(2)}) async-start(bf16[16,8,3072]{2,1,0:T(8,128)(2,1)} %bitcast.30), calls=%async_computation.6 | async-start | bytes 1572864 | tf_op jit(solution)/shard_map/all_to_all | solution.py:315
  183.5 3.9 %collective-permute-start.4 = (bf16[192,128]{1,0:T(8,128)(2,1)S(1)}, bf16[192,128]{1,0:T(8,128)(2,1)S(1)}, u32[]{:S(2)}, u32[]{:S(2)}) collective-permute-start(bf16[192,128]{1,0:T(8,128)(2,1)S(1)} %get-tuple-element.81), channel_id=1, source_target_pairs={{0,16},{16,0},{32,48},{48,32},{1,17},{17,1},{33,49},{49,33},{2,18}... | collective-permute-start | bytes 147464 | tf_op jit(solution)/shard_map/ppermute | solution.py:388
  188.7 3.2 %collective-permute-start.5 = (f32[128,128]{1,0:T(8,128)S(1)}, f32[128,128]{1,0:T(8,128)S(1)}, u32[]{:S(2)}, u32[]{:S(2)}) collective-permute-start(f32[128,128]{1,0:T(8,128)S(1)} %get-tuple-element.86), channel_id=1, source_target_pairs={{0,16},{16,0},{32,48},{48,32},{1,17},{17,1},{33,49},{49,33},{2,18}... | collective-permute-start | bytes 196616 | tf_op jit(solution)/shard_map/ppermute | solution.py:388
  211.7 15.8 %all-to-all-start.8 = ((bf16[16,8,3072]{2,1,0:T(8,128)(2,1)}), bf16[16,8,3072]{2,1,0:T(8,128)(2,1)S(1)}, u32[]{:S(2)}, u32[]{:S(2)}) async-start(bf16[16,8,3072]{2,1,0:T(8,128)(2,1)} %bitcast.40), calls=%async_computation.8 | async-start | bytes 1572864 | tf_op jit(solution)/shard_map/all_to_all | solution.py:315
  229.9 3.9 %collective-permute-start.6 = (bf16[192,128]{1,0:T(8,128)(2,1)S(1)}, bf16[192,128]{1,0:T(8,128)(2,1)S(1)}, u32[]{:S(2)}, u32[]{:S(2)}) collective-permute-start(bf16[192,128]{1,0:T(8,128)(2,1)S(1)} %get-tuple-element.93), channel_id=1, source_target_pairs={{0,16},{16,0},{32,48},{48,32},{1,17},{17,1},{33,49},{49,33},{2,18}... | collective-permute-start | bytes 147464 | tf_op jit(solution)/shard_map/ppermute | solution.py:388
  235.1 3.2 %collective-permute-start.7 = (f32[128,128]{1,0:T(8,128)S(1)}, f32[128,128]{1,0:T(8,128)S(1)}, u32[]{:S(2)}, u32[]{:S(2)}) collective-permute-start(f32[128,128]{1,0:T(8,128)S(1)} %get-tuple-element.98), channel_id=1, source_target_pairs={{0,16},{16,0},{32,48},{48,32},{1,17},{17,1},{33,49},{49,33},{2,18}... | collective-permute-start | bytes 196616 | tf_op jit(solution)/shard_map/ppermute | solution.py:388
  239.8 18.4 %all-to-all-start.9 = ((bf16[16,8,3072]{2,1,0:T(8,128)(2,1)}), bf16[16,8,3072]{2,1,0:T(8,128)(2,1)S(1)}, u32[]{:S(2)}, u32[]{:S(2)}) async-start(bf16[16,8,3072]{2,1,0:T(8,128)(2,1)} %bitcast.44), calls=%async_computation.9 | async-start | bytes 1572864 | tf_op jit(solution)/shard_map/all_to_all | solution.py:315
Sparse Core Ops, SparseCore 0:
  40.2 49.6 all-gather.7
  91.8 42.7 all-gather.9
  136.4 44.6 all-gather.11
  182.8 44.6 all-gather.13

commit v6 on v5

--- a/solution.py
+++ b/solution.py
@@ -30,6 +30,7 @@
 PIECE = AT_SHARED_V + PATCHES // 2
 HALF = HD // 2
 ANY = pl.BlockSpec(memory_space=pl.ANY)
+HBM = pl.BlockSpec(memory_space=pltpu.HBM)
 SMEM = pl.BlockSpec(memory_space=pltpu.SMEM)
 VMEM = pl.BlockSpec(memory_space=pltpu.VMEM)
 SMALL = pltpu.CompilerParams(vmem_limit_bytes=24 * 1024 * 1024)
@@ -90,9 +91,20 @@
         put(member, AT_SHARED_VO, jnp.concatenate([w_v[:, lanes], w_o[:, lanes]], axis=1))
 
 
-def first_kernel(place_ref, rows_ref, shift_ref, scale_ref, normed_ref, blocks_ref):
-    for block in range(BLOCKS):
-        blocks_ref[block] = place_ref[2] + block
+def cut_kernel(received_ref, earlier_ref, *rest):
+    del earlier_ref
+    targets, sems = rest[:-1], rest[-1]
+    copies = [
+        pltpu.make_async_copy(received_ref.at[block + 1], target, sems.at[block])
+        for block, target in enumerate(targets)
+    ]
+    for copy in copies:
+        copy.start()
+    for copy in copies:
+        copy.wait()
+
+
+def first_kernel(rows_ref, shift_ref, scale_ref, normed_ref):
     normed = modulate(rows_ref[...].astype(jnp.float32), shift_ref[...], scale_ref[...])
     twice = jnp.concatenate([normed, normed], axis=0)
     for at in range(0, LOCAL, 2 * OWN):
@@ -318,12 +330,12 @@
 def body(latent, modulation, w_qkv, w_out, stale):
     x_at, y_at = lax.axis_index("x"), lax.axis_index("y")
     pair_at = lax.axis_index("z") * NC + lax.axis_index("c")
-    place = jnp.stack([2 * pair_at, y_at % 2, 0 * y_at]).astype(jnp.int32)
+    place = jnp.stack([2 * pair_at, y_at % 2]).astype(jnp.int32)
 
     sent = pl.pallas_call(
         pack_kernel,
         out_shape=jax.ShapeDtypeStruct((MEMBERS, PIECE, HD), jnp.bfloat16),
-        in_specs=[ANY, ANY, VMEM],
+        in_specs=[HBM, HBM, VMEM],
         out_specs=VMEM,
         scratch_shapes=[
             pltpu.VMEM((ROWS, 3 * D), jnp.bfloat16),
@@ -335,11 +347,10 @@
     )(w_qkv[0], w_out[0].T, jnp.swapaxes(stale[0, :, 0], 0, 1))
     received = exchange(sent, HEAD_AXES).reshape(BLOCKS, NY, PIECE, HD)
 
-    def gather(block):
-        own_piece = lax.dynamic_index_in_dim(received, block, 0, keepdims=False)
+    def gather(own_piece):
         return lax.all_gather(own_piece, REST_AXES, axis=0, tiled=True)
 
-    pieces = [gather(0)]
+    pieces = [gather(received[0])]
 
     terms = to_own_order(lax.all_gather(modulation[0], "x", axis=0, tiled=False))
     wanted = latent.reshape(NZ * NC, 2, D)
@@ -351,18 +362,26 @@
         return terms[block, which][None]
 
     spread = jax.ShapeDtypeStruct((LOCAL, D), jnp.bfloat16)
+    normed = pl.pallas_call(
+        first_kernel,
+        out_shape=spread,
+        in_specs=[VMEM] * 3,
+        out_specs=VMEM,
+        compiler_params=PARAMS,
+        name="first",
+    )(current, term(0, 0), term(0, 1))
+    later = pl.pallas_call(
+        cut_kernel,
+        out_shape=[jax.ShapeDtypeStruct((NY, PIECE, HD), jnp.bfloat16)] * (BLOCKS - 1),
+        in_specs=[ANY, VMEM],
+        out_specs=[HBM] * (BLOCKS - 1),
+        scratch_shapes=[pltpu.SemaphoreType.DMA((BLOCKS - 1,))],
+        name="cut",
+    )(received, normed)
+    pieces += [gather(own_piece) for own_piece in later]
     weight = pltpu.VMEM((SOURCES, ROWS, HD), jnp.bfloat16)
     cache = pltpu.VMEM((SOURCES, PATCHES, HD), jnp.bfloat16)
     owned = jax.ShapeDtypeStruct((OWN, D), jnp.bfloat16)
-    normed, blocks = pl.pallas_call(
-        first_kernel,
-        out_shape=(spread, jax.ShapeDtypeStruct((BLOCKS,), jnp.int32)),
-        in_specs=[SMEM] + [VMEM] * 3,
-        out_specs=(VMEM, SMEM),
-        compiler_params=PARAMS,
-        name="first",
-    )(place, current, term(0, 0), term(0, 1))
-    pieces += [gather(blocks[block]) for block in range(1, BLOCKS)]
     half_cache = jax.ShapeDtypeStruct((SOURCES, PATCHES // 2, HD), jnp.bfloat16)
     kept_weight = jax.ShapeDtypeStruct((SOURCES, ROWS, HD), jnp.bfloat16)
     sums_of = jax.ShapeDtypeStruct((LOCAL, HD), jnp.float32)
@@ -392,12 +411,12 @@
         rows = exchange(normed, HEAD_AXES)
         source = pieces[block]
         kept, given = local(
-            shared_project_kernel, (SMEM, VMEM, ANY), (VMEM, VMEM),
+            shared_project_kernel, (SMEM, VMEM, HBM), (VMEM, VMEM),
             (rows_of(LOCAL + PT), rows_of(LOCAL + PT)), [weight] * 2, 2, 2 * D * HD,
         )(place, rows, source)
         got = swap(given)
         own, keys, values = local(
-            own_project_kernel, (VMEM, ANY), (VMEM, VMEM, VMEM),
+            own_project_kernel, (VMEM, HBM), (VMEM, VMEM, VMEM),
             (rows_of(3 * LOCAL), half_cache, half_cache), [weight] * 3, 5, 3 * D * HD,
         )(rows, source)
         sums, given = local(
@@ -406,7 +425,7 @@
         )(place, kept, got, keys, values)
         got = swap(given)
         attended, w_own, w_vo = local(
-            own_attend_kernel, (SMEM, VMEM, VMEM, ANY), (VMEM, VMEM, VMEM),
+            own_attend_kernel, (SMEM, VMEM, VMEM, HBM), (VMEM, VMEM, VMEM),
             (rows_of(LOCAL), kept_weight, kept_weight), [cache] * 2, 4, 2 * PATCHES * PT * HD,
         )(place, own, sums, source)
         partial = local(
@@ -432,7 +451,18 @@
                 name="last",
             )(parts, current, term(block, 2))
         outputs.append(to_given_order(current))
-    placed = exchange(jnp.concatenate(outputs, axis=0), "x")
+    outputs = jnp.stack(outputs)
+    moved = [lax.dynamic_index_in_dim(outputs, x_at, 0, keepdims=False)]
+    for step in range(1, NX):
+        leaving = lax.dynamic_index_in_dim(outputs, (x_at + step) % NX, 0, keepdims=False)
+        moved.append(lax.ppermute(leaving, "x", [(at, (at + step) % NX) for at in range(NX)]))
+    moved = jnp.stack(moved)
+    placed = jnp.stack(
+        [
+            lax.dynamic_index_in_dim(moved, (x_at - origin) % NX, 0, keepdims=False)
+            for origin in range(NX)
+        ]
+    )
     placed = jnp.swapaxes(placed.reshape(2, NZ * NC, D), 0, 1).reshape(PATCHES, D)
     placed = exchange(placed, REST_AXES)
     return placed[None, :, None]

time: 294 us -> 326 us (1.11)
  Pallas kernels: 44.8 us -> 82.1 us
  blocking collectives: 130 us -> 116 us
  waiting for transfers between devices: 50.1 us -> 63.6 us
  between operations: 19.7 us -> 13.7 us
    pallas_call x13 -> x14, Pallas kernels: 31.8 us -> 69 us  [the longest x1 38 us: body(): pl.pallas_call(cut_kernel, out_shape=[jax.ShapeDtypeStruct((NY, PIECE, HD...]
    all_to_all x5 -> x6, waiting for transfers between devices: 10.8 us -> 41.3 us  [exchange(): return lax.all_to_all(array, axes, split_axis=0, concat_axis=0, tiled=True)]
    all_gather x4, waiting for transfers between devices: 37.6 us -> 13.3 us  [gather(): return lax.all_gather(own_piece, REST_AXES, axis=0, tiled=True)]
    all_to_all x7 -> x5, blocking collectives: 120 us -> 105 us  [exchange(): return lax.all_to_all(array, axes, split_axis=0, concat_axis=0, tiled=True)]
    ppermute x8, waiting for transfers between devices: 0.44 us -> 5.38 us  [swap(): return lax.ppermute(array, 'y', [(at, at ^ 1) for at in range(NY)])]
    all_to_all x5 -> x6, starting transfers between devices: 28 us -> 29.6 us  [exchange(): return lax.all_to_all(array, axes, split_axis=0, concat_axis=0, tiled=True)]
  transfers between devices with their start and end apart: 17 -> 21, of which waited for: 7 -> 15; matrix products, arithmetic and copies ran while one was open for 2% -> 2% of each run, Pallas kernels for 13% -> 23%
where the time goes in v6:
time: 326 us; the launch traced here: 325 us
  blocking collectives  116 us (36%)
  Pallas kernels  82.1 us (25%)
  waiting for transfers between devices  63.6 us (20%)
  starting transfers between devices  37.9 us (12%)
  between operations  13.7 us (4%)
  local copies, waits for them, and re-layouts  10.7 us (3%)
    all_to_all x5, blocking collectives, exchange(): return lax.all_to_all(array, axes, split_axis=0, concat_axis=0, tiled=True)  105 us
    all_to_all x6, waiting for transfers between devices, exchange(): return lax.all_to_all(array, axes, split_axis=0, concat_axis=0, tiled=True)  41.3 us
    pallas_call x1, Pallas kernels, body(): pl.pallas_call(cut_kernel, out_shape=[jax.ShapeDtypeStruct((NY, PIECE, HD...  38 us
    all_to_all x6, starting transfers between devices, exchange(): return lax.all_to_all(array, axes, split_axis=0, concat_axis=0, tiled=True)  29.6 us
    all_gather x4, waiting for transfers between devices, gather(): return lax.all_gather(own_piece, REST_AXES, axis=0, tiled=True)  13.3 us
    pallas_call x4, Pallas kernels, body(): local(own_attend_kernel, (SMEM, VMEM, VMEM, HBM), (VMEM, VMEM, VMEM), (ro...  10.7 us
    pallas_call x4, Pallas kernels, body(): local(own_project_kernel, (VMEM, HBM), (VMEM, VMEM, VMEM), (rows_of(3 * L...  10.5 us
    all_gather x1, blocking collectives, body(): lax.all_gather(modulation[0], 'x', axis=0, tiled=False)  10.5 us
  transfers between devices with their start and end apart: 21, of which 15 were waited for; matrix products, arithmetic and copies ran while one was open for 2% of the time, Pallas kernels for 23%

profile of v6, /device:TPU:1, one launch (start us, length us, event | category | flops | bytes accessed | tf_op | source)
XLA Modules:
  0.0 325.2 jit_solution(1460404595382940828)
XLA Ops:
  6.5 1.1 copy.48
  7.7 1.2 copy-done.1
  8.8 1.0 copy-done.2
  9.8 0.6 pack.1
  10.4 28.9 %all_to_all.105 = bf16[16,384,128]{2,1,0:T(8,128)(2,1)S(1)} all-to-all(bf16[16,384,128]{2,1,0:T(8,128)(2,1)S(1)} %pack.1), channel_id=1, replica_groups=mesh['x'=4,'y'=4,'z'=8,'c'=2] {'x','y'}, dimensions={0} | all-to-all | bytes 3145728 | tf_op jit(solution)/shard_map/all_to_all | solution.py:327
  39.3 0.8 slice.55
  41.0 1.2 reduce.2
  42.2 0.7 reshape.73
  42.9 10.5 %all-to-all-start = ((bf16[16,2,1536]{2,1,0:T(2,128)(2,1)}), bf16[16,2,1536]{2,1,0:T(2,128)(2,1)S(1)}, u32[]{:S(2)}, u32[]{:S(2)}) async-start(bf16[16,2,1536]{2,1,0:T(2,128)(2,1)} %reshape.73), calls=%async_computation | async-start | bytes 196608 | tf_op jit(solution)/shard_map/all_to_all | solution.py:327
  53.4 10.5 %all_gather.15 = f32[4,3,3072]{2,1,0:T(4,128)S(1)} all-gather(f32[1,3,3072]{2,1,0:T(4,128)S(1)} %copy.34), channel_id=1, replica_groups=mesh['x'=4,'y'=4,'z'=8,'c'=2] {'x'}, dimensions={0}, use_global_device_ids=true | all-gather | bytes 184320 | tf_op jit(solution)/shard_map/all_gather | solution.py:355
  66.0 0.9 copy-done
  66.8 38.0 %cut.1 = (bf16[4,384,128]{2,1,0:T(8,128)(2,1)}, bf16[4,384,128]{2,1,0:T(8,128)(2,1)}, bf16[4,384,128]{2,1,0:T(8,128)(2,1)}) custom-call(bf16[4,4,384,128]{3,2,1,0:T(8,128)(2,1)} %bitcast.111, bf16[128,3072]{1,0:T(8,128)(2,1)} %copy-done), custom_call_target="tpu_custom_call" | custom-call | tf_op jit(solution)/shard_map/cut/pallas_call | solution.py:373
  104.9 0.7 all-gather.9.cloned.1.call-update
  106.2 3.6 %all-to-all-start.1 = ((bf16[16,8,3072]{2,1,0:T(8,128)(2,1)}), bf16[16,8,3072]{2,1,0:T(8,128)(2,1)S(1)}, u32[]{:S(2)}, u32[]{:S(2)}) async-start(bf16[16,8,3072]{2,1,0:T(8,128)(2,1)} %bitcast.100), calls=%async_computation.1 | async-start | bytes 1572864 | tf_op jit(solution)/shard_map/all_to_all | solution.py:327
  109.9 12.0 %all-to-all-done.1 = bf16[16,8,3072]{2,1,0:T(8,128)(2,1)S(1)} async-done(((bf16[16,8,3072]{2,1,0:T(8,128)(2,1)}), bf16[16,8,3072]{2,1,0:T(8,128)(2,1)S(1)}, u32[]{:S(2)}, u32[]{:S(2)}) %all-to-all-start.1) | async-done | bytes 786464 | tf_op jit(solution)/shard_map/all_to_all | solution.py:327
  121.9 2.4 shared_project_kernel.4
  124.4 0.7 collective-permute-start
  125.0 2.7 own_project_kernel.4
  127.8 1.3 shared_attend_kernel.4
  129.0 0.9 collective-permute-start.1
  129.9 2.7 own_attend_kernel.4
  132.6 0.6 finish_kernel.4
  133.3 14.3 %all_to_all.106 = bf16[16,8,3072]{2,1,0:T(8,128)(2,1)S(1)} all-to-all(bf16[16,8,3072]{2,1,0:T(8,128)(2,1)S(1)} %bitcast.101), channel_id=1, replica_groups=mesh['x'=4,'y'=4,'z'=8,'c'=2] {'x','y'}, dimensions={0} | all-to-all | bytes 1572864 | tf_op jit(solution)/shard_map/all_to_all | solution.py:327
  147.6 1.3 middle.3
  148.9 3.7 %all-to-all-start.4 = ((bf16[16,8,3072]{2,1,0:T(8,128)(2,1)}), bf16[16,8,3072]{2,1,0:T(8,128)(2,1)S(1)}, u32[]{:S(2)}, u32[]{:S(2)}) async-start(bf16[16,8,3072]{2,1,0:T(8,128)(2,1)} %bitcast.19), calls=%async_computation.4 | async-start | bytes 1572864 | tf_op jit(solution)/shard_map/all_to_all | solution.py:327
  152.6 10.4 %all-to-all-done.4 = bf16[16,8,3072]{2,1,0:T(8,128)(2,1)S(1)} async-done(((bf16[16,8,3072]{2,1,0:T(8,128)(2,1)}), bf16[16,8,3072]{2,1,0:T(8,128)(2,1)S(1)}, u32[]{:S(2)}, u32[]{:S(2)}) %all-to-all-start.4) | async-done | bytes 786464 | tf_op jit(solution)/shard_map/all_to_all | solution.py:327
  163.1 2.4 shared_project_kernel.5
  165.8 2.6 own_project_kernel.5
  168.9 1.3 shared_attend_kernel.5
  170.2 1.0 collective-permute-start.3
  171.2 2.7 own_attend_kernel.5
  174.0 0.6 finish_kernel.5
  174.6 13.6 %all_to_all.107 = bf16[16,8,3072]{2,1,0:T(8,128)(2,1)S(1)} all-to-all(bf16[16,8,3072]{2,1,0:T(8,128)(2,1)S(1)} %bitcast.102), channel_id=1, replica_groups=mesh['x'=4,'y'=4,'z'=8,'c'=2] {'x','y'}, dimensions={0} | all-to-all | bytes 1572864 | tf_op jit(solution)/shard_map/all_to_all | solution.py:327
  188.2 1.3 middle.4
  189.5 3.7 %all-to-all-start.6 = ((bf16[16,8,3072]{2,1,0:T(8,128)(2,1)}), bf16[16,8,3072]{2,1,0:T(8,128)(2,1)S(1)}, u32[]{:S(2)}, u32[]{:S(2)}) async-start(bf16[16,8,3072]{2,1,0:T(8,128)(2,1)} %bitcast.28), calls=%async_computation.6 | async-start | bytes 1572864 | tf_op jit(solution)/shard_map/all_to_all | solution.py:327
  193.2 4.3 %all-gather.9.cloned.1.call-done.pieces_ref = bf16[64,384,128]{2,1,0:T(8,128)(2,1)} async-done(((bf16[4,384,128]{2,1,0:T(8,128)(2,1)}), bf16[64,384,128]{2,1,0:T(8,128)(2,1)}) %all-gather.9.cloned.1.call-update) | async-done | bytes 6291472 | tf_op jit(solution)/shard_map/all_gather | solution.py:351
  197.5 6.1 %all-to-all-done.6 = bf16[16,8,3072]{2,1,0:T(8,128)(2,1)S(1)} async-done(((bf16[16,8,3072]{2,1,0:T(8,128)(2,1)}), bf16[16,8,3072]{2,1,0:T(8,128)(2,1)S(1)}, u32[]{:S(2)}, u32[]{:S(2)}) %all-to-all-start.6) | async-done | bytes 786464 | tf_op jit(solution)/shard_map/all_to_all | solution.py:327
  203.6 2.4 shared_project_kernel.6
  206.4 2.6 own_project_kernel.6
  209.0 2.2 collective-permute-done.4.got_ref
  211.2 1.3 shared_attend_kernel.6
  212.8 2.7 own_attend_kernel.6
  215.5 0.6 collective-permute-done.5.got_ref
  216.0 0.6 finish_kernel.6
  216.7 13.2 %all_to_all.108 = bf16[16,8,3072]{2,1,0:T(8,128)(2,1)S(1)} all-to-all(bf16[16,8,3072]{2,1,0:T(8,128)(2,1)S(1)} %bitcast.103), channel_id=1, replica_groups=mesh['x'=4,'y'=4,'z'=8,'c'=2] {'x','y'}, dimensions={0} | all-to-all | bytes 1572864 | tf_op jit(solution)/shard_map/all_to_all | solution.py:327
  229.9 1.3 middle.5
  231.2 3.7 %all-to-all-start.8 = ((bf16[16,8,3072]{2,1,0:T(8,128)(2,1)}), bf16[16,8,3072]{2,1,0:T(8,128)(2,1)S(1)}, u32[]{:S(2)}, u32[]{:S(2)}) async-start(bf16[16,8,3072]{2,1,0:T(8,128)(2,1)} %bitcast.36), calls=%async_computation.8 | async-start | bytes 1572864 | tf_op jit(solution)/shard_map/all_to_all | solution.py:327
  235.0 9.0 %all-gather.11.cloned.1.call-done.pieces_ref = bf16[64,384,128]{2,1,0:T(8,128)(2,1)} async-done(((bf16[4,384,128]{2,1,0:T(8,128)(2,1)}), bf16[64,384,128]{2,1,0:T(8,128)(2,1)}) %all-gather.11.cloned.1.call-update) | async-done | bytes 6291472 | tf_op jit(solution)/shard_map/all_gather | solution.py:351
  243.9 3.3 %all-to-all-done.8 = bf16[16,8,3072]{2,1,0:T(8,128)(2,1)S(1)} async-done(((bf16[16,8,3072]{2,1,0:T(8,128)(2,1)}), bf16[16,8,3072]{2,1,0:T(8,128)(2,1)S(1)}, u32[]{:S(2)}, u32[]{:S(2)}) %all-to-all-start.8) | async-done | bytes 786464 | tf_op jit(solution)/shard_map/all_to_all | solution.py:327
  247.2 2.4 shared_project_kernel.7
  250.0 2.6 own_project_kernel.7
  252.6 1.3 shared_attend_kernel.7
  253.9 1.2 collective-permute-start.7
  255.5 2.7 own_attend_kernel.7
  258.2 1.9 collective-permute-done.7.got_ref
  260.1 1.5 finish_kernel.7
  261.7 4.2 %all-to-all-start.9 = ((bf16[16,8,3072]{2,1,0:T(8,128)(2,1)}), bf16[16,8,3072]{2,1,0:T(8,128)(2,1)S(1)}, u32[]{:S(2)}, u32[]{:S(2)}) async-start(bf16[16,8,3072]{2,1,0:T(8,128)(2,1)} %bitcast.38), calls=%async_computation.9 | async-start | bytes 1572864 | tf_op jit(solution)/shard_map/all_to_all | solution.py:327
  266.7 9.5 %all-to-all-done.9 = bf16[16,8,3072]{2,1,0:T(8,128)(2,1)S(1)} async-done(((bf16[16,8,3072]{2,1,0:T(8,128)(2,1)}), bf16[16,8,3072]{2,1,0:T(8,128)(2,1)S(1)}, u32[]{:S(2)}, u32[]{:S(2)}) %all-to-all-start.9) | async-done | bytes 786464 | tf_op jit(solution)/shard_map/all_to_all | solution.py:327
  276.9 2.0 collective-permute-start.9
  278.9 0.9 collective-permute-start.10
  279.8 1.8 collective-permute-done.8
  281.6 0.6 collective-permute-done.10
  282.5 35.5 %all_to_all.109 = bf16[16,2,3072]{2,1,0:T(2,128)(2,1)S(1)} all-to-all(bf16[16,2,3072]{2,1,0:T(2,128)(2,1)S(1)} %copy.42), channel_id=1, replica_groups=mesh['x'=4,'y'=4,'z'=8,'c'=2] {'z','c'}, dimensions={0} | all-to-all | bytes 393216 | tf_op jit(solution)/shard_map/all_to_all | solution.py:327
  317.9 0.8 broadcast_in_dim.3
  (68 shorter events, 7.8 us)
Async XLA Ops:
  6.5 33.6 %copy-start.4 = (bf16[32,1,3072]{2,0,1:T(8,128)(2,1)S(1)}, bf16[32,1,3072]{2,0,1:T(8,128)(2,1)}, u32[]{:S(2)}) copy-start(bf16[32,1,3072]{2,0,1:T(8,128)(2,1)} %param.5) | copy-start | bytes 589828
  6.5 46.9 %copy-start.5 = (f32[1,3,3072]{2,0,1:T(1,128)S(1)}, f32[1,3,3072]{2,0,1:T(1,128)}, u32[]{:S(2)}) copy-start(f32[1,3,3072]{2,0,1:T(1,128)} %param.6) | copy-start | bytes 110596
  6.5 115.4 %all-gather.5.cloned.1.call-start = ((), (), s32[]{:S(2)}) async-start(), calls=%async_computation.11 | async-start | bytes 6684672 | tf_op jit(solution)/shard_map/all_gather | solution.py:351
  7.6 1.2 copy-start.1
  8.8 1.0 copy-start.2
  39.3 27.6 %copy-start.3 = (bf16[16,384,128]{2,1,0:T(8,128)(2,1)}, bf16[16,384,128]{2,1,0:T(8,128)(2,1)S(1)}, u32[]{:S(2)}) copy-start(bf16[16,384,128]{2,1,0:T(8,128)(2,1)S(1)} %all_to_all.105) | copy-start | bytes 4718596
  42.9 22.0 %all-to-all-start = ((bf16[16,2,1536]{2,1,0:T(2,128)(2,1)}), bf16[16,2,1536]{2,1,0:T(2,128)(2,1)S(1)}, u32[]{:S(2)}, u32[]{:S(2)}) async-start(bf16[16,2,1536]{2,1,0:T(2,128)(2,1)} %reshape.73), calls=%async_computation | async-start | bytes 196608 | tf_op jit(solution)/shard_map/all_to_all | solution.py:327
  53.4 99.3 %all-gather.7.cloned.1.call-start = ((), (), s32[]{:S(2)}) async-start(), calls=%async_computation.12 | async-start | bytes 6684672 | tf_op jit(solution)/shard_map/all_gather | solution.py:351
  66.0 0.9 copy-start
  104.9 92.7 %all-gather.9.cloned.1.call-start = ((), (), s32[]{:S(2)}) async-start(), calls=%async_computation.13 | async-start | bytes 6684672 | tf_op jit(solution)/shard_map/all_gather | solution.py:351
  105.6 138.3 %all-gather.11.cloned.1.call-start = ((), (), s32[]{:S(2)}) async-start(), calls=%async_computation.14 | async-start | bytes 6684672 | tf_op jit(solution)/shard_map/all_gather | solution.py:351
  106.2 15.8 %all-to-all-start.1 = ((bf16[16,8,3072]{2,1,0:T(8,128)(2,1)}), bf16[16,8,3072]{2,1,0:T(8,128)(2,1)S(1)}, u32[]{:S(2)}, u32[]{:S(2)}) async-start(bf16[16,8,3072]{2,1,0:T(8,128)(2,1)} %bitcast.100), calls=%async_computation.1 | async-start | bytes 1572864 | tf_op jit(solution)/shard_map/all_to_all | solution.py:327
  124.4 3.4 %collective-permute-start = (bf16[192,128]{1,0:T(8,128)(2,1)S(1)}, bf16[192,128]{1,0:T(8,128)(2,1)S(1)}, u32[]{:S(2)}, u32[]{:S(2)}) collective-permute-start(bf16[192,128]{1,0:T(8,128)(2,1)S(1)} %get-tuple-element.56), channel_id=1, source_target_pairs={{0,16},{16,0},{32,48},{48,32},{1,17},{17,1},{33,49},{49,33},{2,18}... | collective-permute-start | bytes 147464 | tf_op jit(solution)/shard_map/ppermute | solution.py:407
  129.0 3.6 %collective-permute-start.1 = (f32[128,128]{1,0:T(8,128)S(1)}, f32[128,128]{1,0:T(8,128)S(1)}, u32[]{:S(2)}, u32[]{:S(2)}) collective-permute-start(f32[128,128]{1,0:T(8,128)S(1)} %get-tuple-element.61), channel_id=1, source_target_pairs={{0,16},{16,0},{32,48},{48,32},{1,17},{17,1},{33,49},{49,33},{2,18}... | collective-permute-start | bytes 196616 | tf_op jit(solution)/shard_map/ppermute | solution.py:407
  148.9 14.2 %all-to-all-start.4 = ((bf16[16,8,3072]{2,1,0:T(8,128)(2,1)}), bf16[16,8,3072]{2,1,0:T(8,128)(2,1)S(1)}, u32[]{:S(2)}, u32[]{:S(2)}) async-start(bf16[16,8,3072]{2,1,0:T(8,128)(2,1)} %bitcast.19), calls=%async_computation.4 | async-start | bytes 1572864 | tf_op jit(solution)/shard_map/all_to_all | solution.py:327
  165.5 3.4 %collective-permute-start.2 = (bf16[192,128]{1,0:T(8,128)(2,1)S(1)}, bf16[192,128]{1,0:T(8,128)(2,1)S(1)}, u32[]{:S(2)}, u32[]{:S(2)}) collective-permute-start(bf16[192,128]{1,0:T(8,128)(2,1)S(1)} %get-tuple-element.69), channel_id=1, source_target_pairs={{0,16},{16,0},{32,48},{48,32},{1,17},{17,1},{33,49},{49,33},{2,18}... | collective-permute-start | bytes 147464 | tf_op jit(solution)/shard_map/ppermute | solution.py:407
  170.2 3.8 %collective-permute-start.3 = (f32[128,128]{1,0:T(8,128)S(1)}, f32[128,128]{1,0:T(8,128)S(1)}, u32[]{:S(2)}, u32[]{:S(2)}) collective-permute-start(f32[128,128]{1,0:T(8,128)S(1)} %get-tuple-element.74), channel_id=1, source_target_pairs={{0,16},{16,0},{32,48},{48,32},{1,17},{17,1},{33,49},{49,33},{2,18}... | collective-permute-start | bytes 196616 | tf_op jit(solution)/shard_map/ppermute | solution.py:407
  189.5 14.1 %all-to-all-start.6 = ((bf16[16,8,3072]{2,1,0:T(8,128)(2,1)}), bf16[16,8,3072]{2,1,0:T(8,128)(2,1)S(1)}, u32[]{:S(2)}, u32[]{:S(2)}) async-start(bf16[16,8,3072]{2,1,0:T(8,128)(2,1)} %bitcast.28), calls=%async_computation.6 | async-start | bytes 1572864 | tf_op jit(solution)/shard_map/all_to_all | solution.py:327
  206.0 5.2 %collective-permute-start.4 = (bf16[192,128]{1,0:T(8,128)(2,1)S(1)}, bf16[192,128]{1,0:T(8,128)(2,1)S(1)}, u32[]{:S(2)}, u32[]{:S(2)}) collective-permute-start(bf16[192,128]{1,0:T(8,128)(2,1)S(1)} %get-tuple-element.82), channel_id=1, source_target_pairs={{0,16},{16,0},{32,48},{48,32},{1,17},{17,1},{33,49},{49,33},{2,18}... | collective-permute-start | bytes 147464 | tf_op jit(solution)/shard_map/ppermute | solution.py:407
  212.4 3.6 %collective-permute-start.5 = (f32[128,128]{1,0:T(8,128)S(1)}, f32[128,128]{1,0:T(8,128)S(1)}, u32[]{:S(2)}, u32[]{:S(2)}) collective-permute-start(f32[128,128]{1,0:T(8,128)S(1)} %get-tuple-element.87), channel_id=1, source_target_pairs={{0,16},{16,0},{32,48},{48,32},{1,17},{17,1},{33,49},{49,33},{2,18}... | collective-permute-start | bytes 196616 | tf_op jit(solution)/shard_map/ppermute | solution.py:407
  231.2 16.0 %all-to-all-start.8 = ((bf16[16,8,3072]{2,1,0:T(8,128)(2,1)}), bf16[16,8,3072]{2,1,0:T(8,128)(2,1)S(1)}, u32[]{:S(2)}, u32[]{:S(2)}) async-start(bf16[16,8,3072]{2,1,0:T(8,128)(2,1)} %bitcast.36), calls=%async_computation.8 | async-start | bytes 1572864 | tf_op jit(solution)/shard_map/all_to_all | solution.py:327
  249.6 3.0 collective-permute-start.6
  253.9 6.2 %collective-permute-start.7 = (f32[128,128]{1,0:T(8,128)S(1)}, f32[128,128]{1,0:T(8,128)S(1)}, u32[]{:S(2)}, u32[]{:S(2)}) collective-permute-start(f32[128,128]{1,0:T(8,128)S(1)} %get-tuple-element.100), channel_id=1, source_target_pairs={{0,16},{16,0},{32,48},{48,32},{1,17},{17,1},{33,49},{49,33},{2,18}... | collective-permute-start | bytes 196616 | tf_op jit(solution)/shard_map/ppermute | solution.py:407
  261.7 14.6 %all-to-all-start.9 = ((bf16[16,8,3072]{2,1,0:T(8,128)(2,1)}), bf16[16,8,3072]{2,1,0:T(8,128)(2,1)S(1)}, u32[]{:S(2)}, u32[]{:S(2)}) async-start(bf16[16,8,3072]{2,1,0:T(8,128)(2,1)} %bitcast.38), calls=%async_computation.9 | async-start | bytes 1572864 | tf_op jit(solution)/shard_map/all_to_all | solution.py:327
  276.8 4.8 %collective-permute-start.8 = (bf16[8,3072]{1,0:T(8,128)(2,1)S(1)}, bf16[8,3072]{1,0:T(8,128)(2,1)S(1)}, u32[]{:S(2)}, u32[]{:S(2)}) collective-permute-start(bf16[8,3072]{1,0:T(8,128)(2,1)S(1)} %get-tuple-element.110), channel_id=1, source_target_pairs={{0,64},{64,128},{128,192},{192,0},{1,65},{65,129},{129,193},{193,1... | collective-permute-start | bytes 147464 | tf_op jit(solution)/shard_map/ppermute | solution.py:458
  276.9 4.7 %collective-permute-start.9 = (bf16[8,3072]{1,0:T(8,128)(2,1)S(1)}, bf16[8,3072]{1,0:T(8,128)(2,1)S(1)}, u32[]{:S(2)}, u32[]{:S(2)}) collective-permute-start(bf16[8,3072]{1,0:T(8,128)(2,1)S(1)} %get-tuple-element.109), channel_id=1, source_target_pairs={{0,128},{64,192},{128,0},{192,64},{1,129},{65,193},{129,1},{193,65... | collective-permute-start | bytes 147464 | tf_op jit(solution)/shard_map/ppermute | solution.py:458
  278.9 3.2 collective-permute-start.10
Sparse Core Ops, SparseCore 0:
  40.2 49.6 all-gather.4
  105.0 45.8 all-gather.6
  152.8 44.7 all-gather.8
  199.2 44.6 all-gather.10

commit v7 on v6

--- a/solution.py
+++ b/solution.py
@@ -30,7 +30,6 @@
 PIECE = AT_SHARED_V + PATCHES // 2
 HALF = HD // 2
 ANY = pl.BlockSpec(memory_space=pl.ANY)
-HBM = pl.BlockSpec(memory_space=pltpu.HBM)
 SMEM = pl.BlockSpec(memory_space=pltpu.SMEM)
 VMEM = pl.BlockSpec(memory_space=pltpu.VMEM)
 SMALL = pltpu.CompilerParams(vmem_limit_bytes=24 * 1024 * 1024)
@@ -91,19 +90,6 @@
         put(member, AT_SHARED_VO, jnp.concatenate([w_v[:, lanes], w_o[:, lanes]], axis=1))
 
 
-def cut_kernel(received_ref, earlier_ref, *rest):
-    del earlier_ref
-    targets, sems = rest[:-1], rest[-1]
-    copies = [
-        pltpu.make_async_copy(received_ref.at[block + 1], target, sems.at[block])
-        for block, target in enumerate(targets)
-    ]
-    for copy in copies:
-        copy.start()
-    for copy in copies:
-        copy.wait()
-
-
 def first_kernel(rows_ref, shift_ref, scale_ref, normed_ref):
     normed = modulate(rows_ref[...].astype(jnp.float32), shift_ref[...], scale_ref[...])
     twice = jnp.concatenate([normed, normed], axis=0)
@@ -335,7 +321,7 @@
     sent = pl.pallas_call(
         pack_kernel,
         out_shape=jax.ShapeDtypeStruct((MEMBERS, PIECE, HD), jnp.bfloat16),
-        in_specs=[HBM, HBM, VMEM],
+        in_specs=[ANY, ANY, VMEM],
         out_specs=VMEM,
         scratch_shapes=[
             pltpu.VMEM((ROWS, 3 * D), jnp.bfloat16),
@@ -347,10 +333,9 @@
     )(w_qkv[0], w_out[0].T, jnp.swapaxes(stale[0, :, 0], 0, 1))
     received = exchange(sent, HEAD_AXES).reshape(BLOCKS, NY, PIECE, HD)
 
-    def gather(own_piece):
-        return lax.all_gather(own_piece, REST_AXES, axis=0, tiled=True)
-
-    pieces = [gather(received[0])]
+    pieces = [
+        lax.all_gather(received[block], REST_AXES, axis=0, tiled=True) for block in range(BLOCKS)
+    ]
 
     terms = to_own_order(lax.all_gather(modulation[0], "x", axis=0, tiled=False))
     wanted = latent.reshape(NZ * NC, 2, D)
@@ -362,6 +347,7 @@
         return terms[block, which][None]
 
     spread = jax.ShapeDtypeStruct((LOCAL, D), jnp.bfloat16)
+    owned = jax.ShapeDtypeStruct((OWN, D), jnp.bfloat16)
     normed = pl.pallas_call(
         first_kernel,
         out_shape=spread,
@@ -370,18 +356,8 @@
         compiler_params=PARAMS,
         name="first",
     )(current, term(0, 0), term(0, 1))
-    later = pl.pallas_call(
-        cut_kernel,
-        out_shape=[jax.ShapeDtypeStruct((NY, PIECE, HD), jnp.bfloat16)] * (BLOCKS - 1),
-        in_specs=[ANY, VMEM],
-        out_specs=[HBM] * (BLOCKS - 1),
-        scratch_shapes=[pltpu.SemaphoreType.DMA((BLOCKS - 1,))],
-        name="cut",
-    )(received, normed)
-    pieces += [gather(own_piece) for own_piece in later]
     weight = pltpu.VMEM((SOURCES, ROWS, HD), jnp.bfloat16)
     cache = pltpu.VMEM((SOURCES, PATCHES, HD), jnp.bfloat16)
-    owned = jax.ShapeDtypeStruct((OWN, D), jnp.bfloat16)
     half_cache = jax.ShapeDtypeStruct((SOURCES, PATCHES // 2, HD), jnp.bfloat16)
     kept_weight = jax.ShapeDtypeStruct((SOURCES, ROWS, HD), jnp.bfloat16)
     sums_of = jax.ShapeDtypeStruct((LOCAL, HD), jnp.float32)
@@ -411,12 +387,12 @@
         rows = exchange(normed, HEAD_AXES)
         source = pieces[block]
         kept, given = local(
-            shared_project_kernel, (SMEM, VMEM, HBM), (VMEM, VMEM),
+            shared_project_kernel, (SMEM, VMEM, ANY), (VMEM, VMEM),
             (rows_of(LOCAL + PT), rows_of(LOCAL + PT)), [weight] * 2, 2, 2 * D * HD,
         )(place, rows, source)
         got = swap(given)
         own, keys, values = local(
-            own_project_kernel, (VMEM, HBM), (VMEM, VMEM, VMEM),
+            own_project_kernel, (VMEM, ANY), (VMEM, VMEM, VMEM),
             (rows_of(3 * LOCAL), half_cache, half_cache), [weight] * 3, 5, 3 * D * HD,
         )(rows, source)
         sums, given = local(
@@ -425,7 +401,7 @@
         )(place, kept, got, keys, values)
         got = swap(given)
         attended, w_own, w_vo = local(
-            own_attend_kernel, (SMEM, VMEM, VMEM, HBM), (VMEM, VMEM, VMEM),
+            own_attend_kernel, (SMEM, VMEM, VMEM, ANY), (VMEM, VMEM, VMEM),
             (rows_of(LOCAL), kept_weight, kept_weight), [cache] * 2, 4, 2 * PATCHES * PT * HD,
         )(place, own, sums, source)
         partial = local(

time: 326 us -> 295 us (0.905)
  Pallas kernels: 82.1 us -> 44.9 us
  waiting for transfers between devices: 63.6 us -> 69.9 us
  blocking collectives: 116 us -> 111 us
  starting transfers between devices: 37.9 us -> 42.2 us
    pallas_call x13 -> x12, Pallas kernels: 68.7 us -> 30.6 us  [the longest x4 10.6 us: body(): local(own_attend_kernel, (SMEM, VMEM, VMEM, ANY), (VMEM, VMEM, VMEM), (ro...]
    all_gather x4, waiting for transfers between devices: 13.3 us -> 41.4 us  [body(): lax.all_gather(received[block], REST_AXES, axis=0, tiled=True)]
    all_to_all x6, waiting for transfers between devices: 41.3 us -> 23.9 us  [exchange(): return lax.all_to_all(array, axes, split_axis=0, concat_axis=0, tiled=True)]
    ppermute x8, waiting for transfers between devices: 5.38 us -> 0.43 us  [swap(): return lax.ppermute(array, 'y', [(at, at ^ 1) for at in range(NY)])]
    all_to_all x5, blocking collectives: 105 us -> 101 us  [exchange(): return lax.all_to_all(array, axes, split_axis=0, concat_axis=0, tiled=True)]
  transfers between devices with their start and end apart: 21 -> 21, of which waited for: 15 -> 11; matrix products, arithmetic and copies ran while one was open for 2% -> 2% of each run, Pallas kernels for 23% -> 13%
where the time goes in v7:
time: 295 us; the launch traced here: 293 us
  blocking collectives  111 us (38%)
  waiting for transfers between devices  69.9 us (24%)
  Pallas kernels  44.9 us (15%)
  starting transfers between devices  42.2 us (14%)
  between operations  13.7 us (5%)
  local copies, waits for them, and re-layouts  10.1 us (3%)
    all_to_all x5, blocking collectives, exchange(): return lax.all_to_all(array, axes, split_axis=0, concat_axis=0, tiled=True)  101 us
    all_gather x4, waiting for transfers between devices, body(): lax.all_gather(received[block], REST_AXES, axis=0, tiled=True)  41.4 us
    all_to_all x6, starting transfers between devices, exchange(): return lax.all_to_all(array, axes, split_axis=0, concat_axis=0, tiled=True)  32 us
    all_to_all x6, waiting for transfers between devices, exchange(): return lax.all_to_all(array, axes, split_axis=0, concat_axis=0, tiled=True)  23.9 us
    pallas_call x4, Pallas kernels, body(): local(own_attend_kernel, (SMEM, VMEM, VMEM, ANY), (VMEM, VMEM, VMEM), (ro...  10.6 us
    all_gather x1, blocking collectives, body(): lax.all_gather(modulation[0], 'x', axis=0, tiled=False)  10.5 us
    pallas_call x4, Pallas kernels, body(): local(own_project_kernel, (VMEM, ANY), (VMEM, VMEM, VMEM), (rows_of(3 * L...  10.4 us
    pallas_call x4, Pallas kernels, body(): local(shared_project_kernel, (SMEM, VMEM, ANY), (VMEM, VMEM), (rows_of(LO...  9.59 us
  transfers between devices with their start and end apart: 21, of which 11 were waited for; matrix products, arithmetic and copies ran while one was open for 2% of the time, Pallas kernels for 13%

profile of v7, /device:TPU:1, one launch (start us, length us, event | category | flops | bytes accessed | tf_op | source)
XLA Modules:
  0.0 293.5 jit_solution(13390547779672605781)
XLA Ops:
  6.5 1.1 copy.48
  7.7 1.2 copy-done
  8.8 1.0 copy-done.1
  9.8 0.6 pack.1
  10.4 28.9 %all_to_all.105 = bf16[16,384,128]{2,1,0:T(8,128)(2,1)S(1)} all-to-all(bf16[16,384,128]{2,1,0:T(8,128)(2,1)S(1)} %pack.1), channel_id=1, replica_groups=mesh['x'=4,'y'=4,'z'=8,'c'=2] {'x','y'}, dimensions={0} | all-to-all | bytes 3145728 | tf_op jit(solution)/shard_map/all_to_all | solution.py:313
  39.3 1.2 fusion
  40.5 0.7 all-gather.7.cloned.1.call-update
  41.3 0.7 all-gather.9.cloned.1.call-update
  42.0 0.5 all-gather.11.cloned.1.call-update
  42.9 0.5 broadcast.11
  43.4 1.2 reduce.2
  44.6 0.7 reshape.76
  45.3 10.5 %all-to-all-start = ((bf16[16,2,1536]{2,1,0:T(2,128)(2,1)}), bf16[16,2,1536]{2,1,0:T(2,128)(2,1)S(1)}, u32[]{:S(2)}, u32[]{:S(2)}) async-start(bf16[16,2,1536]{2,1,0:T(2,128)(2,1)} %reshape.76), calls=%async_computation | async-start | bytes 196608 | tf_op jit(solution)/shard_map/all_to_all | solution.py:313
  55.8 10.5 %all_gather.15 = f32[4,3,3072]{2,1,0:T(4,128)S(1)} all-gather(f32[1,3,3072]{2,1,0:T(4,128)S(1)} %copy.34), channel_id=1, replica_groups=mesh['x'=4,'y'=4,'z'=8,'c'=2] {'x'}, dimensions={0}, use_global_device_ids=true | all-gather | bytes 184320 | tf_op jit(solution)/shard_map/all_gather | solution.py:340
  68.0 1.2 first.1
  69.2 3.6 %all-to-all-start.1 = ((bf16[16,8,3072]{2,1,0:T(8,128)(2,1)}), bf16[16,8,3072]{2,1,0:T(8,128)(2,1)S(1)}, u32[]{:S(2)}, u32[]{:S(2)}) async-start(bf16[16,8,3072]{2,1,0:T(8,128)(2,1)} %bitcast.6), calls=%async_computation.1 | async-start | bytes 1572864 | tf_op jit(solution)/shard_map/all_to_all | solution.py:313
  72.9 12.2 %all-to-all-done.1 = bf16[16,8,3072]{2,1,0:T(8,128)(2,1)S(1)} async-done(((bf16[16,8,3072]{2,1,0:T(8,128)(2,1)}), bf16[16,8,3072]{2,1,0:T(8,128)(2,1)S(1)}, u32[]{:S(2)}, u32[]{:S(2)}) %all-to-all-start.1) | async-done | bytes 786464 | tf_op jit(solution)/shard_map/all_to_all | solution.py:313
  85.1 5.2 %all-gather.5.cloned.1.call-done.pieces_ref = bf16[64,384,128]{2,1,0:T(8,128)(2,1)} async-done(((bf16[4,384,128]{2,1,0:T(8,128)(2,1)}), bf16[64,384,128]{2,1,0:T(8,128)(2,1)}) %all-gather.5.cloned.1.call-update) | async-done | bytes 6291472 | tf_op jit(solution)/shard_map/all_gather | solution.py:337
  90.3 2.4 shared_project_kernel.4
  92.7 1.3 collective-permute-start
  94.0 2.6 own_project_kernel.4
  96.6 1.3 shared_attend_kernel.4
  98.3 2.7 own_attend_kernel.4
  101.1 0.6 finish_kernel.4
  101.7 17.8 %all_to_all.106 = bf16[16,8,3072]{2,1,0:T(8,128)(2,1)S(1)} all-to-all(bf16[16,8,3072]{2,1,0:T(8,128)(2,1)S(1)} %bitcast.99), channel_id=1, replica_groups=mesh['x'=4,'y'=4,'z'=8,'c'=2] {'x','y'}, dimensions={0} | all-to-all | bytes 1572864 | tf_op jit(solution)/shard_map/all_to_all | solution.py:313
  119.5 1.3 middle.3
  120.8 3.8 %all-to-all-start.4 = ((bf16[16,8,3072]{2,1,0:T(8,128)(2,1)}), bf16[16,8,3072]{2,1,0:T(8,128)(2,1)S(1)}, u32[]{:S(2)}, u32[]{:S(2)}) async-start(bf16[16,8,3072]{2,1,0:T(8,128)(2,1)} %bitcast.19), calls=%async_computation.4 | async-start | bytes 1572864 | tf_op jit(solution)/shard_map/all_to_all | solution.py:313
  124.6 12.2 %all-gather.7.cloned.1.call-done.pieces_ref = bf16[64,384,128]{2,1,0:T(8,128)(2,1)} async-done(((bf16[4,384,128]{2,1,0:T(8,128)(2,1)}), bf16[64,384,128]{2,1,0:T(8,128)(2,1)}) %all-gather.7.cloned.1.call-update) | async-done | bytes 6291472 | tf_op jit(solution)/shard_map/all_gather | solution.py:337
  136.8 2.4 shared_project_kernel.5
  139.2 1.3 collective-permute-start.2
  140.5 2.6 own_project_kernel.5
  143.1 1.3 shared_attend_kernel.5
  144.4 0.6 collective-permute-start.3
  145.0 2.7 own_attend_kernel.5
  147.8 0.6 finish_kernel.5
  148.4 17.8 %all_to_all.107 = bf16[16,8,3072]{2,1,0:T(8,128)(2,1)S(1)} all-to-all(bf16[16,8,3072]{2,1,0:T(8,128)(2,1)S(1)} %bitcast.100), channel_id=1, replica_groups=mesh['x'=4,'y'=4,'z'=8,'c'=2] {'x','y'}, dimensions={0} | all-to-all | bytes 1572864 | tf_op jit(solution)/shard_map/all_to_all | solution.py:313
  166.3 1.3 middle.4
  167.5 3.8 %all-to-all-start.6 = ((bf16[16,8,3072]{2,1,0:T(8,128)(2,1)}), bf16[16,8,3072]{2,1,0:T(8,128)(2,1)S(1)}, u32[]{:S(2)}, u32[]{:S(2)}) async-start(bf16[16,8,3072]{2,1,0:T(8,128)(2,1)} %bitcast.27), calls=%async_computation.6 | async-start | bytes 1572864 | tf_op jit(solution)/shard_map/all_to_all | solution.py:313
  171.4 12.0 %all-gather.9.cloned.1.call-done.pieces_ref = bf16[64,384,128]{2,1,0:T(8,128)(2,1)} async-done(((bf16[4,384,128]{2,1,0:T(8,128)(2,1)}), bf16[64,384,128]{2,1,0:T(8,128)(2,1)}) %all-gather.9.cloned.1.call-update) | async-done | bytes 6291472 | tf_op jit(solution)/shard_map/all_gather | solution.py:337
  183.3 2.4 shared_project_kernel.6
  185.8 1.3 collective-permute-start.4
  187.0 2.6 own_project_kernel.6
  189.7 1.3 shared_attend_kernel.6
  191.3 2.7 own_attend_kernel.6
  194.1 0.6 finish_kernel.6
  194.8 17.9 %all_to_all.108 = bf16[16,8,3072]{2,1,0:T(8,128)(2,1)S(1)} all-to-all(bf16[16,8,3072]{2,1,0:T(8,128)(2,1)S(1)} %bitcast.101), channel_id=1, replica_groups=mesh['x'=4,'y'=4,'z'=8,'c'=2] {'x','y'}, dimensions={0} | all-to-all | bytes 1572864 | tf_op jit(solution)/shard_map/all_to_all | solution.py:313
  212.6 1.3 middle.5
  213.9 3.8 %all-to-all-start.8 = ((bf16[16,8,3072]{2,1,0:T(8,128)(2,1)}), bf16[16,8,3072]{2,1,0:T(8,128)(2,1)S(1)}, u32[]{:S(2)}, u32[]{:S(2)}) async-start(bf16[16,8,3072]{2,1,0:T(8,128)(2,1)} %bitcast.35), calls=%async_computation.8 | async-start | bytes 1572864 | tf_op jit(solution)/shard_map/all_to_all | solution.py:313
  217.7 12.0 %all-gather.11.cloned.1.call-done.pieces_ref = bf16[64,384,128]{2,1,0:T(8,128)(2,1)} async-done(((bf16[4,384,128]{2,1,0:T(8,128)(2,1)}), bf16[64,384,128]{2,1,0:T(8,128)(2,1)}) %all-gather.11.cloned.1.call-update) | async-done | bytes 6291472 | tf_op jit(solution)/shard_map/all_gather | solution.py:337
  229.7 2.4 shared_project_kernel.7
  232.1 1.3 collective-permute-start.6
  233.4 2.6 own_project_kernel.7
  236.1 1.3 shared_attend_kernel.7
  237.3 0.4 collective-permute-start.7
  238.1 2.7 own_attend_kernel.7
  240.8 1.5 finish_kernel.7
  242.3 6.5 %all-to-all-start.9 = ((bf16[16,8,3072]{2,1,0:T(8,128)(2,1)}), bf16[16,8,3072]{2,1,0:T(8,128)(2,1)S(1)}, u32[]{:S(2)}, u32[]{:S(2)}) async-start(bf16[16,8,3072]{2,1,0:T(8,128)(2,1)} %bitcast.37), calls=%async_computation.9 | async-start | bytes 1572864 | tf_op jit(solution)/shard_map/all_to_all | solution.py:313
  249.7 11.7 %all-to-all-done.9 = bf16[16,8,3072]{2,1,0:T(8,128)(2,1)S(1)} async-done(((bf16[16,8,3072]{2,1,0:T(8,128)(2,1)}), bf16[16,8,3072]{2,1,0:T(8,128)(2,1)S(1)}, u32[]{:S(2)}, u32[]{:S(2)}) %all-to-all-start.9) | async-done | bytes 786464 | tf_op jit(solution)/shard_map/all_to_all | solution.py:313
  262.0 2.2 collective-permute-start.9
  264.2 0.8 collective-permute-start.10
  265.0 1.7 collective-permute-done.8
  266.7 0.6 collective-permute-done.10
  267.6 18.6 %all_to_all.109 = bf16[16,2,3072]{2,1,0:T(2,128)(2,1)S(1)} all-to-all(bf16[16,2,3072]{2,1,0:T(2,128)(2,1)S(1)} %copy.42), channel_id=1, replica_groups=mesh['x'=4,'y'=4,'z'=8,'c'=2] {'z','c'}, dimensions={0} | all-to-all | bytes 393216 | tf_op jit(solution)/shard_map/all_to_all | solution.py:313
  286.2 0.8 broadcast_in_dim.3
  (63 shorter events, 5.5 us)
Async XLA Ops:
  6.5 36.0 %copy-start.2 = (bf16[32,1,3072]{2,0,1:T(8,128)(2,1)S(1)}, bf16[32,1,3072]{2,0,1:T(8,128)(2,1)}, u32[]{:S(2)}) copy-start(bf16[32,1,3072]{2,0,1:T(8,128)(2,1)} %param.5) | copy-start | bytes 589828
  6.5 83.8 %all-gather.5.cloned.1.call-start = ((), (), s32[]{:S(2)}) async-start(), calls=%async_computation.11 | async-start | bytes 6684672 | tf_op jit(solution)/shard_map/all_gather | solution.py:337
  6.5 49.2 %copy-start.3 = (f32[1,3,3072]{2,0,1:T(1,128)S(1)}, f32[1,3,3072]{2,0,1:T(1,128)}, u32[]{:S(2)}) copy-start(f32[1,3,3072]{2,0,1:T(1,128)} %param.6) | copy-start | bytes 110596
  7.6 1.2 copy-start
  8.8 1.0 copy-start.1
  40.5 96.3 %all-gather.7.cloned.1.call-start = ((), (), s32[]{:S(2)}) async-start(), calls=%async_computation.12 | async-start | bytes 6684672 | tf_op jit(solution)/shard_map/all_gather | solution.py:337
  41.2 142.1 %all-gather.9.cloned.1.call-start = ((), (), s32[]{:S(2)}) async-start(), calls=%async_computation.13 | async-start | bytes 6684672 | tf_op jit(solution)/shard_map/all_gather | solution.py:337
  42.0 187.8 %all-gather.11.cloned.1.call-start = ((), (), s32[]{:S(2)}) async-start(), calls=%async_computation.14 | async-start | bytes 6684672 | tf_op jit(solution)/shard_map/all_gather | solution.py:337
  45.3 21.9 %all-to-all-start = ((bf16[16,2,1536]{2,1,0:T(2,128)(2,1)}), bf16[16,2,1536]{2,1,0:T(2,128)(2,1)S(1)}, u32[]{:S(2)}, u32[]{:S(2)}) async-start(bf16[16,2,1536]{2,1,0:T(2,128)(2,1)} %reshape.76), calls=%async_computation | async-start | bytes 196608 | tf_op jit(solution)/shard_map/all_to_all | solution.py:313
  69.2 15.9 %all-to-all-start.1 = ((bf16[16,8,3072]{2,1,0:T(8,128)(2,1)}), bf16[16,8,3072]{2,1,0:T(8,128)(2,1)S(1)}, u32[]{:S(2)}, u32[]{:S(2)}) async-start(bf16[16,8,3072]{2,1,0:T(8,128)(2,1)} %bitcast.6), calls=%async_computation.1 | async-start | bytes 1572864 | tf_op jit(solution)/shard_map/all_to_all | solution.py:313
  92.7 3.9 %collective-permute-start = (bf16[192,128]{1,0:T(8,128)(2,1)S(1)}, bf16[192,128]{1,0:T(8,128)(2,1)S(1)}, u32[]{:S(2)}, u32[]{:S(2)}) collective-permute-start(bf16[192,128]{1,0:T(8,128)(2,1)S(1)} %get-tuple-element.53), channel_id=1, source_target_pairs={{0,16},{16,0},{32,48},{48,32},{1,17},{17,1},{33,49},{49,33},{2,18}... | collective-permute-start | bytes 147464 | tf_op jit(solution)/shard_map/ppermute | solution.py:383
  97.9 3.2 %collective-permute-start.1 = (f32[128,128]{1,0:T(8,128)S(1)}, f32[128,128]{1,0:T(8,128)S(1)}, u32[]{:S(2)}, u32[]{:S(2)}) collective-permute-start(f32[128,128]{1,0:T(8,128)S(1)} %get-tuple-element.58), channel_id=1, source_target_pairs={{0,16},{16,0},{32,48},{48,32},{1,17},{17,1},{33,49},{49,33},{2,18}... | collective-permute-start | bytes 196616 | tf_op jit(solution)/shard_map/ppermute | solution.py:383
  120.8 16.0 %all-to-all-start.4 = ((bf16[16,8,3072]{2,1,0:T(8,128)(2,1)}), bf16[16,8,3072]{2,1,0:T(8,128)(2,1)S(1)}, u32[]{:S(2)}, u32[]{:S(2)}) async-start(bf16[16,8,3072]{2,1,0:T(8,128)(2,1)} %bitcast.19), calls=%async_computation.4 | async-start | bytes 1572864 | tf_op jit(solution)/shard_map/all_to_all | solution.py:313
  139.2 3.9 %collective-permute-start.2 = (bf16[192,128]{1,0:T(8,128)(2,1)S(1)}, bf16[192,128]{1,0:T(8,128)(2,1)S(1)}, u32[]{:S(2)}, u32[]{:S(2)}) collective-permute-start(bf16[192,128]{1,0:T(8,128)(2,1)S(1)} %get-tuple-element.65), channel_id=1, source_target_pairs={{0,16},{16,0},{32,48},{48,32},{1,17},{17,1},{33,49},{49,33},{2,18}... | collective-permute-start | bytes 147464 | tf_op jit(solution)/shard_map/ppermute | solution.py:383
  144.4 3.4 %collective-permute-start.3 = (f32[128,128]{1,0:T(8,128)S(1)}, f32[128,128]{1,0:T(8,128)S(1)}, u32[]{:S(2)}, u32[]{:S(2)}) collective-permute-start(f32[128,128]{1,0:T(8,128)S(1)} %get-tuple-element.70), channel_id=1, source_target_pairs={{0,16},{16,0},{32,48},{48,32},{1,17},{17,1},{33,49},{49,33},{2,18}... | collective-permute-start | bytes 196616 | tf_op jit(solution)/shard_map/ppermute | solution.py:383
  167.5 15.8 %all-to-all-start.6 = ((bf16[16,8,3072]{2,1,0:T(8,128)(2,1)}), bf16[16,8,3072]{2,1,0:T(8,128)(2,1)S(1)}, u32[]{:S(2)}, u32[]{:S(2)}) async-start(bf16[16,8,3072]{2,1,0:T(8,128)(2,1)} %bitcast.27), calls=%async_computation.6 | async-start | bytes 1572864 | tf_op jit(solution)/shard_map/all_to_all | solution.py:313
  185.8 3.9 %collective-permute-start.4 = (bf16[192,128]{1,0:T(8,128)(2,1)S(1)}, bf16[192,128]{1,0:T(8,128)(2,1)S(1)}, u32[]{:S(2)}, u32[]{:S(2)}) collective-permute-start(bf16[192,128]{1,0:T(8,128)(2,1)S(1)} %get-tuple-element.77), channel_id=1, source_target_pairs={{0,16},{16,0},{32,48},{48,32},{1,17},{17,1},{33,49},{49,33},{2,18}... | collective-permute-start | bytes 147464 | tf_op jit(solution)/shard_map/ppermute | solution.py:383
  190.9 3.2 %collective-permute-start.5 = (f32[128,128]{1,0:T(8,128)S(1)}, f32[128,128]{1,0:T(8,128)S(1)}, u32[]{:S(2)}, u32[]{:S(2)}) collective-permute-start(f32[128,128]{1,0:T(8,128)S(1)} %get-tuple-element.82), channel_id=1, source_target_pairs={{0,16},{16,0},{32,48},{48,32},{1,17},{17,1},{33,49},{49,33},{2,18}... | collective-permute-start | bytes 196616 | tf_op jit(solution)/shard_map/ppermute | solution.py:383
  213.9 15.8 %all-to-all-start.8 = ((bf16[16,8,3072]{2,1,0:T(8,128)(2,1)}), bf16[16,8,3072]{2,1,0:T(8,128)(2,1)S(1)}, u32[]{:S(2)}, u32[]{:S(2)}) async-start(bf16[16,8,3072]{2,1,0:T(8,128)(2,1)} %bitcast.35), calls=%async_computation.8 | async-start | bytes 1572864 | tf_op jit(solution)/shard_map/all_to_all | solution.py:313
  232.1 3.9 %collective-permute-start.6 = (bf16[192,128]{1,0:T(8,128)(2,1)S(1)}, bf16[192,128]{1,0:T(8,128)(2,1)S(1)}, u32[]{:S(2)}, u32[]{:S(2)}) collective-permute-start(bf16[192,128]{1,0:T(8,128)(2,1)S(1)} %get-tuple-element.89), channel_id=1, source_target_pairs={{0,16},{16,0},{32,48},{48,32},{1,17},{17,1},{33,49},{49,33},{2,18}... | collective-permute-start | bytes 147464 | tf_op jit(solution)/shard_map/ppermute | solution.py:383
  237.3 3.5 %collective-permute-start.7 = (f32[128,128]{1,0:T(8,128)S(1)}, f32[128,128]{1,0:T(8,128)S(1)}, u32[]{:S(2)}, u32[]{:S(2)}) collective-permute-start(f32[128,128]{1,0:T(8,128)S(1)} %get-tuple-element.94), channel_id=1, source_target_pairs={{0,16},{16,0},{32,48},{48,32},{1,17},{17,1},{33,49},{49,33},{2,18}... | collective-permute-start | bytes 196616 | tf_op jit(solution)/shard_map/ppermute | solution.py:383
  242.3 19.0 %all-to-all-start.9 = ((bf16[16,8,3072]{2,1,0:T(8,128)(2,1)}), bf16[16,8,3072]{2,1,0:T(8,128)(2,1)S(1)}, u32[]{:S(2)}, u32[]{:S(2)}) async-start(bf16[16,8,3072]{2,1,0:T(8,128)(2,1)} %bitcast.37), calls=%async_computation.9 | async-start | bytes 1572864 | tf_op jit(solution)/shard_map/all_to_all | solution.py:313
  261.9 4.8 %collective-permute-start.8 = (bf16[8,3072]{1,0:T(8,128)(2,1)S(1)}, bf16[8,3072]{1,0:T(8,128)(2,1)S(1)}, u32[]{:S(2)}, u32[]{:S(2)}) collective-permute-start(bf16[8,3072]{1,0:T(8,128)(2,1)S(1)} %get-tuple-element.108), channel_id=1, source_target_pairs={{0,64},{64,128},{128,192},{192,0},{1,65},{65,129},{129,193},{193,1... | collective-permute-start | bytes 147464 | tf_op jit(solution)/shard_map/ppermute | solution.py:434
  262.0 4.7 %collective-permute-start.9 = (bf16[8,3072]{1,0:T(8,128)(2,1)S(1)}, bf16[8,3072]{1,0:T(8,128)(2,1)S(1)}, u32[]{:S(2)}, u32[]{:S(2)}) collective-permute-start(bf16[8,3072]{1,0:T(8,128)(2,1)S(1)} %get-tuple-element.107), channel_id=1, source_target_pairs={{0,128},{64,192},{128,0},{192,64},{1,129},{65,193},{129,1},{193,65... | collective-permute-start | bytes 147464 | tf_op jit(solution)/shard_map/ppermute | solution.py:434
  264.2 3.1 %collective-permute-start.10 = (bf16[8,3072]{1,0:T(8,128)(2,1)S(1)}, bf16[8,3072]{1,0:T(8,128)(2,1)S(1)}, u32[]{:S(2)}, u32[]{:S(2)}) collective-permute-start(bf16[8,3072]{1,0:T(8,128)(2,1)S(1)} %get-tuple-element.106), channel_id=1, source_target_pairs={{0,192},{64,0},{128,64},{192,128},{1,193},{65,1},{129,65},{193,129... | collective-permute-start | bytes 147464 | tf_op jit(solution)/shard_map/ppermute | solution.py:434
Sparse Core Ops, SparseCore 0:
  40.6 49.6 all-gather.4
  92.1 44.6 all-gather.6
  138.6 44.6 all-gather.8
  185.0 44.6 all-gather.10

commit v8 on v7

--- a/solution.py
+++ b/solution.py
@@ -150,12 +150,32 @@
 
 
 def shared_project_kernel(place_ref, rows_ref, pieces_ref, kept_ref, given_ref, w_qk, w_vo, sems):
-    copies = fetch(pieces_ref, sems, [(w_qk, AT_SHARED), (w_vo, AT_SHARED_VO)])
+    parts = 2
+    count = SOURCES // parts
+    copies = []
+    for low in range(0, SOURCES, count):
+        for target, at in ((w_qk, AT_SHARED), (w_vo, AT_SHARED_VO)):
+            copies.append(
+                pltpu.make_async_copy(
+                    pieces_ref.at[low : low + count, at : at + ROWS, :],
+                    target.at[low : low + count],
+                    sems.at[len(copies)],
+                )
+            )
+    for copy in copies:
+        copy.start()
     half = place_ref[1]
-    rows = rows_ref[...]
-    for copy in copies:
-        copy.wait()
-    both = project(rows, w_qk, w_vo)
+    both = jnp.zeros((LOCAL, 2 * HD), jnp.float32)
+    for part in range(parts):
+        copies[2 * part].wait()
+        copies[2 * part + 1].wait()
+        low, width = part * count, count * ROWS
+        some = [w[low : low + count].reshape(width, HD) for w in (w_qk, w_vo)]
+        both = both + jnp.dot(
+            rows_ref[:, part * width : (part + 1) * width],
+            jnp.concatenate(some, axis=1),
+            preferred_element_type=jnp.float32,
+        )
     normed = head_norm(both[:, :HD])
     values = jnp.where(low_lanes(LOCAL), both[:, HD:], 0.0).astype(jnp.bfloat16)
     kept_ref[:LOCAL] = normed
@@ -249,7 +269,11 @@
     swapped = pltpu.roll(gathered, HALF, 1)
     first = low_lanes(LOCAL)
     sums_ref[...] = jnp.where(first, total, jnp.where(half == 0, swapped, gathered))
-    given_ref[...] = jnp.where(first, total, jnp.where(half == 0, gathered, swapped))
+    leading = total.astype(jnp.bfloat16).astype(jnp.float32)
+    lane = lax.broadcasted_iota(jnp.int32, (LOCAL, HD), 1)
+    sent = jnp.where(half == 0, gathered, swapped)
+    sent = jnp.where(first, jnp.where(lane == 0, leading, total - leading), sent)
+    given_ref[...] = sent.astype(jnp.bfloat16)
 
 
 def own_attend_kernel(
@@ -279,8 +303,9 @@
 
 
 def finish_kernel(attended_ref, sums_ref, got_ref, w_own, w_vo, partial_ref):
-    sums = sums_ref[...] + got_ref[...]
-    shared = jnp.where(low_lanes(LOCAL), 0.0, sums / sums[:, :1]).astype(jnp.bfloat16)
+    sums, got = sums_ref[...], got_ref[...].astype(jnp.float32)
+    total = sums[:, :1] + got[:, :1] + got[:, 1:2]
+    shared = jnp.where(low_lanes(LOCAL), 0.0, (sums + got) / total).astype(jnp.bfloat16)
     attention = jnp.concatenate([attended_ref[...], shared], axis=1)
     step = 8
     width = step * ROWS
@@ -388,7 +413,7 @@
         source = pieces[block]
         kept, given = local(
             shared_project_kernel, (SMEM, VMEM, ANY), (VMEM, VMEM),
-            (rows_of(LOCAL + PT), rows_of(LOCAL + PT)), [weight] * 2, 2, 2 * D * HD,
+            (rows_of(LOCAL + PT), rows_of(LOCAL + PT)), [weight] * 2, 4, 2 * D * HD,
         )(place, rows, source)
         got = swap(given)
         own, keys, values = local(
@@ -397,7 +422,7 @@
         )(rows, source)
         sums, given = local(
             shared_attend_kernel, (SMEM,) + (VMEM,) * 4, (VMEM, VMEM),
-            (sums_of, sums_of), [], 0, PATCHES * PT * HD,
+            (sums_of, rows_of(LOCAL)), [], 0, PATCHES * PT * HD,
         )(place, kept, got, keys, values)
         got = swap(given)
         attended, w_own, w_vo = local(

time: 295 us -> 295 us (level)
  transfers between devices with their start and end apart: 21 -> 21, of which waited for: 11 -> 8; matrix products, arithmetic and copies ran while one was open for 2% -> 2% of each run, Pallas kernels for 13% -> 13%
where the time goes in v8:
time: 295 us; the launch traced here: 294 us
  blocking collectives  112 us (38%)
  waiting for transfers between devices  68.5 us (23%)
  Pallas kernels  45.3 us (15%)
  starting transfers between devices  42.8 us (15%)
  between operations  13.7 us (5%)
  local copies, waits for them, and re-layouts  10.1 us (3%)
    all_to_all x5, blocking collectives, exchange(): return lax.all_to_all(array, axes, split_axis=0, concat_axis=0, tiled=True)  101 us
    all_gather x4, waiting for transfers between devices, body(): lax.all_gather(received[block], REST_AXES, axis=0, tiled=True)  40.4 us
    all_to_all x6, starting transfers between devices, exchange(): return lax.all_to_all(array, axes, split_axis=0, concat_axis=0, tiled=True)  32.6 us
    all_to_all x6, waiting for transfers between devices, exchange(): return lax.all_to_all(array, axes, split_axis=0, concat_axis=0, tiled=True)  23.9 us
    pallas_call x4, Pallas kernels, body(): local(own_attend_kernel, (SMEM, VMEM, VMEM, ANY), (VMEM, VMEM, VMEM), (ro...  10.6 us
    all_gather x1, blocking collectives, body(): lax.all_gather(modulation[0], 'x', axis=0, tiled=False)  10.5 us
    pallas_call x4, Pallas kernels, body(): local(own_project_kernel, (VMEM, ANY), (VMEM, VMEM, VMEM), (rows_of(3 * L...  10.4 us
    pallas_call x4, Pallas kernels, body(): local(shared_project_kernel, (SMEM, VMEM, ANY), (VMEM, VMEM), (rows_of(LO...  9.58 us
  transfers between devices with their start and end apart: 21, of which 8 were waited for; matrix products, arithmetic and copies ran while one was open for 2% of the time, Pallas kernels for 13%

profile of v8, /device:TPU:1, one launch (start us, length us, event | category | flops | bytes accessed | tf_op | source)
XLA Modules:
  0.0 293.6 jit_solution(15548880248993396300)
XLA Ops:
  6.5 1.1 copy.48
  7.7 1.2 copy-done
  8.8 1.0 copy-done.1
  9.8 0.6 pack.1
  10.4 28.9 %all_to_all.105 = bf16[16,384,128]{2,1,0:T(8,128)(2,1)S(1)} all-to-all(bf16[16,384,128]{2,1,0:T(8,128)(2,1)S(1)} %pack.1), channel_id=1, replica_groups=mesh['x'=4,'y'=4,'z'=8,'c'=2] {'x','y'}, dimensions={0} | all-to-all | bytes 3145728 | tf_op jit(solution)/shard_map/all_to_all | solution.py:338
  39.3 1.2 fusion
  40.5 0.7 all-gather.7.cloned.1.call-update
  41.3 0.7 all-gather.9.cloned.1.call-update
  42.0 0.5 all-gather.11.cloned.1.call-update
  42.9 0.5 broadcast.11
  43.4 1.2 reduce.2
  44.6 0.7 reshape.76
  45.3 10.5 %all-to-all-start = ((bf16[16,2,1536]{2,1,0:T(2,128)(2,1)}), bf16[16,2,1536]{2,1,0:T(2,128)(2,1)S(1)}, u32[]{:S(2)}, u32[]{:S(2)}) async-start(bf16[16,2,1536]{2,1,0:T(2,128)(2,1)} %reshape.76), calls=%async_computation | async-start | bytes 196608 | tf_op jit(solution)/shard_map/all_to_all | solution.py:338
  55.8 10.5 %all_gather.15 = f32[4,3,3072]{2,1,0:T(4,128)S(1)} all-gather(f32[1,3,3072]{2,1,0:T(4,128)S(1)} %copy.34), channel_id=1, replica_groups=mesh['x'=4,'y'=4,'z'=8,'c'=2] {'x'}, dimensions={0}, use_global_device_ids=true | all-gather | bytes 184320 | tf_op jit(solution)/shard_map/all_gather | solution.py:365
  68.0 1.2 first.1
  69.2 3.6 %all-to-all-start.1 = ((bf16[16,8,3072]{2,1,0:T(8,128)(2,1)}), bf16[16,8,3072]{2,1,0:T(8,128)(2,1)S(1)}, u32[]{:S(2)}, u32[]{:S(2)}) async-start(bf16[16,8,3072]{2,1,0:T(8,128)(2,1)} %bitcast.6), calls=%async_computation.1 | async-start | bytes 1572864 | tf_op jit(solution)/shard_map/all_to_all | solution.py:338
  72.9 12.2 %all-to-all-done.1 = bf16[16,8,3072]{2,1,0:T(8,128)(2,1)S(1)} async-done(((bf16[16,8,3072]{2,1,0:T(8,128)(2,1)}), bf16[16,8,3072]{2,1,0:T(8,128)(2,1)S(1)}, u32[]{:S(2)}, u32[]{:S(2)}) %all-to-all-start.1) | async-done | bytes 786464 | tf_op jit(solution)/shard_map/all_to_all | solution.py:338
  85.1 5.2 %all-gather.5.cloned.1.call-done.pieces_ref = bf16[64,384,128]{2,1,0:T(8,128)(2,1)} async-done(((bf16[4,384,128]{2,1,0:T(8,128)(2,1)}), bf16[64,384,128]{2,1,0:T(8,128)(2,1)}) %all-gather.5.cloned.1.call-update) | async-done | bytes 6291472 | tf_op jit(solution)/shard_map/all_gather | solution.py:362
  90.3 2.4 shared_project_kernel.4
  92.7 1.3 collective-permute-start
  94.0 2.6 own_project_kernel.4
  96.6 1.3 shared_attend_kernel.4
  97.9 0.4 collective-permute-start.1
  98.3 2.7 own_attend_kernel.4
  101.0 0.7 finish_kernel.4
  101.7 18.0 %all_to_all.106 = bf16[16,8,3072]{2,1,0:T(8,128)(2,1)S(1)} all-to-all(bf16[16,8,3072]{2,1,0:T(8,128)(2,1)S(1)} %bitcast.99), channel_id=1, replica_groups=mesh['x'=4,'y'=4,'z'=8,'c'=2] {'x','y'}, dimensions={0} | all-to-all | bytes 1572864 | tf_op jit(solution)/shard_map/all_to_all | solution.py:338
  119.7 1.3 middle.3
  121.0 4.1 %all-to-all-start.4 = ((bf16[16,8,3072]{2,1,0:T(8,128)(2,1)}), bf16[16,8,3072]{2,1,0:T(8,128)(2,1)S(1)}, u32[]{:S(2)}, u32[]{:S(2)}) async-start(bf16[16,8,3072]{2,1,0:T(8,128)(2,1)} %bitcast.19), calls=%async_computation.4 | async-start | bytes 1572864 | tf_op jit(solution)/shard_map/all_to_all | solution.py:338
  125.1 11.7 %all-gather.7.cloned.1.call-done.pieces_ref = bf16[64,384,128]{2,1,0:T(8,128)(2,1)} async-done(((bf16[4,384,128]{2,1,0:T(8,128)(2,1)}), bf16[64,384,128]{2,1,0:T(8,128)(2,1)}) %all-gather.7.cloned.1.call-update) | async-done | bytes 6291472 | tf_op jit(solution)/shard_map/all_gather | solution.py:362
  136.8 2.4 shared_project_kernel.5
  139.2 1.3 collective-permute-start.2
  140.5 2.6 own_project_kernel.5
  143.1 1.3 shared_attend_kernel.5
  144.4 0.6 collective-permute-start.3
  145.0 2.7 own_attend_kernel.5
  147.7 0.7 finish_kernel.5
  148.4 18.0 %all_to_all.107 = bf16[16,8,3072]{2,1,0:T(8,128)(2,1)S(1)} all-to-all(bf16[16,8,3072]{2,1,0:T(8,128)(2,1)S(1)} %bitcast.100), channel_id=1, replica_groups=mesh['x'=4,'y'=4,'z'=8,'c'=2] {'x','y'}, dimensions={0} | all-to-all | bytes 1572864 | tf_op jit(solution)/shard_map/all_to_all | solution.py:338
  166.4 1.3 middle.4
  167.7 4.0 %all-to-all-start.6 = ((bf16[16,8,3072]{2,1,0:T(8,128)(2,1)}), bf16[16,8,3072]{2,1,0:T(8,128)(2,1)S(1)}, u32[]{:S(2)}, u32[]{:S(2)}) async-start(bf16[16,8,3072]{2,1,0:T(8,128)(2,1)} %bitcast.27), calls=%async_computation.6 | async-start | bytes 1572864 | tf_op jit(solution)/shard_map/all_to_all | solution.py:338
  171.7 11.6 %all-gather.9.cloned.1.call-done.pieces_ref = bf16[64,384,128]{2,1,0:T(8,128)(2,1)} async-done(((bf16[4,384,128]{2,1,0:T(8,128)(2,1)}), bf16[64,384,128]{2,1,0:T(8,128)(2,1)}) %all-gather.9.cloned.1.call-update) | async-done | bytes 6291472 | tf_op jit(solution)/shard_map/all_gather | solution.py:362
  183.3 2.4 shared_project_kernel.6
  185.8 1.3 collective-permute-start.4
  187.1 2.6 own_project_kernel.6
  189.7 1.3 shared_attend_kernel.6
  191.3 2.7 own_attend_kernel.6
  194.0 0.7 finish_kernel.6
  194.7 18.0 %all_to_all.108 = bf16[16,8,3072]{2,1,0:T(8,128)(2,1)S(1)} all-to-all(bf16[16,8,3072]{2,1,0:T(8,128)(2,1)S(1)} %bitcast.101), channel_id=1, replica_groups=mesh['x'=4,'y'=4,'z'=8,'c'=2] {'x','y'}, dimensions={0} | all-to-all | bytes 1572864 | tf_op jit(solution)/shard_map/all_to_all | solution.py:338
  212.7 1.3 middle.5
  214.0 3.9 %all-to-all-start.8 = ((bf16[16,8,3072]{2,1,0:T(8,128)(2,1)}), bf16[16,8,3072]{2,1,0:T(8,128)(2,1)S(1)}, u32[]{:S(2)}, u32[]{:S(2)}) async-start(bf16[16,8,3072]{2,1,0:T(8,128)(2,1)} %bitcast.35), calls=%async_computation.8 | async-start | bytes 1572864 | tf_op jit(solution)/shard_map/all_to_all | solution.py:338
  217.9 11.8 %all-gather.11.cloned.1.call-done.pieces_ref = bf16[64,384,128]{2,1,0:T(8,128)(2,1)} async-done(((bf16[4,384,128]{2,1,0:T(8,128)(2,1)}), bf16[64,384,128]{2,1,0:T(8,128)(2,1)}) %all-gather.11.cloned.1.call-update) | async-done | bytes 6291472 | tf_op jit(solution)/shard_map/all_gather | solution.py:362
  229.8 2.4 shared_project_kernel.7
  232.2 1.3 collective-permute-start.6
  233.4 2.6 own_project_kernel.7
  236.1 1.3 shared_attend_kernel.7
  238.1 2.7 own_attend_kernel.7
  240.8 1.6 finish_kernel.7
  242.4 6.5 %all-to-all-start.9 = ((bf16[16,8,3072]{2,1,0:T(8,128)(2,1)}), bf16[16,8,3072]{2,1,0:T(8,128)(2,1)S(1)}, u32[]{:S(2)}, u32[]{:S(2)}) async-start(bf16[16,8,3072]{2,1,0:T(8,128)(2,1)} %bitcast.37), calls=%async_computation.9 | async-start | bytes 1572864 | tf_op jit(solution)/shard_map/all_to_all | solution.py:338
  249.8 11.7 %all-to-all-done.9 = bf16[16,8,3072]{2,1,0:T(8,128)(2,1)S(1)} async-done(((bf16[16,8,3072]{2,1,0:T(8,128)(2,1)}), bf16[16,8,3072]{2,1,0:T(8,128)(2,1)S(1)}, u32[]{:S(2)}, u32[]{:S(2)}) %all-to-all-start.9) | async-done | bytes 786464 | tf_op jit(solution)/shard_map/all_to_all | solution.py:338
  262.1 2.2 collective-permute-start.9
  264.3 0.8 collective-permute-start.10
  265.1 1.7 collective-permute-done.8
  266.8 0.6 collective-permute-done.10
  267.7 18.6 %all_to_all.109 = bf16[16,2,3072]{2,1,0:T(2,128)(2,1)S(1)} all-to-all(bf16[16,2,3072]{2,1,0:T(2,128)(2,1)S(1)} %copy.42), channel_id=1, replica_groups=mesh['x'=4,'y'=4,'z'=8,'c'=2] {'z','c'}, dimensions={0} | all-to-all | bytes 393216 | tf_op jit(solution)/shard_map/all_to_all | solution.py:338
  286.3 0.8 broadcast_in_dim.3
  (63 shorter events, 5.1 us)
Async XLA Ops:
  6.5 36.0 %copy-start.2 = (bf16[32,1,3072]{2,0,1:T(8,128)(2,1)S(1)}, bf16[32,1,3072]{2,0,1:T(8,128)(2,1)}, u32[]{:S(2)}) copy-start(bf16[32,1,3072]{2,0,1:T(8,128)(2,1)} %param.5) | copy-start | bytes 589828
  6.5 83.8 %all-gather.5.cloned.1.call-start = ((), (), s32[]{:S(2)}) async-start(), calls=%async_computation.11 | async-start | bytes 6684672 | tf_op jit(solution)/shard_map/all_gather | solution.py:362
  6.5 49.2 %copy-start.3 = (f32[1,3,3072]{2,0,1:T(1,128)S(1)}, f32[1,3,3072]{2,0,1:T(1,128)}, u32[]{:S(2)}) copy-start(f32[1,3,3072]{2,0,1:T(1,128)} %param.6) | copy-start | bytes 110596
  7.6 1.2 copy-start
  8.8 1.0 copy-start.1
  40.5 96.3 %all-gather.7.cloned.1.call-start = ((), (), s32[]{:S(2)}) async-start(), calls=%async_computation.12 | async-start | bytes 6684672 | tf_op jit(solution)/shard_map/all_gather | solution.py:362
  41.2 142.1 %all-gather.9.cloned.1.call-start = ((), (), s32[]{:S(2)}) async-start(), calls=%async_computation.13 | async-start | bytes 6684672 | tf_op jit(solution)/shard_map/all_gather | solution.py:362
  42.0 187.8 %all-gather.11.cloned.1.call-start = ((), (), s32[]{:S(2)}) async-start(), calls=%async_computation.14 | async-start | bytes 6684672 | tf_op jit(solution)/shard_map/all_gather | solution.py:362
  45.3 21.9 %all-to-all-start = ((bf16[16,2,1536]{2,1,0:T(2,128)(2,1)}), bf16[16,2,1536]{2,1,0:T(2,128)(2,1)S(1)}, u32[]{:S(2)}, u32[]{:S(2)}) async-start(bf16[16,2,1536]{2,1,0:T(2,128)(2,1)} %reshape.76), calls=%async_computation | async-start | bytes 196608 | tf_op jit(solution)/shard_map/all_to_all | solution.py:338
  69.2 15.9 %all-to-all-start.1 = ((bf16[16,8,3072]{2,1,0:T(8,128)(2,1)}), bf16[16,8,3072]{2,1,0:T(8,128)(2,1)S(1)}, u32[]{:S(2)}, u32[]{:S(2)}) async-start(bf16[16,8,3072]{2,1,0:T(8,128)(2,1)} %bitcast.6), calls=%async_computation.1 | async-start | bytes 1572864 | tf_op jit(solution)/shard_map/all_to_all | solution.py:338
  92.7 3.9 %collective-permute-start = (bf16[192,128]{1,0:T(8,128)(2,1)S(1)}, bf16[192,128]{1,0:T(8,128)(2,1)S(1)}, u32[]{:S(2)}, u32[]{:S(2)}) collective-permute-start(bf16[192,128]{1,0:T(8,128)(2,1)S(1)} %get-tuple-element.53), channel_id=1, source_target_pairs={{0,16},{16,0},{32,48},{48,32},{1,17},{17,1},{33,49},{49,33},{2,18}... | collective-permute-start | bytes 147464 | tf_op jit(solution)/shard_map/ppermute | solution.py:408
  97.9 3.1 %collective-permute-start.1 = (bf16[128,128]{1,0:T(8,128)(2,1)S(1)}, bf16[128,128]{1,0:T(8,128)(2,1)S(1)}, u32[]{:S(2)}, u32[]{:S(2)}) collective-permute-start(bf16[128,128]{1,0:T(8,128)(2,1)S(1)} %get-tuple-element.58), channel_id=1, source_target_pairs={{0,16},{16,0},{32,48},{48,32},{1,17},{17,1},{33,49},{49,33},{2,18}... | collective-permute-start | bytes 98312 | tf_op jit(solution)/shard_map/ppermute | solution.py:408
  121.0 15.8 %all-to-all-start.4 = ((bf16[16,8,3072]{2,1,0:T(8,128)(2,1)}), bf16[16,8,3072]{2,1,0:T(8,128)(2,1)S(1)}, u32[]{:S(2)}, u32[]{:S(2)}) async-start(bf16[16,8,3072]{2,1,0:T(8,128)(2,1)} %bitcast.19), calls=%async_computation.4 | async-start | bytes 1572864 | tf_op jit(solution)/shard_map/all_to_all | solution.py:338
  139.2 3.9 %collective-permute-start.2 = (bf16[192,128]{1,0:T(8,128)(2,1)S(1)}, bf16[192,128]{1,0:T(8,128)(2,1)S(1)}, u32[]{:S(2)}, u32[]{:S(2)}) collective-permute-start(bf16[192,128]{1,0:T(8,128)(2,1)S(1)} %get-tuple-element.65), channel_id=1, source_target_pairs={{0,16},{16,0},{32,48},{48,32},{1,17},{17,1},{33,49},{49,33},{2,18}... | collective-permute-start | bytes 147464 | tf_op jit(solution)/shard_map/ppermute | solution.py:408
  144.4 3.2 %collective-permute-start.3 = (bf16[128,128]{1,0:T(8,128)(2,1)S(1)}, bf16[128,128]{1,0:T(8,128)(2,1)S(1)}, u32[]{:S(2)}, u32[]{:S(2)}) collective-permute-start(bf16[128,128]{1,0:T(8,128)(2,1)S(1)} %get-tuple-element.70), channel_id=1, source_target_pairs={{0,16},{16,0},{32,48},{48,32},{1,17},{17,1},{33,49},{49,33},{2,18}... | collective-permute-start | bytes 98312 | tf_op jit(solution)/shard_map/ppermute | solution.py:408
  167.7 15.7 %all-to-all-start.6 = ((bf16[16,8,3072]{2,1,0:T(8,128)(2,1)}), bf16[16,8,3072]{2,1,0:T(8,128)(2,1)S(1)}, u32[]{:S(2)}, u32[]{:S(2)}) async-start(bf16[16,8,3072]{2,1,0:T(8,128)(2,1)} %bitcast.27), calls=%async_computation.6 | async-start | bytes 1572864 | tf_op jit(solution)/shard_map/all_to_all | solution.py:338
  185.8 3.9 %collective-permute-start.4 = (bf16[192,128]{1,0:T(8,128)(2,1)S(1)}, bf16[192,128]{1,0:T(8,128)(2,1)S(1)}, u32[]{:S(2)}, u32[]{:S(2)}) collective-permute-start(bf16[192,128]{1,0:T(8,128)(2,1)S(1)} %get-tuple-element.77), channel_id=1, source_target_pairs={{0,16},{16,0},{32,48},{48,32},{1,17},{17,1},{33,49},{49,33},{2,18}... | collective-permute-start | bytes 147464 | tf_op jit(solution)/shard_map/ppermute | solution.py:408
  190.9 3.1 %collective-permute-start.5 = (bf16[128,128]{1,0:T(8,128)(2,1)S(1)}, bf16[128,128]{1,0:T(8,128)(2,1)S(1)}, u32[]{:S(2)}, u32[]{:S(2)}) collective-permute-start(bf16[128,128]{1,0:T(8,128)(2,1)S(1)} %get-tuple-element.82), channel_id=1, source_target_pairs={{0,16},{16,0},{32,48},{48,32},{1,17},{17,1},{33,49},{49,33},{2,18}... | collective-permute-start | bytes 98312 | tf_op jit(solution)/shard_map/ppermute | solution.py:408
  214.0 15.7 %all-to-all-start.8 = ((bf16[16,8,3072]{2,1,0:T(8,128)(2,1)}), bf16[16,8,3072]{2,1,0:T(8,128)(2,1)S(1)}, u32[]{:S(2)}, u32[]{:S(2)}) async-start(bf16[16,8,3072]{2,1,0:T(8,128)(2,1)} %bitcast.35), calls=%async_computation.8 | async-start | bytes 1572864 | tf_op jit(solution)/shard_map/all_to_all | solution.py:338
  232.2 3.9 %collective-permute-start.6 = (bf16[192,128]{1,0:T(8,128)(2,1)S(1)}, bf16[192,128]{1,0:T(8,128)(2,1)S(1)}, u32[]{:S(2)}, u32[]{:S(2)}) collective-permute-start(bf16[192,128]{1,0:T(8,128)(2,1)S(1)} %get-tuple-element.89), channel_id=1, source_target_pairs={{0,16},{16,0},{32,48},{48,32},{1,17},{17,1},{33,49},{49,33},{2,18}... | collective-permute-start | bytes 147464 | tf_op jit(solution)/shard_map/ppermute | solution.py:408
  237.3 3.5 %collective-permute-start.7 = (bf16[128,128]{1,0:T(8,128)(2,1)S(1)}, bf16[128,128]{1,0:T(8,128)(2,1)S(1)}, u32[]{:S(2)}, u32[]{:S(2)}) collective-permute-start(bf16[128,128]{1,0:T(8,128)(2,1)S(1)} %get-tuple-element.94), channel_id=1, source_target_pairs={{0,16},{16,0},{32,48},{48,32},{1,17},{17,1},{33,49},{49,33},{2,18}... | collective-permute-start | bytes 98312 | tf_op jit(solution)/shard_map/ppermute | solution.py:408
  242.4 19.0 %all-to-all-start.9 = ((bf16[16,8,3072]{2,1,0:T(8,128)(2,1)}), bf16[16,8,3072]{2,1,0:T(8,128)(2,1)S(1)}, u32[]{:S(2)}, u32[]{:S(2)}) async-start(bf16[16,8,3072]{2,1,0:T(8,128)(2,1)} %bitcast.37), calls=%async_computation.9 | async-start | bytes 1572864 | tf_op jit(solution)/shard_map/all_to_all | solution.py:338
  262.0 4.8 %collective-permute-start.8 = (bf16[8,3072]{1,0:T(8,128)(2,1)S(1)}, bf16[8,3072]{1,0:T(8,128)(2,1)S(1)}, u32[]{:S(2)}, u32[]{:S(2)}) collective-permute-start(bf16[8,3072]{1,0:T(8,128)(2,1)S(1)} %get-tuple-element.108), channel_id=1, source_target_pairs={{0,64},{64,128},{128,192},{192,0},{1,65},{65,129},{129,193},{193,1... | collective-permute-start | bytes 147464 | tf_op jit(solution)/shard_map/ppermute | solution.py:459
  262.1 4.7 %collective-permute-start.9 = (bf16[8,3072]{1,0:T(8,128)(2,1)S(1)}, bf16[8,3072]{1,0:T(8,128)(2,1)S(1)}, u32[]{:S(2)}, u32[]{:S(2)}) collective-permute-start(bf16[8,3072]{1,0:T(8,128)(2,1)S(1)} %get-tuple-element.107), channel_id=1, source_target_pairs={{0,128},{64,192},{128,0},{192,64},{1,129},{65,193},{129,1},{193,65... | collective-permute-start | bytes 147464 | tf_op jit(solution)/shard_map/ppermute | solution.py:459
  264.3 3.1 %collective-permute-start.10 = (bf16[8,3072]{1,0:T(8,128)(2,1)S(1)}, bf16[8,3072]{1,0:T(8,128)(2,1)S(1)}, u32[]{:S(2)}, u32[]{:S(2)}) collective-permute-start(bf16[8,3072]{1,0:T(8,128)(2,1)S(1)} %get-tuple-element.106), channel_id=1, source_target_pairs={{0,192},{64,0},{128,64},{192,128},{1,193},{65,1},{129,65},{193,129... | collective-permute-start | bytes 147464 | tf_op jit(solution)/shard_map/ppermute | solution.py:459
Sparse Core Ops, SparseCore 0:
  40.6 49.6 all-gather.4
  92.1 44.6 all-gather.6
  138.6 44.6 all-gather.8
  185.0 44.6 all-gather.10

commit v9 on v7

--- a/solution.py
+++ b/solution.py
@@ -338,10 +338,14 @@
     ]
 
     terms = to_own_order(lax.all_gather(modulation[0], "x", axis=0, tiled=False))
-    wanted = latent.reshape(NZ * NC, 2, D)
-    wanted = lax.dynamic_index_in_dim(wanted, x_at // 2, 1, keepdims=False)
-    mine = exchange(wanted, REST_AXES)
-    current = to_own_order(lax.dynamic_slice_in_dim(mine, (x_at % 2) * OWN, OWN, 0))
+    wanted = latent.reshape(NZ, NC, 2, D)
+    wanted = lax.dynamic_index_in_dim(wanted, x_at // 2, 2, keepdims=False)
+    core_at = lax.axis_index("c")
+    same = lax.dynamic_index_in_dim(wanted, core_at, 1, keepdims=False)
+    other = lax.dynamic_index_in_dim(wanted, 1 - core_at, 1, keepdims=False)
+    other = lax.ppermute(other, "c", [(0, 1), (1, 0)])
+    mine = exchange(jnp.where(core_at == x_at % 2, same, other), "z")
+    current = to_own_order(mine)
 
     def term(block, which):
         return terms[block, which][None]
@@ -439,7 +443,7 @@
             for origin in range(NX)
         ]
     )
-    placed = jnp.swapaxes(placed.reshape(2, NZ * NC, D), 0, 1).reshape(PATCHES, D)
+    placed = placed.reshape(2, NC, NZ, D).transpose(2, 1, 0, 3).reshape(PATCHES, D)
     placed = exchange(placed, REST_AXES)
     return placed[None, :, None]
 

time: 295 us -> 294 us (level)
  blocking collectives: 111 us -> 108 us
    all_to_all x6, waiting for transfers between devices: 23.9 us -> 29.5 us  [exchange(): return lax.all_to_all(array, axes, split_axis=0, concat_axis=0, tiled=True)]
    all_gather x4, waiting for transfers between devices: 41.4 us -> 37.9 us  [body(): lax.all_gather(received[block], REST_AXES, axis=0, tiled=True)]
  transfers between devices with their start and end apart: 21 -> 22, of which waited for: 11 -> 12; matrix products, arithmetic and copies ran while one was open for 2% -> 2% of each run, Pallas kernels for 13% -> 13%
where the time goes in v9:
time: 294 us; the launch traced here: 293 us
  blocking collectives  108 us (37%)
  waiting for transfers between devices  72.7 us (25%)
  Pallas kernels  44.9 us (15%)
  starting transfers between devices  42.2 us (14%)
  between operations  13.7 us (5%)
  local copies, waits for them, and re-layouts  9.8 us (3%)
    all_to_all x5, blocking collectives, exchange(): return lax.all_to_all(array, axes, split_axis=0, concat_axis=0, tiled=True)  99 us
    all_gather x4, waiting for transfers between devices, body(): lax.all_gather(received[block], REST_AXES, axis=0, tiled=True)  37.9 us
    all_to_all x6, starting transfers between devices, exchange(): return lax.all_to_all(array, axes, split_axis=0, concat_axis=0, tiled=True)  29.9 us
    all_to_all x6, waiting for transfers between devices, exchange(): return lax.all_to_all(array, axes, split_axis=0, concat_axis=0, tiled=True)  29.5 us
    pallas_call x4, Pallas kernels, body(): local(own_attend_kernel, (SMEM, VMEM, VMEM, ANY), (VMEM, VMEM, VMEM), (ro...  10.6 us
    pallas_call x4, Pallas kernels, body(): local(own_project_kernel, (VMEM, ANY), (VMEM, VMEM, VMEM), (rows_of(3 * L...  10.4 us
    pallas_call x4, Pallas kernels, body(): local(shared_project_kernel, (SMEM, VMEM, ANY), (VMEM, VMEM), (rows_of(LO...  9.58 us
    all_gather x1, blocking collectives, body(): lax.all_gather(modulation[0], 'x', axis=0, tiled=False)  9.24 us
  transfers between devices with their start and end apart: 22, of which 12 were waited for; matrix products, arithmetic and copies ran while one was open for 2% of the time, Pallas kernels for 13%

profile of v9, /device:TPU:1, one launch (start us, length us, event | category | flops | bytes accessed | tf_op | source)
XLA Modules:
  0.0 292.5 jit_solution(10062247670029695215)
XLA Ops:
  6.5 1.1 copy.52
  7.7 1.2 copy-done
  8.8 1.0 copy-done.1
  9.8 0.6 pack.1
  10.4 28.9 %all_to_all.111 = bf16[16,384,128]{2,1,0:T(8,128)(2,1)S(1)} all-to-all(bf16[16,384,128]{2,1,0:T(8,128)(2,1)S(1)} %pack.1), channel_id=1, replica_groups=mesh['x'=4,'y'=4,'z'=8,'c'=2] {'x','y'}, dimensions={0} | all-to-all | bytes 3145728 | tf_op jit(solution)/shard_map/all_to_all | solution.py:313
  39.3 1.2 fusion.1
  40.5 0.7 all-gather.7.cloned.1.call-update
  41.3 0.7 all-gather.9.cloned.1.call-update
  42.0 0.5 all-gather.11.cloned.1.call-update
  42.9 2.1 collective-permute-start
  45.0 9.2 %all_gather.15 = f32[4,3,3072]{2,1,0:T(4,128)S(1)} all-gather(f32[1,3,3072]{2,1,0:T(4,128)S(1)} %copy.34), channel_id=1, replica_groups=mesh['x'=4,'y'=4,'z'=8,'c'=2] {'x'}, dimensions={0}, use_global_device_ids=true | all-gather | bytes 184320 | tf_op jit(solution)/shard_map/all_gather | solution.py:340
  55.7 0.7 reduce.1
  56.3 0.6 reshape.78
  57.0 8.6 %all-to-all-start = ((bf16[8,2,1536]{2,1,0:T(2,128)(2,1)}), bf16[8,2,1536]{2,1,0:T(2,128)(2,1)S(1)}, u32[]{:S(2)}, u32[]{:S(2)}) async-start(bf16[8,2,1536]{2,1,0:T(2,128)(2,1)} %reshape.78), calls=%async_computation | async-start | bytes 98304 | tf_op jit(solution)/shard_map/all_to_all | solution.py:313
  65.7 7.5 %all-to-all-done = bf16[8,2,1536]{2,1,0:T(2,128)(2,1)S(1)} async-done(((bf16[8,2,1536]{2,1,0:T(2,128)(2,1)}), bf16[8,2,1536]{2,1,0:T(2,128)(2,1)S(1)}, u32[]{:S(2)}, u32[]{:S(2)}) %all-to-all-start) | async-done | bytes 49184 | tf_op jit(solution)/shard_map/all_to_all | solution.py:313
  73.9 1.2 first.1
  75.0 3.6 %all-to-all-start.1 = ((bf16[16,8,3072]{2,1,0:T(8,128)(2,1)}), bf16[16,8,3072]{2,1,0:T(8,128)(2,1)S(1)}, u32[]{:S(2)}, u32[]{:S(2)}) async-start(bf16[16,8,3072]{2,1,0:T(8,128)(2,1)} %bitcast.7), calls=%async_computation.1 | async-start | bytes 1572864 | tf_op jit(solution)/shard_map/all_to_all | solution.py:313
  78.8 10.3 %all-to-all-done.1 = bf16[16,8,3072]{2,1,0:T(8,128)(2,1)S(1)} async-done(((bf16[16,8,3072]{2,1,0:T(8,128)(2,1)}), bf16[16,8,3072]{2,1,0:T(8,128)(2,1)S(1)}, u32[]{:S(2)}, u32[]{:S(2)}) %all-to-all-start.1) | async-done | bytes 786464 | tf_op jit(solution)/shard_map/all_to_all | solution.py:313
  89.3 2.4 shared_project_kernel.4
  91.7 1.3 collective-permute-start.1
  93.0 2.6 own_project_kernel.4
  95.6 1.3 shared_attend_kernel.4
  97.2 2.7 own_attend_kernel.4
  99.9 0.9 collective-permute-done.2.got_ref
  100.8 0.6 finish_kernel.4
  101.4 15.8 %all_to_all.112 = bf16[16,8,3072]{2,1,0:T(8,128)(2,1)S(1)} all-to-all(bf16[16,8,3072]{2,1,0:T(8,128)(2,1)S(1)} %bitcast.109), channel_id=1, replica_groups=mesh['x'=4,'y'=4,'z'=8,'c'=2] {'x','y'}, dimensions={0} | all-to-all | bytes 1572864 | tf_op jit(solution)/shard_map/all_to_all | solution.py:313
  117.2 1.3 middle.3
  118.5 3.7 %all-to-all-start.4 = ((bf16[16,8,3072]{2,1,0:T(8,128)(2,1)}), bf16[16,8,3072]{2,1,0:T(8,128)(2,1)S(1)}, u32[]{:S(2)}, u32[]{:S(2)}) async-start(bf16[16,8,3072]{2,1,0:T(8,128)(2,1)} %bitcast.20), calls=%async_computation.4 | async-start | bytes 1572864 | tf_op jit(solution)/shard_map/all_to_all | solution.py:313
  122.1 13.7 %all-gather.7.cloned.1.call-done.pieces_ref = bf16[64,384,128]{2,1,0:T(8,128)(2,1)} async-done(((bf16[4,384,128]{2,1,0:T(8,128)(2,1)}), bf16[64,384,128]{2,1,0:T(8,128)(2,1)}) %all-gather.7.cloned.1.call-update) | async-done | bytes 6291472 | tf_op jit(solution)/shard_map/all_gather | solution.py:337
  135.9 2.4 shared_project_kernel.5
  138.3 1.3 collective-permute-start.3
  139.6 2.6 own_project_kernel.5
  142.2 1.3 shared_attend_kernel.5
  143.4 0.6 collective-permute-start.4
  144.0 2.7 own_attend_kernel.5
  146.8 0.6 finish_kernel.5
  147.5 17.9 %all_to_all.113 = bf16[16,8,3072]{2,1,0:T(8,128)(2,1)S(1)} all-to-all(bf16[16,8,3072]{2,1,0:T(8,128)(2,1)S(1)} %bitcast.110), channel_id=1, replica_groups=mesh['x'=4,'y'=4,'z'=8,'c'=2] {'x','y'}, dimensions={0} | all-to-all | bytes 1572864 | tf_op jit(solution)/shard_map/all_to_all | solution.py:313
  165.3 1.3 middle.4
  166.6 3.8 %all-to-all-start.6 = ((bf16[16,8,3072]{2,1,0:T(8,128)(2,1)}), bf16[16,8,3072]{2,1,0:T(8,128)(2,1)S(1)}, u32[]{:S(2)}, u32[]{:S(2)}) async-start(bf16[16,8,3072]{2,1,0:T(8,128)(2,1)} %bitcast.28), calls=%async_computation.6 | async-start | bytes 1572864 | tf_op jit(solution)/shard_map/all_to_all | solution.py:313
  170.4 12.0 %all-gather.9.cloned.1.call-done.pieces_ref = bf16[64,384,128]{2,1,0:T(8,128)(2,1)} async-done(((bf16[4,384,128]{2,1,0:T(8,128)(2,1)}), bf16[64,384,128]{2,1,0:T(8,128)(2,1)}) %all-gather.9.cloned.1.call-update) | async-done | bytes 6291472 | tf_op jit(solution)/shard_map/all_gather | solution.py:337
  182.4 2.4 shared_project_kernel.6
  184.8 1.3 collective-permute-start.5
  186.1 2.6 own_project_kernel.6
  188.7 1.3 shared_attend_kernel.6
  190.4 2.7 own_attend_kernel.6
  193.2 0.6 finish_kernel.6
  193.8 17.9 %all_to_all.114 = bf16[16,8,3072]{2,1,0:T(8,128)(2,1)S(1)} all-to-all(bf16[16,8,3072]{2,1,0:T(8,128)(2,1)S(1)} %bitcast.111), channel_id=1, replica_groups=mesh['x'=4,'y'=4,'z'=8,'c'=2] {'x','y'}, dimensions={0} | all-to-all | bytes 1572864 | tf_op jit(solution)/shard_map/all_to_all | solution.py:313
  211.7 1.3 middle.5
  213.0 3.8 %all-to-all-start.8 = ((bf16[16,8,3072]{2,1,0:T(8,128)(2,1)}), bf16[16,8,3072]{2,1,0:T(8,128)(2,1)S(1)}, u32[]{:S(2)}, u32[]{:S(2)}) async-start(bf16[16,8,3072]{2,1,0:T(8,128)(2,1)} %bitcast.36), calls=%async_computation.8 | async-start | bytes 1572864 | tf_op jit(solution)/shard_map/all_to_all | solution.py:313
  216.8 12.0 %all-gather.11.cloned.1.call-done.pieces_ref = bf16[64,384,128]{2,1,0:T(8,128)(2,1)} async-done(((bf16[4,384,128]{2,1,0:T(8,128)(2,1)}), bf16[64,384,128]{2,1,0:T(8,128)(2,1)}) %all-gather.11.cloned.1.call-update) | async-done | bytes 6291472 | tf_op jit(solution)/shard_map/all_gather | solution.py:337
  228.8 2.4 shared_project_kernel.7
  231.2 1.3 collective-permute-start.7
  232.5 2.6 own_project_kernel.7
  235.1 1.3 shared_attend_kernel.7
  237.2 2.7 own_attend_kernel.7
  239.9 1.6 finish_kernel.7
  241.4 6.5 %all-to-all-start.9 = ((bf16[16,8,3072]{2,1,0:T(8,128)(2,1)}), bf16[16,8,3072]{2,1,0:T(8,128)(2,1)S(1)}, u32[]{:S(2)}, u32[]{:S(2)}) async-start(bf16[16,8,3072]{2,1,0:T(8,128)(2,1)} %bitcast.38), calls=%async_computation.9 | async-start | bytes 1572864 | tf_op jit(solution)/shard_map/all_to_all | solution.py:313
  248.7 11.7 %all-to-all-done.9 = bf16[16,8,3072]{2,1,0:T(8,128)(2,1)S(1)} async-done(((bf16[16,8,3072]{2,1,0:T(8,128)(2,1)}), bf16[16,8,3072]{2,1,0:T(8,128)(2,1)S(1)}, u32[]{:S(2)}, u32[]{:S(2)}) %all-to-all-start.9) | async-done | bytes 786464 | tf_op jit(solution)/shard_map/all_to_all | solution.py:313
  261.1 2.2 collective-permute-start.10
  263.2 0.8 collective-permute-start.11
  264.0 1.7 collective-permute-done.9
  265.7 0.6 collective-permute-done.11
  266.6 18.6 %all_to_all.115 = bf16[16,2,3072]{2,1,0:T(2,128)(2,1)S(1)} all-to-all(bf16[16,2,3072]{2,1,0:T(2,128)(2,1)S(1)} %bitcast.121), channel_id=1, replica_groups=mesh['x'=4,'y'=4,'z'=8,'c'=2] {'z','c'}, dimensions={0} | all-to-all | bytes 393216 | tf_op jit(solution)/shard_map/all_to_all | solution.py:313
  285.3 0.8 broadcast_in_dim.3
  (67 shorter events, 6.5 us)
Async XLA Ops:
  6.5 36.0 %copy-start.2 = (bf16[32,1,3072]{2,0,1:T(8,128)(2,1)S(1)}, bf16[32,1,3072]{2,0,1:T(8,128)(2,1)}, u32[]{:S(2)}) copy-start(bf16[32,1,3072]{2,0,1:T(8,128)(2,1)} %param.5) | copy-start | bytes 589828
  6.5 38.5 %copy-start.3 = (f32[1,3,3072]{2,0,1:T(1,128)S(1)}, f32[1,3,3072]{2,0,1:T(1,128)}, u32[]{:S(2)}) copy-start(f32[1,3,3072]{2,0,1:T(1,128)} %param.6) | copy-start | bytes 110596
  6.5 82.7 %all-gather.5.cloned.1.call-start = ((), (), s32[]{:S(2)}) async-start(), calls=%async_computation.11 | async-start | bytes 6684672 | tf_op jit(solution)/shard_map/all_gather | solution.py:337
  7.6 1.2 copy-start
  8.8 1.0 copy-start.1
  40.5 95.4 %all-gather.7.cloned.1.call-start = ((), (), s32[]{:S(2)}) async-start(), calls=%async_computation.12 | async-start | bytes 6684672 | tf_op jit(solution)/shard_map/all_gather | solution.py:337
  41.2 141.2 %all-gather.9.cloned.1.call-start = ((), (), s32[]{:S(2)}) async-start(), calls=%async_computation.13 | async-start | bytes 6684672 | tf_op jit(solution)/shard_map/all_gather | solution.py:337
  42.0 186.8 %all-gather.11.cloned.1.call-start = ((), (), s32[]{:S(2)}) async-start(), calls=%async_computation.14 | async-start | bytes 6684672 | tf_op jit(solution)/shard_map/all_gather | solution.py:337
  42.9 12.2 %collective-permute-start = (bf16[8,3072]{1,0:T(8,128)(2,1)S(1)}, bf16[8,3072]{1,0:T(8,128)(2,1)S(1)}, u32[]{:S(2)}, u32[]{:S(2)}) collective-permute-start(bf16[8,3072]{1,0:T(8,128)(2,1)S(1)} %bitcast.130), channel_id=1, source_target_pairs={{0,1},{1,0},{2,3},{3,2},{4,5},{5,4},{6,7},{7,6},{8,9},{9,8},{10,11... | collective-permute-start | bytes 147464 | tf_op jit(solution)/shard_map/ppermute | solution.py:346
  57.0 16.1 %all-to-all-start = ((bf16[8,2,1536]{2,1,0:T(2,128)(2,1)}), bf16[8,2,1536]{2,1,0:T(2,128)(2,1)S(1)}, u32[]{:S(2)}, u32[]{:S(2)}) async-start(bf16[8,2,1536]{2,1,0:T(2,128)(2,1)} %reshape.78), calls=%async_computation | async-start | bytes 98304 | tf_op jit(solution)/shard_map/all_to_all | solution.py:313
  75.0 14.0 %all-to-all-start.1 = ((bf16[16,8,3072]{2,1,0:T(8,128)(2,1)}), bf16[16,8,3072]{2,1,0:T(8,128)(2,1)S(1)}, u32[]{:S(2)}, u32[]{:S(2)}) async-start(bf16[16,8,3072]{2,1,0:T(8,128)(2,1)} %bitcast.7), calls=%async_computation.1 | async-start | bytes 1572864 | tf_op jit(solution)/shard_map/all_to_all | solution.py:313
  91.7 3.9 %collective-permute-start.1 = (bf16[192,128]{1,0:T(8,128)(2,1)S(1)}, bf16[192,128]{1,0:T(8,128)(2,1)S(1)}, u32[]{:S(2)}, u32[]{:S(2)}) collective-permute-start(bf16[192,128]{1,0:T(8,128)(2,1)S(1)} %get-tuple-element.53), channel_id=1, source_target_pairs={{0,16},{16,0},{32,48},{48,32},{1,17},{17,1},{33,49},{49,33},{2,18}... | collective-permute-start | bytes 147464 | tf_op jit(solution)/shard_map/ppermute | solution.py:387
  96.8 3.9 %collective-permute-start.2 = (f32[128,128]{1,0:T(8,128)S(1)}, f32[128,128]{1,0:T(8,128)S(1)}, u32[]{:S(2)}, u32[]{:S(2)}) collective-permute-start(f32[128,128]{1,0:T(8,128)S(1)} %get-tuple-element.58), channel_id=1, source_target_pairs={{0,16},{16,0},{32,48},{48,32},{1,17},{17,1},{33,49},{49,33},{2,18}... | collective-permute-start | bytes 196616 | tf_op jit(solution)/shard_map/ppermute | solution.py:387
  118.5 17.4 %all-to-all-start.4 = ((bf16[16,8,3072]{2,1,0:T(8,128)(2,1)}), bf16[16,8,3072]{2,1,0:T(8,128)(2,1)S(1)}, u32[]{:S(2)}, u32[]{:S(2)}) async-start(bf16[16,8,3072]{2,1,0:T(8,128)(2,1)} %bitcast.20), calls=%async_computation.4 | async-start | bytes 1572864 | tf_op jit(solution)/shard_map/all_to_all | solution.py:313
  138.3 3.9 %collective-permute-start.3 = (bf16[192,128]{1,0:T(8,128)(2,1)S(1)}, bf16[192,128]{1,0:T(8,128)(2,1)S(1)}, u32[]{:S(2)}, u32[]{:S(2)}) collective-permute-start(bf16[192,128]{1,0:T(8,128)(2,1)S(1)} %get-tuple-element.65), channel_id=1, source_target_pairs={{0,16},{16,0},{32,48},{48,32},{1,17},{17,1},{33,49},{49,33},{2,18}... | collective-permute-start | bytes 147464 | tf_op jit(solution)/shard_map/ppermute | solution.py:387
  143.4 3.4 %collective-permute-start.4 = (f32[128,128]{1,0:T(8,128)S(1)}, f32[128,128]{1,0:T(8,128)S(1)}, u32[]{:S(2)}, u32[]{:S(2)}) collective-permute-start(f32[128,128]{1,0:T(8,128)S(1)} %get-tuple-element.70), channel_id=1, source_target_pairs={{0,16},{16,0},{32,48},{48,32},{1,17},{17,1},{33,49},{49,33},{2,18}... | collective-permute-start | bytes 196616 | tf_op jit(solution)/shard_map/ppermute | solution.py:387
  166.6 15.8 %all-to-all-start.6 = ((bf16[16,8,3072]{2,1,0:T(8,128)(2,1)}), bf16[16,8,3072]{2,1,0:T(8,128)(2,1)S(1)}, u32[]{:S(2)}, u32[]{:S(2)}) async-start(bf16[16,8,3072]{2,1,0:T(8,128)(2,1)} %bitcast.28), calls=%async_computation.6 | async-start | bytes 1572864 | tf_op jit(solution)/shard_map/all_to_all | solution.py:313
  184.8 3.9 %collective-permute-start.5 = (bf16[192,128]{1,0:T(8,128)(2,1)S(1)}, bf16[192,128]{1,0:T(8,128)(2,1)S(1)}, u32[]{:S(2)}, u32[]{:S(2)}) collective-permute-start(bf16[192,128]{1,0:T(8,128)(2,1)S(1)} %get-tuple-element.77), channel_id=1, source_target_pairs={{0,16},{16,0},{32,48},{48,32},{1,17},{17,1},{33,49},{49,33},{2,18}... | collective-permute-start | bytes 147464 | tf_op jit(solution)/shard_map/ppermute | solution.py:387
  190.0 3.2 %collective-permute-start.6 = (f32[128,128]{1,0:T(8,128)S(1)}, f32[128,128]{1,0:T(8,128)S(1)}, u32[]{:S(2)}, u32[]{:S(2)}) collective-permute-start(f32[128,128]{1,0:T(8,128)S(1)} %get-tuple-element.82), channel_id=1, source_target_pairs={{0,16},{16,0},{32,48},{48,32},{1,17},{17,1},{33,49},{49,33},{2,18}... | collective-permute-start | bytes 196616 | tf_op jit(solution)/shard_map/ppermute | solution.py:387
  213.0 15.8 %all-to-all-start.8 = ((bf16[16,8,3072]{2,1,0:T(8,128)(2,1)}), bf16[16,8,3072]{2,1,0:T(8,128)(2,1)S(1)}, u32[]{:S(2)}, u32[]{:S(2)}) async-start(bf16[16,8,3072]{2,1,0:T(8,128)(2,1)} %bitcast.36), calls=%async_computation.8 | async-start | bytes 1572864 | tf_op jit(solution)/shard_map/all_to_all | solution.py:313
  231.2 3.9 %collective-permute-start.7 = (bf16[192,128]{1,0:T(8,128)(2,1)S(1)}, bf16[192,128]{1,0:T(8,128)(2,1)S(1)}, u32[]{:S(2)}, u32[]{:S(2)}) collective-permute-start(bf16[192,128]{1,0:T(8,128)(2,1)S(1)} %get-tuple-element.89), channel_id=1, source_target_pairs={{0,16},{16,0},{32,48},{48,32},{1,17},{17,1},{33,49},{49,33},{2,18}... | collective-permute-start | bytes 147464 | tf_op jit(solution)/shard_map/ppermute | solution.py:387
  236.4 3.5 %collective-permute-start.8 = (f32[128,128]{1,0:T(8,128)S(1)}, f32[128,128]{1,0:T(8,128)S(1)}, u32[]{:S(2)}, u32[]{:S(2)}) collective-permute-start(f32[128,128]{1,0:T(8,128)S(1)} %get-tuple-element.94), channel_id=1, source_target_pairs={{0,16},{16,0},{32,48},{48,32},{1,17},{17,1},{33,49},{49,33},{2,18}... | collective-permute-start | bytes 196616 | tf_op jit(solution)/shard_map/ppermute | solution.py:387
  241.4 19.0 %all-to-all-start.9 = ((bf16[16,8,3072]{2,1,0:T(8,128)(2,1)}), bf16[16,8,3072]{2,1,0:T(8,128)(2,1)S(1)}, u32[]{:S(2)}, u32[]{:S(2)}) async-start(bf16[16,8,3072]{2,1,0:T(8,128)(2,1)} %bitcast.38), calls=%async_computation.9 | async-start | bytes 1572864 | tf_op jit(solution)/shard_map/all_to_all | solution.py:313
  261.0 4.8 %collective-permute-start.9 = (bf16[8,3072]{1,0:T(8,128)(2,1)S(1)}, bf16[8,3072]{1,0:T(8,128)(2,1)S(1)}, u32[]{:S(2)}, u32[]{:S(2)}) collective-permute-start(bf16[8,3072]{1,0:T(8,128)(2,1)S(1)} %get-tuple-element.108), channel_id=1, source_target_pairs={{0,64},{64,128},{128,192},{192,0},{1,65},{65,129},{129,193},{193,1... | collective-permute-start | bytes 147464 | tf_op jit(solution)/shard_map/ppermute | solution.py:438
  261.1 4.7 %collective-permute-start.10 = (bf16[8,3072]{1,0:T(8,128)(2,1)S(1)}, bf16[8,3072]{1,0:T(8,128)(2,1)S(1)}, u32[]{:S(2)}, u32[]{:S(2)}) collective-permute-start(bf16[8,3072]{1,0:T(8,128)(2,1)S(1)} %get-tuple-element.107), channel_id=1, source_target_pairs={{0,128},{64,192},{128,0},{192,64},{1,129},{65,193},{129,1},{193,65... | collective-permute-start | bytes 147464 | tf_op jit(solution)/shard_map/ppermute | solution.py:438
  263.2 3.1 %collective-permute-start.11 = (bf16[8,3072]{1,0:T(8,128)(2,1)S(1)}, bf16[8,3072]{1,0:T(8,128)(2,1)S(1)}, u32[]{:S(2)}, u32[]{:S(2)}) collective-permute-start(bf16[8,3072]{1,0:T(8,128)(2,1)S(1)} %get-tuple-element.106), channel_id=1, source_target_pairs={{0,192},{64,0},{128,64},{192,128},{1,193},{65,1},{129,65},{193,129... | collective-permute-start | bytes 147464 | tf_op jit(solution)/shard_map/ppermute | solution.py:438
Sparse Core Ops, SparseCore 0:
  40.6 48.6 all-gather.4
  91.1 44.7 all-gather.6
  137.7 44.6 all-gather.8
  184.1 44.6 all-gather.10

commit v10 on v9

--- a/solution.py
+++ b/solution.py
@@ -51,10 +51,14 @@
     )
 
 
-def pack_kernel(qkv_from, out_from, stale_ref, sent_ref, qkv_ref, out_ref, sems):
+def pack_kernel(
+    qkv_from, out_from, stale_from, sent_to, qkv_ref, out_ref, stale_ref, sent_ref, sems, sent_sems
+):
     copies = [
-        pltpu.make_async_copy(qkv_from, qkv_ref, sems.at[0]),
-        pltpu.make_async_copy(out_from, out_ref, sems.at[1]),
+        pltpu.make_async_copy(source, target, sems.at[number])
+        for number, (source, target) in enumerate(
+            ((stale_from, stale_ref), (out_from, out_ref), (qkv_from, qkv_ref))
+        )
     ]
     for copy in copies:
         copy.start()
@@ -70,16 +74,17 @@
             triple, half = divmod(member, 2)
             yield member, half, 3 * triple + 2 * half, 3 * triple + 1
 
+    copies[0].wait()
     for member, half, own, shared in each():
-        put(member, AT_K, stale_ref[0, :, columns(own)])
-        put(member, AT_V, stale_ref[1, :, columns(own)])
         some = slice(half * PATCHES // 2, (half + 1) * PATCHES // 2)
-        put(member, AT_SHARED_K, stale_ref[0, some, columns(shared)])
-        put(member, AT_SHARED_V, stale_ref[1, some, columns(shared)])
+        for kind, own_low, shared_low in ((0, AT_K, AT_SHARED_K), (1, AT_V, AT_SHARED_V)):
+            put(member, own_low, stale_ref[:, kind, columns(own)])
+            put(member, shared_low, stale_ref[some, kind, columns(shared)])
     copies[1].wait()
     for member, half, own, shared in each():
         put(member, AT_OUT, out_ref[:, columns(own)])
-    copies[0].wait()
+    copies[2].wait()
+    leaving = []
     for member, half, own, shared in each():
         for part in range(3):
             put(member, part * ROWS, qkv_ref[:, columns(part * HEADS + own)])
@@ -88,6 +93,12 @@
         w_o = out_ref[:, columns(shared)]
         lanes = slice(half * HALF, (half + 1) * HALF)
         put(member, AT_SHARED_VO, jnp.concatenate([w_v[:, lanes], w_o[:, lanes]], axis=1))
+        leaving.append(
+            pltpu.make_async_copy(sent_ref.at[member], sent_to.at[member], sent_sems.at[member])
+        )
+        leaving[-1].start()
+    for copy in leaving:
+        copy.wait()
 
 
 def first_kernel(rows_ref, shift_ref, scale_ref, normed_ref):
@@ -321,16 +332,19 @@
     sent = pl.pallas_call(
         pack_kernel,
         out_shape=jax.ShapeDtypeStruct((MEMBERS, PIECE, HD), jnp.bfloat16),
-        in_specs=[ANY, ANY, VMEM],
-        out_specs=VMEM,
+        in_specs=[ANY] * 3,
+        out_specs=ANY,
         scratch_shapes=[
             pltpu.VMEM((ROWS, 3 * D), jnp.bfloat16),
             pltpu.VMEM((ROWS, D), jnp.bfloat16),
-            pltpu.SemaphoreType.DMA((2,)),
+            pltpu.VMEM((PATCHES, 2, D), jnp.bfloat16),
+            pltpu.VMEM((MEMBERS, PIECE, HD), jnp.bfloat16),
+            pltpu.SemaphoreType.DMA((3,)),
+            pltpu.SemaphoreType.DMA((MEMBERS,)),
         ],
-        compiler_params=PARAMS,
+        compiler_params=pltpu.CompilerParams(vmem_limit_bytes=60 * 1024 * 1024),
         name="pack",
-    )(w_qkv[0], w_out[0].T, jnp.swapaxes(stale[0, :, 0], 0, 1))
+    )(w_qkv[0], w_out[0].T, stale[0, :, 0])
     received = exchange(sent, HEAD_AXES).reshape(BLOCKS, NY, PIECE, HD)
 
     pieces = [

time: 294 us -> 294 us (level)
  local copies, waits for them, and re-layouts: 9.8 us -> 6.58 us
    unnamed x16 -> x11, local copies, waits for them, and re-layouts: 3.97 us -> 0.74 us
where the time goes in v10:
time: 294 us; the launch traced here: 293 us
  blocking collectives  108 us (37%)
  waiting for transfers between devices  72.8 us (25%)
  Pallas kernels  47.6 us (16%)
  starting transfers between devices  42.4 us (14%)
  between operations  13.7 us (5%)
  local copies, waits for them, and re-layouts  6.58 us (2%)
    all_to_all x5, blocking collectives, exchange(): return lax.all_to_all(array, axes, split_axis=0, concat_axis=0, tiled=True)  99.2 us
    all_gather x4, waiting for transfers between devices, body(): lax.all_gather(received[block], REST_AXES, axis=0, tiled=True)  38 us
    all_to_all x6, starting transfers between devices, exchange(): return lax.all_to_all(array, axes, split_axis=0, concat_axis=0, tiled=True)  30 us
    all_to_all x6, waiting for transfers between devices, exchange(): return lax.all_to_all(array, axes, split_axis=0, concat_axis=0, tiled=True)  29.5 us
    pallas_call x4, Pallas kernels, body(): local(own_attend_kernel, (SMEM, VMEM, VMEM, ANY), (VMEM, VMEM, VMEM), (ro...  10.6 us
    pallas_call x4, Pallas kernels, body(): local(own_project_kernel, (VMEM, ANY), (VMEM, VMEM, VMEM), (rows_of(3 * L...  10.4 us
    pallas_call x4, Pallas kernels, body(): local(shared_project_kernel, (SMEM, VMEM, ANY), (VMEM, VMEM), (rows_of(LO...  9.58 us
    all_gather x1, blocking collectives, body(): lax.all_gather(modulation[0], 'x', axis=0, tiled=False)  9.24 us
  transfers between devices with their start and end apart: 22, of which 12 were waited for; matrix products, arithmetic and copies ran while one was open for 2% of the time, Pallas kernels for 13%

profile of v10, /device:TPU:1, one launch (start us, length us, event | category | flops | bytes accessed | tf_op | source)
XLA Modules:
  0.0 292.6 jit_solution(15627634972970529660)
XLA Ops:
  6.5 3.4 %pack.1 = bf16[16,384,128]{2,1,0:T(8,128)(2,1)} custom-call(bf16[48,9216]{1,0:T(8,128)(2,1)} %bitcast.113, bf16[48,3072]{1,0:T(8,128)(2,1)} %bitcast.122, bf16[32,2,3072]{2,1,0:T(2,128)(2,1)} %bitcast.121), custom_call_target="tpu_custom_call" | custom-call | tf_op jit(solution)/shard_map/pack/pallas_call | solution.py:332
  9.9 29.1 %all_to_all.111 = bf16[16,384,128]{2,1,0:T(8,128)(2,1)S(1)} all-to-all(bf16[16,384,128]{2,1,0:T(8,128)(2,1)} %pack.1), channel_id=1, replica_groups=mesh['x'=4,'y'=4,'z'=8,'c'=2] {'x','y'}, dimensions={0} | all-to-all | bytes 3145728 | tf_op jit(solution)/shard_map/all_to_all | solution.py:324
  39.0 1.2 fusion.1
  40.3 0.7 all-gather.7.cloned.1.call-update
  41.0 0.7 all-gather.9.cloned.1.call-update
  41.7 0.5 all-gather.11.cloned.1.call-update
  42.6 2.1 collective-permute-start
  44.8 9.2 %all_gather.15 = f32[4,3,3072]{2,1,0:T(4,128)S(1)} all-gather(f32[1,3,3072]{2,1,0:T(4,128)S(1)} %copy.30), channel_id=1, replica_groups=mesh['x'=4,'y'=4,'z'=8,'c'=2] {'x'}, dimensions={0}, use_global_device_ids=true | all-gather | bytes 184320 | tf_op jit(solution)/shard_map/all_gather | solution.py:354
  54.9 0.5 broadcast.11
  55.4 0.7 reduce.1
  56.1 0.6 reshape.78
  56.7 8.6 %all-to-all-start = ((bf16[8,2,1536]{2,1,0:T(2,128)(2,1)}), bf16[8,2,1536]{2,1,0:T(2,128)(2,1)S(1)}, u32[]{:S(2)}, u32[]{:S(2)}) async-start(bf16[8,2,1536]{2,1,0:T(2,128)(2,1)} %reshape.78), calls=%async_computation | async-start | bytes 98304 | tf_op jit(solution)/shard_map/all_to_all | solution.py:324
  65.4 7.5 %all-to-all-done = bf16[8,2,1536]{2,1,0:T(2,128)(2,1)S(1)} async-done(((bf16[8,2,1536]{2,1,0:T(2,128)(2,1)}), bf16[8,2,1536]{2,1,0:T(2,128)(2,1)S(1)}, u32[]{:S(2)}, u32[]{:S(2)}) %all-to-all-start) | async-done | bytes 49184 | tf_op jit(solution)/shard_map/all_to_all | solution.py:324
  73.6 1.2 first.1
  74.8 3.6 %all-to-all-start.1 = ((bf16[16,8,3072]{2,1,0:T(8,128)(2,1)}), bf16[16,8,3072]{2,1,0:T(8,128)(2,1)S(1)}, u32[]{:S(2)}, u32[]{:S(2)}) async-start(bf16[16,8,3072]{2,1,0:T(8,128)(2,1)} %bitcast.7), calls=%async_computation.1 | async-start | bytes 1572864 | tf_op jit(solution)/shard_map/all_to_all | solution.py:324
  78.5 10.3 %all-to-all-done.1 = bf16[16,8,3072]{2,1,0:T(8,128)(2,1)S(1)} async-done(((bf16[16,8,3072]{2,1,0:T(8,128)(2,1)}), bf16[16,8,3072]{2,1,0:T(8,128)(2,1)S(1)}, u32[]{:S(2)}, u32[]{:S(2)}) %all-to-all-start.1) | async-done | bytes 786464 | tf_op jit(solution)/shard_map/all_to_all | solution.py:324
  89.0 2.4 shared_project_kernel.4
  91.4 1.3 collective-permute-start.1
  92.7 2.6 own_project_kernel.4
  95.3 1.3 shared_attend_kernel.4
  96.6 0.4 collective-permute-start.2
  97.0 2.7 own_attend_kernel.4
  99.6 0.9 collective-permute-done.2.got_ref
  100.5 0.6 finish_kernel.4
  101.1 15.8 %all_to_all.112 = bf16[16,8,3072]{2,1,0:T(8,128)(2,1)S(1)} all-to-all(bf16[16,8,3072]{2,1,0:T(8,128)(2,1)S(1)} %bitcast.105), channel_id=1, replica_groups=mesh['x'=4,'y'=4,'z'=8,'c'=2] {'x','y'}, dimensions={0} | all-to-all | bytes 1572864 | tf_op jit(solution)/shard_map/all_to_all | solution.py:324
  116.9 1.3 middle.3
  118.2 3.7 %all-to-all-start.4 = ((bf16[16,8,3072]{2,1,0:T(8,128)(2,1)}), bf16[16,8,3072]{2,1,0:T(8,128)(2,1)S(1)}, u32[]{:S(2)}, u32[]{:S(2)}) async-start(bf16[16,8,3072]{2,1,0:T(8,128)(2,1)} %bitcast.19), calls=%async_computation.4 | async-start | bytes 1572864 | tf_op jit(solution)/shard_map/all_to_all | solution.py:324
  121.9 13.7 %all-gather.7.cloned.1.call-done.pieces_ref = bf16[64,384,128]{2,1,0:T(8,128)(2,1)} async-done(((bf16[4,384,128]{2,1,0:T(8,128)(2,1)}), bf16[64,384,128]{2,1,0:T(8,128)(2,1)}) %all-gather.7.cloned.1.call-update) | async-done | bytes 6291472 | tf_op jit(solution)/shard_map/all_gather | solution.py:351
  135.6 2.4 shared_project_kernel.5
  138.0 1.5 collective-permute-start.3
  139.5 2.6 own_project_kernel.5
  142.1 1.3 shared_attend_kernel.5
  143.8 2.7 own_attend_kernel.5
  146.6 0.6 finish_kernel.5
  147.2 17.9 %all_to_all.113 = bf16[16,8,3072]{2,1,0:T(8,128)(2,1)S(1)} all-to-all(bf16[16,8,3072]{2,1,0:T(8,128)(2,1)S(1)} %bitcast.106), channel_id=1, replica_groups=mesh['x'=4,'y'=4,'z'=8,'c'=2] {'x','y'}, dimensions={0} | all-to-all | bytes 1572864 | tf_op jit(solution)/shard_map/all_to_all | solution.py:324
  165.0 1.3 middle.4
  166.3 3.8 %all-to-all-start.6 = ((bf16[16,8,3072]{2,1,0:T(8,128)(2,1)}), bf16[16,8,3072]{2,1,0:T(8,128)(2,1)S(1)}, u32[]{:S(2)}, u32[]{:S(2)}) async-start(bf16[16,8,3072]{2,1,0:T(8,128)(2,1)} %bitcast.27), calls=%async_computation.6 | async-start | bytes 1572864 | tf_op jit(solution)/shard_map/all_to_all | solution.py:324
  170.1 12.1 %all-gather.9.cloned.1.call-done.pieces_ref = bf16[64,384,128]{2,1,0:T(8,128)(2,1)} async-done(((bf16[4,384,128]{2,1,0:T(8,128)(2,1)}), bf16[64,384,128]{2,1,0:T(8,128)(2,1)}) %all-gather.9.cloned.1.call-update) | async-done | bytes 6291472 | tf_op jit(solution)/shard_map/all_gather | solution.py:351
  182.2 2.4 shared_project_kernel.6
  184.6 1.3 collective-permute-start.5
  185.9 2.6 own_project_kernel.6
  188.5 1.3 shared_attend_kernel.6
  189.8 0.4 collective-permute-start.6
  190.2 2.7 own_attend_kernel.6
  193.0 0.6 finish_kernel.6
  193.6 17.9 %all_to_all.114 = bf16[16,8,3072]{2,1,0:T(8,128)(2,1)S(1)} all-to-all(bf16[16,8,3072]{2,1,0:T(8,128)(2,1)S(1)} %bitcast.107), channel_id=1, replica_groups=mesh['x'=4,'y'=4,'z'=8,'c'=2] {'x','y'}, dimensions={0} | all-to-all | bytes 1572864 | tf_op jit(solution)/shard_map/all_to_all | solution.py:324
  211.5 1.3 middle.5
  212.8 3.8 %all-to-all-start.8 = ((bf16[16,8,3072]{2,1,0:T(8,128)(2,1)}), bf16[16,8,3072]{2,1,0:T(8,128)(2,1)S(1)}, u32[]{:S(2)}, u32[]{:S(2)}) async-start(bf16[16,8,3072]{2,1,0:T(8,128)(2,1)} %bitcast.35), calls=%async_computation.8 | async-start | bytes 1572864 | tf_op jit(solution)/shard_map/all_to_all | solution.py:324
  216.6 12.1 %all-gather.11.cloned.1.call-done.pieces_ref = bf16[64,384,128]{2,1,0:T(8,128)(2,1)} async-done(((bf16[4,384,128]{2,1,0:T(8,128)(2,1)}), bf16[64,384,128]{2,1,0:T(8,128)(2,1)}) %all-gather.11.cloned.1.call-update) | async-done | bytes 6291472 | tf_op jit(solution)/shard_map/all_gather | solution.py:351
  228.6 2.4 shared_project_kernel.7
  231.0 1.3 collective-permute-start.7
  232.3 2.6 own_project_kernel.7
  235.0 1.3 shared_attend_kernel.7
  236.2 0.6 collective-permute-start.8
  237.2 2.7 own_attend_kernel.7
  239.9 1.5 finish_kernel.7
  241.4 6.5 %all-to-all-start.9 = ((bf16[16,8,3072]{2,1,0:T(8,128)(2,1)}), bf16[16,8,3072]{2,1,0:T(8,128)(2,1)S(1)}, u32[]{:S(2)}, u32[]{:S(2)}) async-start(bf16[16,8,3072]{2,1,0:T(8,128)(2,1)} %bitcast.37), calls=%async_computation.9 | async-start | bytes 1572864 | tf_op jit(solution)/shard_map/all_to_all | solution.py:324
  248.8 11.7 %all-to-all-done.9 = bf16[16,8,3072]{2,1,0:T(8,128)(2,1)S(1)} async-done(((bf16[16,8,3072]{2,1,0:T(8,128)(2,1)}), bf16[16,8,3072]{2,1,0:T(8,128)(2,1)S(1)}, u32[]{:S(2)}, u32[]{:S(2)}) %all-to-all-start.9) | async-done | bytes 786464 | tf_op jit(solution)/shard_map/all_to_all | solution.py:324
  261.1 2.2 collective-permute-start.10
  263.3 0.8 collective-permute-start.11
  264.1 1.7 collective-permute-done.9
  265.8 0.6 collective-permute-done.11
  266.7 18.7 %all_to_all.115 = bf16[16,2,3072]{2,1,0:T(2,128)(2,1)S(1)} all-to-all(bf16[16,2,3072]{2,1,0:T(2,128)(2,1)S(1)} %bitcast.115), channel_id=1, replica_groups=mesh['x'=4,'y'=4,'z'=8,'c'=2] {'z','c'}, dimensions={0} | all-to-all | bytes 393216 | tf_op jit(solution)/shard_map/all_to_all | solution.py:324
  285.3 0.8 broadcast_in_dim.3
  (62 shorter events, 5.1 us)
Async XLA Ops:
  6.5 35.8 %copy-start = (bf16[32,1,3072]{2,0,1:T(8,128)(2,1)S(1)}, bf16[32,1,3072]{2,0,1:T(8,128)(2,1)}, u32[]{:S(2)}) copy-start(bf16[32,1,3072]{2,0,1:T(8,128)(2,1)} %param.5) | copy-start | bytes 589828
  6.5 38.2 %copy-start.1 = (f32[1,3,3072]{2,0,1:T(1,128)S(1)}, f32[1,3,3072]{2,0,1:T(1,128)}, u32[]{:S(2)}) copy-start(f32[1,3,3072]{2,0,1:T(1,128)} %param.6) | copy-start | bytes 110596
  6.5 82.5 %all-gather.5.cloned.1.call-start = ((), (), s32[]{:S(2)}) async-start(), calls=%async_computation.11 | async-start | bytes 6684672 | tf_op jit(solution)/shard_map/all_gather | solution.py:351
  40.2 95.4 %all-gather.7.cloned.1.call-start = ((), (), s32[]{:S(2)}) async-start(), calls=%async_computation.12 | async-start | bytes 6684672 | tf_op jit(solution)/shard_map/all_gather | solution.py:351
  41.0 141.2 %all-gather.9.cloned.1.call-start = ((), (), s32[]{:S(2)}) async-start(), calls=%async_computation.13 | async-start | bytes 6684672 | tf_op jit(solution)/shard_map/all_gather | solution.py:351
  41.7 186.9 %all-gather.11.cloned.1.call-start = ((), (), s32[]{:S(2)}) async-start(), calls=%async_computation.14 | async-start | bytes 6684672 | tf_op jit(solution)/shard_map/all_gather | solution.py:351
  42.6 12.2 %collective-permute-start = (bf16[8,3072]{1,0:T(8,128)(2,1)S(1)}, bf16[8,3072]{1,0:T(8,128)(2,1)S(1)}, u32[]{:S(2)}, u32[]{:S(2)}) collective-permute-start(bf16[8,3072]{1,0:T(8,128)(2,1)S(1)} %bitcast.126), channel_id=1, source_target_pairs={{0,1},{1,0},{2,3},{3,2},{4,5},{5,4},{6,7},{7,6},{8,9},{9,8},{10,11... | collective-permute-start | bytes 147464 | tf_op jit(solution)/shard_map/ppermute | solution.py:360
  56.7 16.1 %all-to-all-start = ((bf16[8,2,1536]{2,1,0:T(2,128)(2,1)}), bf16[8,2,1536]{2,1,0:T(2,128)(2,1)S(1)}, u32[]{:S(2)}, u32[]{:S(2)}) async-start(bf16[8,2,1536]{2,1,0:T(2,128)(2,1)} %reshape.78), calls=%async_computation | async-start | bytes 98304 | tf_op jit(solution)/shard_map/all_to_all | solution.py:324
  74.8 14.0 %all-to-all-start.1 = ((bf16[16,8,3072]{2,1,0:T(8,128)(2,1)}), bf16[16,8,3072]{2,1,0:T(8,128)(2,1)S(1)}, u32[]{:S(2)}, u32[]{:S(2)}) async-start(bf16[16,8,3072]{2,1,0:T(8,128)(2,1)} %bitcast.7), calls=%async_computation.1 | async-start | bytes 1572864 | tf_op jit(solution)/shard_map/all_to_all | solution.py:324
  91.4 3.9 %collective-permute-start.1 = (bf16[192,128]{1,0:T(8,128)(2,1)S(1)}, bf16[192,128]{1,0:T(8,128)(2,1)S(1)}, u32[]{:S(2)}, u32[]{:S(2)}) collective-permute-start(bf16[192,128]{1,0:T(8,128)(2,1)S(1)} %get-tuple-element.53), channel_id=1, source_target_pairs={{0,16},{16,0},{32,48},{48,32},{1,17},{17,1},{33,49},{49,33},{2,18}... | collective-permute-start | bytes 147464 | tf_op jit(solution)/shard_map/ppermute | solution.py:401
  96.6 3.9 %collective-permute-start.2 = (f32[128,128]{1,0:T(8,128)S(1)}, f32[128,128]{1,0:T(8,128)S(1)}, u32[]{:S(2)}, u32[]{:S(2)}) collective-permute-start(f32[128,128]{1,0:T(8,128)S(1)} %get-tuple-element.58), channel_id=1, source_target_pairs={{0,16},{16,0},{32,48},{48,32},{1,17},{17,1},{33,49},{49,33},{2,18}... | collective-permute-start | bytes 196616 | tf_op jit(solution)/shard_map/ppermute | solution.py:401
  118.2 17.4 %all-to-all-start.4 = ((bf16[16,8,3072]{2,1,0:T(8,128)(2,1)}), bf16[16,8,3072]{2,1,0:T(8,128)(2,1)S(1)}, u32[]{:S(2)}, u32[]{:S(2)}) async-start(bf16[16,8,3072]{2,1,0:T(8,128)(2,1)} %bitcast.19), calls=%async_computation.4 | async-start | bytes 1572864 | tf_op jit(solution)/shard_map/all_to_all | solution.py:324
  138.0 4.1 %collective-permute-start.3 = (bf16[192,128]{1,0:T(8,128)(2,1)S(1)}, bf16[192,128]{1,0:T(8,128)(2,1)S(1)}, u32[]{:S(2)}, u32[]{:S(2)}) collective-permute-start(bf16[192,128]{1,0:T(8,128)(2,1)S(1)} %get-tuple-element.65), channel_id=1, source_target_pairs={{0,16},{16,0},{32,48},{48,32},{1,17},{17,1},{33,49},{49,33},{2,18}... | collective-permute-start | bytes 147464 | tf_op jit(solution)/shard_map/ppermute | solution.py:401
  143.4 3.2 %collective-permute-start.4 = (f32[128,128]{1,0:T(8,128)S(1)}, f32[128,128]{1,0:T(8,128)S(1)}, u32[]{:S(2)}, u32[]{:S(2)}) collective-permute-start(f32[128,128]{1,0:T(8,128)S(1)} %get-tuple-element.70), channel_id=1, source_target_pairs={{0,16},{16,0},{32,48},{48,32},{1,17},{17,1},{33,49},{49,33},{2,18}... | collective-permute-start | bytes 196616 | tf_op jit(solution)/shard_map/ppermute | solution.py:401
  166.3 15.9 %all-to-all-start.6 = ((bf16[16,8,3072]{2,1,0:T(8,128)(2,1)}), bf16[16,8,3072]{2,1,0:T(8,128)(2,1)S(1)}, u32[]{:S(2)}, u32[]{:S(2)}) async-start(bf16[16,8,3072]{2,1,0:T(8,128)(2,1)} %bitcast.27), calls=%async_computation.6 | async-start | bytes 1572864 | tf_op jit(solution)/shard_map/all_to_all | solution.py:324
  184.6 3.9 %collective-permute-start.5 = (bf16[192,128]{1,0:T(8,128)(2,1)S(1)}, bf16[192,128]{1,0:T(8,128)(2,1)S(1)}, u32[]{:S(2)}, u32[]{:S(2)}) collective-permute-start(bf16[192,128]{1,0:T(8,128)(2,1)S(1)} %get-tuple-element.77), channel_id=1, source_target_pairs={{0,16},{16,0},{32,48},{48,32},{1,17},{17,1},{33,49},{49,33},{2,18}... | collective-permute-start | bytes 147464 | tf_op jit(solution)/shard_map/ppermute | solution.py:401
  189.8 3.2 %collective-permute-start.6 = (f32[128,128]{1,0:T(8,128)S(1)}, f32[128,128]{1,0:T(8,128)S(1)}, u32[]{:S(2)}, u32[]{:S(2)}) collective-permute-start(f32[128,128]{1,0:T(8,128)S(1)} %get-tuple-element.82), channel_id=1, source_target_pairs={{0,16},{16,0},{32,48},{48,32},{1,17},{17,1},{33,49},{49,33},{2,18}... | collective-permute-start | bytes 196616 | tf_op jit(solution)/shard_map/ppermute | solution.py:401
  212.8 15.9 %all-to-all-start.8 = ((bf16[16,8,3072]{2,1,0:T(8,128)(2,1)}), bf16[16,8,3072]{2,1,0:T(8,128)(2,1)S(1)}, u32[]{:S(2)}, u32[]{:S(2)}) async-start(bf16[16,8,3072]{2,1,0:T(8,128)(2,1)} %bitcast.35), calls=%async_computation.8 | async-start | bytes 1572864 | tf_op jit(solution)/shard_map/all_to_all | solution.py:324
  231.0 3.9 %collective-permute-start.7 = (bf16[192,128]{1,0:T(8,128)(2,1)S(1)}, bf16[192,128]{1,0:T(8,128)(2,1)S(1)}, u32[]{:S(2)}, u32[]{:S(2)}) collective-permute-start(bf16[192,128]{1,0:T(8,128)(2,1)S(1)} %get-tuple-element.89), channel_id=1, source_target_pairs={{0,16},{16,0},{32,48},{48,32},{1,17},{17,1},{33,49},{49,33},{2,18}... | collective-permute-start | bytes 147464 | tf_op jit(solution)/shard_map/ppermute | solution.py:401
  236.2 3.7 %collective-permute-start.8 = (f32[128,128]{1,0:T(8,128)S(1)}, f32[128,128]{1,0:T(8,128)S(1)}, u32[]{:S(2)}, u32[]{:S(2)}) collective-permute-start(f32[128,128]{1,0:T(8,128)S(1)} %get-tuple-element.94), channel_id=1, source_target_pairs={{0,16},{16,0},{32,48},{48,32},{1,17},{17,1},{33,49},{49,33},{2,18}... | collective-permute-start | bytes 196616 | tf_op jit(solution)/shard_map/ppermute | solution.py:401
  241.4 19.0 %all-to-all-start.9 = ((bf16[16,8,3072]{2,1,0:T(8,128)(2,1)}), bf16[16,8,3072]{2,1,0:T(8,128)(2,1)S(1)}, u32[]{:S(2)}, u32[]{:S(2)}) async-start(bf16[16,8,3072]{2,1,0:T(8,128)(2,1)} %bitcast.37), calls=%async_computation.9 | async-start | bytes 1572864 | tf_op jit(solution)/shard_map/all_to_all | solution.py:324
  261.0 4.8 %collective-permute-start.9 = (bf16[8,3072]{1,0:T(8,128)(2,1)S(1)}, bf16[8,3072]{1,0:T(8,128)(2,1)S(1)}, u32[]{:S(2)}, u32[]{:S(2)}) collective-permute-start(bf16[8,3072]{1,0:T(8,128)(2,1)S(1)} %get-tuple-element.108), channel_id=1, source_target_pairs={{0,64},{64,128},{128,192},{192,0},{1,65},{65,129},{129,193},{193,1... | collective-permute-start | bytes 147464 | tf_op jit(solution)/shard_map/ppermute | solution.py:452
  261.1 4.7 %collective-permute-start.10 = (bf16[8,3072]{1,0:T(8,128)(2,1)S(1)}, bf16[8,3072]{1,0:T(8,128)(2,1)S(1)}, u32[]{:S(2)}, u32[]{:S(2)}) collective-permute-start(bf16[8,3072]{1,0:T(8,128)(2,1)S(1)} %get-tuple-element.107), channel_id=1, source_target_pairs={{0,128},{64,192},{128,0},{192,64},{1,129},{65,193},{129,1},{193,65... | collective-permute-start | bytes 147464 | tf_op jit(solution)/shard_map/ppermute | solution.py:452
  263.3 3.1 %collective-permute-start.11 = (bf16[8,3072]{1,0:T(8,128)(2,1)S(1)}, bf16[8,3072]{1,0:T(8,128)(2,1)S(1)}, u32[]{:S(2)}, u32[]{:S(2)}) collective-permute-start(bf16[8,3072]{1,0:T(8,128)(2,1)S(1)} %get-tuple-element.106), channel_id=1, source_target_pairs={{0,192},{64,0},{128,64},{192,128},{1,193},{65,1},{129,65},{193,129... | collective-permute-start | bytes 147464 | tf_op jit(solution)/shard_map/ppermute | solution.py:452
Sparse Core Ops, SparseCore 0:
  40.3 48.6 all-gather.4
  90.8 44.7 all-gather.6
  137.4 44.7 all-gather.8
  183.9 44.7 all-gather.10

commit v11 on v10

--- a/solution.py
+++ b/solution.py
@@ -351,7 +351,18 @@
         lax.all_gather(received[block], REST_AXES, axis=0, tiled=True) for block in range(BLOCKS)
     ]
 
-    terms = to_own_order(lax.all_gather(modulation[0], "x", axis=0, tiled=False))
+    given = to_own_order(modulation[0])
+    known = jnp.stack(
+        [given]
+        + [
+            lax.ppermute(given, "x", [(at, (at + step) % NX) for at in range(NX)])
+            for step in range(1, NX)
+        ]
+    )
+    terms = [
+        lax.dynamic_index_in_dim(known, (x_at - block) % NX, 0, keepdims=False)
+        for block in range(BLOCKS)
+    ]
     wanted = latent.reshape(NZ, NC, 2, D)
     wanted = lax.dynamic_index_in_dim(wanted, x_at // 2, 2, keepdims=False)
     core_at = lax.axis_index("c")
@@ -362,7 +373,7 @@
     current = to_own_order(mine)
 
     def term(block, which):
-        return terms[block, which][None]
+        return terms[block][which][None]
 
     spread = jax.ShapeDtypeStruct((LOCAL, D), jnp.bfloat16)
     owned = jax.ShapeDtypeStruct((OWN, D), jnp.bfloat16)

time: 294 us -> 294 us (level)
  blocking collectives: 108 us -> 101 us
  starting transfers between devices: 42.4 us -> 46.6 us
  waiting for transfers between devices: 72.8 us -> 75.9 us
    all_gather x1 -> x0, blocking collectives: 9.24 us -> none  [body(): lax.all_gather(modulation[0], 'x', axis=0, tiled=False)]
    all_gather x4, waiting for transfers between devices: 38 us -> 41.1 us  [body(): lax.all_gather(received[block], REST_AXES, axis=0, tiled=True)]
    ppermute x0 -> x3, starting transfers between devices: none -> 3.04 us  [body(): lax.ppermute(given, 'x', [(at, (at + step) % NX) for at in range(NX)])]
  transfers between devices with their start and end apart: 22 -> 25, of which waited for: 12 -> 13; matrix products, arithmetic and copies ran while one was open for 2% -> 2% of each run, Pallas kernels for 13% -> 13%
where the time goes in v11:
time: 294 us; the launch traced here: 293 us
  blocking collectives  101 us (34%)
  waiting for transfers between devices  75.9 us (26%)
  Pallas kernels  47.6 us (16%)
  starting transfers between devices  46.6 us (16%)
  between operations  13.7 us (5%)
  local copies, waits for them, and re-layouts  6.22 us (2%)
    all_to_all x5, blocking collectives, exchange(): return lax.all_to_all(array, axes, split_axis=0, concat_axis=0, tiled=True)  101 us
    all_gather x4, waiting for transfers between devices, body(): lax.all_gather(received[block], REST_AXES, axis=0, tiled=True)  41.1 us
    all_to_all x6, starting transfers between devices, exchange(): return lax.all_to_all(array, axes, split_axis=0, concat_axis=0, tiled=True)  30.4 us
    all_to_all x6, waiting for transfers between devices, exchange(): return lax.all_to_all(array, axes, split_axis=0, concat_axis=0, tiled=True)  29.5 us
    pallas_call x4, Pallas kernels, body(): local(own_attend_kernel, (SMEM, VMEM, VMEM, ANY), (VMEM, VMEM, VMEM), (ro...  10.6 us
    pallas_call x4, Pallas kernels, body(): local(own_project_kernel, (VMEM, ANY), (VMEM, VMEM, VMEM), (rows_of(3 * L...  10.4 us
    pallas_call x4, Pallas kernels, body(): local(shared_project_kernel, (SMEM, VMEM, ANY), (VMEM, VMEM), (rows_of(LO...  9.58 us
    ppermute x8, starting transfers between devices, swap(): return lax.ppermute(array, 'y', [(at, at ^ 1) for at in range(NY)])  6.98 us
  transfers between devices with their start and end apart: 25, of which 13 were waited for; matrix products, arithmetic and copies ran while one was open for 2% of the time, Pallas kernels for 13%

profile of v11, /device:TPU:1, one launch (start us, length us, event | category | flops | bytes accessed | tf_op | source)
XLA Modules:
  0.0 292.5 jit_solution(11052235920729340932)
XLA Ops:
  6.5 3.4 %pack.1 = bf16[16,384,128]{2,1,0:T(8,128)(2,1)} custom-call(bf16[48,9216]{1,0:T(8,128)(2,1)} %bitcast.113, bf16[48,3072]{1,0:T(8,128)(2,1)} %bitcast.124, bf16[32,2,3072]{2,1,0:T(2,128)(2,1)} %bitcast.123), custom_call_target="tpu_custom_call" | custom-call | tf_op jit(solution)/shard_map/pack/pallas_call | solution.py:332
  9.9 29.1 %all_to_all.111 = bf16[16,384,128]{2,1,0:T(8,128)(2,1)S(1)} all-to-all(bf16[16,384,128]{2,1,0:T(8,128)(2,1)} %pack.1), channel_id=1, replica_groups=mesh['x'=4,'y'=4,'z'=8,'c'=2] {'x','y'}, dimensions={0} | all-to-all | bytes 3145728 | tf_op jit(solution)/shard_map/all_to_all | solution.py:324
  39.0 1.2 fusion.1
  40.3 0.7 all-gather.7.cloned.1.call-update
  41.0 0.7 all-gather.9.cloned.1.call-update
  41.7 0.5 all-gather.11.cloned.1.call-update
  42.8 2.2 collective-permute-start.2
  45.0 0.7 collective-permute-start.3
  46.1 3.0 %collective-permute-start = (bf16[8,3072]{1,0:T(8,128)(2,1)S(1)}, bf16[8,3072]{1,0:T(8,128)(2,1)S(1)}, u32[]{:S(2)}, u32[]{:S(2)}) collective-permute-start(bf16[8,3072]{1,0:T(8,128)(2,1)S(1)} %bitcast.131), channel_id=1, source_target_pairs={{0,1},{1,0},{2,3},{3,2},{4,5},{5,4},{6,7},{7,6},{8,9},{9,8},{10,11... | collective-permute-start | bytes 147464 | tf_op jit(solution)/shard_map/ppermute | solution.py:371
  49.4 0.6 collective-permute-done
  50.0 0.5 broadcast.12
  50.5 0.7 reduce.2
  51.2 0.6 reshape.87
  51.8 8.2 %all-to-all-start = ((bf16[8,2,1536]{2,1,0:T(2,128)(2,1)}), bf16[8,2,1536]{2,1,0:T(2,128)(2,1)S(1)}, u32[]{:S(2)}, u32[]{:S(2)}) async-start(bf16[8,2,1536]{2,1,0:T(2,128)(2,1)} %reshape.87), calls=%async_computation | async-start | bytes 98304 | tf_op jit(solution)/shard_map/all_to_all | solution.py:324
  60.1 7.4 %all-to-all-done = bf16[8,2,1536]{2,1,0:T(2,128)(2,1)S(1)} async-done(((bf16[8,2,1536]{2,1,0:T(2,128)(2,1)}), bf16[8,2,1536]{2,1,0:T(2,128)(2,1)S(1)}, u32[]{:S(2)}, u32[]{:S(2)}) %all-to-all-start) | async-done | bytes 49184 | tf_op jit(solution)/shard_map/all_to_all | solution.py:324
  68.3 1.2 first.1
  69.5 4.3 %all-to-all-start.1 = ((bf16[16,8,3072]{2,1,0:T(8,128)(2,1)}), bf16[16,8,3072]{2,1,0:T(8,128)(2,1)S(1)}, u32[]{:S(2)}, u32[]{:S(2)}) async-start(bf16[16,8,3072]{2,1,0:T(8,128)(2,1)} %bitcast.10), calls=%async_computation.1 | async-start | bytes 1572864 | tf_op jit(solution)/shard_map/all_to_all | solution.py:324
  73.9 10.4 %all-to-all-done.1 = bf16[16,8,3072]{2,1,0:T(8,128)(2,1)S(1)} async-done(((bf16[16,8,3072]{2,1,0:T(8,128)(2,1)}), bf16[16,8,3072]{2,1,0:T(8,128)(2,1)S(1)}, u32[]{:S(2)}, u32[]{:S(2)}) %all-to-all-start.1) | async-done | bytes 786464 | tf_op jit(solution)/shard_map/all_to_all | solution.py:324
  84.3 4.7 %all-gather.5.cloned.1.call-done.pieces_ref = bf16[64,384,128]{2,1,0:T(8,128)(2,1)} async-done(((bf16[4,384,128]{2,1,0:T(8,128)(2,1)}), bf16[64,384,128]{2,1,0:T(8,128)(2,1)}) %all-gather.5.cloned.1.call-update) | async-done | bytes 6291472 | tf_op jit(solution)/shard_map/all_gather | solution.py:351
  89.0 2.4 shared_project_kernel.4
  91.4 1.3 collective-permute-start.4
  92.7 2.6 own_project_kernel.4
  95.3 1.3 shared_attend_kernel.4
  97.0 2.7 own_attend_kernel.4
  99.8 0.6 finish_kernel.4
  100.4 17.9 %all_to_all.112 = bf16[16,8,3072]{2,1,0:T(8,128)(2,1)S(1)} all-to-all(bf16[16,8,3072]{2,1,0:T(8,128)(2,1)S(1)} %bitcast.106), channel_id=1, replica_groups=mesh['x'=4,'y'=4,'z'=8,'c'=2] {'x','y'}, dimensions={0} | all-to-all | bytes 1572864 | tf_op jit(solution)/shard_map/all_to_all | solution.py:324
  118.3 1.3 middle.3
  119.6 3.8 %all-to-all-start.4 = ((bf16[16,8,3072]{2,1,0:T(8,128)(2,1)}), bf16[16,8,3072]{2,1,0:T(8,128)(2,1)S(1)}, u32[]{:S(2)}, u32[]{:S(2)}) async-start(bf16[16,8,3072]{2,1,0:T(8,128)(2,1)} %bitcast.22), calls=%async_computation.4 | async-start | bytes 1572864 | tf_op jit(solution)/shard_map/all_to_all | solution.py:324
  123.5 12.1 %all-gather.7.cloned.1.call-done.pieces_ref = bf16[64,384,128]{2,1,0:T(8,128)(2,1)} async-done(((bf16[4,384,128]{2,1,0:T(8,128)(2,1)}), bf16[64,384,128]{2,1,0:T(8,128)(2,1)}) %all-gather.7.cloned.1.call-update) | async-done | bytes 6291472 | tf_op jit(solution)/shard_map/all_gather | solution.py:351
  135.6 2.4 shared_project_kernel.5
  138.0 1.3 collective-permute-start.6
  139.3 2.6 own_project_kernel.5
  141.9 1.3 shared_attend_kernel.5
  143.6 2.7 own_attend_kernel.5
  146.4 0.6 finish_kernel.5
  147.0 17.8 %all_to_all.113 = bf16[16,8,3072]{2,1,0:T(8,128)(2,1)S(1)} all-to-all(bf16[16,8,3072]{2,1,0:T(8,128)(2,1)S(1)} %bitcast.107), channel_id=1, replica_groups=mesh['x'=4,'y'=4,'z'=8,'c'=2] {'x','y'}, dimensions={0} | all-to-all | bytes 1572864 | tf_op jit(solution)/shard_map/all_to_all | solution.py:324
  164.8 1.3 middle.4
  166.1 3.8 %all-to-all-start.6 = ((bf16[16,8,3072]{2,1,0:T(8,128)(2,1)}), bf16[16,8,3072]{2,1,0:T(8,128)(2,1)S(1)}, u32[]{:S(2)}, u32[]{:S(2)}) async-start(bf16[16,8,3072]{2,1,0:T(8,128)(2,1)} %bitcast.30), calls=%async_computation.6 | async-start | bytes 1572864 | tf_op jit(solution)/shard_map/all_to_all | solution.py:324
  169.9 12.2 %all-gather.9.cloned.1.call-done.pieces_ref = bf16[64,384,128]{2,1,0:T(8,128)(2,1)} async-done(((bf16[4,384,128]{2,1,0:T(8,128)(2,1)}), bf16[64,384,128]{2,1,0:T(8,128)(2,1)}) %all-gather.9.cloned.1.call-update) | async-done | bytes 6291472 | tf_op jit(solution)/shard_map/all_gather | solution.py:351
  182.1 2.4 shared_project_kernel.6
  184.5 1.3 collective-permute-start.8
  185.8 2.6 own_project_kernel.6
  188.4 1.3 shared_attend_kernel.6
  190.1 2.7 own_attend_kernel.6
  192.9 0.6 finish_kernel.6
  193.5 17.8 %all_to_all.114 = bf16[16,8,3072]{2,1,0:T(8,128)(2,1)S(1)} all-to-all(bf16[16,8,3072]{2,1,0:T(8,128)(2,1)S(1)} %bitcast.108), channel_id=1, replica_groups=mesh['x'=4,'y'=4,'z'=8,'c'=2] {'x','y'}, dimensions={0} | all-to-all | bytes 1572864 | tf_op jit(solution)/shard_map/all_to_all | solution.py:324
  211.4 1.3 middle.5
  212.7 3.8 %all-to-all-start.8 = ((bf16[16,8,3072]{2,1,0:T(8,128)(2,1)}), bf16[16,8,3072]{2,1,0:T(8,128)(2,1)S(1)}, u32[]{:S(2)}, u32[]{:S(2)}) async-start(bf16[16,8,3072]{2,1,0:T(8,128)(2,1)} %bitcast.38), calls=%async_computation.8 | async-start | bytes 1572864 | tf_op jit(solution)/shard_map/all_to_all | solution.py:324
  216.5 12.1 %all-gather.11.cloned.1.call-done.pieces_ref = bf16[64,384,128]{2,1,0:T(8,128)(2,1)} async-done(((bf16[4,384,128]{2,1,0:T(8,128)(2,1)}), bf16[64,384,128]{2,1,0:T(8,128)(2,1)}) %all-gather.11.cloned.1.call-update) | async-done | bytes 6291472 | tf_op jit(solution)/shard_map/all_gather | solution.py:351
  228.6 2.4 shared_project_kernel.7
  231.0 1.3 collective-permute-start.10
  232.2 2.6 own_project_kernel.7
  234.9 1.3 shared_attend_kernel.7
  236.1 0.6 collective-permute-start.11
  237.1 2.7 own_attend_kernel.7
  239.8 1.5 finish_kernel.7
  241.4 6.5 %all-to-all-start.9 = ((bf16[16,8,3072]{2,1,0:T(8,128)(2,1)}), bf16[16,8,3072]{2,1,0:T(8,128)(2,1)S(1)}, u32[]{:S(2)}, u32[]{:S(2)}) async-start(bf16[16,8,3072]{2,1,0:T(8,128)(2,1)} %bitcast.40), calls=%async_computation.9 | async-start | bytes 1572864 | tf_op jit(solution)/shard_map/all_to_all | solution.py:324
  248.7 11.7 %all-to-all-done.9 = bf16[16,8,3072]{2,1,0:T(8,128)(2,1)S(1)} async-done(((bf16[16,8,3072]{2,1,0:T(8,128)(2,1)}), bf16[16,8,3072]{2,1,0:T(8,128)(2,1)S(1)}, u32[]{:S(2)}, u32[]{:S(2)}) %all-to-all-start.9) | async-done | bytes 786464 | tf_op jit(solution)/shard_map/all_to_all | solution.py:324
  261.0 2.2 collective-permute-start.13
  263.2 0.8 collective-permute-start.14
  264.0 1.7 collective-permute-done.12
  265.7 0.6 collective-permute-done.14
  266.6 18.7 %all_to_all.115 = bf16[16,2,3072]{2,1,0:T(2,128)(2,1)S(1)} all-to-all(bf16[16,2,3072]{2,1,0:T(2,128)(2,1)S(1)} %bitcast.117), channel_id=1, replica_groups=mesh['x'=4,'y'=4,'z'=8,'c'=2] {'z','c'}, dimensions={0} | all-to-all | bytes 393216 | tf_op jit(solution)/shard_map/all_to_all | solution.py:324
  285.3 0.8 broadcast_in_dim.3
  (68 shorter events, 5.8 us)
Async XLA Ops:
  6.5 35.7 %copy-start.1 = (f32[1,3,3072]{2,0,1:T(1,128)S(1)}, f32[1,3,3072]{2,0,1:T(1,128)}, u32[]{:S(2)}) copy-start(f32[1,3,3072]{2,0,1:T(1,128)} %param.6) | copy-start | bytes 110596
  6.5 39.2 %copy-start = (bf16[32,1,3072]{2,0,1:T(8,128)(2,1)S(1)}, bf16[32,1,3072]{2,0,1:T(8,128)(2,1)}, u32[]{:S(2)}) copy-start(bf16[32,1,3072]{2,0,1:T(8,128)(2,1)} %param.5) | copy-start | bytes 589828
  6.5 82.5 %all-gather.5.cloned.1.call-start = ((), (), s32[]{:S(2)}) async-start(), calls=%async_computation.11 | async-start | bytes 6684672 | tf_op jit(solution)/shard_map/all_gather | solution.py:351
  40.2 95.4 %all-gather.7.cloned.1.call-start = ((), (), s32[]{:S(2)}) async-start(), calls=%async_computation.12 | async-start | bytes 6684672 | tf_op jit(solution)/shard_map/all_gather | solution.py:351
  41.0 141.2 %all-gather.9.cloned.1.call-start = ((), (), s32[]{:S(2)}) async-start(), calls=%async_computation.13 | async-start | bytes 6684672 | tf_op jit(solution)/shard_map/all_gather | solution.py:351
  41.7 186.9 %all-gather.11.cloned.1.call-start = ((), (), s32[]{:S(2)}) async-start(), calls=%async_computation.14 | async-start | bytes 6684672 | tf_op jit(solution)/shard_map/all_gather | solution.py:351
  42.7 6.6 %collective-permute-start.1 = (f32[3,3072]{1,0:T(4,128)S(1)}, f32[3,3072]{1,0:T(4,128)S(1)}, u32[]{:S(2)}, u32[]{:S(2)}) collective-permute-start(f32[3,3072]{1,0:T(4,128)S(1)} %reshape.79), channel_id=1, source_target_pairs={{0,64},{64,128},{128,192},{192,0},{1,65},{65,129},{129,193},{193,1... | collective-permute-start | bytes 110600 | tf_op jit(solution)/shard_map/ppermute | solution.py:358
  42.8 6.5 %collective-permute-start.2 = (f32[3,3072]{1,0:T(4,128)S(1)}, f32[3,3072]{1,0:T(4,128)S(1)}, u32[]{:S(2)}, u32[]{:S(2)}) collective-permute-start(f32[3,3072]{1,0:T(4,128)S(1)} %reshape.79), channel_id=1, source_target_pairs={{0,128},{64,192},{128,0},{192,64},{1,129},{65,193},{129,1},{193,65... | collective-permute-start | bytes 110600 | tf_op jit(solution)/shard_map/ppermute | solution.py:358
  45.0 4.3 %collective-permute-start.3 = (f32[3,3072]{1,0:T(4,128)S(1)}, f32[3,3072]{1,0:T(4,128)S(1)}, u32[]{:S(2)}, u32[]{:S(2)}) collective-permute-start(f32[3,3072]{1,0:T(4,128)S(1)} %reshape.79), channel_id=1, source_target_pairs={{0,192},{64,0},{128,64},{192,128},{1,193},{65,1},{129,65},{193,129... | collective-permute-start | bytes 110600 | tf_op jit(solution)/shard_map/ppermute | solution.py:358
  46.1 3.9 %collective-permute-start = (bf16[8,3072]{1,0:T(8,128)(2,1)S(1)}, bf16[8,3072]{1,0:T(8,128)(2,1)S(1)}, u32[]{:S(2)}, u32[]{:S(2)}) collective-permute-start(bf16[8,3072]{1,0:T(8,128)(2,1)S(1)} %bitcast.131), channel_id=1, source_target_pairs={{0,1},{1,0},{2,3},{3,2},{4,5},{5,4},{6,7},{7,6},{8,9},{9,8},{10,11... | collective-permute-start | bytes 147464 | tf_op jit(solution)/shard_map/ppermute | solution.py:371
  51.8 15.8 %all-to-all-start = ((bf16[8,2,1536]{2,1,0:T(2,128)(2,1)}), bf16[8,2,1536]{2,1,0:T(2,128)(2,1)S(1)}, u32[]{:S(2)}, u32[]{:S(2)}) async-start(bf16[8,2,1536]{2,1,0:T(2,128)(2,1)} %reshape.87), calls=%async_computation | async-start | bytes 98304 | tf_op jit(solution)/shard_map/all_to_all | solution.py:324
  69.5 14.8 %all-to-all-start.1 = ((bf16[16,8,3072]{2,1,0:T(8,128)(2,1)}), bf16[16,8,3072]{2,1,0:T(8,128)(2,1)S(1)}, u32[]{:S(2)}, u32[]{:S(2)}) async-start(bf16[16,8,3072]{2,1,0:T(8,128)(2,1)} %bitcast.10), calls=%async_computation.1 | async-start | bytes 1572864 | tf_op jit(solution)/shard_map/all_to_all | solution.py:324
  91.4 3.9 %collective-permute-start.4 = (bf16[192,128]{1,0:T(8,128)(2,1)S(1)}, bf16[192,128]{1,0:T(8,128)(2,1)S(1)}, u32[]{:S(2)}, u32[]{:S(2)}) collective-permute-start(bf16[192,128]{1,0:T(8,128)(2,1)S(1)} %get-tuple-element.53), channel_id=1, source_target_pairs={{0,16},{16,0},{32,48},{48,32},{1,17},{17,1},{33,49},{49,33},{2,18}... | collective-permute-start | bytes 147464 | tf_op jit(solution)/shard_map/ppermute | solution.py:412
  96.6 3.2 %collective-permute-start.5 = (f32[128,128]{1,0:T(8,128)S(1)}, f32[128,128]{1,0:T(8,128)S(1)}, u32[]{:S(2)}, u32[]{:S(2)}) collective-permute-start(f32[128,128]{1,0:T(8,128)S(1)} %get-tuple-element.58), channel_id=1, source_target_pairs={{0,16},{16,0},{32,48},{48,32},{1,17},{17,1},{33,49},{49,33},{2,18}... | collective-permute-start | bytes 196616 | tf_op jit(solution)/shard_map/ppermute | solution.py:412
  119.6 16.0 %all-to-all-start.4 = ((bf16[16,8,3072]{2,1,0:T(8,128)(2,1)}), bf16[16,8,3072]{2,1,0:T(8,128)(2,1)S(1)}, u32[]{:S(2)}, u32[]{:S(2)}) async-start(bf16[16,8,3072]{2,1,0:T(8,128)(2,1)} %bitcast.22), calls=%async_computation.4 | async-start | bytes 1572864 | tf_op jit(solution)/shard_map/all_to_all | solution.py:324
  138.0 3.9 %collective-permute-start.6 = (bf16[192,128]{1,0:T(8,128)(2,1)S(1)}, bf16[192,128]{1,0:T(8,128)(2,1)S(1)}, u32[]{:S(2)}, u32[]{:S(2)}) collective-permute-start(bf16[192,128]{1,0:T(8,128)(2,1)S(1)} %get-tuple-element.65), channel_id=1, source_target_pairs={{0,16},{16,0},{32,48},{48,32},{1,17},{17,1},{33,49},{49,33},{2,18}... | collective-permute-start | bytes 147464 | tf_op jit(solution)/shard_map/ppermute | solution.py:412
  143.2 3.2 %collective-permute-start.7 = (f32[128,128]{1,0:T(8,128)S(1)}, f32[128,128]{1,0:T(8,128)S(1)}, u32[]{:S(2)}, u32[]{:S(2)}) collective-permute-start(f32[128,128]{1,0:T(8,128)S(1)} %get-tuple-element.70), channel_id=1, source_target_pairs={{0,16},{16,0},{32,48},{48,32},{1,17},{17,1},{33,49},{49,33},{2,18}... | collective-permute-start | bytes 196616 | tf_op jit(solution)/shard_map/ppermute | solution.py:412
  166.1 16.0 %all-to-all-start.6 = ((bf16[16,8,3072]{2,1,0:T(8,128)(2,1)}), bf16[16,8,3072]{2,1,0:T(8,128)(2,1)S(1)}, u32[]{:S(2)}, u32[]{:S(2)}) async-start(bf16[16,8,3072]{2,1,0:T(8,128)(2,1)} %bitcast.30), calls=%async_computation.6 | async-start | bytes 1572864 | tf_op jit(solution)/shard_map/all_to_all | solution.py:324
  184.5 3.9 %collective-permute-start.8 = (bf16[192,128]{1,0:T(8,128)(2,1)S(1)}, bf16[192,128]{1,0:T(8,128)(2,1)S(1)}, u32[]{:S(2)}, u32[]{:S(2)}) collective-permute-start(bf16[192,128]{1,0:T(8,128)(2,1)S(1)} %get-tuple-element.77), channel_id=1, source_target_pairs={{0,16},{16,0},{32,48},{48,32},{1,17},{17,1},{33,49},{49,33},{2,18}... | collective-permute-start | bytes 147464 | tf_op jit(solution)/shard_map/ppermute | solution.py:412
  189.7 3.2 %collective-permute-start.9 = (f32[128,128]{1,0:T(8,128)S(1)}, f32[128,128]{1,0:T(8,128)S(1)}, u32[]{:S(2)}, u32[]{:S(2)}) collective-permute-start(f32[128,128]{1,0:T(8,128)S(1)} %get-tuple-element.82), channel_id=1, source_target_pairs={{0,16},{16,0},{32,48},{48,32},{1,17},{17,1},{33,49},{49,33},{2,18}... | collective-permute-start | bytes 196616 | tf_op jit(solution)/shard_map/ppermute | solution.py:412
  212.7 15.9 %all-to-all-start.8 = ((bf16[16,8,3072]{2,1,0:T(8,128)(2,1)}), bf16[16,8,3072]{2,1,0:T(8,128)(2,1)S(1)}, u32[]{:S(2)}, u32[]{:S(2)}) async-start(bf16[16,8,3072]{2,1,0:T(8,128)(2,1)} %bitcast.38), calls=%async_computation.8 | async-start | bytes 1572864 | tf_op jit(solution)/shard_map/all_to_all | solution.py:324
  231.0 3.9 %collective-permute-start.10 = (bf16[192,128]{1,0:T(8,128)(2,1)S(1)}, bf16[192,128]{1,0:T(8,128)(2,1)S(1)}, u32[]{:S(2)}, u32[]{:S(2)}) collective-permute-start(bf16[192,128]{1,0:T(8,128)(2,1)S(1)} %get-tuple-element.89), channel_id=1, source_target_pairs={{0,16},{16,0},{32,48},{48,32},{1,17},{17,1},{33,49},{49,33},{2,18}... | collective-permute-start | bytes 147464 | tf_op jit(solution)/shard_map/ppermute | solution.py:412
  236.1 3.7 %collective-permute-start.11 = (f32[128,128]{1,0:T(8,128)S(1)}, f32[128,128]{1,0:T(8,128)S(1)}, u32[]{:S(2)}, u32[]{:S(2)}) collective-permute-start(f32[128,128]{1,0:T(8,128)S(1)} %get-tuple-element.94), channel_id=1, source_target_pairs={{0,16},{16,0},{32,48},{48,32},{1,17},{17,1},{33,49},{49,33},{2,18}... | collective-permute-start | bytes 196616 | tf_op jit(solution)/shard_map/ppermute | solution.py:412
  241.4 19.0 %all-to-all-start.9 = ((bf16[16,8,3072]{2,1,0:T(8,128)(2,1)}), bf16[16,8,3072]{2,1,0:T(8,128)(2,1)S(1)}, u32[]{:S(2)}, u32[]{:S(2)}) async-start(bf16[16,8,3072]{2,1,0:T(8,128)(2,1)} %bitcast.40), calls=%async_computation.9 | async-start | bytes 1572864 | tf_op jit(solution)/shard_map/all_to_all | solution.py:324
  260.9 4.8 %collective-permute-start.12 = (bf16[8,3072]{1,0:T(8,128)(2,1)S(1)}, bf16[8,3072]{1,0:T(8,128)(2,1)S(1)}, u32[]{:S(2)}, u32[]{:S(2)}) collective-permute-start(bf16[8,3072]{1,0:T(8,128)(2,1)S(1)} %get-tuple-element.108), channel_id=1, source_target_pairs={{0,64},{64,128},{128,192},{192,0},{1,65},{65,129},{129,193},{193,1... | collective-permute-start | bytes 147464 | tf_op jit(solution)/shard_map/ppermute | solution.py:463
  261.0 4.7 %collective-permute-start.13 = (bf16[8,3072]{1,0:T(8,128)(2,1)S(1)}, bf16[8,3072]{1,0:T(8,128)(2,1)S(1)}, u32[]{:S(2)}, u32[]{:S(2)}) collective-permute-start(bf16[8,3072]{1,0:T(8,128)(2,1)S(1)} %get-tuple-element.107), channel_id=1, source_target_pairs={{0,128},{64,192},{128,0},{192,64},{1,129},{65,193},{129,1},{193,65... | collective-permute-start | bytes 147464 | tf_op jit(solution)/shard_map/ppermute | solution.py:463
  263.2 3.1 %collective-permute-start.14 = (bf16[8,3072]{1,0:T(8,128)(2,1)S(1)}, bf16[8,3072]{1,0:T(8,128)(2,1)S(1)}, u32[]{:S(2)}, u32[]{:S(2)}) collective-permute-start(bf16[8,3072]{1,0:T(8,128)(2,1)S(1)} %get-tuple-element.106), channel_id=1, source_target_pairs={{0,192},{64,0},{128,64},{192,128},{1,193},{65,1},{129,65},{193,129... | collective-permute-start | bytes 147464 | tf_op jit(solution)/shard_map/ppermute | solution.py:463
Sparse Core Ops, SparseCore 0:
  40.3 48.6 all-gather.4
  90.8 44.6 all-gather.6
  137.4 44.6 all-gather.8
  183.8 44.7 all-gather.10

commit v12 on v11

--- a/solution.py
+++ b/solution.py
@@ -101,6 +101,12 @@
         copy.wait()
 
 
+def later_kernel(received_ref, earlier_ref, *targets):
+    del earlier_ref
+    for block, target in enumerate(targets):
+        target[...] = received_ref[block + 1]
+
+
 def first_kernel(rows_ref, shift_ref, scale_ref, normed_ref):
     normed = modulate(rows_ref[...].astype(jnp.float32), shift_ref[...], scale_ref[...])
     twice = jnp.concatenate([normed, normed], axis=0)
@@ -347,9 +353,10 @@
     )(w_qkv[0], w_out[0].T, stale[0, :, 0])
     received = exchange(sent, HEAD_AXES).reshape(BLOCKS, NY, PIECE, HD)
 
-    pieces = [
-        lax.all_gather(received[block], REST_AXES, axis=0, tiled=True) for block in range(BLOCKS)
-    ]
+    def gather(own_piece):
+        return lax.all_gather(own_piece, REST_AXES, axis=0, tiled=True)
+
+    pieces = [gather(received[0])]
 
     given = to_own_order(modulation[0])
     known = jnp.stack(
@@ -385,6 +392,15 @@
         compiler_params=PARAMS,
         name="first",
     )(current, term(0, 0), term(0, 1))
+    later = pl.pallas_call(
+        later_kernel,
+        out_shape=[jax.ShapeDtypeStruct((NY, PIECE, HD), jnp.bfloat16)] * (BLOCKS - 1),
+        in_specs=[VMEM, VMEM],
+        out_specs=[VMEM] * (BLOCKS - 1),
+        compiler_params=SMALL,
+        name="later",
+    )(received, normed)
+    pieces += [gather(own_piece) for own_piece in later]
     weight = pltpu.VMEM((SOURCES, ROWS, HD), jnp.bfloat16)
     cache = pltpu.VMEM((SOURCES, PATCHES, HD), jnp.bfloat16)
     half_cache = jax.ShapeDtypeStruct((SOURCES, PATCHES // 2, HD), jnp.bfloat16)

time: 294 us -> 293 us (level)
  transfers between devices with their start and end apart: 25 -> 25, of which waited for: 13 -> 13; matrix products, arithmetic and copies ran while one was open for 2% -> 2% of each run, Pallas kernels for 13% -> 14%
where the time goes in v12:
time: 293 us; the launch traced here: 292 us
  blocking collectives  101 us (34%)
  waiting for transfers between devices  73.5 us (25%)
  Pallas kernels  49.9 us (17%)
  starting transfers between devices  46.6 us (16%)
  between operations  13.7 us (5%)
  local copies, waits for them, and re-layouts  5.83 us (2%)
    all_to_all x5, blocking collectives, exchange(): return lax.all_to_all(array, axes, split_axis=0, concat_axis=0, tiled=True)  101 us
    all_gather x4, waiting for transfers between devices, gather(): return lax.all_gather(own_piece, REST_AXES, axis=0, tiled=True)  39.5 us
    all_to_all x6, starting transfers between devices, exchange(): return lax.all_to_all(array, axes, split_axis=0, concat_axis=0, tiled=True)  30.4 us
    all_to_all x6, waiting for transfers between devices, exchange(): return lax.all_to_all(array, axes, split_axis=0, concat_axis=0, tiled=True)  29.5 us
    pallas_call x4, Pallas kernels, body(): local(own_attend_kernel, (SMEM, VMEM, VMEM, ANY), (VMEM, VMEM, VMEM), (ro...  10.6 us
    pallas_call x4, Pallas kernels, body(): local(own_project_kernel, (VMEM, ANY), (VMEM, VMEM, VMEM), (rows_of(3 * L...  10.4 us
    pallas_call x4, Pallas kernels, body(): local(shared_project_kernel, (SMEM, VMEM, ANY), (VMEM, VMEM), (rows_of(LO...  9.58 us
    ppermute x8, starting transfers between devices, swap(): return lax.ppermute(array, 'y', [(at, at ^ 1) for at in range(NY)])  7.01 us
  transfers between devices with their start and end apart: 25, of which 13 were waited for; matrix products, arithmetic and copies ran while one was open for 2% of the time, Pallas kernels for 14%

profile of v12, /device:TPU:1, one launch (start us, length us, event | category | flops | bytes accessed | tf_op | source)
XLA Modules:
  0.0 292.1 jit_solution(8416890853351332912)
XLA Ops:
  6.5 3.4 %pack.1 = bf16[16,384,128]{2,1,0:T(8,128)(2,1)} custom-call(bf16[48,9216]{1,0:T(8,128)(2,1)} %bitcast.115, bf16[48,3072]{1,0:T(8,128)(2,1)} %bitcast.126, bf16[32,2,3072]{2,1,0:T(2,128)(2,1)} %bitcast.125), custom_call_target="tpu_custom_call" | custom-call | tf_op jit(solution)/shard_map/pack/pallas_call | solution.py:338
  9.9 29.1 %all_to_all.111 = bf16[16,384,128]{2,1,0:T(8,128)(2,1)S(1)} all-to-all(bf16[16,384,128]{2,1,0:T(8,128)(2,1)} %pack.1), channel_id=1, replica_groups=mesh['x'=4,'y'=4,'z'=8,'c'=2] {'x','y'}, dimensions={0} | all-to-all | bytes 3145728 | tf_op jit(solution)/shard_map/all_to_all | solution.py:330
  39.0 0.8 slice.101
  40.3 2.2 collective-permute-start.2
  42.5 0.7 collective-permute-start.3
  43.6 3.0 %collective-permute-start = (bf16[8,3072]{1,0:T(8,128)(2,1)S(1)}, bf16[8,3072]{1,0:T(8,128)(2,1)S(1)}, u32[]{:S(2)}, u32[]{:S(2)}) collective-permute-start(bf16[8,3072]{1,0:T(8,128)(2,1)S(1)} %bitcast.133), channel_id=1, source_target_pairs={{0,1},{1,0},{2,3},{3,2},{4,5},{5,4},{6,7},{7,6},{8,9},{9,8},{10,11... | collective-permute-start | bytes 147464 | tf_op jit(solution)/shard_map/ppermute | solution.py:378
  46.9 0.6 collective-permute-done
  47.5 0.5 broadcast.12
  48.0 0.7 reduce.2
  48.7 0.6 reshape.84
  49.4 8.2 %all-to-all-start = ((bf16[8,2,1536]{2,1,0:T(2,128)(2,1)}), bf16[8,2,1536]{2,1,0:T(2,128)(2,1)S(1)}, u32[]{:S(2)}, u32[]{:S(2)}) async-start(bf16[8,2,1536]{2,1,0:T(2,128)(2,1)} %reshape.84), calls=%async_computation | async-start | bytes 98304 | tf_op jit(solution)/shard_map/all_to_all | solution.py:330
  57.7 7.4 %all-to-all-done = bf16[8,2,1536]{2,1,0:T(2,128)(2,1)S(1)} async-done(((bf16[8,2,1536]{2,1,0:T(2,128)(2,1)}), bf16[8,2,1536]{2,1,0:T(2,128)(2,1)S(1)}, u32[]{:S(2)}, u32[]{:S(2)}) %all-to-all-start) | async-done | bytes 49184 | tf_op jit(solution)/shard_map/all_to_all | solution.py:330
  65.9 1.2 first.1.earlier_ref
  67.0 2.3 later.1
  69.4 0.7 all-gather.9.cloned.1.call-update
  70.1 0.5 all-gather.11.cloned.1.call-update
  70.6 4.3 %all-to-all-start.1 = ((bf16[16,8,3072]{2,1,0:T(8,128)(2,1)}), bf16[16,8,3072]{2,1,0:T(8,128)(2,1)S(1)}, u32[]{:S(2)}, u32[]{:S(2)}) async-start(bf16[16,8,3072]{2,1,0:T(8,128)(2,1)} %bitcast.10), calls=%async_computation.1 | async-start | bytes 1572864 | tf_op jit(solution)/shard_map/all_to_all | solution.py:330
  75.0 10.4 %all-to-all-done.1 = bf16[16,8,3072]{2,1,0:T(8,128)(2,1)S(1)} async-done(((bf16[16,8,3072]{2,1,0:T(8,128)(2,1)}), bf16[16,8,3072]{2,1,0:T(8,128)(2,1)S(1)}, u32[]{:S(2)}, u32[]{:S(2)}) %all-to-all-start.1) | async-done | bytes 786464 | tf_op jit(solution)/shard_map/all_to_all | solution.py:330
  85.5 3.1 %all-gather.5.cloned.1.call-done.pieces_ref = bf16[64,384,128]{2,1,0:T(8,128)(2,1)} async-done(((bf16[4,384,128]{2,1,0:T(8,128)(2,1)}), bf16[64,384,128]{2,1,0:T(8,128)(2,1)}) %all-gather.5.cloned.1.call-update) | async-done | bytes 6291472 | tf_op jit(solution)/shard_map/all_gather | solution.py:357
  88.6 2.4 shared_project_kernel.4
  91.0 1.3 collective-permute-start.4
  92.3 2.6 own_project_kernel.4
  94.9 1.3 shared_attend_kernel.4
  96.6 2.7 own_attend_kernel.4
  99.4 0.6 finish_kernel.4
  100.0 17.8 %all_to_all.112 = bf16[16,8,3072]{2,1,0:T(8,128)(2,1)S(1)} all-to-all(bf16[16,8,3072]{2,1,0:T(8,128)(2,1)S(1)} %bitcast.108), channel_id=1, replica_groups=mesh['x'=4,'y'=4,'z'=8,'c'=2] {'x','y'}, dimensions={0} | all-to-all | bytes 1572864 | tf_op jit(solution)/shard_map/all_to_all | solution.py:330
  117.9 1.3 middle.3
  119.2 3.8 %all-to-all-start.4 = ((bf16[16,8,3072]{2,1,0:T(8,128)(2,1)}), bf16[16,8,3072]{2,1,0:T(8,128)(2,1)S(1)}, u32[]{:S(2)}, u32[]{:S(2)}) async-start(bf16[16,8,3072]{2,1,0:T(8,128)(2,1)} %bitcast.22), calls=%async_computation.4 | async-start | bytes 1572864 | tf_op jit(solution)/shard_map/all_to_all | solution.py:330
  123.0 12.1 %all-gather.7.cloned.1.call-done.pieces_ref = bf16[64,384,128]{2,1,0:T(8,128)(2,1)} async-done(((bf16[4,384,128]{2,1,0:T(8,128)(2,1)}), bf16[64,384,128]{2,1,0:T(8,128)(2,1)}) %all-gather.7.cloned.1.call-update) | async-done | bytes 6291472 | tf_op jit(solution)/shard_map/all_gather | solution.py:357
  135.1 2.4 shared_project_kernel.5
  137.5 1.3 collective-permute-start.6
  138.8 2.6 own_project_kernel.5
  141.5 1.3 shared_attend_kernel.5
  143.1 2.7 own_attend_kernel.5
  145.9 0.6 finish_kernel.5
  146.6 17.8 %all_to_all.113 = bf16[16,8,3072]{2,1,0:T(8,128)(2,1)S(1)} all-to-all(bf16[16,8,3072]{2,1,0:T(8,128)(2,1)S(1)} %bitcast.109), channel_id=1, replica_groups=mesh['x'=4,'y'=4,'z'=8,'c'=2] {'x','y'}, dimensions={0} | all-to-all | bytes 1572864 | tf_op jit(solution)/shard_map/all_to_all | solution.py:330
  164.4 1.3 middle.4
  165.7 3.8 %all-to-all-start.6 = ((bf16[16,8,3072]{2,1,0:T(8,128)(2,1)}), bf16[16,8,3072]{2,1,0:T(8,128)(2,1)S(1)}, u32[]{:S(2)}, u32[]{:S(2)}) async-start(bf16[16,8,3072]{2,1,0:T(8,128)(2,1)} %bitcast.31), calls=%async_computation.6 | async-start | bytes 1572864 | tf_op jit(solution)/shard_map/all_to_all | solution.py:330
  169.5 12.2 %all-gather.9.cloned.1.call-done.pieces_ref = bf16[64,384,128]{2,1,0:T(8,128)(2,1)} async-done(((bf16[4,384,128]{2,1,0:T(8,128)(2,1)}), bf16[64,384,128]{2,1,0:T(8,128)(2,1)}) %all-gather.9.cloned.1.call-update) | async-done | bytes 6291472 | tf_op jit(solution)/shard_map/all_gather | solution.py:357
  181.7 2.4 shared_project_kernel.6
  184.1 1.3 collective-permute-start.8
  185.4 2.6 own_project_kernel.6
  188.1 1.3 shared_attend_kernel.6
  189.7 2.7 own_attend_kernel.6
  192.5 0.6 finish_kernel.6
  193.1 17.8 %all_to_all.114 = bf16[16,8,3072]{2,1,0:T(8,128)(2,1)S(1)} all-to-all(bf16[16,8,3072]{2,1,0:T(8,128)(2,1)S(1)} %bitcast.110), channel_id=1, replica_groups=mesh['x'=4,'y'=4,'z'=8,'c'=2] {'x','y'}, dimensions={0} | all-to-all | bytes 1572864 | tf_op jit(solution)/shard_map/all_to_all | solution.py:330
  211.0 1.3 middle.5
  212.3 3.8 %all-to-all-start.8 = ((bf16[16,8,3072]{2,1,0:T(8,128)(2,1)}), bf16[16,8,3072]{2,1,0:T(8,128)(2,1)S(1)}, u32[]{:S(2)}, u32[]{:S(2)}) async-start(bf16[16,8,3072]{2,1,0:T(8,128)(2,1)} %bitcast.39), calls=%async_computation.8 | async-start | bytes 1572864 | tf_op jit(solution)/shard_map/all_to_all | solution.py:330
  216.1 12.0 %all-gather.11.cloned.1.call-done.pieces_ref = bf16[64,384,128]{2,1,0:T(8,128)(2,1)} async-done(((bf16[4,384,128]{2,1,0:T(8,128)(2,1)}), bf16[64,384,128]{2,1,0:T(8,128)(2,1)}) %all-gather.11.cloned.1.call-update) | async-done | bytes 6291472 | tf_op jit(solution)/shard_map/all_gather | solution.py:357
  228.1 2.4 shared_project_kernel.7
  230.5 1.3 collective-permute-start.10
  231.8 2.6 own_project_kernel.7
  234.4 1.3 shared_attend_kernel.7
  235.7 0.6 collective-permute-start.11
  236.7 2.7 own_attend_kernel.7
  239.4 1.5 finish_kernel.7
  240.9 6.5 %all-to-all-start.9 = ((bf16[16,8,3072]{2,1,0:T(8,128)(2,1)}), bf16[16,8,3072]{2,1,0:T(8,128)(2,1)S(1)}, u32[]{:S(2)}, u32[]{:S(2)}) async-start(bf16[16,8,3072]{2,1,0:T(8,128)(2,1)} %bitcast.41), calls=%async_computation.9 | async-start | bytes 1572864 | tf_op jit(solution)/shard_map/all_to_all | solution.py:330
  248.2 11.7 %all-to-all-done.9 = bf16[16,8,3072]{2,1,0:T(8,128)(2,1)S(1)} async-done(((bf16[16,8,3072]{2,1,0:T(8,128)(2,1)}), bf16[16,8,3072]{2,1,0:T(8,128)(2,1)S(1)}, u32[]{:S(2)}, u32[]{:S(2)}) %all-to-all-start.9) | async-done | bytes 786464 | tf_op jit(solution)/shard_map/all_to_all | solution.py:330
  260.6 2.2 collective-permute-start.13
  262.8 0.8 collective-permute-start.14
  263.6 1.7 collective-permute-done.12
  265.3 0.6 collective-permute-done.14
  266.1 18.6 %all_to_all.115 = bf16[16,2,3072]{2,1,0:T(2,128)(2,1)S(1)} all-to-all(bf16[16,2,3072]{2,1,0:T(2,128)(2,1)S(1)} %bitcast.119), channel_id=1, replica_groups=mesh['x'=4,'y'=4,'z'=8,'c'=2] {'z','c'}, dimensions={0} | all-to-all | bytes 393216 | tf_op jit(solution)/shard_map/all_to_all | solution.py:330
  284.8 0.8 broadcast_in_dim.3
  (69 shorter events, 5.8 us)
Async XLA Ops:
  6.5 33.3 %copy-start.1 = (f32[1,3,3072]{2,0,1:T(1,128)S(1)}, f32[1,3,3072]{2,0,1:T(1,128)}, u32[]{:S(2)}) copy-start(f32[1,3,3072]{2,0,1:T(1,128)} %param.6) | copy-start | bytes 110596
  6.5 36.7 %copy-start = (bf16[32,1,3072]{2,0,1:T(8,128)(2,1)S(1)}, bf16[32,1,3072]{2,0,1:T(8,128)(2,1)}, u32[]{:S(2)}) copy-start(bf16[32,1,3072]{2,0,1:T(8,128)(2,1)} %param.5) | copy-start | bytes 589828
  6.5 82.1 %all-gather.5.cloned.1.call-start = ((), (), s32[]{:S(2)}) async-start(), calls=%async_computation.11 | async-start | bytes 6684672 | tf_op jit(solution)/shard_map/all_gather | solution.py:357
  40.2 6.6 %collective-permute-start.1 = (f32[3,3072]{1,0:T(4,128)S(1)}, f32[3,3072]{1,0:T(4,128)S(1)}, u32[]{:S(2)}, u32[]{:S(2)}) collective-permute-start(f32[3,3072]{1,0:T(4,128)S(1)} %reshape.75), channel_id=1, source_target_pairs={{0,64},{64,128},{128,192},{192,0},{1,65},{65,129},{129,193},{193,1... | collective-permute-start | bytes 110600 | tf_op jit(solution)/shard_map/ppermute | solution.py:365
  40.3 6.5 %collective-permute-start.2 = (f32[3,3072]{1,0:T(4,128)S(1)}, f32[3,3072]{1,0:T(4,128)S(1)}, u32[]{:S(2)}, u32[]{:S(2)}) collective-permute-start(f32[3,3072]{1,0:T(4,128)S(1)} %reshape.75), channel_id=1, source_target_pairs={{0,128},{64,192},{128,0},{192,64},{1,129},{65,193},{129,1},{193,65... | collective-permute-start | bytes 110600 | tf_op jit(solution)/shard_map/ppermute | solution.py:365
  42.5 4.3 %collective-permute-start.3 = (f32[3,3072]{1,0:T(4,128)S(1)}, f32[3,3072]{1,0:T(4,128)S(1)}, u32[]{:S(2)}, u32[]{:S(2)}) collective-permute-start(f32[3,3072]{1,0:T(4,128)S(1)} %reshape.75), channel_id=1, source_target_pairs={{0,192},{64,0},{128,64},{192,128},{1,193},{65,1},{129,65},{193,129... | collective-permute-start | bytes 110600 | tf_op jit(solution)/shard_map/ppermute | solution.py:365
  43.6 3.9 %collective-permute-start = (bf16[8,3072]{1,0:T(8,128)(2,1)S(1)}, bf16[8,3072]{1,0:T(8,128)(2,1)S(1)}, u32[]{:S(2)}, u32[]{:S(2)}) collective-permute-start(bf16[8,3072]{1,0:T(8,128)(2,1)S(1)} %bitcast.133), channel_id=1, source_target_pairs={{0,1},{1,0},{2,3},{3,2},{4,5},{5,4},{6,7},{7,6},{8,9},{9,8},{10,11... | collective-permute-start | bytes 147464 | tf_op jit(solution)/shard_map/ppermute | solution.py:378
  49.4 15.8 %all-to-all-start = ((bf16[8,2,1536]{2,1,0:T(2,128)(2,1)}), bf16[8,2,1536]{2,1,0:T(2,128)(2,1)S(1)}, u32[]{:S(2)}, u32[]{:S(2)}) async-start(bf16[8,2,1536]{2,1,0:T(2,128)(2,1)} %reshape.84), calls=%async_computation | async-start | bytes 98304 | tf_op jit(solution)/shard_map/all_to_all | solution.py:330
  57.5 77.6 %all-gather.7.cloned.1.call-start = ((), (), s32[]{:S(2)}) async-start(), calls=%async_computation.12 | async-start | bytes 6684672 | tf_op jit(solution)/shard_map/all_gather | solution.py:357
  69.3 112.4 %all-gather.9.cloned.1.call-start = ((), (), s32[]{:S(2)}) async-start(), calls=%async_computation.13 | async-start | bytes 6684672 | tf_op jit(solution)/shard_map/all_gather | solution.py:357
  70.1 158.0 %all-gather.11.cloned.1.call-start = ((), (), s32[]{:S(2)}) async-start(), calls=%async_computation.14 | async-start | bytes 6684672 | tf_op jit(solution)/shard_map/all_gather | solution.py:357
  70.6 14.8 %all-to-all-start.1 = ((bf16[16,8,3072]{2,1,0:T(8,128)(2,1)}), bf16[16,8,3072]{2,1,0:T(8,128)(2,1)S(1)}, u32[]{:S(2)}, u32[]{:S(2)}) async-start(bf16[16,8,3072]{2,1,0:T(8,128)(2,1)} %bitcast.10), calls=%async_computation.1 | async-start | bytes 1572864 | tf_op jit(solution)/shard_map/all_to_all | solution.py:330
  91.0 3.9 %collective-permute-start.4 = (bf16[192,128]{1,0:T(8,128)(2,1)S(1)}, bf16[192,128]{1,0:T(8,128)(2,1)S(1)}, u32[]{:S(2)}, u32[]{:S(2)}) collective-permute-start(bf16[192,128]{1,0:T(8,128)(2,1)S(1)} %get-tuple-element.56), channel_id=1, source_target_pairs={{0,16},{16,0},{32,48},{48,32},{1,17},{17,1},{33,49},{49,33},{2,18}... | collective-permute-start | bytes 147464 | tf_op jit(solution)/shard_map/ppermute | solution.py:428
  96.2 3.2 %collective-permute-start.5 = (f32[128,128]{1,0:T(8,128)S(1)}, f32[128,128]{1,0:T(8,128)S(1)}, u32[]{:S(2)}, u32[]{:S(2)}) collective-permute-start(f32[128,128]{1,0:T(8,128)S(1)} %get-tuple-element.61), channel_id=1, source_target_pairs={{0,16},{16,0},{32,48},{48,32},{1,17},{17,1},{33,49},{49,33},{2,18}... | collective-permute-start | bytes 196616 | tf_op jit(solution)/shard_map/ppermute | solution.py:428
  119.2 16.0 %all-to-all-start.4 = ((bf16[16,8,3072]{2,1,0:T(8,128)(2,1)}), bf16[16,8,3072]{2,1,0:T(8,128)(2,1)S(1)}, u32[]{:S(2)}, u32[]{:S(2)}) async-start(bf16[16,8,3072]{2,1,0:T(8,128)(2,1)} %bitcast.22), calls=%async_computation.4 | async-start | bytes 1572864 | tf_op jit(solution)/shard_map/all_to_all | solution.py:330
  137.5 3.9 %collective-permute-start.6 = (bf16[192,128]{1,0:T(8,128)(2,1)S(1)}, bf16[192,128]{1,0:T(8,128)(2,1)S(1)}, u32[]{:S(2)}, u32[]{:S(2)}) collective-permute-start(bf16[192,128]{1,0:T(8,128)(2,1)S(1)} %get-tuple-element.69), channel_id=1, source_target_pairs={{0,16},{16,0},{32,48},{48,32},{1,17},{17,1},{33,49},{49,33},{2,18}... | collective-permute-start | bytes 147464 | tf_op jit(solution)/shard_map/ppermute | solution.py:428
  142.7 3.2 %collective-permute-start.7 = (f32[128,128]{1,0:T(8,128)S(1)}, f32[128,128]{1,0:T(8,128)S(1)}, u32[]{:S(2)}, u32[]{:S(2)}) collective-permute-start(f32[128,128]{1,0:T(8,128)S(1)} %get-tuple-element.74), channel_id=1, source_target_pairs={{0,16},{16,0},{32,48},{48,32},{1,17},{17,1},{33,49},{49,33},{2,18}... | collective-permute-start | bytes 196616 | tf_op jit(solution)/shard_map/ppermute | solution.py:428
  165.7 16.0 %all-to-all-start.6 = ((bf16[16,8,3072]{2,1,0:T(8,128)(2,1)}), bf16[16,8,3072]{2,1,0:T(8,128)(2,1)S(1)}, u32[]{:S(2)}, u32[]{:S(2)}) async-start(bf16[16,8,3072]{2,1,0:T(8,128)(2,1)} %bitcast.31), calls=%async_computation.6 | async-start | bytes 1572864 | tf_op jit(solution)/shard_map/all_to_all | solution.py:330
  184.1 3.9 %collective-permute-start.8 = (bf16[192,128]{1,0:T(8,128)(2,1)S(1)}, bf16[192,128]{1,0:T(8,128)(2,1)S(1)}, u32[]{:S(2)}, u32[]{:S(2)}) collective-permute-start(bf16[192,128]{1,0:T(8,128)(2,1)S(1)} %get-tuple-element.82), channel_id=1, source_target_pairs={{0,16},{16,0},{32,48},{48,32},{1,17},{17,1},{33,49},{49,33},{2,18}... | collective-permute-start | bytes 147464 | tf_op jit(solution)/shard_map/ppermute | solution.py:428
  189.3 3.2 %collective-permute-start.9 = (f32[128,128]{1,0:T(8,128)S(1)}, f32[128,128]{1,0:T(8,128)S(1)}, u32[]{:S(2)}, u32[]{:S(2)}) collective-permute-start(f32[128,128]{1,0:T(8,128)S(1)} %get-tuple-element.87), channel_id=1, source_target_pairs={{0,16},{16,0},{32,48},{48,32},{1,17},{17,1},{33,49},{49,33},{2,18}... | collective-permute-start | bytes 196616 | tf_op jit(solution)/shard_map/ppermute | solution.py:428
  212.3 15.8 %all-to-all-start.8 = ((bf16[16,8,3072]{2,1,0:T(8,128)(2,1)}), bf16[16,8,3072]{2,1,0:T(8,128)(2,1)S(1)}, u32[]{:S(2)}, u32[]{:S(2)}) async-start(bf16[16,8,3072]{2,1,0:T(8,128)(2,1)} %bitcast.39), calls=%async_computation.8 | async-start | bytes 1572864 | tf_op jit(solution)/shard_map/all_to_all | solution.py:330
  230.5 3.9 %collective-permute-start.10 = (bf16[192,128]{1,0:T(8,128)(2,1)S(1)}, bf16[192,128]{1,0:T(8,128)(2,1)S(1)}, u32[]{:S(2)}, u32[]{:S(2)}) collective-permute-start(bf16[192,128]{1,0:T(8,128)(2,1)S(1)} %get-tuple-element.95), channel_id=1, source_target_pairs={{0,16},{16,0},{32,48},{48,32},{1,17},{17,1},{33,49},{49,33},{2,18}... | collective-permute-start | bytes 147464 | tf_op jit(solution)/shard_map/ppermute | solution.py:428
  235.7 3.7 %collective-permute-start.11 = (f32[128,128]{1,0:T(8,128)S(1)}, f32[128,128]{1,0:T(8,128)S(1)}, u32[]{:S(2)}, u32[]{:S(2)}) collective-permute-start(f32[128,128]{1,0:T(8,128)S(1)} %get-tuple-element.100), channel_id=1, source_target_pairs={{0,16},{16,0},{32,48},{48,32},{1,17},{17,1},{33,49},{49,33},{2,18}... | collective-permute-start | bytes 196616 | tf_op jit(solution)/shard_map/ppermute | solution.py:428
  240.9 19.0 %all-to-all-start.9 = ((bf16[16,8,3072]{2,1,0:T(8,128)(2,1)}), bf16[16,8,3072]{2,1,0:T(8,128)(2,1)S(1)}, u32[]{:S(2)}, u32[]{:S(2)}) async-start(bf16[16,8,3072]{2,1,0:T(8,128)(2,1)} %bitcast.41), calls=%async_computation.9 | async-start | bytes 1572864 | tf_op jit(solution)/shard_map/all_to_all | solution.py:330
  260.5 4.8 %collective-permute-start.12 = (bf16[8,3072]{1,0:T(8,128)(2,1)S(1)}, bf16[8,3072]{1,0:T(8,128)(2,1)S(1)}, u32[]{:S(2)}, u32[]{:S(2)}) collective-permute-start(bf16[8,3072]{1,0:T(8,128)(2,1)S(1)} %get-tuple-element.110), channel_id=1, source_target_pairs={{0,64},{64,128},{128,192},{192,0},{1,65},{65,129},{129,193},{193,1... | collective-permute-start | bytes 147464 | tf_op jit(solution)/shard_map/ppermute | solution.py:479
  260.6 4.7 %collective-permute-start.13 = (bf16[8,3072]{1,0:T(8,128)(2,1)S(1)}, bf16[8,3072]{1,0:T(8,128)(2,1)S(1)}, u32[]{:S(2)}, u32[]{:S(2)}) collective-permute-start(bf16[8,3072]{1,0:T(8,128)(2,1)S(1)} %get-tuple-element.109), channel_id=1, source_target_pairs={{0,128},{64,192},{128,0},{192,64},{1,129},{65,193},{129,1},{193,65... | collective-permute-start | bytes 147464 | tf_op jit(solution)/shard_map/ppermute | solution.py:479
  262.8 3.1 %collective-permute-start.14 = (bf16[8,3072]{1,0:T(8,128)(2,1)S(1)}, bf16[8,3072]{1,0:T(8,128)(2,1)S(1)}, u32[]{:S(2)}, u32[]{:S(2)}) collective-permute-start(bf16[8,3072]{1,0:T(8,128)(2,1)S(1)} %get-tuple-element.108), channel_id=1, source_target_pairs={{0,192},{64,0},{128,64},{192,128},{1,193},{65,1},{129,65},{193,129... | collective-permute-start | bytes 147464 | tf_op jit(solution)/shard_map/ppermute | solution.py:479
Sparse Core Ops, SparseCore 0:
  39.9 48.6 all-gather.4
  90.4 44.6 all-gather.6
  137.0 44.6 all-gather.8
  183.4 44.6 all-gather.10

commit v13 on v12

--- a/solution.py
+++ b/solution.py
@@ -392,15 +392,6 @@
         compiler_params=PARAMS,
         name="first",
     )(current, term(0, 0), term(0, 1))
-    later = pl.pallas_call(
-        later_kernel,
-        out_shape=[jax.ShapeDtypeStruct((NY, PIECE, HD), jnp.bfloat16)] * (BLOCKS - 1),
-        in_specs=[VMEM, VMEM],
-        out_specs=[VMEM] * (BLOCKS - 1),
-        compiler_params=SMALL,
-        name="later",
-    )(received, normed)
-    pieces += [gather(own_piece) for own_piece in later]
     weight = pltpu.VMEM((SOURCES, ROWS, HD), jnp.bfloat16)
     cache = pltpu.VMEM((SOURCES, PATCHES, HD), jnp.bfloat16)
     half_cache = jax.ShapeDtypeStruct((SOURCES, PATCHES // 2, HD), jnp.bfloat16)
@@ -430,6 +421,16 @@
     outputs = []
     for block in range(BLOCKS):
         rows = exchange(normed, HEAD_AXES)
+        if block == 0:
+            later = pl.pallas_call(
+                later_kernel,
+                out_shape=[jax.ShapeDtypeStruct((NY, PIECE, HD), jnp.bfloat16)] * (BLOCKS - 1),
+                in_specs=[VMEM, VMEM],
+                out_specs=[VMEM] * (BLOCKS - 1),
+                compiler_params=SMALL,
+                name="later",
+            )(received, rows)
+            pieces += [gather(own_piece) for own_piece in later]
         source = pieces[block]
         kept, given = local(
             shared_project_kernel, (SMEM, VMEM, ANY), (VMEM, VMEM),

time: 293 us -> 293 us (level)
  blocking collectives: 101 us -> 116 us
  waiting for transfers between devices: 73.5 us -> 65.5 us
  starting transfers between devices: 46.6 us -> 42.3 us
    all_to_all x5 -> x6, blocking collectives: 101 us -> 116 us  [exchange(): return lax.all_to_all(array, axes, split_axis=0, concat_axis=0, tiled=True)]
    all_to_all x6 -> x5, waiting for transfers between devices: 29.5 us -> 19.1 us  [exchange(): return lax.all_to_all(array, axes, split_axis=0, concat_axis=0, tiled=True)]
    all_to_all x6 -> x5, starting transfers between devices: 30.4 us -> 26.1 us  [exchange(): return lax.all_to_all(array, axes, split_axis=0, concat_axis=0, tiled=True)]
  transfers between devices with their start and end apart: 25 -> 24, of which waited for: 13 -> 12; matrix products, arithmetic and copies ran while one was open for 2% -> 2% of each run, Pallas kernels for 14% -> 13%
where the time goes in v13:
time: 293 us; the launch traced here: 292 us
  blocking collectives  116 us (40%)
  waiting for transfers between devices  65.5 us (22%)
  Pallas kernels  47.8 us (16%)
  starting transfers between devices  42.3 us (14%)
  between operations  13.7 us (5%)
  local copies, waits for them, and re-layouts  5.87 us (2%)
    all_to_all x6, blocking collectives, exchange(): return lax.all_to_all(array, axes, split_axis=0, concat_axis=0, tiled=True)  116 us
    all_gather x4, waiting for transfers between devices, gather(): return lax.all_gather(own_piece, REST_AXES, axis=0, tiled=True)  41.9 us
    all_to_all x5, starting transfers between devices, exchange(): return lax.all_to_all(array, axes, split_axis=0, concat_axis=0, tiled=True)  26.1 us
    all_to_all x5, waiting for transfers between devices, exchange(): return lax.all_to_all(array, axes, split_axis=0, concat_axis=0, tiled=True)  19.1 us
    pallas_call x4, Pallas kernels, body(): local(own_attend_kernel, (SMEM, VMEM, VMEM, ANY), (VMEM, VMEM, VMEM), (ro...  10.6 us
    pallas_call x4, Pallas kernels, body(): local(own_project_kernel, (VMEM, ANY), (VMEM, VMEM, VMEM), (rows_of(3 * L...  10.4 us
    pallas_call x4, Pallas kernels, body(): local(shared_project_kernel, (SMEM, VMEM, ANY), (VMEM, VMEM), (rows_of(LO...  9.58 us
    ppermute x8, starting transfers between devices, swap(): return lax.ppermute(array, 'y', [(at, at ^ 1) for at in range(NY)])  7.01 us
  transfers between devices with their start and end apart: 24, of which 12 were waited for; matrix products, arithmetic and copies ran while one was open for 2% of the time, Pallas kernels for 13%

profile of v13, /device:TPU:1, one launch (start us, length us, event | category | flops | bytes accessed | tf_op | source)
XLA Modules:
  0.0 292.1 jit_solution(996206242791516762)
XLA Ops:
  6.5 3.3 %pack.1 = bf16[16,384,128]{2,1,0:T(8,128)(2,1)} custom-call(bf16[48,9216]{1,0:T(8,128)(2,1)} %bitcast.117, bf16[48,3072]{1,0:T(8,128)(2,1)} %bitcast.128, bf16[32,2,3072]{2,1,0:T(2,128)(2,1)} %bitcast.127), custom_call_target="tpu_custom_call" | custom-call | tf_op jit(solution)/shard_map/pack/pallas_call | solution.py:338
  9.9 29.1 %all_to_all.111 = bf16[16,384,128]{2,1,0:T(8,128)(2,1)S(1)} all-to-all(bf16[16,384,128]{2,1,0:T(8,128)(2,1)} %pack.1), channel_id=1, replica_groups=mesh['x'=4,'y'=4,'z'=8,'c'=2] {'x','y'}, dimensions={0} | all-to-all | bytes 3145728 | tf_op jit(solution)/shard_map/all_to_all | solution.py:330
  39.0 0.8 slice.101
  40.3 2.2 collective-permute-start.2
  42.6 0.7 collective-permute-start.3
  43.6 3.0 %collective-permute-start = (bf16[8,3072]{1,0:T(8,128)(2,1)S(1)}, bf16[8,3072]{1,0:T(8,128)(2,1)S(1)}, u32[]{:S(2)}, u32[]{:S(2)}) collective-permute-start(bf16[8,3072]{1,0:T(8,128)(2,1)S(1)} %bitcast.135), channel_id=1, source_target_pairs={{0,1},{1,0},{2,3},{3,2},{4,5},{5,4},{6,7},{7,6},{8,9},{9,8},{10,11... | collective-permute-start | bytes 147464 | tf_op jit(solution)/shard_map/ppermute | solution.py:378
  46.9 0.6 collective-permute-done
  47.5 0.5 broadcast.12
  48.1 0.7 reduce.2
  48.7 0.6 reshape.84
  49.4 8.2 %all-to-all-start = ((bf16[8,2,1536]{2,1,0:T(2,128)(2,1)}), bf16[8,2,1536]{2,1,0:T(2,128)(2,1)S(1)}, u32[]{:S(2)}, u32[]{:S(2)}) async-start(bf16[8,2,1536]{2,1,0:T(2,128)(2,1)} %reshape.84), calls=%async_computation | async-start | bytes 98304 | tf_op jit(solution)/shard_map/all_to_all | solution.py:330
  57.7 7.4 %all-to-all-done = bf16[8,2,1536]{2,1,0:T(2,128)(2,1)S(1)} async-done(((bf16[8,2,1536]{2,1,0:T(2,128)(2,1)}), bf16[8,2,1536]{2,1,0:T(2,128)(2,1)S(1)}, u32[]{:S(2)}, u32[]{:S(2)}) %all-to-all-start) | async-done | bytes 49184 | tf_op jit(solution)/shard_map/all_to_all | solution.py:330
  66.2 14.3 %all_to_all.112 = bf16[16,8,3072]{2,1,0:T(8,128)(2,1)S(1)} all-to-all(bf16[16,8,3072]{2,1,0:T(8,128)(2,1)S(1)} %bitcast.116), channel_id=1, replica_groups=mesh['x'=4,'y'=4,'z'=8,'c'=2] {'x','y'}, dimensions={0} | all-to-all | bytes 1572864 | tf_op jit(solution)/shard_map/all_to_all | solution.py:330
  80.5 1.1 later.1
  81.7 0.7 all-gather.9.cloned.1.call-update
  82.5 0.5 all-gather.11.cloned.1.call-update
  83.1 5.5 %all-gather.5.cloned.1.call-done.pieces_ref = bf16[64,384,128]{2,1,0:T(8,128)(2,1)} async-done(((bf16[4,384,128]{2,1,0:T(8,128)(2,1)}), bf16[64,384,128]{2,1,0:T(8,128)(2,1)}) %all-gather.5.cloned.1.call-update) | async-done | bytes 6291472 | tf_op jit(solution)/shard_map/all_gather | solution.py:357
  88.6 2.4 shared_project_kernel.4
  91.0 1.3 collective-permute-start.4
  92.3 2.6 own_project_kernel.4
  94.9 1.3 shared_attend_kernel.4
  96.2 0.4 collective-permute-start.5
  96.6 2.7 own_attend_kernel.4
  99.4 0.6 finish_kernel.4
  100.0 17.8 %all_to_all.113 = bf16[16,8,3072]{2,1,0:T(8,128)(2,1)S(1)} all-to-all(bf16[16,8,3072]{2,1,0:T(8,128)(2,1)S(1)} %bitcast.109), channel_id=1, replica_groups=mesh['x'=4,'y'=4,'z'=8,'c'=2] {'x','y'}, dimensions={0} | all-to-all | bytes 1572864 | tf_op jit(solution)/shard_map/all_to_all | solution.py:330
  117.9 1.3 middle.3
  119.2 3.8 %all-to-all-start.4 = ((bf16[16,8,3072]{2,1,0:T(8,128)(2,1)}), bf16[16,8,3072]{2,1,0:T(8,128)(2,1)S(1)}, u32[]{:S(2)}, u32[]{:S(2)}) async-start(bf16[16,8,3072]{2,1,0:T(8,128)(2,1)} %bitcast.22), calls=%async_computation.4 | async-start | bytes 1572864 | tf_op jit(solution)/shard_map/all_to_all | solution.py:330
  123.0 12.1 %all-gather.7.cloned.1.call-done.pieces_ref = bf16[64,384,128]{2,1,0:T(8,128)(2,1)} async-done(((bf16[4,384,128]{2,1,0:T(8,128)(2,1)}), bf16[64,384,128]{2,1,0:T(8,128)(2,1)}) %all-gather.7.cloned.1.call-update) | async-done | bytes 6291472 | tf_op jit(solution)/shard_map/all_gather | solution.py:357
  135.2 2.4 shared_project_kernel.5
  137.6 1.3 collective-permute-start.6
  138.8 2.6 own_project_kernel.5
  141.5 1.3 shared_attend_kernel.5
  142.7 0.4 collective-permute-start.7
  143.1 2.7 own_attend_kernel.5
  145.9 0.6 finish_kernel.5
  146.6 17.9 %all_to_all.114 = bf16[16,8,3072]{2,1,0:T(8,128)(2,1)S(1)} all-to-all(bf16[16,8,3072]{2,1,0:T(8,128)(2,1)S(1)} %bitcast.110), channel_id=1, replica_groups=mesh['x'=4,'y'=4,'z'=8,'c'=2] {'x','y'}, dimensions={0} | all-to-all | bytes 1572864 | tf_op jit(solution)/shard_map/all_to_all | solution.py:330
  164.4 1.3 middle.4
  165.7 3.8 %all-to-all-start.6 = ((bf16[16,8,3072]{2,1,0:T(8,128)(2,1)}), bf16[16,8,3072]{2,1,0:T(8,128)(2,1)S(1)}, u32[]{:S(2)}, u32[]{:S(2)}) async-start(bf16[16,8,3072]{2,1,0:T(8,128)(2,1)} %bitcast.31), calls=%async_computation.6 | async-start | bytes 1572864 | tf_op jit(solution)/shard_map/all_to_all | solution.py:330
  169.5 12.2 %all-gather.9.cloned.1.call-done.pieces_ref = bf16[64,384,128]{2,1,0:T(8,128)(2,1)} async-done(((bf16[4,384,128]{2,1,0:T(8,128)(2,1)}), bf16[64,384,128]{2,1,0:T(8,128)(2,1)}) %all-gather.9.cloned.1.call-update) | async-done | bytes 6291472 | tf_op jit(solution)/shard_map/all_gather | solution.py:357
  181.7 2.4 shared_project_kernel.6
  184.1 1.3 collective-permute-start.8
  185.4 2.6 own_project_kernel.6
  188.1 1.3 shared_attend_kernel.6
  189.7 2.7 own_attend_kernel.6
  192.5 0.6 finish_kernel.6
  193.1 17.8 %all_to_all.115 = bf16[16,8,3072]{2,1,0:T(8,128)(2,1)S(1)} all-to-all(bf16[16,8,3072]{2,1,0:T(8,128)(2,1)S(1)} %bitcast.111), channel_id=1, replica_groups=mesh['x'=4,'y'=4,'z'=8,'c'=2] {'x','y'}, dimensions={0} | all-to-all | bytes 1572864 | tf_op jit(solution)/shard_map/all_to_all | solution.py:330
  211.0 1.3 middle.5
  212.3 3.8 %all-to-all-start.8 = ((bf16[16,8,3072]{2,1,0:T(8,128)(2,1)}), bf16[16,8,3072]{2,1,0:T(8,128)(2,1)S(1)}, u32[]{:S(2)}, u32[]{:S(2)}) async-start(bf16[16,8,3072]{2,1,0:T(8,128)(2,1)} %bitcast.39), calls=%async_computation.8 | async-start | bytes 1572864 | tf_op jit(solution)/shard_map/all_to_all | solution.py:330
  216.1 12.0 %all-gather.11.cloned.1.call-done.pieces_ref = bf16[64,384,128]{2,1,0:T(8,128)(2,1)} async-done(((bf16[4,384,128]{2,1,0:T(8,128)(2,1)}), bf16[64,384,128]{2,1,0:T(8,128)(2,1)}) %all-gather.11.cloned.1.call-update) | async-done | bytes 6291472 | tf_op jit(solution)/shard_map/all_gather | solution.py:357
  228.1 2.4 shared_project_kernel.7
  230.5 1.3 collective-permute-start.10
  231.8 2.6 own_project_kernel.7
  234.4 1.3 shared_attend_kernel.7
  235.7 0.6 collective-permute-start.11
  236.7 2.7 own_attend_kernel.7
  239.4 1.5 finish_kernel.7
  240.9 6.5 %all-to-all-start.9 = ((bf16[16,8,3072]{2,1,0:T(8,128)(2,1)}), bf16[16,8,3072]{2,1,0:T(8,128)(2,1)S(1)}, u32[]{:S(2)}, u32[]{:S(2)}) async-start(bf16[16,8,3072]{2,1,0:T(8,128)(2,1)} %bitcast.41), calls=%async_computation.9 | async-start | bytes 1572864 | tf_op jit(solution)/shard_map/all_to_all | solution.py:330
  248.2 11.7 %all-to-all-done.9 = bf16[16,8,3072]{2,1,0:T(8,128)(2,1)S(1)} async-done(((bf16[16,8,3072]{2,1,0:T(8,128)(2,1)}), bf16[16,8,3072]{2,1,0:T(8,128)(2,1)S(1)}, u32[]{:S(2)}, u32[]{:S(2)}) %all-to-all-start.9) | async-done | bytes 786464 | tf_op jit(solution)/shard_map/all_to_all | solution.py:330
  260.6 2.2 collective-permute-start.13
  262.7 0.8 collective-permute-start.14
  263.6 1.7 collective-permute-done.12
  265.2 0.6 collective-permute-done.14
  266.1 18.6 %all_to_all.116 = bf16[16,2,3072]{2,1,0:T(2,128)(2,1)S(1)} all-to-all(bf16[16,2,3072]{2,1,0:T(2,128)(2,1)S(1)} %bitcast.121), channel_id=1, replica_groups=mesh['x'=4,'y'=4,'z'=8,'c'=2] {'z','c'}, dimensions={0} | all-to-all | bytes 393216 | tf_op jit(solution)/shard_map/all_to_all | solution.py:330
  284.8 0.8 broadcast_in_dim.3
  (68 shorter events, 5.3 us)
Async XLA Ops:
  6.5 33.3 %copy-start.1 = (f32[1,3,3072]{2,0,1:T(1,128)S(1)}, f32[1,3,3072]{2,0,1:T(1,128)}, u32[]{:S(2)}) copy-start(f32[1,3,3072]{2,0,1:T(1,128)} %param.6) | copy-start | bytes 110596
  6.5 36.8 %copy-start = (bf16[32,1,3072]{2,0,1:T(8,128)(2,1)S(1)}, bf16[32,1,3072]{2,0,1:T(8,128)(2,1)}, u32[]{:S(2)}) copy-start(bf16[32,1,3072]{2,0,1:T(8,128)(2,1)} %param.5) | copy-start | bytes 589828
  6.5 82.1 %all-gather.5.cloned.1.call-start = ((), (), s32[]{:S(2)}) async-start(), calls=%async_computation.11 | async-start | bytes 6684672 | tf_op jit(solution)/shard_map/all_gather | solution.py:357
  40.2 6.6 %collective-permute-start.1 = (f32[3,3072]{1,0:T(4,128)S(1)}, f32[3,3072]{1,0:T(4,128)S(1)}, u32[]{:S(2)}, u32[]{:S(2)}) collective-permute-start(f32[3,3072]{1,0:T(4,128)S(1)} %reshape.75), channel_id=1, source_target_pairs={{0,64},{64,128},{128,192},{192,0},{1,65},{65,129},{129,193},{193,1... | collective-permute-start | bytes 110600 | tf_op jit(solution)/shard_map/ppermute | solution.py:365
  40.3 6.5 %collective-permute-start.2 = (f32[3,3072]{1,0:T(4,128)S(1)}, f32[3,3072]{1,0:T(4,128)S(1)}, u32[]{:S(2)}, u32[]{:S(2)}) collective-permute-start(f32[3,3072]{1,0:T(4,128)S(1)} %reshape.75), channel_id=1, source_target_pairs={{0,128},{64,192},{128,0},{192,64},{1,129},{65,193},{129,1},{193,65... | collective-permute-start | bytes 110600 | tf_op jit(solution)/shard_map/ppermute | solution.py:365
  42.6 4.3 %collective-permute-start.3 = (f32[3,3072]{1,0:T(4,128)S(1)}, f32[3,3072]{1,0:T(4,128)S(1)}, u32[]{:S(2)}, u32[]{:S(2)}) collective-permute-start(f32[3,3072]{1,0:T(4,128)S(1)} %reshape.75), channel_id=1, source_target_pairs={{0,192},{64,0},{128,64},{192,128},{1,193},{65,1},{129,65},{193,129... | collective-permute-start | bytes 110600 | tf_op jit(solution)/shard_map/ppermute | solution.py:365
  43.6 3.9 %collective-permute-start = (bf16[8,3072]{1,0:T(8,128)(2,1)S(1)}, bf16[8,3072]{1,0:T(8,128)(2,1)S(1)}, u32[]{:S(2)}, u32[]{:S(2)}) collective-permute-start(bf16[8,3072]{1,0:T(8,128)(2,1)S(1)} %bitcast.135), channel_id=1, source_target_pairs={{0,1},{1,0},{2,3},{3,2},{4,5},{5,4},{6,7},{7,6},{8,9},{9,8},{10,11... | collective-permute-start | bytes 147464 | tf_op jit(solution)/shard_map/ppermute | solution.py:378
  49.4 15.8 %all-to-all-start = ((bf16[8,2,1536]{2,1,0:T(2,128)(2,1)}), bf16[8,2,1536]{2,1,0:T(2,128)(2,1)S(1)}, u32[]{:S(2)}, u32[]{:S(2)}) async-start(bf16[8,2,1536]{2,1,0:T(2,128)(2,1)} %reshape.84), calls=%async_computation | async-start | bytes 98304 | tf_op jit(solution)/shard_map/all_to_all | solution.py:330
  57.6 77.6 %all-gather.7.cloned.1.call-start = ((), (), s32[]{:S(2)}) async-start(), calls=%async_computation.12 | async-start | bytes 6684672 | tf_op jit(solution)/shard_map/all_gather | solution.py:357
  81.7 100.0 %all-gather.9.cloned.1.call-start = ((), (), s32[]{:S(2)}) async-start(), calls=%async_computation.13 | async-start | bytes 6684672 | tf_op jit(solution)/shard_map/all_gather | solution.py:357
  82.4 145.7 %all-gather.11.cloned.1.call-start = ((), (), s32[]{:S(2)}) async-start(), calls=%async_computation.14 | async-start | bytes 6684672 | tf_op jit(solution)/shard_map/all_gather | solution.py:357
  91.0 3.9 %collective-permute-start.4 = (bf16[192,128]{1,0:T(8,128)(2,1)S(1)}, bf16[192,128]{1,0:T(8,128)(2,1)S(1)}, u32[]{:S(2)}, u32[]{:S(2)}) collective-permute-start(bf16[192,128]{1,0:T(8,128)(2,1)S(1)} %get-tuple-element.56), channel_id=1, source_target_pairs={{0,16},{16,0},{32,48},{48,32},{1,17},{17,1},{33,49},{49,33},{2,18}... | collective-permute-start | bytes 147464 | tf_op jit(solution)/shard_map/ppermute | solution.py:419
  96.2 3.2 %collective-permute-start.5 = (f32[128,128]{1,0:T(8,128)S(1)}, f32[128,128]{1,0:T(8,128)S(1)}, u32[]{:S(2)}, u32[]{:S(2)}) collective-permute-start(f32[128,128]{1,0:T(8,128)S(1)} %get-tuple-element.61), channel_id=1, source_target_pairs={{0,16},{16,0},{32,48},{48,32},{1,17},{17,1},{33,49},{49,33},{2,18}... | collective-permute-start | bytes 196616 | tf_op jit(solution)/shard_map/ppermute | solution.py:419
  119.2 16.0 %all-to-all-start.4 = ((bf16[16,8,3072]{2,1,0:T(8,128)(2,1)}), bf16[16,8,3072]{2,1,0:T(8,128)(2,1)S(1)}, u32[]{:S(2)}, u32[]{:S(2)}) async-start(bf16[16,8,3072]{2,1,0:T(8,128)(2,1)} %bitcast.22), calls=%async_computation.4 | async-start | bytes 1572864 | tf_op jit(solution)/shard_map/all_to_all | solution.py:330
  137.6 3.9 %collective-permute-start.6 = (bf16[192,128]{1,0:T(8,128)(2,1)S(1)}, bf16[192,128]{1,0:T(8,128)(2,1)S(1)}, u32[]{:S(2)}, u32[]{:S(2)}) collective-permute-start(bf16[192,128]{1,0:T(8,128)(2,1)S(1)} %get-tuple-element.69), channel_id=1, source_target_pairs={{0,16},{16,0},{32,48},{48,32},{1,17},{17,1},{33,49},{49,33},{2,18}... | collective-permute-start | bytes 147464 | tf_op jit(solution)/shard_map/ppermute | solution.py:419
  142.7 3.2 %collective-permute-start.7 = (f32[128,128]{1,0:T(8,128)S(1)}, f32[128,128]{1,0:T(8,128)S(1)}, u32[]{:S(2)}, u32[]{:S(2)}) collective-permute-start(f32[128,128]{1,0:T(8,128)S(1)} %get-tuple-element.74), channel_id=1, source_target_pairs={{0,16},{16,0},{32,48},{48,32},{1,17},{17,1},{33,49},{49,33},{2,18}... | collective-permute-start | bytes 196616 | tf_op jit(solution)/shard_map/ppermute | solution.py:419
  165.7 16.0 %all-to-all-start.6 = ((bf16[16,8,3072]{2,1,0:T(8,128)(2,1)}), bf16[16,8,3072]{2,1,0:T(8,128)(2,1)S(1)}, u32[]{:S(2)}, u32[]{:S(2)}) async-start(bf16[16,8,3072]{2,1,0:T(8,128)(2,1)} %bitcast.31), calls=%async_computation.6 | async-start | bytes 1572864 | tf_op jit(solution)/shard_map/all_to_all | solution.py:330
  184.1 3.9 %collective-permute-start.8 = (bf16[192,128]{1,0:T(8,128)(2,1)S(1)}, bf16[192,128]{1,0:T(8,128)(2,1)S(1)}, u32[]{:S(2)}, u32[]{:S(2)}) collective-permute-start(bf16[192,128]{1,0:T(8,128)(2,1)S(1)} %get-tuple-element.82), channel_id=1, source_target_pairs={{0,16},{16,0},{32,48},{48,32},{1,17},{17,1},{33,49},{49,33},{2,18}... | collective-permute-start | bytes 147464 | tf_op jit(solution)/shard_map/ppermute | solution.py:419
  189.3 3.2 %collective-permute-start.9 = (f32[128,128]{1,0:T(8,128)S(1)}, f32[128,128]{1,0:T(8,128)S(1)}, u32[]{:S(2)}, u32[]{:S(2)}) collective-permute-start(f32[128,128]{1,0:T(8,128)S(1)} %get-tuple-element.87), channel_id=1, source_target_pairs={{0,16},{16,0},{32,48},{48,32},{1,17},{17,1},{33,49},{49,33},{2,18}... | collective-permute-start | bytes 196616 | tf_op jit(solution)/shard_map/ppermute | solution.py:419
  212.3 15.8 %all-to-all-start.8 = ((bf16[16,8,3072]{2,1,0:T(8,128)(2,1)}), bf16[16,8,3072]{2,1,0:T(8,128)(2,1)S(1)}, u32[]{:S(2)}, u32[]{:S(2)}) async-start(bf16[16,8,3072]{2,1,0:T(8,128)(2,1)} %bitcast.39), calls=%async_computation.8 | async-start | bytes 1572864 | tf_op jit(solution)/shard_map/all_to_all | solution.py:330
  230.5 3.9 %collective-permute-start.10 = (bf16[192,128]{1,0:T(8,128)(2,1)S(1)}, bf16[192,128]{1,0:T(8,128)(2,1)S(1)}, u32[]{:S(2)}, u32[]{:S(2)}) collective-permute-start(bf16[192,128]{1,0:T(8,128)(2,1)S(1)} %get-tuple-element.95), channel_id=1, source_target_pairs={{0,16},{16,0},{32,48},{48,32},{1,17},{17,1},{33,49},{49,33},{2,18}... | collective-permute-start | bytes 147464 | tf_op jit(solution)/shard_map/ppermute | solution.py:419
  235.7 3.7 %collective-permute-start.11 = (f32[128,128]{1,0:T(8,128)S(1)}, f32[128,128]{1,0:T(8,128)S(1)}, u32[]{:S(2)}, u32[]{:S(2)}) collective-permute-start(f32[128,128]{1,0:T(8,128)S(1)} %get-tuple-element.100), channel_id=1, source_target_pairs={{0,16},{16,0},{32,48},{48,32},{1,17},{17,1},{33,49},{49,33},{2,18}... | collective-permute-start | bytes 196616 | tf_op jit(solution)/shard_map/ppermute | solution.py:419
  240.9 19.0 %all-to-all-start.9 = ((bf16[16,8,3072]{2,1,0:T(8,128)(2,1)}), bf16[16,8,3072]{2,1,0:T(8,128)(2,1)S(1)}, u32[]{:S(2)}, u32[]{:S(2)}) async-start(bf16[16,8,3072]{2,1,0:T(8,128)(2,1)} %bitcast.41), calls=%async_computation.9 | async-start | bytes 1572864 | tf_op jit(solution)/shard_map/all_to_all | solution.py:330
  260.5 4.8 %collective-permute-start.12 = (bf16[8,3072]{1,0:T(8,128)(2,1)S(1)}, bf16[8,3072]{1,0:T(8,128)(2,1)S(1)}, u32[]{:S(2)}, u32[]{:S(2)}) collective-permute-start(bf16[8,3072]{1,0:T(8,128)(2,1)S(1)} %get-tuple-element.110), channel_id=1, source_target_pairs={{0,64},{64,128},{128,192},{192,0},{1,65},{65,129},{129,193},{193,1... | collective-permute-start | bytes 147464 | tf_op jit(solution)/shard_map/ppermute | solution.py:480
  260.6 4.7 %collective-permute-start.13 = (bf16[8,3072]{1,0:T(8,128)(2,1)S(1)}, bf16[8,3072]{1,0:T(8,128)(2,1)S(1)}, u32[]{:S(2)}, u32[]{:S(2)}) collective-permute-start(bf16[8,3072]{1,0:T(8,128)(2,1)S(1)} %get-tuple-element.109), channel_id=1, source_target_pairs={{0,128},{64,192},{128,0},{192,64},{1,129},{65,193},{129,1},{193,65... | collective-permute-start | bytes 147464 | tf_op jit(solution)/shard_map/ppermute | solution.py:480
  262.7 3.1 %collective-permute-start.14 = (bf16[8,3072]{1,0:T(8,128)(2,1)S(1)}, bf16[8,3072]{1,0:T(8,128)(2,1)S(1)}, u32[]{:S(2)}, u32[]{:S(2)}) collective-permute-start(bf16[8,3072]{1,0:T(8,128)(2,1)S(1)} %get-tuple-element.108), channel_id=1, source_target_pairs={{0,192},{64,0},{128,64},{192,128},{1,193},{65,1},{129,65},{193,129... | collective-permute-start | bytes 147464 | tf_op jit(solution)/shard_map/ppermute | solution.py:480
Sparse Core Ops, SparseCore 0:
  39.9 48.6 all-gather.4
  90.4 44.6 all-gather.6
  137.0 44.6 all-gather.8
  183.4 44.6 all-gather.10
